TPU v7x, 32 devices: a whole 2x2x4 slice. The times are simulated.
32 devices in a mesh: win: 2 (over x), seq: 8 (over z, y), ch: 2 (over core).
Axes of the slice: x: 2, y: 2, z: 4, core: 2. Of those that a mesh axis runs over, the one named last changes fastest.
Arguments:
- tokens: int32 [8192], P(('win', 'seq')), parts along dimension 0, may hold values from 0 to 3
- hidden: bfloat16 [8192, 1024], P(('win', 'seq')), parts along dimension 0, may hold values from -6 to 6
- embedding: bfloat16 [4, 1024], replicated, may hold values from -3 to 3
- w_gate: bfloat16 [1024, 2048], P(None, 'ch'), may hold values from -0.1875 to 0.1875
- w_inner: bfloat16 [1024, 2048], P(None, 'ch'), may hold values from -0.1875 to 0.1875
- w_state: bfloat16 [1024, 256], replicated, may hold values from -0.1875 to 0.1875
- w_step: bfloat16 [1024, 32], P(None, 'ch'), may hold values from -0.75 to 0.75
- conv_inner: float32 [4, 2048], P(None, 'ch'), may hold values from -3 to 3
- conv_state: float32 [4, 256], replicated, may hold values from -3 to 3
- step_bias: float32 [32], P('ch'), may hold values from -1 to 1
- decay_rate: float32 [32], P('ch'), may hold values from 1.2207031e-05 to 0.05, as said below
- norm_gain: float32 [2048], P('ch'), may hold values from 0.1 to 1.9
- w_output: bfloat16 [2048, 1024], P('ch'), may hold values from -0.125 to 0.125
Outputs:
- mixed: bfloat16 [8192, 1024], P(('win', 'seq'), 'ch'), parts along dimension 0
There are 2 independent parts, one for each index of `win`. A program takes and returns all parts, laid end to end along the dimension named above; an argument that names none is the same for every part. Nothing has to cross between parts.
Inputs may be any that keep to these rules, and one draw needn't show every extreme that they name: `decay_rate`: each head's decay rate per unit step.
All inputs are finite; a program needn't handle non-finite values.
Results may differ from a plain program's by a relative error of at most 0.013.
Values may be sent and summed in bfloat16 or wider, within the bound.
No kernel may reach another device: no remote copies, remote signals or barrier semaphores. Data moves between devices by JAX's collectives and lax.ppermute only.
A program may use at most 128 MiB of HBM per device.

v0:
```python
import functools

import jax
import jax.numpy as jnp
from jax import lax
from jax.experimental import pallas as pl
from jax.experimental.pallas import tpu as pltpu
from jax.sharding import PartitionSpec as P

F32 = jnp.float32
BF16 = jnp.bfloat16
EPS = 1e-05
HALO = 16
EXTRA = 16
CHUNK = 128
TILE = 256
VMEM_LIMIT = 40 * 1024 * 1024


def params(limit=VMEM_LIMIT, dims=("arbitrary",)):
    return pltpu.CompilerParams(vmem_limit_bytes=limit, dimension_semantics=dims)


def dot(a, b):
    return jnp.dot(a, b, preferred_element_type=F32)


def dot_nt(a, b):
    return lax.dot_general(a, b, (((1,), (1,)), ((), ())), preferred_element_type=F32)


def dot_tn(a, b):
    return lax.dot_general(a, b, (((0,), (0,)), ((), ())), preferred_element_type=F32)


def flip_matrix(size):
    rows = lax.broadcasted_iota(jnp.int32, (size, size), 0)
    columns = lax.broadcasted_iota(jnp.int32, (size, size), 1)
    return jnp.where(rows + columns == size - 1, 1.0, 0.0).astype(BF16)


def flip_lanes(value):
    width = value.shape[1]
    anti = flip_matrix(TILE)
    count = width // TILE
    blocks = [
        dot(value[:, (count - 1 - k) * TILE : (count - k) * TILE], anti).astype(BF16)
        for k in range(count)
    ]
    return jnp.concatenate(blocks, axis=1)


def normalise(rows):
    wide = rows.astype(F32)
    return (wide * lax.rsqrt(jnp.mean(wide * wide, axis=-1, keepdims=True) + EPS)).astype(BF16)


def silu(v):
    return v / (1.0 + jnp.exp(-v))


def two_parts(value):
    high = value.astype(BF16)
    low = (value - high.astype(F32)).astype(BF16)
    return jnp.concatenate([high, low], axis=1)


def spread(value, width, head_size, first_head):
    heads = value.shape[1]
    source = lax.broadcasted_iota(jnp.int32, (2 * heads, width), 0)
    source = jnp.where(source >= heads, source - heads, source)
    target = lax.broadcasted_iota(jnp.int32, (2 * heads, width), 1) // head_size + first_head
    onehot = jnp.where(source == target, 1.0, 0.0).astype(BF16)
    return dot(two_parts(value), onehot)


def gate_kernel(merged_ref, wg_ref, nf_ref, nb_ref, gf_ref, gb_ref):
    @pl.when(pl.program_id(0) == 0)
    def _():
        normed = normalise(merged_ref[...])
        nf_ref[...] = normed
        nb_ref[...] = flip_lanes(normed)

    weights = wg_ref[...]
    for rows_ref, out_ref in ((nf_ref, gf_ref), (nb_ref, gb_ref)):
        gate = dot(rows_ref[...], weights).astype(BF16).astype(F32)
        out_ref[...] = silu(gate).astype(BF16)


def gate_call(merged, w_gate):
    rows, width = merged.shape
    inner = w_gate.shape[1]
    whole = pl.BlockSpec((rows, width), lambda g: (0, 0))
    tile = pl.BlockSpec((rows, TILE), lambda g: (0, g))
    return pl.pallas_call(
        gate_kernel,
        grid=(inner // TILE,),
        in_specs=[whole, pl.BlockSpec((width, TILE), lambda g: (0, g))],
        out_specs=[whole, whole, tile, tile],
        out_shape=[jax.ShapeDtypeStruct((rows, width), BF16)] * 2
        + [jax.ShapeDtypeStruct((rows, inner), BF16)] * 2,
        compiler_params=params(),
        name="gate",
    )(merged, w_gate)


def conv_silu(rows_ref, weights, rows, backward):
    taps = weights.shape[0]
    total = None
    for k in range(taps):
        offset = (taps - 1 - k) if backward else HALO - (taps - 1) + k
        term = weights[k : k + 1, :] * rows_ref[offset : offset + rows, :]
        total = term if total is None else total + term
    return silu(total).astype(BF16)


def local_kernel(
    backward,
    head_size,
    normed_ref,
    halo_ref,
    wi_ref,
    ws_ref,
    wt_ref,
    ci_ref,
    cs_ref,
    bias_ref,
    rate_ref,
    xs_ref,
    bc_ref,
    cum_ref,
    cumt_ref,
    state_ref,
    ext_ref,
    rows_ref,
    step_ref,
    bt_ref,
):
    rows = normed_ref.shape[0]
    states = bc_ref.shape[1] // 2
    g = pl.program_id(0)

    @pl.when(g == 0)
    def _():
        halo = normalise(halo_ref[...])
        main = normed_ref[...]
        if backward:
            ext_ref[:rows, :] = main
            ext_ref[rows:, :] = flip_lanes(halo)
        else:
            ext_ref[:HALO, :] = halo
            ext_ref[HALO:, :] = main
        rows_ref[...] = dot(ext_ref[...], ws_ref[...]).astype(BF16).astype(F32)
        state_conv = conv_silu(rows_ref, cs_ref[...], rows, backward)
        bc_ref[...] = state_conv
        bt_ref[...] = state_conv[:, :states].astype(F32).T.astype(BF16)
        raw = dot(main, wt_ref[...]) + bias_ref[...]
        step = jnp.maximum(raw, 0.0) + jnp.log1p(jnp.exp(-jnp.abs(raw)))
        step_ref[...] = step
        logdecay = -step * rate_ref[...]
        high = logdecay.astype(BF16)
        rest = logdecay - high.astype(F32)
        mid = rest.astype(BF16)
        low = (rest - mid.astype(F32)).astype(BF16)
        parts = jnp.concatenate([high, mid, low], axis=1)
        heads = step.shape[1]
        to = lax.broadcasted_iota(jnp.int32, (rows, rows), 0)
        frm = lax.broadcasted_iota(jnp.int32, (rows, rows), 1)
        reach = (to <= frm) if backward else (to >= frm)
        sums = dot(jnp.where(reach, 1.0, 0.0).astype(BF16), parts)
        cum = sums[:, :heads] + sums[:, heads : 2 * heads] + sums[:, 2 * heads :]
        cum_ref[...] = cum
        cumt_ref[...] = cum.T

    projected = dot(ext_ref[...], wi_ref[...]).astype(BF16).astype(F32)
    rows_ref[...] = projected
    x = conv_silu(rows_ref, ci_ref[...], rows, backward).astype(F32)
    first = g * (TILE // head_size)
    xs = x * spread(step_ref[...], TILE, head_size, first)
    xs_ref[...] = xs.astype(BF16)
    cum = cum_ref[...]
    total = cum[:1, :] if backward else cum[rows - 1 :, :]
    left = spread(jnp.exp(total - cum), TILE, head_size, first)
    state_ref[:states, :] = dot(bt_ref[...], (xs * left).astype(BF16)).astype(BF16)
    whole = spread(jnp.broadcast_to(jnp.exp(total), (EXTRA, total.shape[1])), TILE, head_size, first)
    high = whole.astype(BF16).astype(F32)
    place = lax.broadcasted_iota(jnp.int32, whole.shape, 0)
    state_ref[states:, :] = jnp.where(place == 0, high, whole - high).astype(BF16)


def local_call(backward, normed, halo, w_inner, w_state, w_step, ci, cs, bias, rate):
    rows, width = normed.shape
    inner = w_inner.shape[1]
    heads = w_step.shape[1]
    both = w_state.shape[1]
    states = both // 2
    taps = ci.shape[0]

    def whole(*shape):
        return pl.BlockSpec(shape, lambda g: (0, 0))

    def tile(count):
        return pl.BlockSpec((count, TILE), lambda g: (0, g))

    return pl.pallas_call(
        functools.partial(local_kernel, backward, inner // heads),
        grid=(inner // TILE,),
        in_specs=[
            whole(rows, width),
            whole(HALO, width),
            tile(width),
            whole(width, both),
            whole(width, heads),
            tile(taps),
            whole(taps, both),
            whole(1, heads),
            whole(1, heads),
        ],
        out_specs=[
            tile(rows),
            whole(rows, both),
            whole(rows, heads),
            whole(heads, rows),
            tile(states + EXTRA),
        ],
        out_shape=[
            jax.ShapeDtypeStruct((rows, inner), BF16),
            jax.ShapeDtypeStruct((rows, both), BF16),
            jax.ShapeDtypeStruct((rows, heads), F32),
            jax.ShapeDtypeStruct((heads, rows), F32),
            jax.ShapeDtypeStruct((states + EXTRA, inner), BF16),
        ],
        scratch_shapes=[
            pltpu.VMEM((rows + HALO, width), BF16),
            pltpu.VMEM((rows + HALO, TILE), F32),
            pltpu.VMEM((rows, heads), F32),
            pltpu.VMEM((states, rows), BF16),
        ],
        compiler_params=params(),
        name="local_b" if backward else "local_f",
    )(normed, halo, w_inner, w_state, w_step, ci, cs, bias, rate)


def inside_kernel(backward, head_size, xs_ref, bc_ref, cum_ref, cumt_ref, y_ref, state_ref, prev_ref):
    length, inner = xs_ref.shape
    states = bc_ref.shape[1] // 2
    heads = cum_ref.shape[1]

    @pl.when(pl.program_id(0) == 0)
    def _():
        state_ref[...] = jnp.zeros_like(state_ref)
        prev_ref[...] = jnp.zeros_like(prev_ref)

    bmat = bc_ref[:, :states]
    cmat = bc_ref[:, states:]
    to = lax.broadcasted_iota(jnp.int32, (length, length), 0)
    frm = lax.broadcasted_iota(jnp.int32, (length, length), 1)
    reach = (to <= frm) if backward else (to >= frm)
    scores = jnp.where(reach, dot_nt(cmat, bmat), 0.0)
    cum = cum_ref[...]
    cumt = cumt_ref[...]
    last = 0 if backward else length - 1
    end = cum[last : last + 1, :]
    since = spread(jnp.exp(cum - prev_ref[...]), inner, head_size, 0)
    left = spread(jnp.exp(end - cum), inner, head_size, 0)
    state = state_ref[...]
    carried = dot(cmat, state.astype(BF16)) * since
    xs = xs_ref[...]
    scaled = (xs.astype(F32) * left).astype(BF16)
    state_ref[...] = state * since[last : last + 1, :] + dot_tn(bmat, scaled)
    prev_ref[...] = end
    pair = 2 * head_size
    lane = lax.broadcasted_iota(jnp.int32, (length, pair), 1)
    for p in range(heads // 2):
        weights = []
        for h in (2 * p, 2 * p + 1):
            apart = jnp.minimum(cum[:, h : h + 1] - cumt[h : h + 1, :], 0.0)
            weights.append((jnp.exp(apart) * scores).astype(BF16))
        mine = xs[:, p * pair : (p + 1) * pair]
        none = jnp.zeros_like(mine)
        stacked = jnp.concatenate(
            [jnp.where(lane < head_size, mine, none), jnp.where(lane < head_size, none, mine)], axis=0
        )
        inside = dot(jnp.concatenate(weights, axis=1), stacked)
        y_ref[:, p * pair : (p + 1) * pair] = (
            inside + carried[:, p * pair : (p + 1) * pair]
        ).astype(BF16)


def inside_call(backward, xs, bc, cum, cumt):
    rows, inner = xs.shape
    heads = cum.shape[1]
    both = bc.shape[1]
    count = rows // CHUNK
    at = (lambda c: count - 1 - c) if backward else (lambda c: c)

    def block(width):
        return pl.BlockSpec((CHUNK, width), lambda c: (at(c), 0))

    return pl.pallas_call(
        functools.partial(inside_kernel, backward, inner // heads),
        grid=(count,),
        in_specs=[
            block(inner),
            block(both),
            block(heads),
            pl.BlockSpec((heads, CHUNK), lambda c: (0, at(c))),
        ],
        out_specs=block(inner),
        out_shape=jax.ShapeDtypeStruct((rows, inner), BF16),
        scratch_shapes=[pltpu.VMEM((both // 2, inner), F32), pltpu.VMEM((1, heads), F32)],
        compiler_params=params(),
        name="inside_b" if backward else "inside_f",
    )(xs, bc, cum, cumt)


def parts_of(payload):
    states = payload.shape[0] - EXTRA
    wide = payload.astype(F32)
    return wide[:states], wide[states : states + 1] + wide[states + 1 : states + 2]


def write_payload(out_ref, state, decay):
    states = state.shape[0]
    out_ref[:states, :] = state.astype(BF16)
    decay = jnp.broadcast_to(decay, (EXTRA, decay.shape[1]))
    high = decay.astype(BF16).astype(F32)
    place = lax.broadcasted_iota(jnp.int32, decay.shape, 0)
    out_ref[states:, :] = jnp.where(place == 0, high, decay - high).astype(BF16)


def pair_kernel(first_ref, mine_ref, other_ref, out_ref):
    mine, mine_a = parts_of(mine_ref[...])
    other, other_a = parts_of(other_ref[...])
    is_first = first_ref[0] == 1
    early = jnp.where(is_first, mine, other)
    late = jnp.where(is_first, other, mine)
    late_a = jnp.where(is_first, other_a, mine_a)
    write_payload(out_ref, late_a * early + late, mine_a * other_a)


def chain_kernel(pair_ref, before_ref, out_ref):
    pair, pair_a = parts_of(pair_ref[...])
    before, before_a = parts_of(before_ref[...])
    write_payload(out_ref, pair_a * before + pair, pair_a * before_a)


def longer_kernel(before_ref, farther_ref, out_ref):
    before, before_a = parts_of(before_ref[...])
    farther, farther_a = parts_of(farther_ref[...])
    write_payload(out_ref, before + before_a * farther, before_a * farther_a)


def entry_kernel(first_ref, mine_ref, other_ref, before_ref, farther_ref, keep_ref, send_ref):
    mine, mine_a = parts_of(mine_ref[...])
    other, other_a = parts_of(other_ref[...])
    before, before_a = parts_of(before_ref[...])
    farther, _ = parts_of(farther_ref[...])
    is_first = first_ref[0] == 1
    entry_first = before + before_a * farther
    early = jnp.where(is_first, mine, other)
    early_a = jnp.where(is_first, mine_a, other_a)
    entry_second = early_a * entry_first + early
    keep_ref[...] = jnp.where(is_first, entry_first, entry_second).astype(BF16)
    send_ref[...] = jnp.where(is_first, entry_second, entry_first).astype(BF16)


def small_call(kernel, name, flags, arrays, shapes):
    vmem = pl.BlockSpec(memory_space=pltpu.VMEM)
    smem = pl.BlockSpec(memory_space=pltpu.SMEM)
    return pl.pallas_call(
        kernel,
        in_specs=[smem] * len(flags) + [vmem] * len(arrays),
        out_specs=[vmem] * len(shapes),
        out_shape=[jax.ShapeDtypeStruct(s, BF16) for s in shapes],
        compiler_params=pltpu.CompilerParams(vmem_limit_bytes=16 * 1024 * 1024),
        name=name,
    )(*flags, *arrays)


def entering(backward, state):
    tag = "_b" if backward else "_f"
    count = lax.axis_size("seq")
    place = lax.axis_index("seq")
    parity = place % 2
    first = (parity if backward else 1 - parity).astype(jnp.int32).reshape(1)
    height, inner = state.shape
    half = inner // 2
    swap = [(i, i ^ 1) for i in range(count)]
    send = lax.dynamic_slice_in_dim(state, (1 - parity) * half, half, 1)
    mine = lax.dynamic_slice_in_dim(state, parity * half, half, 1)
    other = lax.ppermute(send, "seq", swap)
    shape = (height, half)
    (pair,) = small_call(pair_kernel, "pair" + tag, [first], [mine, other], [shape])
    before = None
    running = pair
    apart = 2
    while apart < count:
        by = -apart if backward else apart
        hops = [(i, i + by) for i in range(count) if 0 <= i + by < count]
        arrived = lax.ppermute(running, "seq", hops)
        last = apart * 2 >= count
        if before is None and last:
            farther = jnp.zeros(shape, BF16)
            before = arrived
        elif last:
            farther = arrived
        else:
            if before is None:
                before = arrived
            else:
                (before,) = small_call(longer_kernel, "longer" + tag, [], [before, arrived], [shape])
            (running,) = small_call(chain_kernel, "chain" + tag, [], [pair, before], [shape])
        apart *= 2
    entry = (height - EXTRA, half)
    keep, out = small_call(
        entry_kernel, "entry" + tag, [first], [mine, other, before, farther], [entry, entry]
    )
    return keep, lax.ppermute(out, "seq", swap)


def finish_kernel(
    head_size, place_ref, y_ref, bc_ref, cum_ref, keep_ref, other_ref, gate_ref, gain_ref, wo_ref, own_ref, send_ref, sq_ref
):
    rows, inner = y_ref.shape
    states = bc_ref.shape[1] // 2
    cmat = bc_ref[:, states:]
    swap = place_ref[0] == 1
    keep = keep_ref[...]
    other = other_ref[...]
    entry = jnp.concatenate([jnp.where(swap, other, keep), jnp.where(swap, keep, other)], axis=1)
    carried = dot(cmat, entry) * spread(jnp.exp(cum_ref[...]), inner, head_size, 0)
    gated = (y_ref[...].astype(F32) + carried) * gate_ref[...].astype(F32)
    squares = jnp.sum(gated * gated, axis=-1, keepdims=True)
    scaled = (gated * gain_ref[...]).astype(BF16)
    half = own_ref.shape[1]
    spare = sq_ref.shape[1]
    squares = jnp.broadcast_to(squares, (rows, spare))
    sq_ref[...] = squares
    high = squares.astype(BF16).astype(F32)
    lane = lax.broadcasted_iota(jnp.int32, squares.shape, 1)
    send_ref[:, half:] = jnp.where(lane == 0, high, squares - high).astype(BF16)
    result = dot(scaled, wo_ref[...])
    low, up = result[:, :half], result[:, half:]
    second = place_ref[1] == 1
    own_ref[...] = jnp.where(second, up, low)
    send_ref[:, :half] = jnp.where(second, low, up).astype(BF16)


def finish_call(name, place, y, bc, cum, keep, other, gate, gain, w_output):
    rows, inner = y.shape
    width = w_output.shape[1]
    half = width // 2
    heads = cum.shape[1]
    block_rows = TILE

    def block(columns):
        return pl.BlockSpec((block_rows, columns), lambda r: (r, 0))

    def whole(a):
        return pl.BlockSpec(a.shape, lambda r: (0, 0))

    return pl.pallas_call(
        functools.partial(finish_kernel, inner // heads),
        grid=(rows // block_rows,),
        in_specs=[
            pl.BlockSpec(memory_space=pltpu.SMEM),
            block(inner),
            block(bc.shape[1]),
            block(heads),
            whole(keep),
            whole(other),
            block(inner),
            whole(gain),
            whole(w_output),
        ],
        out_specs=[block(half), block(half + 128), block(128)],
        out_shape=[
            jax.ShapeDtypeStruct((rows, half), F32),
            jax.ShapeDtypeStruct((rows, half + 128), BF16),
            jax.ShapeDtypeStruct((rows, 128), F32),
        ],
        compiler_params=params(),
        name=name,
    )(place, y, bc, cum, keep, other, gate, gain, w_output)


def sum_kernel(full_width, of_ref, sf_ref, rf_ref, ob_ref, sb_ref, rb_ref, out_ref):
    half = out_ref.shape[1]
    total = None
    for own_ref, sq_ref, recv_ref in ((of_ref, sf_ref, rf_ref), (ob_ref, sb_ref, rb_ref)):
        theirs = recv_ref[:, half : half + 1].astype(F32) + recv_ref[:, half + 1 : half + 2].astype(F32)
        squares = sq_ref[:, :1] + theirs
        scale = lax.rsqrt(squares / full_width + EPS)
        part = (own_ref[...] + recv_ref[:, :half].astype(F32)) * scale
        total = part if total is None else total + part
    out_ref[...] = total.astype(BF16)


def sum_call(full_width, arrays):
    rows, half = arrays[0].shape
    block_rows = 128
    return pl.pallas_call(
        functools.partial(sum_kernel, full_width),
        grid=(rows // block_rows,),
        in_specs=[pl.BlockSpec((block_rows, a.shape[1]), lambda r: (r, 0)) for a in arrays],
        out_specs=pl.BlockSpec((block_rows, half), lambda r: (r, 0)),
        out_shape=jax.ShapeDtypeStruct((rows, half), BF16),
        compiler_params=params(),
        name="total",
    )(*arrays)


def flip_kernel(w_ref, out_ref):
    out_ref[...] = dot(w_ref[...], flip_matrix(TILE)).astype(BF16)


def flip_call(w):
    rows, width = w.shape
    count = width // TILE
    return pl.pallas_call(
        flip_kernel,
        grid=(count,),
        in_specs=[pl.BlockSpec((rows, TILE), lambda g: (0, count - 1 - g))],
        out_specs=pl.BlockSpec((rows, TILE), lambda g: (0, g)),
        out_shape=jax.ShapeDtypeStruct((rows, width), BF16),
        compiler_params=params(),
        name="flip",
    )(w)


def body(
    tokens,
    hidden,
    embedding,
    w_gate,
    w_inner,
    w_state,
    w_step,
    conv_inner,
    conv_state,
    step_bias,
    decay_rate,
    norm_gain,
    w_output,
):
    rows = hidden.shape[0]
    count = lax.axis_size("seq")
    base = jnp.zeros(hidden.shape, F32)
    for t in range(embedding.shape[0]):
        base = jnp.where((tokens == t)[:, None], embedding[t].astype(F32)[None, :], base)
    merged = (hidden.astype(F32) + base).astype(BF16)
    halo_f = lax.ppermute(merged[rows - HALO :], "seq", [(i, i + 1) for i in range(count - 1)])
    halo_b = lax.ppermute(merged[:HALO], "seq", [(i + 1, i) for i in range(count - 1)])
    normed_f, normed_b, gate_f, gate_b = gate_call(merged, w_gate)
    bias = step_bias.reshape(1, -1)
    rate = decay_rate.reshape(1, -1)
    gain = norm_gain.reshape(1, -1)
    place = jnp.stack([lax.axis_index("seq") % 2, lax.axis_index("ch")]).astype(jnp.int32)
    weights = (w_inner, w_state, w_step, conv_inner, conv_state, bias, rate)
    xs_f, bc_f, cum_f, cumt_f, state_f = local_call(False, normed_f, halo_f, *weights)
    xs_b, bc_b, cum_b, cumt_b, state_b = local_call(True, normed_b, halo_b, *weights)
    keep_f, other_f = entering(False, state_f)
    keep_b, other_b = entering(True, state_b)
    y_f = inside_call(False, xs_f, bc_f, cum_f, cumt_f)
    y_b = inside_call(True, xs_b, bc_b, cum_b, cumt_b)
    w_back = flip_call(w_output)
    swap = [(0, 1), (1, 0)]
    own_f, send_f, sq_f = finish_call("finish_f", place, y_f, bc_f, cum_f, keep_f, other_f, gate_f, gain, w_output)
    recv_f = lax.ppermute(send_f, "ch", swap)
    own_b, send_b, sq_b = finish_call("finish_b", place, y_b, bc_b, cum_b, keep_b, other_b, gate_b, gain, w_back)
    recv_b = lax.ppermute(send_b, "ch", swap)
    full_width = w_inner.shape[1] * lax.axis_size("ch")
    return sum_call(float(full_width), (own_f, sq_f, recv_f, own_b, sq_b, recv_b))


def solution(mesh):
    return jax.shard_map(
        body,
        mesh=mesh,
        in_specs=(
            P(("win", "seq")),
            P(("win", "seq"), None),
            P(),
            P(None, "ch"),
            P(None, "ch"),
            P(),
            P(None, "ch"),
            P(None, "ch"),
            P(),
            P("ch"),
            P("ch"),
            P("ch"),
            P("ch", None),
        ),
        out_specs=P(("win", "seq"), "ch"),
        check_vma=False,
    )
```

profile of v0, /device:TPU:0, one launch (start us, length us, event | category | flops | bytes accessed | tf_op | source)
XLA Modules:
  0.0 85.3 jit_solution(4102715671344251350)
XLA Ops:
  1.6 2.4 %add_convert_fusion.merged_ref = bf16[512,1024]{1,0:T(8,128)(2,1)S(1)} fusion(bf16[512,1024]{1,0:T(8,128)(2,1)} %param.14, f32[1024]{0:T(1024)S(1)} %bitcast.18, f32[1024]{0:T(1024)S(1)} %bitcast.19, f32[1024]{0:T(1024)S(1)} %bitcast.17, f32[1024]{0:T(1024)S(1)} %bitcast.16, pred[512]{0:T(512)(128)(4,1)S(1)} %get-tuple-element.65, ...), kind=kLoop, calls=%fused_computation | loop fusion | flops 3670016 | bytes 2115584 | tf_op jit(solution)/shard_map/convert_element_type | solution.py:552
  4.1 5.0 %collective-permute-start = (bf16[16,1024]{1,0:T(8,128)(2,1)S(1)}, bf16[16,1024]{1,0:T(8,128)(2,1)S(1)}, u32[]{:S(2)}, u32[]{:S(2)}) collective-permute-start(bf16[16,1024]{1,0:T(8,128)(2,1)S(1)} %get-tuple-element.54), channel_id=1, source_target_pairs={{0,2},{2,4},{4,6},{6,8},{8,10},{10,12},{12,14},{1,3},{3,5},{5,7},{... | collective-permute-start | bytes 98312 | tf_op jit(solution)/shard_map/ppermute | solution.py:553
  9.1 1.3 %collective-permute-start.6 = (bf16[16,1024]{1,0:T(8,128)(2,1)S(1)}, bf16[16,1024]{1,0:T(8,128)(2,1)S(1)}, u32[]{:S(2)}, u32[]{:S(2)}) collective-permute-start(bf16[16,1024]{1,0:T(8,128)(2,1)S(1)} %get-tuple-element.53), channel_id=1, source_target_pairs={{2,0},{4,2},{6,4},{8,6},{10,8},{12,10},{14,12},{3,1},{5,3},{7,5},{... | collective-permute-start | bytes 98312 | tf_op jit(solution)/shard_map/ppermute | solution.py:554
  10.4 1.6 %copy-done.2 = bf16[1024,1024]{1,0:T(8,128)(2,1)S(1)} copy-done((bf16[1024,1024]{1,0:T(8,128)(2,1)S(1)}, bf16[1024,1024]{1,0:T(8,128)(2,1)}, u32[]{:S(2)}) %copy-start.2) | copy-done | bytes 2097176
  12.0 4.8 %gate.1 = (bf16[512,1024]{1,0:T(8,128)(2,1)S(1)}, bf16[512,1024]{1,0:T(8,128)(2,1)S(1)}, bf16[512,1024]{1,0:T(8,128)(2,1)S(1)}, bf16[512,1024]{1,0:T(8,128)(2,1)S(1)}) custom-call(bf16[512,1024]{1,0:T(8,128)(2,1)S(1)} %add_convert_fusion.merged_ref, bf16[1024,1024]{1,0:T(8,128)(2,1)S(1)} %copy-done.2), custom_call_target="tpu_custom_call" | custom-call | tf_op jit(solution)/shard_map/gate/pallas_call | solution.py:95
  20.9 1.0 %copy-done.3 = bf16[1024,256]{1,0:T(8,128)(2,1)S(1)} copy-done((bf16[1024,256]{1,0:T(8,128)(2,1)S(1)}, bf16[1024,256]{1,0:T(8,128)(2,1)}, u32[]{:S(2)}) %copy-start.3) | copy-done | bytes 524312
  22.0 1.2 %copy-done.13 = bf16[512,1024]{1,0:T(8,128)(2,1)S(1)} copy-done((bf16[512,1024]{1,0:T(8,128)(2,1)S(1)}, bf16[512,1024]{1,0:T(8,128)(2,1)}, u32[]{:S(2)}) %copy-start.13) | copy-done | bytes 1048600
  23.2 7.3 %local_f.1 = (bf16[512,1024]{1,0:T(8,128)(2,1)S(1)}, bf16[512,256]{1,0:T(8,128)(2,1)S(1)}, f32[512,16]{1,0:T(8,128)S(1)}, f32[16,512]{1,0:T(8,128)S(1)}, bf16[144,1024]{1,0:T(8,128)(2,1)S(1)}) custom-call(bf16[512,1024]{1,0:T(8,128)(2,1)S(1)} %copy-done.13, bf16[16,1024]{1,0:T(8,128)(2,1)S(1)} %collective-permute-done.halo_ref, ...), custom_call_target="tpu_custom_call" | custom-call | tf_op jit(solution)/shard_map/local_f/pallas_call | solution.py:205
  31.2 2.7 %collective-permute-start.1 = (bf16[144,512]{1,0:T(8,128)(2,1)S(1)}, bf16[144,512]{1,0:T(8,128)(2,1)S(1)}, u32[]{:S(2)}, u32[]{:S(2)}) collective-permute-start(bf16[144,512]{1,0:T(8,128)(2,1)S(1)} %get-tuple-element.57), channel_id=1, source_target_pairs={{0,2},{2,0},{4,6},{6,4},{8,10},{10,8},{12,14},{14,12},{1,3},{3,1},... | collective-permute-start | bytes 442376 | tf_op jit(solution)/shard_map/ppermute | solution.py:392
  33.9 7.5 %local_b.1 = (bf16[512,1024]{1,0:T(8,128)(2,1)S(1)}, bf16[512,256]{1,0:T(8,128)(2,1)S(1)}, f32[512,16]{1,0:T(8,128)S(1)}, f32[16,512]{1,0:T(8,128)S(1)}, bf16[144,1024]{1,0:T(8,128)(2,1)S(1)}) custom-call(bf16[512,1024]{1,0:T(8,128)(2,1)S(1)} %copy-done.11, bf16[16,1024]{1,0:T(8,128)(2,1)S(1)} %collective-permute-done.6.halo_ref, ...), custom_call_target="tpu_custom_call" | custom-call | tf_op jit(solution)/shard_map/local_b/pallas_call | solution.py:205
  41.7 4.8 %collective-permute-start.2 = (bf16[144,512]{1,0:T(8,128)(2,1)S(1)}, bf16[144,512]{1,0:T(8,128)(2,1)S(1)}, u32[]{:S(2)}, u32[]{:S(2)}) collective-permute-start(bf16[144,512]{1,0:T(8,128)(2,1)S(1)} %pair_f.1.pair_ref), channel_id=1, source_target_pairs={{0,4},{2,6},{4,8},{6,10},{8,12},{10,14},{1,5},{3,7},{5,9},{7,11},{... | collective-permute-start | bytes 442376 | tf_op jit(solution)/shard_map/ppermute | solution.py:401
  46.8 1.3 %collective-permute-start.8 = (bf16[144,512]{1,0:T(8,128)(2,1)S(1)}, bf16[144,512]{1,0:T(8,128)(2,1)S(1)}, u32[]{:S(2)}, u32[]{:S(2)}) collective-permute-start(bf16[144,512]{1,0:T(8,128)(2,1)S(1)} %pair_b.1.pair_ref), channel_id=1, source_target_pairs={{4,0},{6,2},{8,4},{10,6},{12,8},{14,10},{5,1},{7,3},{9,5},{11,7},{... | collective-permute-start | bytes 442376 | tf_op jit(solution)/shard_map/ppermute | solution.py:401
  48.1 1.1 %collective-permute-done.2.before_ref = bf16[144,512]{1,0:T(8,128)(2,1)S(1)} collective-permute-done((bf16[144,512]{1,0:T(8,128)(2,1)S(1)}, bf16[144,512]{1,0:T(8,128)(2,1)S(1)}, u32[]{:S(2)}, u32[]{:S(2)}) %collective-permute-start.2) | collective-permute-done | bytes 147488 | tf_op jit(solution)/shard_map/ppermute | solution.py:401
  49.3 5.4 %collective-permute-start.3 = (bf16[144,512]{1,0:T(8,128)(2,1)S(1)}, bf16[144,512]{1,0:T(8,128)(2,1)S(1)}, u32[]{:S(2)}, u32[]{:S(2)}) collective-permute-start(bf16[144,512]{1,0:T(8,128)(2,1)S(1)} %chain_f.1), channel_id=1, source_target_pairs={{0,8},{2,10},{4,12},{6,14},{1,9},{3,11},{5,13},{7,15},{16,24},{18,... | collective-permute-start | bytes 442376 | tf_op jit(solution)/shard_map/ppermute | solution.py:401
  54.8 1.5 %collective-permute-start.9 = (bf16[144,512]{1,0:T(8,128)(2,1)S(1)}, bf16[144,512]{1,0:T(8,128)(2,1)S(1)}, u32[]{:S(2)}, u32[]{:S(2)}) collective-permute-start(bf16[144,512]{1,0:T(8,128)(2,1)S(1)} %chain_b.1), channel_id=1, source_target_pairs={{8,0},{10,2},{12,4},{14,6},{9,1},{11,3},{13,5},{15,7},{24,16},{26,... | collective-permute-start | bytes 442376 | tf_op jit(solution)/shard_map/ppermute | solution.py:401
  56.2 1.1 %collective-permute-done.3.farther_ref = bf16[144,512]{1,0:T(8,128)(2,1)S(1)} collective-permute-done((bf16[144,512]{1,0:T(8,128)(2,1)S(1)}, bf16[144,512]{1,0:T(8,128)(2,1)S(1)}, u32[]{:S(2)}, u32[]{:S(2)}) %collective-permute-start.3) | collective-permute-done | bytes 147488 | tf_op jit(solution)/shard_map/ppermute | solution.py:401
  58.8 5.4 %collective-permute-done.9.farther_ref = bf16[144,512]{1,0:T(8,128)(2,1)S(1)} collective-permute-done((bf16[144,512]{1,0:T(8,128)(2,1)S(1)}, bf16[144,512]{1,0:T(8,128)(2,1)S(1)}, u32[]{:S(2)}, u32[]{:S(2)}) %collective-permute-start.9) | collective-permute-done | bytes 147488 | tf_op jit(solution)/shard_map/ppermute | solution.py:401
  65.9 1.8 %flip.1.wo_ref = bf16[1024,1024]{1,0:T(8,128)(2,1)S(1)} custom-call(bf16[1024,1024]{1,0:T(8,128)(2,1)S(1)} %copy-done), custom_call_target="tpu_custom_call" | custom-call | tf_op jit(solution)/shard_map/flip/pallas_call | solution.py:521
  67.8 3.2 %inside_f.1.y_ref = bf16[512,1024]{1,0:T(8,128)(2,1)S(1)} custom-call(bf16[512,1024]{1,0:T(8,128)(2,1)S(1)} %get-tuple-element.30.xs_ref, bf16[512,256]{1,0:T(8,128)(2,1)S(1)} %copy-done.15, f32[512,16]{1,0:T(8,128)S(1)} %copy-done.17, f32[16,512]{1,0:T(8,128)S(1)} %copy-done.26), custom_call_target="tpu_custom_call" | custom-call | tf_op jit(solution)/shard_map/inside_f/pallas_call | solution.py:300
  71.0 3.2 %inside_b.1.y_ref = bf16[512,1024]{1,0:T(8,128)(2,1)S(1)} custom-call(bf16[512,1024]{1,0:T(8,128)(2,1)S(1)} %copy-done.9, bf16[512,256]{1,0:T(8,128)(2,1)S(1)} %copy-done.19, f32[512,16]{1,0:T(8,128)S(1)} %copy-done.21, f32[16,512]{1,0:T(8,128)S(1)} %copy-done.28), custom_call_target="tpu_custom_call" | custom-call | tf_op jit(solution)/shard_map/inside_b/pallas_call | solution.py:300
  74.3 3.4 %finish_f.1 = (f32[512,512]{1,0:T(8,128)S(1)}, bf16[512,640]{1,0:T(8,128)(2,1)S(1)}, f32[512,128]{1,0:T(8,128)S(1)}) custom-call(s32[2]{0:T(128)S(1)} %pad_add_fusion.place_ref, bf16[512,1024]{1,0:T(8,128)(2,1)S(1)} %inside_f.1.y_ref, bf16[512,256]{1,0:T(8,128)(2,1)S(1)} %copy-done.15, f32[512,16]{1,0:T(8,128)S(1)} %copy-done.17, ...), custom_call_target="tpu_custom_call" | custom-call | tf_op jit(solution)/shard_map/finish_f/pallas_call | solution.py:463
  77.8 3.3 %finish_b.1 = (f32[512,512]{1,0:T(8,128)S(1)}, bf16[512,640]{1,0:T(8,128)(2,1)S(1)}, f32[512,128]{1,0:T(8,128)S(1)}) custom-call(s32[2]{0:T(128)S(1)} %pad_add_fusion.place_ref, bf16[512,1024]{1,0:T(8,128)(2,1)S(1)} %inside_b.1.y_ref, bf16[512,256]{1,0:T(8,128)(2,1)S(1)} %copy-done.19, f32[512,16]{1,0:T(8,128)S(1)} %copy-done.21, ...), custom_call_target="tpu_custom_call" | custom-call | tf_op jit(solution)/shard_map/finish_b/pallas_call | solution.py:463
  81.7 1.7 %collective-permute-done.11.rb_ref = bf16[512,640]{1,0:T(8,128)(2,1)S(1)} collective-permute-done((bf16[512,640]{1,0:T(8,128)(2,1)S(1)}, bf16[512,640]{1,0:T(8,128)(2,1)S(1)}, u32[]{:S(2)}, u32[]{:S(2)}) %collective-permute-start.11) | collective-permute-done | bytes 655392 | tf_op jit(solution)/shard_map/ppermute | solution.py:572
  83.4 1.9 %total.1 = bf16[512,512]{1,0:T(8,128)(2,1)} custom-call(f32[512,512]{1,0:T(8,128)S(1)} %get-tuple-element.38.of_ref, f32[512,128]{1,0:T(8,128)S(1)} %get-tuple-element.39.sf_ref, bf16[512,640]{1,0:T(8,128)(2,1)S(1)} %collective-permute-done.5.rf_ref, f32[512,512]{1,0:T(8,128)S(1)} %get-tuple-element.50.ob_ref, f32[512,128]{1,0:T(8,128)S(1)} %get-tuple-element.51.sb_ref, ...), custom_call_target="tpu_custom_call" | custom-call | tf_op jit(solution)/shard_map/total/pallas_call | solution.py:503
  (91 shorter events, 10.7 us)
Async XLA Ops:
  1.6 19.1 %copy-start.33 = (bf16[1024,16]{0,1:T(8,128)(2,1)S(1)}, bf16[1024,16]{0,1:T(8,128)(2,1)}, u32[]{:S(2)}) copy-start(bf16[1024,16]{0,1:T(8,128)(2,1)} %param.19) | copy-start | bytes 98308
  1.6 19.3 %copy-start.24 = (f32[4,1024]{1,0:T(4,128)S(1)}, f32[4,1024]{1,0:T(4,128)}, u32[]{:S(2)}) copy-start(f32[4,1024]{1,0:T(4,128)} %ci_ref.3) | copy-start | bytes 49156
  1.6 19.3 %copy-start.29 = (f32[4,256]{1,0:T(4,128)S(1)}, f32[4,256]{1,0:T(4,128)}, u32[]{:S(2)}) copy-start(f32[4,256]{1,0:T(4,128)} %cs_ref.3) | copy-start | bytes 12292
  1.6 19.3 %copy-start.31 = (f32[16]{0:T(128)S(1)}, f32[16]{0:T(128)}, u32[]{:S(2)}) copy-start(f32[16]{0:T(128)} %param.22) | copy-start | bytes 196
  1.6 19.3 %copy-start.32 = (f32[16]{0:T(128)S(1)}, f32[16]{0:T(128)}, u32[]{:S(2)}) copy-start(f32[16]{0:T(128)} %param.23) | copy-start | bytes 196
  4.0 16.9 %copy-start.1 = (bf16[1024,1024]{1,0:T(8,128)(2,1)S(1)}, bf16[1024,1024]{1,0:T(8,128)(2,1)}, u32[]{:S(2)}) copy-start(bf16[1024,1024]{1,0:T(8,128)(2,1)} %wi_ref.3) | copy-start | bytes 6291460
  4.1 16.8 %collective-permute-start = (bf16[16,1024]{1,0:T(8,128)(2,1)S(1)}, bf16[16,1024]{1,0:T(8,128)(2,1)S(1)}, u32[]{:S(2)}, u32[]{:S(2)}) collective-permute-start(bf16[16,1024]{1,0:T(8,128)(2,1)S(1)} %get-tuple-element.54), channel_id=1, source_target_pairs={{0,2},{2,4},{4,6},{6,8},{8,10},{10,12},{12,14},{1,3},{3,5},{5,7},{... | collective-permute-start | bytes 98312 | tf_op jit(solution)/shard_map/ppermute | solution.py:553
  9.1 24.8 %collective-permute-start.6 = (bf16[16,1024]{1,0:T(8,128)(2,1)S(1)}, bf16[16,1024]{1,0:T(8,128)(2,1)S(1)}, u32[]{:S(2)}, u32[]{:S(2)}) collective-permute-start(bf16[16,1024]{1,0:T(8,128)(2,1)S(1)} %get-tuple-element.53), channel_id=1, source_target_pairs={{2,0},{4,2},{6,4},{8,6},{10,8},{12,10},{14,12},{3,1},{5,3},{7,5},{... | collective-permute-start | bytes 98312 | tf_op jit(solution)/shard_map/ppermute | solution.py:554
  23.2 10.7 %copy-start.11 = (bf16[512,1024]{1,0:T(8,128)(2,1)S(1)}, bf16[512,1024]{1,0:T(8,128)(2,1)}, u32[]{:S(2)}) copy-start(bf16[512,1024]{1,0:T(8,128)(2,1)} %copy-done.10) | copy-start | bytes 3145732
  31.2 10.5 %collective-permute-start.1 = (bf16[144,512]{1,0:T(8,128)(2,1)S(1)}, bf16[144,512]{1,0:T(8,128)(2,1)S(1)}, u32[]{:S(2)}, u32[]{:S(2)}) collective-permute-start(bf16[144,512]{1,0:T(8,128)(2,1)S(1)} %get-tuple-element.57), channel_id=1, source_target_pairs={{0,2},{2,0},{4,6},{6,4},{8,10},{10,8},{12,14},{14,12},{1,3},{3,1},... | collective-permute-start | bytes 442376 | tf_op jit(solution)/shard_map/ppermute | solution.py:392
  41.5 23.6 %copy-start.8 = (bf16[512,1024]{1,0:T(8,128)(2,1)}, bf16[512,1024]{1,0:T(8,128)(2,1)S(1)}, u32[]{:S(2)}) copy-start(bf16[512,1024]{1,0:T(8,128)(2,1)S(1)} %get-tuple-element.42.xs_ref) | copy-start | bytes 3145732
  41.5 23.6 %copy-start.18 = (bf16[512,256]{1,0:T(8,128)(2,1)}, bf16[512,256]{1,0:T(8,128)(2,1)S(1)}, u32[]{:S(2)}) copy-start(bf16[512,256]{1,0:T(8,128)(2,1)S(1)} %get-tuple-element.43.bc_ref) | copy-start | bytes 786436
  41.5 23.6 %copy-start.20 = (f32[512,16]{1,0:T(8,128)}, f32[512,16]{1,0:T(8,128)S(1)}, u32[]{:S(2)}) copy-start(f32[512,16]{1,0:T(8,128)S(1)} %get-tuple-element.44.cum_ref) | copy-start | bytes 98308
  41.5 23.6 %copy-start.27 = (f32[16,512]{1,0:T(8,128)}, f32[16,512]{1,0:T(8,128)S(1)}, u32[]{:S(2)}) copy-start(f32[16,512]{1,0:T(8,128)S(1)} %get-tuple-element.45.cumt_ref) | copy-start | bytes 98308
  41.5 24.4 %copy-start = (bf16[1024,1024]{1,0:T(8,128)(2,1)S(1)}, bf16[1024,1024]{1,0:T(8,128)(2,1)}, u32[]{:S(2)}) copy-start(bf16[1024,1024]{1,0:T(8,128)(2,1)} %w_ref.1) | copy-start | bytes 6291460
  41.5 5.2 %collective-permute-start.7 = (bf16[144,512]{1,0:T(8,128)(2,1)S(1)}, bf16[144,512]{1,0:T(8,128)(2,1)S(1)}, u32[]{:S(2)}, u32[]{:S(2)}) collective-permute-start(bf16[144,512]{1,0:T(8,128)(2,1)S(1)} %get-tuple-element.55), channel_id=1, source_target_pairs={{0,2},{2,0},{4,6},{6,4},{8,10},{10,8},{12,14},{14,12},{1,3},{3,1},... | collective-permute-start | bytes 442376 | tf_op jit(solution)/shard_map/ppermute | solution.py:392
  41.7 7.5 %collective-permute-start.2 = (bf16[144,512]{1,0:T(8,128)(2,1)S(1)}, bf16[144,512]{1,0:T(8,128)(2,1)S(1)}, u32[]{:S(2)}, u32[]{:S(2)}) collective-permute-start(bf16[144,512]{1,0:T(8,128)(2,1)S(1)} %pair_f.1.pair_ref), channel_id=1, source_target_pairs={{0,4},{2,6},{4,8},{6,10},{8,12},{10,14},{1,5},{3,7},{5,9},{7,11},{... | collective-permute-start | bytes 442376 | tf_op jit(solution)/shard_map/ppermute | solution.py:401
  46.8 7.9 %collective-permute-start.8 = (bf16[144,512]{1,0:T(8,128)(2,1)S(1)}, bf16[144,512]{1,0:T(8,128)(2,1)S(1)}, u32[]{:S(2)}, u32[]{:S(2)}) collective-permute-start(bf16[144,512]{1,0:T(8,128)(2,1)S(1)} %pair_b.1.pair_ref), channel_id=1, source_target_pairs={{4,0},{6,2},{8,4},{10,6},{12,8},{14,10},{5,1},{7,3},{9,5},{11,7},{... | collective-permute-start | bytes 442376 | tf_op jit(solution)/shard_map/ppermute | solution.py:401
  49.3 8.1 %collective-permute-start.3 = (bf16[144,512]{1,0:T(8,128)(2,1)S(1)}, bf16[144,512]{1,0:T(8,128)(2,1)S(1)}, u32[]{:S(2)}, u32[]{:S(2)}) collective-permute-start(bf16[144,512]{1,0:T(8,128)(2,1)S(1)} %chain_f.1), channel_id=1, source_target_pairs={{0,8},{2,10},{4,12},{6,14},{1,9},{3,11},{5,13},{7,15},{16,24},{18,... | collective-permute-start | bytes 442376 | tf_op jit(solution)/shard_map/ppermute | solution.py:401
  54.8 9.5 %collective-permute-start.9 = (bf16[144,512]{1,0:T(8,128)(2,1)S(1)}, bf16[144,512]{1,0:T(8,128)(2,1)S(1)}, u32[]{:S(2)}, u32[]{:S(2)}) collective-permute-start(bf16[144,512]{1,0:T(8,128)(2,1)S(1)} %chain_b.1), channel_id=1, source_target_pairs={{8,0},{10,2},{12,4},{14,6},{9,1},{11,3},{13,5},{15,7},{24,16},{26,... | collective-permute-start | bytes 442376 | tf_op jit(solution)/shard_map/ppermute | solution.py:401
  58.1 16.2 %collective-permute-start.4 = (bf16[128,512]{1,0:T(8,128)(2,1)}, bf16[128,512]{1,0:T(8,128)(2,1)}, u32[]{:S(2)}, u32[]{:S(2)}) collective-permute-start(bf16[128,512]{1,0:T(8,128)(2,1)} %get-tuple-element.36), channel_id=1, source_target_pairs={{0,2},{2,0},{4,6},{6,4},{8,10},{10,8},{12,14},{14,12},{1,3},{3,1},... | collective-permute-start | bytes 393224 | tf_op jit(solution)/shard_map/ppermute | solution.py:419
  65.1 12.7 %collective-permute-start.10 = (bf16[128,512]{1,0:T(8,128)(2,1)}, bf16[128,512]{1,0:T(8,128)(2,1)}, u32[]{:S(2)}, u32[]{:S(2)}) collective-permute-start(bf16[128,512]{1,0:T(8,128)(2,1)} %get-tuple-element.48), channel_id=1, source_target_pairs={{0,2},{2,0},{4,6},{6,4},{8,10},{10,8},{12,14},{14,12},{1,3},{3,1},... | collective-permute-start | bytes 393224 | tf_op jit(solution)/shard_map/ppermute | solution.py:419
  77.7 4.0 %collective-permute-start.5 = (bf16[512,640]{1,0:T(8,128)(2,1)S(1)}, bf16[512,640]{1,0:T(8,128)(2,1)S(1)}, u32[]{:S(2)}, u32[]{:S(2)}) collective-permute-start(bf16[512,640]{1,0:T(8,128)(2,1)S(1)} %get-tuple-element.40), channel_id=1, source_target_pairs={{0,1},{1,0},{2,3},{3,2},{4,5},{5,4},{6,7},{7,6},{8,9},{9,8},{10,11... | collective-permute-start | bytes 1966088 | tf_op jit(solution)/shard_map/ppermute | solution.py:570
  81.2 2.2 %collective-permute-start.11 = (bf16[512,640]{1,0:T(8,128)(2,1)S(1)}, bf16[512,640]{1,0:T(8,128)(2,1)S(1)}, u32[]{:S(2)}, u32[]{:S(2)}) collective-permute-start(bf16[512,640]{1,0:T(8,128)(2,1)S(1)} %get-tuple-element.52), channel_id=1, source_target_pairs={{0,1},{1,0},{2,3},{3,2},{4,5},{5,4},{6,7},{7,6},{8,9},{9,8},{10,11... | collective-permute-start | bytes 1966088 | tf_op jit(solution)/shard_map/ppermute | solution.py:572
  (22 other events, 77.9 us)
where the time goes:
time: 85.8 us; the launch traced here: 85.3 us
  Pallas kernels  38.1 us (44%)
  starting transfers between devices  24.3 us (28%)
  waiting for transfers between devices  9.55 us (11%)
  local copies, waits for them, and re-layouts  8.73 us (10%)
  other arithmetic  4.06 us (5%)
    pallas_call x2, Pallas kernels, local_call(): pl.pallas_call(functools.partial(local_kernel, backward, inner // heads),...  14.8 us
    ppermute x4, starting transfers between devices, entering(): arrived = lax.ppermute(running, 'seq', hops)  13 us
    unnamed x69, local copies, waits for them, and re-layouts  8.67 us
    ppermute x4, waiting for transfers between devices, entering(): arrived = lax.ppermute(running, 'seq', hops)  7.65 us
    pallas_call x2, Pallas kernels, finish_call(): pl.pallas_call(functools.partial(finish_kernel, inner // heads), grid=(ro...  6.74 us
    pallas_call x2, Pallas kernels, inside_call(): pl.pallas_call(functools.partial(inside_kernel, backward, inner // heads)...  6.38 us
    ppermute x1, starting transfers between devices, body(): lax.ppermute(merged[rows - HALO:], 'seq', [(i, i + 1) for i in range(coun...  5 us
    pallas_call x1, Pallas kernels, gate_call(): pl.pallas_call(gate_kernel, grid=(inner // TILE,), in_specs=[whole, pl.Bl...  4.76 us
  transfers between devices with their start and end apart: 12, of which 5 were waited for; matrix products, arithmetic and copies ran while one was open for 0% of the time, Pallas kernels for 42%

commit v1 on v0

v1 whole, which is shorter than its diff:
```python
import functools

import jax
import jax.numpy as jnp
from jax import lax
from jax.experimental import pallas as pl
from jax.experimental.pallas import tpu as pltpu
from jax.sharding import PartitionSpec as P

F32 = jnp.float32
BF16 = jnp.bfloat16
EPS = 1e-05
HALO = 16
EXTRA = 16
CHUNK = 128
TILE = 256
MB = 1024 * 1024


def call(kernel, name, *, vmem, cost, scalars=(), grid=(), in_specs, out_specs, out_shape, scratch=()):
    flops, moved, special = cost
    return pl.pallas_call(
        kernel,
        grid_spec=pltpu.PrefetchScalarGridSpec(
            num_scalar_prefetch=len(scalars),
            grid=grid,
            in_specs=in_specs,
            out_specs=out_specs,
            scratch_shapes=scratch,
        ),
        out_shape=out_shape,
        compiler_params=pltpu.CompilerParams(
            vmem_limit_bytes=vmem * MB, dimension_semantics=("arbitrary",) * len(grid)
        ),
        cost_estimate=pl.CostEstimate(flops=flops, bytes_accessed=moved, transcendentals=special),
        name=name,
    )


def micros(us):
    return (int(us * 1.1e9), int(us * 1e6), 0)


def dot(a, b):
    return jnp.dot(a, b, preferred_element_type=F32)


def dot_nt(a, b):
    return lax.dot_general(a, b, (((1,), (1,)), ((), ())), preferred_element_type=F32)


def dot_tn(a, b):
    return lax.dot_general(a, b, (((0,), (0,)), ((), ())), preferred_element_type=F32)


def flip_matrix(size):
    rows = lax.broadcasted_iota(jnp.int32, (size, size), 0)
    columns = lax.broadcasted_iota(jnp.int32, (size, size), 1)
    return jnp.where(rows + columns == size - 1, 1.0, 0.0).astype(BF16)


def flip_both(value):
    rows, width = value.shape
    turned = dot(flip_matrix(rows), value).astype(BF16)
    anti = flip_matrix(TILE)
    count = width // TILE
    blocks = [
        dot(turned[:, (count - 1 - k) * TILE : (count - k) * TILE], anti).astype(BF16)
        for k in range(count)
    ]
    return jnp.concatenate(blocks, axis=1)


def silu(v):
    half = 0.5 * v
    return half + half * jnp.tanh(half)


def two_parts(value):
    high = value.astype(BF16)
    low = (value - high.astype(F32)).astype(BF16)
    return jnp.concatenate([high, low], axis=1)


def spread(value, width, head_size, first_head):
    heads = value.shape[1]
    source = lax.broadcasted_iota(jnp.int32, (2 * heads, width), 0)
    source = jnp.where(source >= heads, source - heads, source)
    target = lax.broadcasted_iota(jnp.int32, (2 * heads, width), 1) // head_size + first_head
    onehot = jnp.where(source == target, 1.0, 0.0).astype(BF16)
    return dot(two_parts(value), onehot)


def prepare_kernel(back_ref, tokens_ref, hidden_ref, emb_ref, out_ref, tail_ref):
    length = hidden_ref.shape[0]
    kinds = emb_ref.shape[0]
    back = back_ref[0] == 1
    r = pl.program_id(0)
    final = pl.num_programs(0) - 1
    kind = lax.broadcasted_iota(jnp.int32, (kinds, length), 0)
    onehot = jnp.where(kind == tokens_ref[...], 1.0, 0.0).astype(BF16)
    merged = (hidden_ref[...].astype(F32) + dot_tn(onehot, emb_ref[...])).astype(BF16).astype(F32)
    mean = jnp.mean(merged * merged, axis=-1, keepdims=True)
    normed = (merged * lax.rsqrt(mean + EPS)).astype(BF16)

    @pl.when(back)
    def _():
        out_ref[...] = flip_both(normed)

    @pl.when(jnp.logical_not(back))
    def _():
        out_ref[...] = normed

    @pl.when(r == jnp.where(back, 0, final))
    def _():
        tail_ref[...] = out_ref[length - HALO :, :]


def prepare_call(back, tokens, hidden, embedding):
    rows, width = hidden.shape
    count = rows // CHUNK

    def turned(r, back):
        return (jnp.where(back[0] == 1, count - 1 - r, r), 0)

    return call(
        prepare_kernel,
        "prepare",
        vmem=12,
        cost=micros(1.5),
        scalars=(back,),
        grid=(count,),
        in_specs=[
            pl.BlockSpec((1, CHUNK), lambda r, back: (0, r)),
            pl.BlockSpec((CHUNK, width), lambda r, back: (r, 0)),
            pl.BlockSpec(embedding.shape, lambda r, back: (0, 0)),
        ],
        out_specs=[
            pl.BlockSpec((CHUNK, width), turned),
            pl.BlockSpec((HALO, width), lambda r, back: (0, 0)),
        ],
        out_shape=[
            jax.ShapeDtypeStruct((rows, width), BF16),
            jax.ShapeDtypeStruct((HALO, width), BF16),
        ],
    )(back, tokens.reshape(1, rows), hidden, embedding)


def gate_kernel(rows_ref, wg_ref, out_ref):
    gate = dot(rows_ref[...], wg_ref[...]).astype(BF16).astype(F32)
    out_ref[...] = silu(gate).astype(BF16)


def gate_call(tag, normed, w_gate):
    rows, width = normed.shape
    inner = w_gate.shape[1]
    return call(
        gate_kernel,
        "gate_" + tag,
        vmem=8,
        cost=micros(2.4),
        grid=(inner // TILE,),
        in_specs=[
            pl.BlockSpec((rows, width), lambda g: (0, 0)),
            pl.BlockSpec((width, TILE), lambda g: (0, g)),
        ],
        out_specs=pl.BlockSpec((rows, TILE), lambda g: (0, g)),
        out_shape=jax.ShapeDtypeStruct((rows, inner), BF16),
    )(normed, w_gate)


def conv_silu(rows_ref, weights, rows):
    taps = weights.shape[0]
    total = None
    for k in range(taps):
        offset = HALO - (taps - 1) + k
        term = weights[k : k + 1, :] * rows_ref[offset : offset + rows, :]
        total = term if total is None else total + term
    return silu(total).astype(BF16)


def maps_kernel(normed_ref, halo_ref, ws_ref, cs_ref, bc_ref, bt_ref, rows_ref):
    rows = normed_ref.shape[0]
    states = bc_ref.shape[1] // 2
    rows_ref[:HALO, :] = dot(halo_ref[...], ws_ref[...]).astype(BF16).astype(F32)
    rows_ref[HALO:, :] = dot(normed_ref[...], ws_ref[...]).astype(BF16).astype(F32)
    state_conv = conv_silu(rows_ref, cs_ref[...], rows)
    bc_ref[...] = state_conv
    bt_ref[...] = state_conv[:, :states].astype(F32).T.astype(BF16)


def maps_call(normed, halo, w_state, conv_state):
    rows = normed.shape[0]
    both = w_state.shape[1]
    vmem = pl.BlockSpec(memory_space=pltpu.VMEM)
    return call(
        maps_kernel,
        "maps",
        vmem=8,
        cost=micros(1.5),
        in_specs=[vmem] * 4,
        out_specs=[vmem] * 2,
        out_shape=[
            jax.ShapeDtypeStruct((rows, both), BF16),
            jax.ShapeDtypeStruct((both // 2, rows), BF16),
        ],
        scratch=[pltpu.VMEM((rows + HALO, both), F32)],
    )(normed, halo, w_state, conv_state)


def local_kernel(
    head_size,
    normed_ref,
    halo_ref,
    bt_ref,
    wi_ref,
    wt_ref,
    small_ref,
    xs_ref,
    cum_ref,
    cumt_ref,
    state_ref,
    rows_ref,
    step_ref,
):
    rows = normed_ref.shape[0]
    states = bt_ref.shape[0]
    heads = wt_ref.shape[0]
    taps = SMALL_TAPS
    g = pl.program_id(0)

    @pl.when(g == 0)
    def _():
        bias = small_ref[taps + 1 : taps + 2, :heads]
        rate = small_ref[taps + 2 : taps + 3, :heads]
        raw = dot_nt(normed_ref[...], wt_ref[...]) + bias
        step = jnp.maximum(raw, 0.0) + jnp.log1p(jnp.exp(-jnp.abs(raw)))
        step_ref[...] = step
        logdecay = -step * rate
        high = logdecay.astype(BF16)
        rest = logdecay - high.astype(F32)
        mid = rest.astype(BF16)
        low = (rest - mid.astype(F32)).astype(BF16)
        parts = jnp.concatenate([high, mid, low], axis=1)
        to = lax.broadcasted_iota(jnp.int32, (rows, rows), 0)
        frm = lax.broadcasted_iota(jnp.int32, (rows, rows), 1)
        sums = dot(jnp.where(to >= frm, 1.0, 0.0).astype(BF16), parts)
        cum = sums[:, :heads] + sums[:, heads : 2 * heads] + sums[:, 2 * heads :]
        cum_ref[...] = cum
        cumt_ref[...] = cum.T

    weights = wi_ref[...]
    rows_ref[:HALO, :] = dot(halo_ref[...], weights).astype(BF16).astype(F32)
    rows_ref[HALO:, :] = dot(normed_ref[...], weights).astype(BF16).astype(F32)
    columns = pl.ds(pl.multiple_of(g * TILE, TILE), TILE)
    x = conv_silu(rows_ref, small_ref[:taps, columns], rows).astype(F32)
    first = g * (TILE // head_size)
    xs = x * spread(step_ref[...], TILE, head_size, first)
    xs_ref[...] = xs.astype(BF16)
    cum = cum_ref[...]
    total = cum[rows - 1 :, :]
    left = spread(jnp.exp(total - cum), TILE, head_size, first)
    state_ref[:states, :] = dot(bt_ref[...], (xs * left).astype(BF16)).astype(BF16)
    whole = spread(jnp.broadcast_to(jnp.exp(total), (EXTRA, heads)), TILE, head_size, first)
    high = whole.astype(BF16).astype(F32)
    place = lax.broadcasted_iota(jnp.int32, whole.shape, 0)
    state_ref[states:, :] = jnp.where(place == 0, high, whole - high).astype(BF16)


SMALL_TAPS = 4
SMALL_ROWS = 8


def small_params(conv, gain, bias, rate):
    inner = gain.shape[0]
    rest = SMALL_ROWS - SMALL_TAPS - 3

    def row(a):
        return jnp.pad(a, (0, inner - a.shape[0]))[None, :]

    return jnp.concatenate([conv, row(gain), row(bias), row(rate), jnp.zeros((rest, inner), F32)], axis=0)


def local_call(tag, normed, halo, bt, w_inner, w_step_t, small):
    rows, width = normed.shape
    inner = w_inner.shape[1]
    heads = w_step_t.shape[0]
    states = bt.shape[0]

    def whole(a):
        return pl.BlockSpec(a.shape, lambda g: (0, 0))

    def tile(count):
        return pl.BlockSpec((count, TILE), lambda g: (0, g))

    return call(
        functools.partial(local_kernel, inner // heads),
        "local_" + tag,
        vmem=12,
        cost=micros(5.0),
        grid=(inner // TILE,),
        in_specs=[whole(normed), whole(halo), whole(bt), tile(width), whole(w_step_t), whole(small)],
        out_specs=[
            tile(rows),
            pl.BlockSpec((rows, heads), lambda g: (0, 0)),
            pl.BlockSpec((heads, rows), lambda g: (0, 0)),
            tile(states + EXTRA),
        ],
        out_shape=[
            jax.ShapeDtypeStruct((rows, inner), BF16),
            jax.ShapeDtypeStruct((rows, heads), F32),
            jax.ShapeDtypeStruct((heads, rows), F32),
            jax.ShapeDtypeStruct((states + EXTRA, inner), BF16),
        ],
        scratch=[pltpu.VMEM((rows + HALO, TILE), F32), pltpu.VMEM((rows, heads), F32)],
    )(normed, halo, bt, w_inner, w_step_t, small)


def inside_kernel(head_size, xs_ref, bc_ref, cum_ref, cumt_ref, y_ref, state_ref, prev_ref):
    length, inner = xs_ref.shape
    states = bc_ref.shape[1] // 2
    heads = cum_ref.shape[1]

    @pl.when(pl.program_id(0) == 0)
    def _():
        state_ref[...] = jnp.zeros_like(state_ref)
        prev_ref[...] = jnp.zeros_like(prev_ref)

    bmat = bc_ref[:, :states]
    cmat = bc_ref[:, states:]
    to = lax.broadcasted_iota(jnp.int32, (length, length), 0)
    frm = lax.broadcasted_iota(jnp.int32, (length, length), 1)
    scores = jnp.where(to >= frm, dot_nt(cmat, bmat), 0.0)
    cum = cum_ref[...]
    cumt = cumt_ref[...]
    last = length - 1
    end = cum[last:, :]
    since = spread(jnp.exp(cum - prev_ref[...]), inner, head_size, 0)
    left = spread(jnp.exp(end - cum), inner, head_size, 0)
    state = state_ref[...]
    carried = dot(cmat, state.astype(BF16)) * since
    xs = xs_ref[...]
    scaled = (xs.astype(F32) * left).astype(BF16)
    state_ref[...] = state * since[last:, :] + dot_tn(bmat, scaled)
    prev_ref[...] = end
    pair = 2 * head_size
    lane = lax.broadcasted_iota(jnp.int32, (length, pair), 1)
    for p in range(heads // 2):
        weights = []
        for h in (2 * p, 2 * p + 1):
            apart = jnp.minimum(cum[:, h : h + 1] - cumt[h : h + 1, :], 0.0)
            weights.append((jnp.exp(apart) * scores).astype(BF16))
        mine = xs[:, p * pair : (p + 1) * pair]
        none = jnp.zeros_like(mine)
        stacked = jnp.concatenate(
            [jnp.where(lane < head_size, mine, none), jnp.where(lane < head_size, none, mine)], axis=0
        )
        inside = dot(jnp.concatenate(weights, axis=1), stacked)
        y_ref[:, p * pair : (p + 1) * pair] = (
            inside + carried[:, p * pair : (p + 1) * pair]
        ).astype(BF16)


def inside_call(tag, xs, bc, cum, cumt):
    rows, inner = xs.shape
    heads = cum.shape[1]
    both = bc.shape[1]

    def block(width):
        return pl.BlockSpec((CHUNK, width), lambda c: (c, 0))

    return call(
        functools.partial(inside_kernel, inner // heads),
        "inside_" + tag,
        vmem=8,
        cost=micros(3.2),
        grid=(rows // CHUNK,),
        in_specs=[
            block(inner),
            block(both),
            block(heads),
            pl.BlockSpec((heads, CHUNK), lambda c: (0, c)),
        ],
        out_specs=block(inner),
        out_shape=jax.ShapeDtypeStruct((rows, inner), BF16),
        scratch=[pltpu.VMEM((both // 2, inner), F32), pltpu.VMEM((1, heads), F32)],
    )(xs, bc, cum, cumt)


def parts_of(payload):
    states = payload.shape[0] - EXTRA
    wide = payload.astype(F32)
    return wide[:states], wide[states : states + 1] + wide[states + 1 : states + 2]


def write_payload(out_ref, state, decay):
    states = state.shape[0]
    out_ref[:states, :] = state.astype(BF16)
    decay = jnp.broadcast_to(decay, (EXTRA, decay.shape[1]))
    high = decay.astype(BF16).astype(F32)
    place = lax.broadcasted_iota(jnp.int32, decay.shape, 0)
    out_ref[states:, :] = jnp.where(place == 0, high, decay - high).astype(BF16)


def pair_kernel(first_ref, mine_ref, other_ref, out_ref):
    mine, mine_a = parts_of(mine_ref[...])
    other, other_a = parts_of(other_ref[...])
    is_first = first_ref[0] == 1
    early = jnp.where(is_first, mine, other)
    late = jnp.where(is_first, other, mine)
    late_a = jnp.where(is_first, other_a, mine_a)
    write_payload(out_ref, late_a * early + late, mine_a * other_a)


def chain_kernel(pair_ref, before_ref, out_ref):
    pair, pair_a = parts_of(pair_ref[...])
    before, before_a = parts_of(before_ref[...])
    write_payload(out_ref, pair_a * before + pair, pair_a * before_a)


def longer_kernel(before_ref, farther_ref, out_ref):
    before, before_a = parts_of(before_ref[...])
    farther, farther_a = parts_of(farther_ref[...])
    write_payload(out_ref, before + before_a * farther, before_a * farther_a)


def entry_kernel(first_ref, mine_ref, other_ref, before_ref, farther_ref, keep_ref, send_ref):
    mine, mine_a = parts_of(mine_ref[...])
    other, other_a = parts_of(other_ref[...])
    before, before_a = parts_of(before_ref[...])
    farther, _ = parts_of(farther_ref[...])
    is_first = first_ref[0] == 1
    entry_first = before + before_a * farther
    early = jnp.where(is_first, mine, other)
    early_a = jnp.where(is_first, mine_a, other_a)
    entry_second = early_a * entry_first + early
    keep_ref[...] = jnp.where(is_first, entry_first, entry_second).astype(BF16)
    send_ref[...] = jnp.where(is_first, entry_second, entry_first).astype(BF16)


def small_call(kernel, name, flags, arrays, shapes):
    vmem = pl.BlockSpec(memory_space=pltpu.VMEM)
    smem = pl.BlockSpec(memory_space=pltpu.SMEM)
    return call(
        kernel,
        name,
        vmem=4,
        cost=micros(0.5),
        in_specs=[smem] * len(flags) + [vmem] * len(arrays),
        out_specs=[vmem] * len(shapes),
        out_shape=[jax.ShapeDtypeStruct(s, BF16) for s in shapes],
    )(*flags, *arrays)


def onward(value, by):
    count = lax.axis_size("seq")
    cores = lax.axis_size("ch")
    pairs = []
    for core in range(cores):
        step = -by if core == 1 else by
        pairs += [
            (i * cores + core, (i + step) * cores + core) for i in range(count) if 0 <= i + step < count
        ]
    return lax.ppermute(value, ("seq", "ch"), pairs)


def entering(tag, back, state):
    count = lax.axis_size("seq")
    parity = lax.axis_index("seq") % 2
    first = jnp.where(back == 1, parity, 1 - parity).astype(jnp.int32)
    height, inner = state.shape
    half = inner // 2
    swap = [(i, i ^ 1) for i in range(count)]
    send = lax.dynamic_slice_in_dim(state, (1 - parity) * half, half, 1)
    mine = lax.dynamic_slice_in_dim(state, parity * half, half, 1)
    other = lax.ppermute(send, "seq", swap)
    shape = (height, half)
    (pair,) = small_call(pair_kernel, "pair_" + tag, [first], [mine, other], [shape])
    before = None
    farther = None
    running = pair
    apart = 2
    while apart < count:
        arrived = onward(running, apart)
        last = apart * 2 >= count
        if before is None:
            before = arrived
        elif last:
            farther = arrived
        else:
            (before,) = small_call(longer_kernel, "longer_" + tag, [], [before, arrived], [shape])
        if not last:
            (running,) = small_call(chain_kernel, "chain_" + tag, [], [pair, before], [shape])
        apart *= 2
    if before is None:
        before = jnp.zeros(shape, BF16)
    if farther is None:
        farther = jnp.zeros(shape, BF16)
    entry = (height - EXTRA, half)
    keep, out = small_call(
        entry_kernel, "entry_" + tag, [first], [mine, other, before, farther], [entry, entry]
    )
    return keep, lax.ppermute(out, "seq", swap)


def gated_part(head_size, swap, y_ref, bc_ref, cum_ref, keep_ref, other_ref, gate_ref, small_ref, wo_ref):
    inner = y_ref.shape[1]
    states = bc_ref.shape[1] // 2
    cmat = bc_ref[:, states:]
    keep = keep_ref[...]
    other = other_ref[...]
    entry = jnp.concatenate([jnp.where(swap, other, keep), jnp.where(swap, keep, other)], axis=1)
    carried = dot(cmat, entry) * spread(jnp.exp(cum_ref[...]), inner, head_size, 0)
    gated = (y_ref[...].astype(F32) + carried) * gate_ref[...].astype(F32)
    squares = jnp.sum(gated * gated, axis=-1, keepdims=True)
    gain = small_ref[SMALL_TAPS : SMALL_TAPS + 1, :]
    return dot((gated * gain).astype(BF16), wo_ref[...]), squares


def part_kernel(head_size, flags_ref, *refs):
    *ins, out_ref, sq_ref = refs
    result, squares = gated_part(head_size, flags_ref[0] == 1, *ins)
    out_ref[...] = result
    sq_ref[...] = jnp.broadcast_to(squares, sq_ref.shape)


def finish_kernel(head_size, full_width, flags_ref, *refs):
    *ins, part_ref, psq_ref, own_ref, send_ref = refs
    result, squares = gated_part(head_size, flags_ref[0] == 1, *ins)
    squares = squares + psq_ref[:, :1]
    result = (result + part_ref[...]) * lax.rsqrt(squares / full_width + EPS)
    result = result.astype(BF16)
    half = own_ref.shape[1]

    @pl.when(flags_ref[1] == 1)
    def _():
        turned = flip_both(result)
        own_ref[...] = turned[:, half:]
        send_ref[...] = turned[:, :half]

    @pl.when(flags_ref[1] != 1)
    def _():
        own_ref[...] = result[:, :half]
        send_ref[...] = result[:, half:]


def finish_call(flags, y, bc, cum, keep, other, gate, small, w_output, full_width=None, partial=None):
    rows, inner = y.shape
    width = w_output.shape[1]
    half = width // 2
    heads = cum.shape[1]
    count = rows // TILE

    def block(columns):
        return pl.BlockSpec((TILE, columns), lambda r, flags: (r, 0))

    def whole(a):
        return pl.BlockSpec(a.shape, lambda r, flags: (0, 0))

    def turned(r, flags):
        return (jnp.where(flags[1] == 1, count - 1 - r, r), 0)

    in_specs = [
        block(inner),
        block(bc.shape[1]),
        block(heads),
        whole(keep),
        whole(other),
        block(inner),
        whole(small),
        whole(w_output),
    ]
    arrays = [y, bc, cum, keep, other, gate, small, w_output]
    if partial is None:
        kernel = functools.partial(part_kernel, inner // heads)
        out_specs = [block(width), block(128)]
        out_shape = [jax.ShapeDtypeStruct((rows, width), F32), jax.ShapeDtypeStruct((rows, 128), F32)]
    else:
        kernel = functools.partial(finish_kernel, inner // heads, full_width)
        in_specs += [block(width), block(128)]
        arrays += list(partial)
        out_specs = [pl.BlockSpec((TILE, half), turned)] * 2
        out_shape = [jax.ShapeDtypeStruct((rows, half), BF16)] * 2
    return call(
        kernel,
        "part" if partial is None else "finish",
        vmem=16,
        cost=micros(3.5),
        scalars=(flags,),
        grid=(count,),
        in_specs=in_specs,
        out_specs=out_specs,
        out_shape=out_shape,
    )(flags, *arrays)


def body(
    tokens,
    hidden,
    embedding,
    w_gate,
    w_inner,
    w_state,
    w_step,
    conv_inner,
    conv_state,
    step_bias,
    decay_rate,
    norm_gain,
    w_output,
):
    swap = [(0, 1), (1, 0)]

    def theirs(a):
        return lax.ppermute(a, "ch", swap)

    back = lax.axis_index("ch").astype(jnp.int32).reshape(1)
    parity = (lax.axis_index("seq") % 2).astype(jnp.int32).reshape(1)
    flags = jnp.concatenate([parity, back])
    normed, tail = prepare_call(back, tokens, hidden, embedding)
    halo = onward(tail, 1)
    small = small_params(conv_inner, norm_gain, step_bias, decay_rate)
    own = (w_inner, w_step.T, small)
    other = tuple(theirs(a) for a in own)
    w_gate_2 = theirs(w_gate)
    w_output_2 = theirs(w_output)
    gate_1 = gate_call("own", normed, w_gate)
    bc, bt = maps_call(normed, halo, w_state, conv_state)
    xs_1, cum_1, cumt_1, state_1 = local_call("own", normed, halo, bt, *own)
    xs_2, cum_2, cumt_2, state_2 = local_call("other", normed, halo, bt, *other)
    entry_1 = entering("own", back, state_1)
    entry_2 = entering("other", back, state_2)
    y_1 = inside_call("own", xs_1, bc, cum_1, cumt_1)
    y_2 = inside_call("other", xs_2, bc, cum_2, cumt_2)
    gate_2 = gate_call("other", normed, w_gate_2)
    partial = finish_call(flags, y_1, bc, cum_1, *entry_1, gate_1, small, w_output)
    full_width = float(w_inner.shape[1] * lax.axis_size("ch"))
    mine, send = finish_call(
        flags, y_2, bc, cum_2, *entry_2, gate_2, other[2], w_output_2, full_width, partial
    )
    return (mine.astype(F32) + theirs(send).astype(F32)).astype(BF16)


def solution(mesh):
    return jax.shard_map(
        body,
        mesh=mesh,
        in_specs=(
            P(("win", "seq")),
            P(("win", "seq"), None),
            P(),
            P(None, "ch"),
            P(None, "ch"),
            P(),
            P(None, "ch"),
            P(None, "ch"),
            P(),
            P("ch"),
            P("ch"),
            P("ch"),
            P("ch", None),
        ),
        out_specs=P(("win", "seq"), "ch"),
        check_vma=False,
    )
```

time: 85.8 us -> 86.4 us (level)
  starting transfers between devices: 24.3 us -> 32.9 us
  Pallas kernels: 38.1 us -> 33.9 us
  other arithmetic: 4.06 us -> 1.01 us
  local copies, waits for them, and re-layouts: 8.73 us -> 5.82 us
  waiting for transfers between devices: 9.55 us -> 11.5 us
    ppermute x8 -> x11, starting transfers between devices: 19.9 us -> 26.6 us  [the longest x5 25.4 us: onward(): return lax.ppermute(value, ('seq', 'ch'), pairs)]
    ppermute x2, waiting for transfers between devices: 0.17 us -> 4.78 us  [entering(): other = lax.ppermute(send, 'seq', swap)]
    pallas_call x15 -> x16, Pallas kernels: 38.1 us -> 33.9 us  [the longest x2 13.9 us: local_call(): call(functools.partial(local_kernel, inner // heads), 'local_' + tag, vme...]
    ppermute x8 -> x11, waiting for transfers between devices: 9.37 us -> 5.71 us  [the longest x5 3.8 us: onward(): return lax.ppermute(value, ('seq', 'ch'), pairs)]
    unnamed x69 -> x32, local copies, waits for them, and re-layouts: 8.67 us -> 5.71 us
    convert_element_type x1, other arithmetic: 2.43 us -> 0.93 us  [body(): return (mine.astype(F32) + theirs(send).astype(F32)).astype(BF16)]
    ppermute x2, starting transfers between devices: 1.57 us -> 2.72 us  [entering(): return (keep, lax.ppermute(out, 'seq', swap))]
    ppermute x2, waiting for transfers between devices: 0.01 us -> 1.04 us  [entering(): return (keep, lax.ppermute(out, 'seq', swap))]
  transfers between devices with their start and end apart: 12 -> 15, of which waited for: 5 -> 7; matrix products, arithmetic and copies ran while one was open for 0% -> 0% of each run, Pallas kernels for 42% -> 36%
where the time goes in v1:
time: 86.4 us; the launch traced here: 85.6 us
  Pallas kernels  33.9 us (39%)
  starting transfers between devices  32.9 us (38%)
  waiting for transfers between devices  11.5 us (13%)
  local copies, waits for them, and re-layouts  5.82 us (7%)
  other arithmetic  1.01 us (1%)
    ppermute x5, starting transfers between devices, onward(): return lax.ppermute(value, ('seq', 'ch'), pairs)  25.4 us
    pallas_call x2, Pallas kernels, local_call(): call(functools.partial(local_kernel, inner // heads), 'local_' + tag, vme...  13.9 us
    pallas_call x2, Pallas kernels, inside_call(): call(functools.partial(inside_kernel, inner // heads), 'inside_' + tag, v...  6.55 us
    pallas_call x2, Pallas kernels, finish_call(): call(kernel, 'part' if partial is None else 'finish', vmem=16, cost=micro...  5.92 us
    unnamed x32, local copies, waits for them, and re-layouts  5.71 us
    ppermute x2, waiting for transfers between devices, entering(): other = lax.ppermute(send, 'seq', swap)  4.78 us
    pallas_call x2, Pallas kernels, gate_call(): call(gate_kernel, 'gate_' + tag, vmem=8, cost=micros(2.4), grid=(inner //...  4.42 us
    ppermute x5, waiting for transfers between devices, onward(): return lax.ppermute(value, ('seq', 'ch'), pairs)  3.8 us
  transfers between devices with their start and end apart: 15, of which 7 were waited for; matrix products, arithmetic and copies ran while one was open for 0% of the time, Pallas kernels for 36%

profile of v1, /device:TPU:0, one launch (start us, length us, event | category | flops | bytes accessed | tf_op | source)
XLA Modules:
  0.0 85.6 jit_solution(13027207499108182285)
XLA Ops:
  0.5 1.2 %copy-done.3 = bf16[512,1024]{1,0:T(8,128)(2,1)S(1)} copy-done((bf16[512,1024]{1,0:T(8,128)(2,1)S(1)}, bf16[512,1024]{1,0:T(8,128)(2,1)}, u32[]{:S(2)}) %copy-start.3) | copy-done | bytes 1048600
  3.1 1.7 %prepare.1 = (bf16[512,1024]{1,0:T(8,128)(2,1)S(1)}, bf16[16,1024]{1,0:T(8,128)(2,1)S(1)}) custom-call(s32[1]{0:T(128)} %bitcast.1.back_ref, s32[1,512]{1,0:T(1,128)S(1)} %bitcast.10, bf16[512,1024]{1,0:T(8,128)(2,1)S(1)} %copy-done.3, bf16[4,1024]{1,0:T(4,128)(2,1)S(1)} %copy-done.6), custom_call_target="tpu_custom_call" | custom-call | flops 1650000000 | bytes 1500000 | tf_op jit(solution)/shard_map/prepare/pallas_call | solution.py:126
  5.7 4.4 %collective-permute-start = (bf16[16,1024]{1,0:T(8,128)(2,1)S(1)}, bf16[16,1024]{1,0:T(8,128)(2,1)S(1)}, u32[]{:S(2)}, u32[]{:S(2)}) collective-permute-start(bf16[16,1024]{1,0:T(8,128)(2,1)S(1)} %get-tuple-element.26), channel_id=1, source_target_pairs={{0,2},{2,4},{4,6},{6,8},{8,10},{10,12},{12,14},{3,1},{5,3},{7,5},{... | collective-permute-start | bytes 98312 | tf_op jit(solution)/shard_map/ppermute | solution.py:464
  10.3 1.4 %collective-permute-done.halo_ref = bf16[16,1024]{1,0:T(8,128)(2,1)S(1)} collective-permute-done((bf16[16,1024]{1,0:T(8,128)(2,1)S(1)}, bf16[16,1024]{1,0:T(8,128)(2,1)S(1)}, u32[]{:S(2)}, u32[]{:S(2)}) %collective-permute-start) | collective-permute-done | bytes 32800 | tf_op jit(solution)/shard_map/ppermute | solution.py:464
  11.8 1.2 %copy-done.10 = bf16[512,1024]{1,0:T(8,128)(2,1)S(1)} copy-done((bf16[512,1024]{1,0:T(8,128)(2,1)S(1)}, bf16[512,1024]{1,0:T(8,128)(2,1)}, u32[]{:S(2)}) %copy-start.10) | copy-done | bytes 1048600
  14.9 6.9 %local_own.1 = (bf16[512,1024]{1,0:T(8,128)(2,1)S(1)}, f32[512,16]{1,0:T(8,128)S(1)}, f32[16,512]{1,0:T(8,128)S(1)}, bf16[144,1024]{1,0:T(8,128)(2,1)S(1)}) custom-call(bf16[512,1024]{1,0:T(8,128)(2,1)S(1)} %copy-done.11, bf16[16,1024]{1,0:T(8,128)(2,1)S(1)} %collective-permute-done.halo_ref, bf16[128,512]{1,0:T(8,128)(2,1)S(1)} %get-tuple-element.27.bt_ref, ...), custom_call_target="tpu_custom_call" | custom-call | flops 5500000256 | bytes 5000000 | tf_op jit(solution)/shard_map/local_own/pallas_call | solution.py:296
  21.8 2.4 %collective-permute-start.10 = (bf16[144,512]{1,0:T(8,128)(2,1)S(1)}, bf16[144,512]{1,0:T(8,128)(2,1)S(1)}, u32[]{:S(2)}, u32[]{:S(2)}) collective-permute-start(bf16[144,512]{1,0:T(8,128)(2,1)S(1)} %get-tuple-element.45), channel_id=1, source_target_pairs={{0,2},{2,0},{4,6},{6,4},{8,10},{10,8},{12,14},{14,12},{1,3},{3,1},... | collective-permute-start | bytes 442376 | tf_op jit(solution)/shard_map/ppermute | solution.py:476
  24.2 3.7 %collective-permute-done.10.other_ref = bf16[144,512]{1,0:T(8,128)(2,1)S(1)} collective-permute-done((bf16[144,512]{1,0:T(8,128)(2,1)S(1)}, bf16[144,512]{1,0:T(8,128)(2,1)S(1)}, u32[]{:S(2)}, u32[]{:S(2)}) %collective-permute-start.10) | collective-permute-done | bytes 147488 | tf_op jit(solution)/shard_map/ppermute | solution.py:476
  28.0 5.4 %collective-permute-start.11 = (bf16[144,512]{1,0:T(8,128)(2,1)S(1)}, bf16[144,512]{1,0:T(8,128)(2,1)S(1)}, u32[]{:S(2)}, u32[]{:S(2)}) collective-permute-start(bf16[144,512]{1,0:T(8,128)(2,1)S(1)} %pair_own.1.pair_ref), channel_id=1, source_target_pairs={{0,4},{2,6},{4,8},{6,10},{8,12},{10,14},{5,1},{7,3},{9,5},{11,7},{... | collective-permute-start | bytes 442376 | tf_op jit(solution)/shard_map/ppermute | solution.py:464
  34.1 2.0 %collective-permute-done.11.before_ref = bf16[144,512]{1,0:T(8,128)(2,1)S(1)} collective-permute-done((bf16[144,512]{1,0:T(8,128)(2,1)S(1)}, bf16[144,512]{1,0:T(8,128)(2,1)S(1)}, u32[]{:S(2)}, u32[]{:S(2)}) %collective-permute-start.11) | collective-permute-done | bytes 147488 | tf_op jit(solution)/shard_map/ppermute | solution.py:464
  36.2 5.5 %collective-permute-start.12 = (bf16[144,512]{1,0:T(8,128)(2,1)S(1)}, bf16[144,512]{1,0:T(8,128)(2,1)S(1)}, u32[]{:S(2)}, u32[]{:S(2)}) collective-permute-start(bf16[144,512]{1,0:T(8,128)(2,1)S(1)} %chain_own.1), channel_id=1, source_target_pairs={{0,8},{2,10},{4,12},{6,14},{9,1},{11,3},{13,5},{15,7},{16,24},{18,... | collective-permute-start | bytes 442376 | tf_op jit(solution)/shard_map/ppermute | solution.py:464
  41.7 2.2 %gate_own.1.refs_5_ = bf16[512,1024]{1,0:T(8,128)(2,1)S(1)} custom-call(bf16[512,1024]{1,0:T(8,128)(2,1)S(1)} %copy-done.11, bf16[1024,1024]{1,0:T(8,128)(2,1)S(1)} %copy-done.1), custom_call_target="tpu_custom_call" | custom-call | flops 2640000000 | bytes 2400000 | tf_op jit(solution)/shard_map/gate_own/pallas_call | solution.py:157
  45.5 6.9 %local_other.1 = (bf16[512,1024]{1,0:T(8,128)(2,1)S(1)}, f32[512,16]{1,0:T(8,128)S(1)}, f32[16,512]{1,0:T(8,128)S(1)}, bf16[144,1024]{1,0:T(8,128)(2,1)S(1)}) custom-call(bf16[512,1024]{1,0:T(8,128)(2,1)S(1)} %copy-done.11, bf16[16,1024]{1,0:T(8,128)(2,1)S(1)} %collective-permute-done.halo_ref, bf16[128,512]{1,0:T(8,128)(2,1)S(1)} %get-tuple-element.27.bt_ref, ...), custom_call_target="tpu_custom_call" | custom-call | flops 5500000256 | bytes 5000000 | tf_op jit(solution)/shard_map/local_other/pallas_call | solution.py:296
  52.5 1.2 %collective-permute-start.4 = (bf16[144,512]{1,0:T(8,128)(2,1)S(1)}, bf16[144,512]{1,0:T(8,128)(2,1)S(1)}, u32[]{:S(2)}, u32[]{:S(2)}) collective-permute-start(bf16[144,512]{1,0:T(8,128)(2,1)S(1)} %get-tuple-element.47), channel_id=1, source_target_pairs={{0,2},{2,0},{4,6},{6,4},{8,10},{10,8},{12,14},{14,12},{1,3},{3,1},... | collective-permute-start | bytes 442376 | tf_op jit(solution)/shard_map/ppermute | solution.py:476
  53.7 3.3 %inside_own.1.refs_0_ = bf16[512,1024]{1,0:T(8,128)(2,1)S(1)} custom-call(bf16[512,1024]{1,0:T(8,128)(2,1)S(1)} %get-tuple-element.35.xs_ref, bf16[512,256]{1,0:T(8,128)(2,1)S(1)} %get-tuple-element.29.bc_ref.refs_1_, f32[512,16]{1,0:T(8,128)S(1)} %get-tuple-element.36.cum_ref.refs_2_, f32[16,512]{1,0:T(8,128)S(1)} %get-tuple-element.37.cumt_ref), custom_call_target="tpu_custom_call" | custom-call | flops 3520000000 | bytes 3200000 | tf_op jit(solution)/shard_map/inside_own/pallas_call | solution.py:372
  57.0 1.1 %collective-permute-done.4.other_ref = bf16[144,512]{1,0:T(8,128)(2,1)S(1)} collective-permute-done((bf16[144,512]{1,0:T(8,128)(2,1)S(1)}, bf16[144,512]{1,0:T(8,128)(2,1)S(1)}, u32[]{:S(2)}, u32[]{:S(2)}) %collective-permute-start.4) | collective-permute-done | bytes 147488 | tf_op jit(solution)/shard_map/ppermute | solution.py:476
  58.1 4.6 %collective-permute-start.5 = (bf16[144,512]{1,0:T(8,128)(2,1)S(1)}, bf16[144,512]{1,0:T(8,128)(2,1)S(1)}, u32[]{:S(2)}, u32[]{:S(2)}) collective-permute-start(bf16[144,512]{1,0:T(8,128)(2,1)S(1)} %pair_other.1.pair_ref), channel_id=1, source_target_pairs={{0,4},{2,6},{4,8},{6,10},{8,12},{10,14},{5,1},{7,3},{9,5},{11,7},{... | collective-permute-start | bytes 442376 | tf_op jit(solution)/shard_map/ppermute | solution.py:464
  62.7 2.9 %part.1 = (f32[512,1024]{1,0:T(8,128)S(1)}, f32[512,128]{1,0:T(8,128)S(1)}) custom-call(s32[2]{0:T(128)S(1)} %pad_add_fusion.flags_ref, bf16[512,1024]{1,0:T(8,128)(2,1)S(1)} %inside_own.1.refs_0_, bf16[512,256]{1,0:T(8,128)(2,1)S(1)} %get-tuple-element.29.bc_ref.refs_1_, f32[512,16]{1,0:T(8,128)S(1)} %get-tuple-element.36.cum_ref.refs_2_, ...), custom_call_target="tpu_custom_call" | custom-call | flops 3849999872 | bytes 3500000 | tf_op jit(solution)/shard_map/part/pallas_call | solution.py:584
  65.7 5.5 %collective-permute-start.6 = (bf16[144,512]{1,0:T(8,128)(2,1)S(1)}, bf16[144,512]{1,0:T(8,128)(2,1)S(1)}, u32[]{:S(2)}, u32[]{:S(2)}) collective-permute-start(bf16[144,512]{1,0:T(8,128)(2,1)S(1)} %chain_other.1), channel_id=1, source_target_pairs={{0,8},{2,10},{4,12},{6,14},{9,1},{11,3},{13,5},{15,7},{16,24},{18,... | collective-permute-start | bytes 442376 | tf_op jit(solution)/shard_map/ppermute | solution.py:464
  71.2 3.3 %inside_other.1.refs_0_ = bf16[512,1024]{1,0:T(8,128)(2,1)S(1)} custom-call(bf16[512,1024]{1,0:T(8,128)(2,1)S(1)} %get-tuple-element.28.xs_ref, bf16[512,256]{1,0:T(8,128)(2,1)S(1)} %get-tuple-element.29.bc_ref.refs_1_, f32[512,16]{1,0:T(8,128)S(1)} %get-tuple-element.30.cum_ref.refs_2_, f32[16,512]{1,0:T(8,128)S(1)} %get-tuple-element.31.cumt_ref), custom_call_target="tpu_custom_call" | custom-call | flops 3520000000 | bytes 3200000 | tf_op jit(solution)/shard_map/inside_other/pallas_call | solution.py:372
  74.6 1.8 %collective-permute-start.7 = (bf16[128,512]{1,0:T(8,128)(2,1)S(1)}, bf16[128,512]{1,0:T(8,128)(2,1)S(1)}, u32[]{:S(2)}, u32[]{:S(2)}) collective-permute-start(bf16[128,512]{1,0:T(8,128)(2,1)S(1)} %get-tuple-element.34), channel_id=1, source_target_pairs={{0,2},{2,0},{4,6},{6,4},{8,10},{10,8},{12,14},{14,12},{1,3},{3,1},... | collective-permute-start | bytes 393224 | tf_op jit(solution)/shard_map/ppermute | solution.py:503
  76.3 2.2 %gate_other.1.refs_5_ = bf16[512,1024]{1,0:T(8,128)(2,1)S(1)} custom-call(bf16[512,1024]{1,0:T(8,128)(2,1)S(1)} %copy-done.11, bf16[1024,1024]{1,0:T(8,128)(2,1)S(1)} %collective-permute-done.8.wg_ref), custom_call_target="tpu_custom_call" | custom-call | flops 2640000000 | bytes 2400000 | tf_op jit(solution)/shard_map/gate_other/pallas_call | solution.py:157
  79.6 3.0 %finish.1 = (bf16[512,512]{1,0:T(8,128)(2,1)S(1)}, bf16[512,512]{1,0:T(8,128)(2,1)S(1)}) custom-call(s32[2]{0:T(128)S(1)} %pad_add_fusion.flags_ref, bf16[512,1024]{1,0:T(8,128)(2,1)S(1)} %inside_other.1.refs_0_, bf16[512,256]{1,0:T(8,128)(2,1)S(1)} %get-tuple-element.29.bc_ref.refs_1_, f32[512,16]{1,0:T(8,128)S(1)} %get-tuple-element.30.cum_ref.refs_2_, ...), custom_call_target="tpu_custom_call" | custom-call | flops 3849999872 | bytes 3500000 | tf_op jit(solution)/shard_map/finish/pallas_call | solution.py:584
  82.7 1.9 %collective-permute-done.14 = bf16[512,512]{1,0:T(8,128)(2,1)S(1)} collective-permute-done((bf16[512,512]{1,0:T(8,128)(2,1)S(1)}, bf16[512,512]{1,0:T(8,128)(2,1)S(1)}, u32[]{:S(2)}, u32[]{:S(2)}) %collective-permute-start.14) | collective-permute-done | bytes 524320 | tf_op jit(solution)/shard_map/ppermute | solution.py:615
  (62 shorter events, 9.4 us)
Async XLA Ops:
  0.0 45.5 %collective-permute-start.1 = (bf16[1024,1024]{1,0:T(8,128)(2,1)}, bf16[1024,1024]{1,0:T(8,128)(2,1)S(1)}, u32[]{:S(2)}, u32[]{:S(2)}) collective-permute-start(bf16[1024,1024]{1,0:T(8,128)(2,1)} %wi_ref.1), channel_id=1, source_target_pairs={{0,1},{1,0},{2,3},{3,2},{4,5},{5,4},{6,7},{7,6},{8,9},{9,8},{10,11... | collective-permute-start | bytes 6291464 | tf_op jit(solution)/shard_map/ppermute | solution.py:615
  3.1 7.1 %copy-start.14 = (f32[16]{0:T(128)S(1)}, f32[16]{0:T(128)}, u32[]{:S(2)}) copy-start(f32[16]{0:T(128)} %param.22) | copy-start | bytes 196
  3.1 7.2 %copy-start.15 = (f32[16]{0:T(128)S(1)}, f32[16]{0:T(128)}, u32[]{:S(2)}) copy-start(f32[16]{0:T(128)} %param.23) | copy-start | bytes 196
  3.1 7.2 %copy-start.12 = (f32[4,1024]{1,0:T(4,128)S(1)}, f32[4,1024]{1,0:T(4,128)}, u32[]{:S(2)}) copy-start(f32[4,1024]{1,0:T(4,128)} %param.20) | copy-start | bytes 49156
  3.1 7.2 %copy-start.13 = (f32[1024]{0:T(1024)S(1)}, f32[1024]{0:T(1024)}, u32[]{:S(2)}) copy-start(f32[1024]{0:T(1024)} %param.24) | copy-start | bytes 12292
  3.1 8.7 %copy-start.4 = (bf16[1024,256]{1,0:T(8,128)(2,1)S(1)}, bf16[1024,256]{1,0:T(8,128)(2,1)}, u32[]{:S(2)}) copy-start(bf16[1024,256]{1,0:T(8,128)(2,1)} %ws_ref.1) | copy-start | bytes 1572868
  3.1 8.7 %copy-start.7 = (f32[4,256]{1,0:T(4,128)S(1)}, f32[4,256]{1,0:T(4,128)}, u32[]{:S(2)}) copy-start(f32[4,256]{1,0:T(4,128)} %cs_ref.1) | copy-start | bytes 12292
  5.7 6.0 %collective-permute-start = (bf16[16,1024]{1,0:T(8,128)(2,1)S(1)}, bf16[16,1024]{1,0:T(8,128)(2,1)S(1)}, u32[]{:S(2)}, u32[]{:S(2)}) collective-permute-start(bf16[16,1024]{1,0:T(8,128)(2,1)S(1)} %get-tuple-element.26), channel_id=1, source_target_pairs={{0,2},{2,4},{4,6},{6,8},{8,10},{10,12},{12,14},{3,1},{5,3},{7,5},{... | collective-permute-start | bytes 98312 | tf_op jit(solution)/shard_map/ppermute | solution.py:464
  13.0 1.9 %copy-start.11 = (bf16[512,1024]{1,0:T(8,128)(2,1)S(1)}, bf16[512,1024]{1,0:T(8,128)(2,1)}, u32[]{:S(2)}) copy-start(bf16[512,1024]{1,0:T(8,128)(2,1)} %copy-done.9) | copy-start | bytes 3145732
  21.8 12.3 %copy-start.1 = (bf16[1024,1024]{1,0:T(8,128)(2,1)S(1)}, bf16[1024,1024]{1,0:T(8,128)(2,1)}, u32[]{:S(2)}) copy-start(bf16[1024,1024]{1,0:T(8,128)(2,1)} %wg_ref.1) | copy-start | bytes 6291460
  21.8 6.1 %collective-permute-start.10 = (bf16[144,512]{1,0:T(8,128)(2,1)S(1)}, bf16[144,512]{1,0:T(8,128)(2,1)S(1)}, u32[]{:S(2)}, u32[]{:S(2)}) collective-permute-start(bf16[144,512]{1,0:T(8,128)(2,1)S(1)} %get-tuple-element.45), channel_id=1, source_target_pairs={{0,2},{2,0},{4,6},{6,4},{8,10},{10,8},{12,14},{14,12},{1,3},{3,1},... | collective-permute-start | bytes 442376 | tf_op jit(solution)/shard_map/ppermute | solution.py:476
  28.0 8.1 %collective-permute-start.11 = (bf16[144,512]{1,0:T(8,128)(2,1)S(1)}, bf16[144,512]{1,0:T(8,128)(2,1)S(1)}, u32[]{:S(2)}, u32[]{:S(2)}) collective-permute-start(bf16[144,512]{1,0:T(8,128)(2,1)S(1)} %pair_own.1.pair_ref), channel_id=1, source_target_pairs={{0,4},{2,6},{4,8},{6,10},{8,12},{10,14},{5,1},{7,3},{9,5},{11,7},{... | collective-permute-start | bytes 442376 | tf_op jit(solution)/shard_map/ppermute | solution.py:464
  33.5 11.1 %collective-permute-start.3 = (f32[8,1024]{1,0:T(8,128)S(1)}, f32[8,1024]{1,0:T(8,128)S(1)}, u32[]{:S(2)}, u32[]{:S(2)}) collective-permute-start(f32[8,1024]{1,0:T(8,128)S(1)} %concatenate.7.small_ref.refs_6_), channel_id=1, source_target_pairs={{0,1},{1,0},{2,3},{3,2},{4,5},{5,4},{6,7},{7,6},{8,9},{9,8},{10,11... | collective-permute-start | bytes 98312 | tf_op jit(solution)/shard_map/ppermute | solution.py:615
  33.6 11.9 %collective-permute-start.2 = (bf16[16,1024]{1,0:T(8,128)(2,1)S(1)}, bf16[16,1024]{1,0:T(8,128)(2,1)S(1)}, u32[]{:S(2)}, u32[]{:S(2)}) collective-permute-start(bf16[16,1024]{1,0:T(8,128)(2,1)S(1)} %bitcast.9), channel_id=1, source_target_pairs={{0,1},{1,0},{2,3},{3,2},{4,5},{5,4},{6,7},{7,6},{8,9},{9,8},{10,11... | collective-permute-start | bytes 98312 | tf_op jit(solution)/shard_map/ppermute | solution.py:615
  34.1 42.3 %collective-permute-start.8 = (bf16[1024,1024]{1,0:T(8,128)(2,1)S(1)}, bf16[1024,1024]{1,0:T(8,128)(2,1)S(1)}, u32[]{:S(2)}, u32[]{:S(2)}) collective-permute-start(bf16[1024,1024]{1,0:T(8,128)(2,1)S(1)} %copy-done.1), channel_id=1, source_target_pairs={{0,1},{1,0},{2,3},{3,2},{4,5},{5,4},{6,7},{7,6},{8,9},{9,8},{10,11... | collective-permute-start | bytes 6291464 | tf_op jit(solution)/shard_map/ppermute | solution.py:615
  36.2 8.2 %copy-start.2 = (bf16[1024,1024]{1,0:T(8,128)(2,1)S(1)}, bf16[1024,1024]{1,0:T(8,128)(2,1)}, u32[]{:S(2)}) copy-start(bf16[1024,1024]{1,0:T(8,128)(2,1)} %refs_7_.1) | copy-start | bytes 6291460
  36.2 8.2 %collective-permute-start.12 = (bf16[144,512]{1,0:T(8,128)(2,1)S(1)}, bf16[144,512]{1,0:T(8,128)(2,1)S(1)}, u32[]{:S(2)}, u32[]{:S(2)}) collective-permute-start(bf16[144,512]{1,0:T(8,128)(2,1)S(1)} %chain_own.1), channel_id=1, source_target_pairs={{0,8},{2,10},{4,12},{6,14},{9,1},{11,3},{13,5},{15,7},{16,24},{18,... | collective-permute-start | bytes 442376 | tf_op jit(solution)/shard_map/ppermute | solution.py:464
  44.4 34.1 %collective-permute-start.9 = (bf16[1024,1024]{1,0:T(8,128)(2,1)S(1)}, bf16[1024,1024]{1,0:T(8,128)(2,1)S(1)}, u32[]{:S(2)}, u32[]{:S(2)}) collective-permute-start(bf16[1024,1024]{1,0:T(8,128)(2,1)S(1)} %copy-done.2), channel_id=1, source_target_pairs={{0,1},{1,0},{2,3},{3,2},{4,5},{5,4},{6,7},{7,6},{8,9},{9,8},{10,11... | collective-permute-start | bytes 6291464 | tf_op jit(solution)/shard_map/ppermute | solution.py:615
  44.5 18.1 %collective-permute-start.13 = (bf16[128,512]{1,0:T(8,128)(2,1)S(1)}, bf16[128,512]{1,0:T(8,128)(2,1)S(1)}, u32[]{:S(2)}, u32[]{:S(2)}) collective-permute-start(bf16[128,512]{1,0:T(8,128)(2,1)S(1)} %get-tuple-element.40), channel_id=1, source_target_pairs={{0,2},{2,0},{4,6},{6,4},{8,10},{10,8},{12,14},{14,12},{1,3},{3,1},... | collective-permute-start | bytes 393224 | tf_op jit(solution)/shard_map/ppermute | solution.py:503
  52.5 5.5 %collective-permute-start.4 = (bf16[144,512]{1,0:T(8,128)(2,1)S(1)}, bf16[144,512]{1,0:T(8,128)(2,1)S(1)}, u32[]{:S(2)}, u32[]{:S(2)}) collective-permute-start(bf16[144,512]{1,0:T(8,128)(2,1)S(1)} %get-tuple-element.47), channel_id=1, source_target_pairs={{0,2},{2,0},{4,6},{6,4},{8,10},{10,8},{12,14},{14,12},{1,3},{3,1},... | collective-permute-start | bytes 442376 | tf_op jit(solution)/shard_map/ppermute | solution.py:476
  58.1 7.5 %collective-permute-start.5 = (bf16[144,512]{1,0:T(8,128)(2,1)S(1)}, bf16[144,512]{1,0:T(8,128)(2,1)S(1)}, u32[]{:S(2)}, u32[]{:S(2)}) collective-permute-start(bf16[144,512]{1,0:T(8,128)(2,1)S(1)} %pair_other.1.pair_ref), channel_id=1, source_target_pairs={{0,4},{2,6},{4,8},{6,10},{8,12},{10,14},{5,1},{7,3},{9,5},{11,7},{... | collective-permute-start | bytes 442376 | tf_op jit(solution)/shard_map/ppermute | solution.py:464
  65.7 8.8 %collective-permute-start.6 = (bf16[144,512]{1,0:T(8,128)(2,1)S(1)}, bf16[144,512]{1,0:T(8,128)(2,1)S(1)}, u32[]{:S(2)}, u32[]{:S(2)}) collective-permute-start(bf16[144,512]{1,0:T(8,128)(2,1)S(1)} %chain_other.1), channel_id=1, source_target_pairs={{0,8},{2,10},{4,12},{6,14},{9,1},{11,3},{13,5},{15,7},{16,24},{18,... | collective-permute-start | bytes 442376 | tf_op jit(solution)/shard_map/ppermute | solution.py:464
  74.6 5.0 %collective-permute-start.7 = (bf16[128,512]{1,0:T(8,128)(2,1)S(1)}, bf16[128,512]{1,0:T(8,128)(2,1)S(1)}, u32[]{:S(2)}, u32[]{:S(2)}) collective-permute-start(bf16[128,512]{1,0:T(8,128)(2,1)S(1)} %get-tuple-element.34), channel_id=1, source_target_pairs={{0,2},{2,0},{4,6},{6,4},{8,10},{10,8},{12,14},{14,12},{1,3},{3,1},... | collective-permute-start | bytes 393224 | tf_op jit(solution)/shard_map/ppermute | solution.py:503
  82.6 2.0 %collective-permute-start.14 = (bf16[512,512]{1,0:T(8,128)(2,1)S(1)}, bf16[512,512]{1,0:T(8,128)(2,1)S(1)}, u32[]{:S(2)}, u32[]{:S(2)}) collective-permute-start(bf16[512,512]{1,0:T(8,128)(2,1)S(1)} %get-tuple-element.44), channel_id=1, source_target_pairs={{0,1},{1,0},{2,3},{3,2},{4,5},{5,4},{6,7},{7,6},{8,9},{9,8},{10,11... | collective-permute-start | bytes 1572872 | tf_op jit(solution)/shard_map/ppermute | solution.py:615
  (7 other events, 8.0 us)

commit v2 on v1

v2 whole, which is shorter than its diff:
```python
import functools

import jax
import jax.numpy as jnp
from jax import lax
from jax.experimental import pallas as pl
from jax.experimental.pallas import tpu as pltpu
from jax.sharding import PartitionSpec as P

F32 = jnp.float32
BF16 = jnp.bfloat16
EPS = 1e-05
HALO = 16
EXTRA = 16
CHUNK = 128
TILE = 256
MB = 1024 * 1024


def call(
    kernel, name, *, vmem, cost, scalars=(), grid=(), in_specs, out_specs, out_shape, scratch=(), after=()
):
    flops, moved, special = cost
    first = len(scalars) + len(in_specs)

    def body(*refs):
        kernel(*refs[:first], *refs[first + len(after) :])

    run = pl.pallas_call(
        body,
        grid_spec=pltpu.PrefetchScalarGridSpec(
            num_scalar_prefetch=len(scalars),
            grid=grid,
            in_specs=list(in_specs) + [pl.BlockSpec(memory_space=pl.ANY)] * len(after),
            out_specs=out_specs,
            scratch_shapes=scratch,
        ),
        out_shape=out_shape,
        compiler_params=pltpu.CompilerParams(
            vmem_limit_bytes=vmem * MB, dimension_semantics=("arbitrary",) * len(grid)
        ),
        cost_estimate=pl.CostEstimate(flops=flops, bytes_accessed=moved, transcendentals=special),
        name=name,
    )
    return lambda *arrays: run(*arrays, *after)


def micros(us):
    return (int(us * 1.1e9), int(us * 1e6), 0)


def dot(a, b):
    return jnp.dot(a, b, preferred_element_type=F32)


def dot_nt(a, b):
    return lax.dot_general(a, b, (((1,), (1,)), ((), ())), preferred_element_type=F32)


def dot_tn(a, b):
    return lax.dot_general(a, b, (((0,), (0,)), ((), ())), preferred_element_type=F32)


def flip_matrix(size):
    rows = lax.broadcasted_iota(jnp.int32, (size, size), 0)
    columns = lax.broadcasted_iota(jnp.int32, (size, size), 1)
    return jnp.where(rows + columns == size - 1, 1.0, 0.0).astype(BF16)


def flip_both(value):
    rows, width = value.shape
    turned = dot(flip_matrix(rows), value).astype(BF16)
    anti = flip_matrix(TILE)
    count = width // TILE
    blocks = [
        dot(turned[:, (count - 1 - k) * TILE : (count - k) * TILE], anti).astype(BF16)
        for k in range(count)
    ]
    return jnp.concatenate(blocks, axis=1)


def silu(v):
    half = 0.5 * v
    return half + half * jnp.tanh(half)


def two_parts(value):
    high = value.astype(BF16)
    low = (value - high.astype(F32)).astype(BF16)
    return jnp.concatenate([high, low], axis=1)


def spread(value, width, head_size, first_head):
    heads = value.shape[1]
    source = lax.broadcasted_iota(jnp.int32, (2 * heads, width), 0)
    source = jnp.where(source >= heads, source - heads, source)
    target = lax.broadcasted_iota(jnp.int32, (2 * heads, width), 1) // head_size + first_head
    onehot = jnp.where(source == target, 1.0, 0.0).astype(BF16)
    return dot(two_parts(value), onehot)


def prepare_kernel(
    back_ref,
    tokens_hbm,
    hidden_hbm,
    emb_hbm,
    conv_ref,
    gain_ref,
    bias_ref,
    rate_ref,
    out_ref,
    tail_ref,
    small_ref,
    tokens_ref,
    hidden_ref,
    emb_ref,
    sems,
):
    rows = hidden_ref.shape[0]
    kinds = emb_ref.shape[0]
    taps, inner = conv_ref.shape
    heads = bias_ref.shape[1]
    count = rows // CHUNK
    back = back_ref[0] == 1
    copies = [
        pltpu.make_async_copy(tokens_hbm, tokens_ref, sems.at[0]),
        pltpu.make_async_copy(emb_hbm, emb_ref, sems.at[1]),
    ]
    for r in range(count):
        part = pl.ds(r * CHUNK, CHUNK)
        copies.append(pltpu.make_async_copy(hidden_hbm.at[part, :], hidden_ref.at[part, :], sems.at[2 + r]))
    for copy in copies:
        copy.start()
    small_ref[:taps, :] = conv_ref[...]
    small_ref[taps : taps + 1, :] = gain_ref[...]
    small_ref[taps + 1 :, :] = jnp.zeros((SMALL_ROWS - taps - 1, inner), F32)
    small_ref[taps + 1 : taps + 2, :heads] = bias_ref[...]
    small_ref[taps + 2 : taps + 3, :heads] = rate_ref[...]
    copies[0].wait()
    copies[1].wait()
    kind = lax.broadcasted_iota(jnp.int32, (kinds, rows), 0)
    onehot = jnp.where(kind == tokens_ref[...], 1.0, 0.0).astype(BF16)
    for r in range(count):
        copies[2 + r].wait()
        low, high = r * CHUNK, (r + 1) * CHUNK
        base = dot_tn(onehot[:, low:high], emb_ref[...])
        merged = (hidden_ref[low:high, :].astype(F32) + base).astype(BF16).astype(F32)
        mean = jnp.mean(merged * merged, axis=-1, keepdims=True)
        normed = (merged * lax.rsqrt(mean + EPS)).astype(BF16)

        @pl.when(back)
        def _():
            turned = flip_both(normed)
            out_ref[rows - high : rows - low, :] = turned
            if r == 0:
                tail_ref[...] = turned[CHUNK - HALO :, :]

        @pl.when(jnp.logical_not(back))
        def _():
            out_ref[low:high, :] = normed
            if r == count - 1:
                tail_ref[...] = normed[CHUNK - HALO :, :]


def prepare_call(back, tokens, hidden, embedding, conv, gain, bias, rate):
    rows, width = hidden.shape
    inner = conv.shape[1]
    vmem = pl.BlockSpec(memory_space=pltpu.VMEM)
    hbm = pl.BlockSpec(memory_space=pltpu.HBM)
    return call(
        prepare_kernel,
        "prepare",
        vmem=12,
        cost=micros(1.5),
        scalars=(back,),
        grid=(),
        in_specs=[hbm] * 3 + [vmem] * 4,
        out_specs=[vmem] * 3,
        out_shape=[
            jax.ShapeDtypeStruct((rows, width), BF16),
            jax.ShapeDtypeStruct((HALO, width), BF16),
            jax.ShapeDtypeStruct((SMALL_ROWS, inner), F32),
        ],
        scratch=[
            pltpu.VMEM((1, rows), jnp.int32),
            pltpu.VMEM((rows, width), BF16),
            pltpu.VMEM(embedding.shape, BF16),
            pltpu.SemaphoreType.DMA((2 + rows // CHUNK,)),
        ],
    )(
        back,
        tokens.reshape(1, rows),
        hidden,
        embedding,
        conv,
        gain.reshape(1, -1),
        bias.reshape(1, -1),
        rate.reshape(1, -1),
    )


def gate_kernel(rows_ref, wg_ref, out_ref):
    gate = dot(rows_ref[...], wg_ref[...]).astype(BF16).astype(F32)
    out_ref[...] = silu(gate).astype(BF16)


def gate_call(tag, normed, w_gate, after=()):
    rows, width = normed.shape
    inner = w_gate.shape[1]
    return call(
        gate_kernel,
        "gate_" + tag,
        vmem=8,
        cost=micros(2.4),
        grid=(inner // TILE,),
        in_specs=[
            pl.BlockSpec((rows, width), lambda g: (0, 0)),
            pl.BlockSpec((width, TILE), lambda g: (0, g)),
        ],
        out_specs=pl.BlockSpec((rows, TILE), lambda g: (0, g)),
        out_shape=jax.ShapeDtypeStruct((rows, inner), BF16),
        after=after,
    )(normed, w_gate)


def conv_silu(rows_ref, weights, rows):
    taps = weights.shape[0]
    total = None
    for k in range(taps):
        offset = HALO - (taps - 1) + k
        term = weights[k : k + 1, :] * rows_ref[offset : offset + rows, :]
        total = term if total is None else total + term
    return silu(total).astype(BF16)


def maps_kernel(place_ref, normed_ref, halo_ref, ws_ref, cs_ref, bc_ref, bt_ref, rows_ref):
    rows = normed_ref.shape[0]
    states = bc_ref.shape[1] // 2
    before = dot(halo_ref[...], ws_ref[...]).astype(BF16).astype(F32)
    rows_ref[:HALO, :] = jnp.where(place_ref[0] >= 1, before, 0.0)
    rows_ref[HALO:, :] = dot(normed_ref[...], ws_ref[...]).astype(BF16).astype(F32)
    state_conv = conv_silu(rows_ref, cs_ref[...], rows)
    bc_ref[...] = state_conv
    bt_ref[...] = state_conv[:, :states].astype(F32).T.astype(BF16)


def maps_call(place, normed, halo, w_state, conv_state, after=()):
    rows = normed.shape[0]
    both = w_state.shape[1]
    vmem = pl.BlockSpec(memory_space=pltpu.VMEM)
    return call(
        maps_kernel,
        "maps",
        vmem=8,
        cost=micros(1.5),
        scalars=(place,),
        in_specs=[vmem] * 4,
        out_specs=[vmem] * 2,
        out_shape=[
            jax.ShapeDtypeStruct((rows, both), BF16),
            jax.ShapeDtypeStruct((both // 2, rows), BF16),
        ],
        scratch=[pltpu.VMEM((rows + HALO, both), F32)],
        after=after,
    )(place, normed, halo, w_state, conv_state)


def local_kernel(
    head_size,
    place_ref,
    parity_ref,
    normed_ref,
    halo_ref,
    bt_ref,
    wi_ref,
    wt_ref,
    small_ref,
    xs_ref,
    cum_ref,
    cumt_ref,
    send_ref,
    mine_ref,
    rows_ref,
    step_ref,
):
    rows = normed_ref.shape[0]
    states = bt_ref.shape[0]
    heads = wt_ref.shape[0]
    taps = SMALL_TAPS
    tiles = pl.num_programs(0)
    g = pl.program_id(0)
    tile = tile_at(g, tiles, parity_ref)

    @pl.when(g == 0)
    def _():
        bias = small_ref[taps + 1 : taps + 2, :heads]
        rate = small_ref[taps + 2 : taps + 3, :heads]
        raw = dot_nt(normed_ref[...], wt_ref[...]) + bias
        step = jnp.maximum(raw, 0.0) + jnp.log1p(jnp.exp(-jnp.abs(raw)))
        step_ref[...] = step
        logdecay = -step * rate
        high = logdecay.astype(BF16)
        rest = logdecay - high.astype(F32)
        mid = rest.astype(BF16)
        low = (rest - mid.astype(F32)).astype(BF16)
        parts = jnp.concatenate([high, mid, low], axis=1)
        to = lax.broadcasted_iota(jnp.int32, (rows, rows), 0)
        frm = lax.broadcasted_iota(jnp.int32, (rows, rows), 1)
        sums = dot(jnp.where(to >= frm, 1.0, 0.0).astype(BF16), parts)
        cum = sums[:, :heads] + sums[:, heads : 2 * heads] + sums[:, 2 * heads :]
        cum_ref[...] = cum
        cumt_ref[...] = cum.T

    weights = wi_ref[...]
    before = dot(halo_ref[...], weights).astype(BF16).astype(F32)
    rows_ref[:HALO, :] = jnp.where(place_ref[0] >= 1, before, 0.0)
    rows_ref[HALO:, :] = dot(normed_ref[...], weights).astype(BF16).astype(F32)
    columns = pl.ds(pl.multiple_of(tile * TILE, TILE), TILE)
    x = conv_silu(rows_ref, small_ref[:taps, columns], rows).astype(F32)
    first = tile * (TILE // head_size)
    xs = x * spread(step_ref[...], TILE, head_size, first)
    xs_ref[...] = xs.astype(BF16)
    cum = cum_ref[...]
    total = cum[rows - 1 :, :]
    left = spread(jnp.exp(total - cum), TILE, head_size, first)
    state = dot(bt_ref[...], (xs * left).astype(BF16))
    decay = spread(jnp.exp(total), TILE, head_size, first)

    @pl.when(g < tiles // 2)
    def _():
        write_payload(send_ref, state, decay)

    @pl.when(g >= tiles // 2)
    def _():
        write_payload(mine_ref, state, decay)


def tile_at(g, tiles, parity_ref):
    return lax.rem(g + (1 - parity_ref[0]) * (tiles // 2), tiles)


SMALL_TAPS = 4
SMALL_ROWS = 8


def local_call(tag, place, parity, normed, halo, bt, w_inner, w_step_t, small, after=()):
    rows, width = normed.shape
    inner = w_inner.shape[1]
    heads = w_step_t.shape[0]
    states = bt.shape[0]
    tiles = inner // TILE
    half = tiles // 2

    def whole(a):
        return pl.BlockSpec(a.shape, lambda g, place, parity: (0, 0))

    def tile(count):
        return pl.BlockSpec((count, TILE), lambda g, place, parity: (0, tile_at(g, tiles, parity)))

    payload = (states + EXTRA, TILE)
    return call(
        functools.partial(local_kernel, inner // heads),
        "local_" + tag,
        vmem=12,
        cost=micros(5.0),
        scalars=(place, parity),
        grid=(tiles,),
        in_specs=[whole(normed), whole(halo), whole(bt), tile(width), whole(w_step_t), whole(small)],
        out_specs=[
            tile(rows),
            pl.BlockSpec((rows, heads), lambda g, place, parity: (0, 0)),
            pl.BlockSpec((heads, rows), lambda g, place, parity: (0, 0)),
            pl.BlockSpec(payload, lambda g, place, parity: (0, jnp.minimum(g, half - 1))),
            pl.BlockSpec(payload, lambda g, place, parity: (0, jnp.maximum(g - half, 0))),
        ],
        out_shape=[
            jax.ShapeDtypeStruct((rows, inner), BF16),
            jax.ShapeDtypeStruct((rows, heads), F32),
            jax.ShapeDtypeStruct((heads, rows), F32),
            jax.ShapeDtypeStruct((states + EXTRA, inner // 2), BF16),
            jax.ShapeDtypeStruct((states + EXTRA, inner // 2), BF16),
        ],
        scratch=[pltpu.VMEM((rows + HALO, TILE), F32), pltpu.VMEM((rows, heads), F32)],
        after=after,
    )(place, parity, normed, halo, bt, w_inner, w_step_t, small)


def inside_kernel(head_size, xs_ref, bc_ref, cum_ref, cumt_ref, y_ref, state_ref, prev_ref):
    length, inner = xs_ref.shape
    states = bc_ref.shape[1] // 2
    heads = cum_ref.shape[1]

    @pl.when(pl.program_id(0) == 0)
    def _():
        state_ref[...] = jnp.zeros_like(state_ref)
        prev_ref[...] = jnp.zeros_like(prev_ref)

    bmat = bc_ref[:, :states]
    cmat = bc_ref[:, states:]
    to = lax.broadcasted_iota(jnp.int32, (length, length), 0)
    frm = lax.broadcasted_iota(jnp.int32, (length, length), 1)
    scores = jnp.where(to >= frm, dot_nt(cmat, bmat), 0.0)
    cum = cum_ref[...]
    cumt = cumt_ref[...]
    last = length - 1
    end = cum[last:, :]
    since = spread(jnp.exp(cum - prev_ref[...]), inner, head_size, 0)
    left = spread(jnp.exp(end - cum), inner, head_size, 0)
    state = state_ref[...]
    carried = dot(cmat, state.astype(BF16)) * since
    xs = xs_ref[...]
    scaled = (xs.astype(F32) * left).astype(BF16)
    state_ref[...] = state * since[last:, :] + dot_tn(bmat, scaled)
    prev_ref[...] = end
    pair = 2 * head_size
    lane = lax.broadcasted_iota(jnp.int32, (length, pair), 1)
    for p in range(heads // 2):
        weights = []
        for h in (2 * p, 2 * p + 1):
            apart = jnp.minimum(cum[:, h : h + 1] - cumt[h : h + 1, :], 0.0)
            weights.append((jnp.exp(apart) * scores).astype(BF16))
        mine = xs[:, p * pair : (p + 1) * pair]
        none = jnp.zeros_like(mine)
        stacked = jnp.concatenate(
            [jnp.where(lane < head_size, mine, none), jnp.where(lane < head_size, none, mine)], axis=0
        )
        inside = dot(jnp.concatenate(weights, axis=1), stacked)
        y_ref[:, p * pair : (p + 1) * pair] = (
            inside + carried[:, p * pair : (p + 1) * pair]
        ).astype(BF16)


def inside_call(tag, xs, bc, cum, cumt, after=()):
    rows, inner = xs.shape
    heads = cum.shape[1]
    both = bc.shape[1]

    def block(width):
        return pl.BlockSpec((CHUNK, width), lambda c: (c, 0))

    return call(
        functools.partial(inside_kernel, inner // heads),
        "inside_" + tag,
        vmem=8,
        cost=micros(3.2),
        grid=(rows // CHUNK,),
        in_specs=[
            block(inner),
            block(both),
            block(heads),
            pl.BlockSpec((heads, CHUNK), lambda c: (0, c)),
        ],
        out_specs=block(inner),
        out_shape=jax.ShapeDtypeStruct((rows, inner), BF16),
        scratch=[pltpu.VMEM((both // 2, inner), F32), pltpu.VMEM((1, heads), F32)],
        after=after,
    )(xs, bc, cum, cumt)


def parts_of(ref, known=None):
    states = ref.shape[0] - EXTRA
    state = ref[:states, :].astype(F32)
    extra = ref[states:, :].astype(F32)
    decay = extra[:1] + extra[1:2]
    if known is None:
        return state, decay
    return jnp.where(known, state, 0.0), jnp.where(known, decay, 0.0)


def write_payload(out_ref, state, decay):
    states = state.shape[0]
    out_ref[:states, :] = state.astype(BF16)
    decay = jnp.broadcast_to(decay, (EXTRA, decay.shape[1]))
    high = decay.astype(BF16).astype(F32)
    place = lax.broadcasted_iota(jnp.int32, decay.shape, 0)
    out_ref[states:, :] = jnp.where(place == 0, high, decay - high).astype(BF16)


def pair_kernel(place_ref, mine_ref, other_ref, out_ref):
    mine, mine_a = parts_of(mine_ref)
    other, other_a = parts_of(other_ref)
    is_first = lax.rem(place_ref[0], 2) == 0
    early = jnp.where(is_first, mine, other)
    late = jnp.where(is_first, other, mine)
    late_a = jnp.where(is_first, other_a, mine_a)
    write_payload(out_ref, late_a * early + late, mine_a * other_a)


def chain_kernel(reach, place_ref, pair_ref, before_ref, out_ref):
    pair, pair_a = parts_of(pair_ref)
    before, before_a = parts_of(before_ref, place_ref[0] >= reach)
    write_payload(out_ref, pair_a * before + pair, pair_a * before_a)


def longer_kernel(reach, farther_reach, place_ref, before_ref, farther_ref, out_ref):
    before, before_a = parts_of(before_ref, place_ref[0] >= reach)
    farther, farther_a = parts_of(farther_ref, place_ref[0] >= farther_reach)
    write_payload(out_ref, before + before_a * farther, before_a * farther_a)


def entry_kernel(reach, farther_reach, place_ref, mine_ref, other_ref, before_ref, farther_ref, keep_ref, send_ref):
    mine, mine_a = parts_of(mine_ref)
    other, other_a = parts_of(other_ref)
    before, before_a = parts_of(before_ref, place_ref[0] >= reach)
    farther, _ = parts_of(farther_ref, place_ref[0] >= farther_reach)
    is_first = lax.rem(place_ref[0], 2) == 0
    entry_first = before + before_a * farther
    early = jnp.where(is_first, mine, other)
    early_a = jnp.where(is_first, mine_a, other_a)
    entry_second = early_a * entry_first + early
    keep_ref[...] = jnp.where(is_first, entry_first, entry_second).astype(BF16)
    send_ref[...] = jnp.where(is_first, entry_second, entry_first).astype(BF16)


def small_call(kernel, name, place, arrays, shapes, after=()):
    vmem = pl.BlockSpec(memory_space=pltpu.VMEM)
    return call(
        kernel,
        name,
        vmem=4,
        cost=micros(0.5),
        scalars=(place,),
        in_specs=[vmem] * len(arrays),
        out_specs=[vmem] * len(shapes),
        out_shape=[jax.ShapeDtypeStruct(s, BF16) for s in shapes],
        after=after,
    )(place, *arrays)


def onward(value, by):
    count = lax.axis_size("seq")
    pairs = []
    for i in range(count):
        up = (i + by, 0) if i + by < count else (i, 1)
        down = (i - by, 1) if i - by >= 0 else (i, 0)
        pairs += [(2 * i, 2 * up[0] + up[1]), (2 * i + 1, 2 * down[0] + down[1])]
    return lax.ppermute(value, ("seq", "ch"), pairs)


class Chain:
    def __init__(self, tag, place, send, mine):
        self.tag, self.place, self.mine = tag, place, mine
        self.count = lax.axis_size("seq")
        self.swap = [(i, i ^ 1) for i in range(self.count)]
        self.other = lax.ppermute(send, "seq", self.swap)
        self.before = self.farther = None
        self.reach = self.farther_reach = 0
        self.apart = 2

    def pair(self, after):
        (self.pair_state,) = small_call(
            pair_kernel, "pair_" + self.tag, self.place, [self.mine, self.other], [self.mine.shape], after
        )
        self.running = self.pair_state
        self.hop()
        return self.pair_state

    def hop(self):
        if self.apart < self.count:
            self.arrived = onward(self.running, self.apart)

    def middle(self, after):
        while self.apart * 2 < self.count:
            self.take(after)
            (self.running,) = small_call(
                functools.partial(chain_kernel, self.reach),
                "chain_" + self.tag,
                self.place,
                [self.pair_state, self.before],
                [self.mine.shape],
                after,
            )
            self.apart *= 2
            self.hop()
        return self.running

    def take(self, after=()):
        if self.before is None:
            self.before, self.reach = self.arrived, self.apart
        else:
            (self.before,) = small_call(
                functools.partial(longer_kernel, self.reach, self.apart),
                "longer_" + self.tag,
                self.place,
                [self.before, self.arrived],
                [self.mine.shape],
                after,
            )
            self.reach = 0

    def entry(self, after):
        shape = self.mine.shape
        if self.apart < self.count:
            if self.before is None:
                self.before, self.reach = self.arrived, self.apart
                self.farther, self.farther_reach = self.arrived, self.count
            else:
                self.farther, self.farther_reach = self.arrived, self.apart
        else:
            self.before = self.farther = self.mine
            self.reach = self.farther_reach = self.count
        half = (shape[0] - EXTRA, shape[1])
        keep, out = small_call(
            functools.partial(entry_kernel, self.reach, self.farther_reach),
            "entry_" + self.tag,
            self.place,
            [self.mine, self.other, self.before, self.farther],
            [half, half],
            after,
        )
        return keep, lax.ppermute(out, "seq", self.swap)


def gated_part(head_size, swap, y_ref, bc_ref, cum_ref, keep_ref, other_ref, gate_ref, small_ref, wo_ref):
    inner = y_ref.shape[1]
    states = bc_ref.shape[1] // 2
    cmat = bc_ref[:, states:]
    keep = keep_ref[...]
    other = other_ref[...]
    entry = jnp.concatenate([jnp.where(swap, other, keep), jnp.where(swap, keep, other)], axis=1)
    carried = dot(cmat, entry) * spread(jnp.exp(cum_ref[...]), inner, head_size, 0)
    gated = (y_ref[...].astype(F32) + carried) * gate_ref[...].astype(F32)
    squares = jnp.sum(gated * gated, axis=-1, keepdims=True)
    gain = small_ref[SMALL_TAPS : SMALL_TAPS + 1, :]
    return dot((gated * gain).astype(BF16), wo_ref[...]), squares


def part_kernel(head_size, back_ref, parity_ref, *refs):
    *ins, out_ref, sq_ref = refs
    result, squares = gated_part(head_size, parity_ref[0] == 1, *ins)
    out_ref[...] = result
    sq_ref[...] = jnp.broadcast_to(squares, sq_ref.shape)


def finish_kernel(head_size, full_width, back_ref, parity_ref, *refs):
    *ins, part_ref, psq_ref, own_ref, send_ref = refs
    result, squares = gated_part(head_size, parity_ref[0] == 1, *ins)
    squares = squares + psq_ref[:, :1]
    result = (result + part_ref[...]) * lax.rsqrt(squares / full_width + EPS)
    result = result.astype(BF16)
    half = own_ref.shape[1]

    @pl.when(back_ref[0] == 1)
    def _():
        turned = flip_both(result)
        own_ref[...] = turned[:, half:]
        send_ref[...] = turned[:, :half]

    @pl.when(back_ref[0] != 1)
    def _():
        own_ref[...] = result[:, :half]
        send_ref[...] = result[:, half:]


def finish_call(back, parity, y, bc, cum, keep, other, gate, small, w_output, full_width=None, partial=None, after=()):
    rows, inner = y.shape
    width = w_output.shape[1]
    half = width // 2
    heads = cum.shape[1]
    count = rows // TILE

    def block(columns):
        return pl.BlockSpec((TILE, columns), lambda r, back, parity: (r, 0))

    def whole(a):
        return pl.BlockSpec(a.shape, lambda r, back, parity: (0, 0))

    def turned(r, back, parity):
        return (jnp.where(back[0] == 1, count - 1 - r, r), 0)

    in_specs = [
        block(inner),
        block(bc.shape[1]),
        block(heads),
        whole(keep),
        whole(other),
        block(inner),
        whole(small),
        whole(w_output),
    ]
    arrays = [y, bc, cum, keep, other, gate, small, w_output]
    if partial is None:
        kernel = functools.partial(part_kernel, inner // heads)
        out_specs = [block(width), block(128)]
        out_shape = [jax.ShapeDtypeStruct((rows, width), F32), jax.ShapeDtypeStruct((rows, 128), F32)]
    else:
        kernel = functools.partial(finish_kernel, inner // heads, full_width)
        in_specs += [block(width), block(128)]
        arrays += list(partial)
        out_specs = [pl.BlockSpec((TILE, half), turned)] * 2
        out_shape = [jax.ShapeDtypeStruct((rows, half), BF16)] * 2
    return call(
        kernel,
        "part" if partial is None else "finish",
        vmem=16,
        cost=micros(3.5),
        scalars=(back, parity),
        grid=(count,),
        in_specs=in_specs,
        out_specs=out_specs,
        out_shape=out_shape,
        after=after,
    )(back, parity, *arrays)


def total_kernel(mine_ref, theirs_ref, out_ref):
    out_ref[...] = (mine_ref[...].astype(F32) + theirs_ref[...].astype(F32)).astype(BF16)


def total_call(mine, theirs):
    rows, half = mine.shape
    block = pl.BlockSpec((CHUNK, half), lambda r: (r, 0))
    return call(
        total_kernel,
        "total",
        vmem=4,
        cost=micros(0.8),
        grid=(rows // CHUNK,),
        in_specs=[block, block],
        out_specs=block,
        out_shape=jax.ShapeDtypeStruct((rows, half), BF16),
    )(mine, theirs)


def body(
    tokens,
    hidden,
    embedding,
    w_gate,
    w_inner,
    w_state,
    w_step,
    conv_inner,
    conv_state,
    step_bias,
    decay_rate,
    norm_gain,
    w_output,
):
    swap = [(0, 1), (1, 0)]

    def theirs(a):
        return lax.ppermute(a, "ch", swap)

    core = lax.axis_index("ch").astype(jnp.int32)
    index = lax.axis_index("seq").astype(jnp.int32)
    last = lax.axis_size("seq") - 1
    back = core.reshape(1)
    parity = (index % 2).reshape(1)
    place = (index + core * (last - 2 * index)).reshape(1)
    w_inner_2 = theirs(w_inner)
    normed, tail, small = prepare_call(
        back, tokens, hidden, embedding, conv_inner, norm_gain, step_bias, decay_rate
    )
    halo = onward(tail, 1)
    small_2 = theirs(small)
    w_step_t = w_step.T
    w_step_2 = theirs(w_step_t)
    w_gate_2 = theirs(w_gate)
    w_output_2 = theirs(w_output)
    gate_1 = gate_call("own", normed, w_gate)
    bc, bt = maps_call(place, normed, halo, w_state, conv_state, after=[gate_1])
    xs_1, cum_1, cumt_1, send_1, mine_1 = local_call(
        "own", place, parity, normed, halo, bt, w_inner, w_step_t, small
    )
    chain_1 = Chain("own", place, send_1, mine_1)
    xs_2, cum_2, cumt_2, send_2, mine_2 = local_call(
        "other", place, parity, normed, halo, bt, w_inner_2, w_step_2, small_2, after=[mine_1]
    )
    chain_2 = Chain("other", place, send_2, mine_2)
    done = chain_1.pair(after=[xs_2])
    y_1 = inside_call("own", xs_1, bc, cum_1, cumt_1, after=[done])
    done = chain_1.middle(after=[y_1])
    done = chain_2.pair(after=[done])
    entry_1 = chain_1.entry(after=[done])
    y_2 = inside_call("other", xs_2, bc, cum_2, cumt_2, after=[entry_1[0]])
    done = chain_2.middle(after=[y_2])
    gate_2 = gate_call("other", normed, w_gate_2, after=[done])
    entry_2 = chain_2.entry(after=[gate_2])
    partial = finish_call(
        back, parity, y_1, bc, cum_1, *entry_1, gate_1, small, w_output, after=[entry_2[0]]
    )
    full_width = float(w_inner.shape[1] * lax.axis_size("ch"))
    mine, send = finish_call(
        back, parity, y_2, bc, cum_2, *entry_2, gate_2, small_2, w_output_2, full_width, partial
    )
    return total_call(mine, theirs(send))


def solution(mesh):
    return jax.shard_map(
        body,
        mesh=mesh,
        in_specs=(
            P(("win", "seq")),
            P(("win", "seq"), None),
            P(),
            P(None, "ch"),
            P(None, "ch"),
            P(),
            P(None, "ch"),
            P(None, "ch"),
            P(),
            P("ch"),
            P("ch"),
            P("ch"),
            P("ch", None),
        ),
        out_specs=P(("win", "seq"), "ch"),
        check_vma=False,
    )
```

time: 86.4 us -> 71.5 us (0.83)
  starting transfers between devices: 32.9 us -> 17.9 us
  waiting for transfers between devices: 11.5 us -> 5.3 us
  local copies, waits for them, and re-layouts: 5.82 us -> 10.7 us
  Pallas kernels: 33.9 us -> 37 us
  other arithmetic: 1.01 us -> 0 us
    ppermute x5, starting transfers between devices: 25.4 us -> 11.4 us  [onward(): return lax.ppermute(value, ('seq', 'ch'), pairs)]
    unnamed x32 -> x38, local copies, waits for them, and re-layouts: 5.71 us -> 10.7 us
    ppermute x4, waiting for transfers between devices: 5.82 us -> 1.49 us  [the longest x2 1.48 us: entry(): return (keep, lax.ppermute(out, 'seq', self.swap))]
    pallas_call x16 -> x17, Pallas kernels: 33.9 us -> 37 us  [call(): return lambda *arrays: run(*arrays, *after)]
    ppermute x5, waiting for transfers between devices: 3.8 us -> 1.91 us  [onward(): return lax.ppermute(value, ('seq', 'ch'), pairs)]
    ppermute x4, starting transfers between devices: 6.3 us -> 5.03 us  [the longest x2 3.04 us: __init__(): self.other = lax.ppermute(send, 'seq', self.swap)]
    convert_element_type x1 -> x0, other arithmetic: 0.93 us -> none  [body(): return (mine.astype(F32) + theirs(send).astype(F32)).astype(BF16)]
  transfers between devices with their start and end apart: 15 -> 15, of which waited for: 7 -> 3; matrix products, arithmetic and copies ran while one was open for 0% -> 0% of each run, Pallas kernels for 36% -> 46%
where the time goes in v2:
time: 71.5 us; the launch traced here: 71.1 us
  Pallas kernels  37 us (52%)
  starting transfers between devices  17.9 us (25%)
  local copies, waits for them, and re-layouts  10.7 us (15%)
  waiting for transfers between devices  5.3 us (7%)
    pallas_call x17, Pallas kernels, call(): return lambda *arrays: run(*arrays, *after)  37 us
    ppermute x5, starting transfers between devices, onward(): return lax.ppermute(value, ('seq', 'ch'), pairs)  11.4 us
    unnamed x38, local copies, waits for them, and re-layouts  10.7 us
    ppermute x2, starting transfers between devices, __init__(): self.other = lax.ppermute(send, 'seq', self.swap)  3.04 us
    ppermute x2, starting transfers between devices, entry(): return (keep, lax.ppermute(out, 'seq', self.swap))  1.99 us
    ppermute x6, waiting for transfers between devices, theirs(): return lax.ppermute(a, 'ch', swap)  1.91 us
    ppermute x5, waiting for transfers between devices, onward(): return lax.ppermute(value, ('seq', 'ch'), pairs)  1.91 us
    ppermute x6, starting transfers between devices, theirs(): return lax.ppermute(a, 'ch', swap)  1.54 us
  transfers between devices with their start and end apart: 15, of which 3 were waited for; matrix products, arithmetic and copies ran while one was open for 0% of the time, Pallas kernels for 46%

profile of v2, /device:TPU:0, one launch (start us, length us, event | category | flops | bytes accessed | tf_op | source)
XLA Modules:
  0.0 71.1 jit_solution(12482388751020251755)
XLA Ops:
  0.5 1.2 %copy-done.3 = bf16[512,1024]{1,0:T(8,128)(2,1)S(1)} copy-done((bf16[512,1024]{1,0:T(8,128)(2,1)S(1)}, bf16[512,1024]{1,0:T(8,128)(2,1)}, u32[]{:S(2)}) %copy-start.3) | copy-done | bytes 1048600
  5.8 1.7 %prepare.1 = (bf16[512,1024]{1,0:T(8,128)(2,1)S(1)}, bf16[16,1024]{1,0:T(8,128)(2,1)S(1)}, f32[8,1024]{1,0:T(8,128)S(1)}) custom-call(s32[1]{0:T(128)} %bitcast.refs_0_, s32[1,512]{1,0:T(1,128)S(1)} %bitcast.11, bf16[512,1024]{1,0:T(8,128)(2,1)S(1)} %copy-done.3, bf16[4,1024]{1,0:T(4,128)(2,1)S(1)} %copy-done.7, f32[4,1024]{1,0:T(4,128)S(1)} %copy-done.6, ...), custom_call_target="tpu_custom_call" | custom-call | flops 1650000000 | bytes 1500000 | tf_op jit(solution)/shard_map/prepare/pallas_call | solution.py:45
  7.5 2.6 %collective-permute-start = (bf16[16,1024]{1,0:T(8,128)(2,1)S(1)}, bf16[16,1024]{1,0:T(8,128)(2,1)S(1)}, u32[]{:S(2)}, u32[]{:S(2)}) collective-permute-start(bf16[16,1024]{1,0:T(8,128)(2,1)S(1)} %get-tuple-element.29), channel_id=1, source_target_pairs={{0,2},{1,0},{2,4},{3,1},{4,6},{5,3},{6,8},{7,5},{8,10},{9,7},{10,1... | collective-permute-start | bytes 98312 | tf_op jit(solution)/shard_map/ppermute | solution.py:537
  10.7 2.2 %gate_own.1.refs_5_.refs_7_ = bf16[512,1024]{1,0:T(8,128)(2,1)S(1)} custom-call(bf16[512,1024]{1,0:T(8,128)(2,1)S(1)} %get-tuple-element.28.refs_0_.refs_1_.refs_2_, bf16[1024,1024]{1,0:T(8,128)(2,1)S(1)} %copy-done.1), custom_call_target="tpu_custom_call" | custom-call | flops 2640000000 | bytes 2400000 | tf_op jit(solution)/shard_map/gate_own/pallas_call | solution.py:45
  12.9 1.0 %copy-done.13 = bf16[512,1024]{1,0:T(8,128)(2,1)} copy-done((bf16[512,1024]{1,0:T(8,128)(2,1)}, bf16[512,1024]{1,0:T(8,128)(2,1)S(1)}, u32[]{:S(2)}) %copy-start.13) | copy-done | bytes 1048600
  15.4 1.2 %copy-done.14 = bf16[512,1024]{1,0:T(8,128)(2,1)S(1)} copy-done((bf16[512,1024]{1,0:T(8,128)(2,1)S(1)}, bf16[512,1024]{1,0:T(8,128)(2,1)}, u32[]{:S(2)}) %copy-start.14) | copy-done | bytes 1048600
  16.6 1.2 %copy-done.17 = bf16[512,1024]{1,0:T(8,128)(2,1)S(1)} copy-done((bf16[512,1024]{1,0:T(8,128)(2,1)S(1)}, bf16[512,1024]{1,0:T(8,128)(2,1)}, u32[]{:S(2)}) %copy-start.17) | copy-done | bytes 1048600
  19.7 7.2 %local_own.1 = (bf16[512,1024]{1,0:T(8,128)(2,1)S(1)}, f32[512,16]{1,0:T(8,128)S(1)}, f32[16,512]{1,0:T(8,128)S(1)}, bf16[144,512]{1,0:T(8,128)(2,1)S(1)}, bf16[144,512]{1,0:T(8,128)(2,1)S(1)}) custom-call(s32[1]{0:T(128)} %bitcast.2.refs_0_, s32[1]{0:T(128)} %bitcast.1.refs_1_, bf16[512,1024]{1,0:T(8,128)(2,1)S(1)} %copy-done.18, ...), custom_call_target="tpu_custom_call" | custom-call | flops 5500000256 | bytes 5000000 | tf_op jit(solution)/shard_map/local_own/pallas_call | solution.py:45
  26.9 1.6 %collective-permute-start.4 = (bf16[144,512]{1,0:T(8,128)(2,1)S(1)}, bf16[144,512]{1,0:T(8,128)(2,1)S(1)}, u32[]{:S(2)}, u32[]{:S(2)}) collective-permute-start(bf16[144,512]{1,0:T(8,128)(2,1)S(1)} %get-tuple-element.37), channel_id=1, source_target_pairs={{0,2},{2,0},{4,6},{6,4},{8,10},{10,8},{12,14},{14,12},{1,3},{3,1},... | collective-permute-start | bytes 442376 | tf_op jit(solution)/shard_map/ppermute | solution.py:545
  28.5 7.9 %local_other.1 = (bf16[512,1024]{1,0:T(8,128)(2,1)S(1)}, f32[512,16]{1,0:T(8,128)S(1)}, f32[16,512]{1,0:T(8,128)S(1)}, bf16[144,512]{1,0:T(8,128)(2,1)S(1)}, bf16[144,512]{1,0:T(8,128)(2,1)S(1)}) custom-call(s32[1]{0:T(128)} %bitcast.2.refs_0_, s32[1]{0:T(128)} %bitcast.1.refs_1_, bf16[512,1024]{1,0:T(8,128)(2,1)S(1)} %copy-done.18, ...), custom_call_target="tpu_custom_call" | custom-call | flops 5500000256 | bytes 5000000 | tf_op jit(solution)/shard_map/local_other/pallas_call | solution.py:45
  36.6 1.7 %collective-permute-start.5 = (bf16[144,512]{1,0:T(8,128)(2,1)S(1)}, bf16[144,512]{1,0:T(8,128)(2,1)S(1)}, u32[]{:S(2)}, u32[]{:S(2)}) collective-permute-start(bf16[144,512]{1,0:T(8,128)(2,1)S(1)} %pair_own.1.refs_4_.refs_1_), channel_id=1, source_target_pairs={{0,4},{1,0},{2,6},{3,2},{4,8},{5,1},{6,10},{7,3},{8,12},{9,5},{10,... | collective-permute-start | bytes 442376 | tf_op jit(solution)/shard_map/ppermute | solution.py:537
  38.3 1.4 %collective-permute-start.7 = (bf16[144,512]{1,0:T(8,128)(2,1)S(1)}, bf16[144,512]{1,0:T(8,128)(2,1)S(1)}, u32[]{:S(2)}, u32[]{:S(2)}) collective-permute-start(bf16[144,512]{1,0:T(8,128)(2,1)S(1)} %get-tuple-element.42), channel_id=1, source_target_pairs={{0,2},{2,0},{4,6},{6,4},{8,10},{10,8},{12,14},{14,12},{1,3},{3,1},... | collective-permute-start | bytes 442376 | tf_op jit(solution)/shard_map/ppermute | solution.py:545
  39.7 3.2 %inside_own.1.refs_3_.refs_2_ = bf16[512,1024]{1,0:T(8,128)(2,1)S(1)} custom-call(bf16[512,1024]{1,0:T(8,128)(2,1)S(1)} %get-tuple-element.38.refs_0_, bf16[512,256]{1,0:T(8,128)(2,1)S(1)} %get-tuple-element.34.refs_1_.refs_3_, f32[512,16]{1,0:T(8,128)S(1)} %get-tuple-element.39.refs_2_.refs_4_, f32[16,512]{1,0:T(8,128)S(1)} %get-tuple-element.40.refs_3_, ...), custom_call_target="tpu_custom_call" | custom-call | flops 3520000000 | bytes 3200000 | tf_op jit(solution)/shard_map/inside_own/pallas_call | solution.py:45
  43.0 2.7 %collective-permute-start.6 = (bf16[144,512]{1,0:T(8,128)(2,1)S(1)}, bf16[144,512]{1,0:T(8,128)(2,1)S(1)}, u32[]{:S(2)}, u32[]{:S(2)}) collective-permute-start(bf16[144,512]{1,0:T(8,128)(2,1)S(1)} %chain_own.1.refs_3_), channel_id=1, source_target_pairs={{0,8},{1,0},{2,10},{3,2},{4,12},{5,4},{6,14},{7,6},{8,9},{9,1},{10... | collective-permute-start | bytes 442376 | tf_op jit(solution)/shard_map/ppermute | solution.py:537
  46.4 1.9 %collective-permute-done.6.refs_4_ = bf16[144,512]{1,0:T(8,128)(2,1)S(1)} collective-permute-done((bf16[144,512]{1,0:T(8,128)(2,1)S(1)}, bf16[144,512]{1,0:T(8,128)(2,1)S(1)}, u32[]{:S(2)}, u32[]{:S(2)}) %collective-permute-start.6) | collective-permute-done | bytes 147488 | tf_op jit(solution)/shard_map/ppermute | solution.py:537
  48.5 3.2 %inside_other.1.refs_3_.refs_2_ = bf16[512,1024]{1,0:T(8,128)(2,1)S(1)} custom-call(bf16[512,1024]{1,0:T(8,128)(2,1)S(1)} %get-tuple-element.33.refs_3_.refs_0_, bf16[512,256]{1,0:T(8,128)(2,1)S(1)} %get-tuple-element.34.refs_1_.refs_3_, f32[512,16]{1,0:T(8,128)S(1)} %get-tuple-element.35.refs_2_.refs_4_, f32[16,512]{1,0:T(8,128)S(1)} %get-tuple-element.36.refs_3_, ...), custom_call_target="tpu_custom_call" | custom-call | flops 3520000000 | bytes 3200000 | tf_op jit(solution)/shard_map/inside_other/pallas_call | solution.py:45
  51.8 3.7 %collective-permute-start.9 = (bf16[144,512]{1,0:T(8,128)(2,1)S(1)}, bf16[144,512]{1,0:T(8,128)(2,1)S(1)}, u32[]{:S(2)}, u32[]{:S(2)}) collective-permute-start(bf16[144,512]{1,0:T(8,128)(2,1)S(1)} %chain_other.1.refs_2_), channel_id=1, source_target_pairs={{0,8},{1,0},{2,10},{3,2},{4,12},{5,4},{6,14},{7,6},{8,9},{9,1},{10... | collective-permute-start | bytes 442376 | tf_op jit(solution)/shard_map/ppermute | solution.py:537
  56.3 3.7 %gate_other.1.refs_5_.refs_7_ = bf16[512,1024]{1,0:T(8,128)(2,1)S(1)} custom-call(bf16[512,1024]{1,0:T(8,128)(2,1)S(1)} %copy-done.18, bf16[1024,1024]{1,0:T(8,128)(2,1)} %collective-permute-done.10.refs_1_, bf16[144,512]{1,0:T(8,128)(2,1)S(1)} %chain_other.1.refs_2_), custom_call_target="tpu_custom_call" | custom-call | flops 2640000000 | bytes 2400000 | tf_op jit(solution)/shard_map/gate_other/pallas_call | solution.py:45
  60.1 1.2 %collective-permute-start.11 = (bf16[128,512]{1,0:T(8,128)(2,1)S(1)}, bf16[128,512]{1,0:T(8,128)(2,1)S(1)}, u32[]{:S(2)}, u32[]{:S(2)}) collective-permute-start(bf16[128,512]{1,0:T(8,128)(2,1)S(1)} %get-tuple-element.45), channel_id=1, source_target_pairs={{0,2},{2,0},{4,6},{6,4},{8,10},{10,8},{12,14},{14,12},{1,3},{3,1},... | collective-permute-start | bytes 393224 | tf_op jit(solution)/shard_map/ppermute | solution.py:611
  61.3 2.4 %part.1 = (f32[512,1024]{1,0:T(8,128)S(1)}, f32[512,128]{1,0:T(8,128)S(1)}) custom-call(s32[1]{0:T(128)} %bitcast.refs_0_, s32[1]{0:T(128)} %bitcast.1.refs_1_, bf16[512,1024]{1,0:T(8,128)(2,1)S(1)} %inside_own.1.refs_3_.refs_2_, bf16[512,256]{1,0:T(8,128)(2,1)S(1)} %get-tuple-element.34.refs_1_.refs_3_, f32[512,16]{1,0:T(8,128)S(1)} %get-tuple-element.39.refs_2_.refs_4_, ...), custom_call_target="tpu_custom_call" | custom-call | flops 3849999872 | bytes 3500000 | tf_op jit(solution)/shard_map/part/pallas_call | solution.py:45
  63.7 1.5 %collective-permute-done.11.refs_6_ = bf16[128,512]{1,0:T(8,128)(2,1)S(1)} collective-permute-done((bf16[128,512]{1,0:T(8,128)(2,1)S(1)}, bf16[128,512]{1,0:T(8,128)(2,1)S(1)}, u32[]{:S(2)}, u32[]{:S(2)}) %collective-permute-start.11) | collective-permute-done | bytes 131104 | tf_op jit(solution)/shard_map/ppermute | solution.py:611
  65.2 2.5 %finish.1 = (bf16[512,512]{1,0:T(8,128)(2,1)S(1)}, bf16[512,512]{1,0:T(8,128)(2,1)S(1)}) custom-call(s32[1]{0:T(128)} %bitcast.refs_0_, s32[1]{0:T(128)} %bitcast.1.refs_1_, bf16[512,1024]{1,0:T(8,128)(2,1)S(1)} %inside_other.1.refs_3_.refs_2_, bf16[512,256]{1,0:T(8,128)(2,1)S(1)} %get-tuple-element.34.refs_1_.refs_3_, ...), custom_call_target="tpu_custom_call" | custom-call | flops 3849999872 | bytes 3500000 | tf_op jit(solution)/shard_map/finish/pallas_call | solution.py:45
  67.8 1.9 %collective-permute-done.14.refs_1_ = bf16[512,512]{1,0:T(8,128)(2,1)S(1)} collective-permute-done((bf16[512,512]{1,0:T(8,128)(2,1)S(1)}, bf16[512,512]{1,0:T(8,128)(2,1)S(1)}, u32[]{:S(2)}, u32[]{:S(2)}) %collective-permute-start.14) | collective-permute-done | bytes 524320 | tf_op jit(solution)/shard_map/ppermute | solution.py:743
  69.7 1.4 %total.1 = bf16[512,512]{1,0:T(8,128)(2,1)} custom-call(bf16[512,512]{1,0:T(8,128)(2,1)S(1)} %get-tuple-element.49.refs_0_, bf16[512,512]{1,0:T(8,128)(2,1)S(1)} %collective-permute-done.14.refs_1_), custom_call_target="tpu_custom_call" | custom-call | flops 880000000 | bytes 800000 | tf_op jit(solution)/shard_map/total/pallas_call | solution.py:45
  (61 shorter events, 10.6 us)
Async XLA Ops:
  0.0 28.5 %collective-permute-start.1 = (bf16[1024,1024]{1,0:T(8,128)(2,1)}, bf16[1024,1024]{1,0:T(8,128)(2,1)}, u32[]{:S(2)}, u32[]{:S(2)}) collective-permute-start(bf16[1024,1024]{1,0:T(8,128)(2,1)} %refs_5_.1), channel_id=1, source_target_pairs={{0,1},{1,0},{2,3},{3,2},{4,5},{5,4},{6,7},{7,6},{8,9},{9,8},{10,11... | collective-permute-start | bytes 6291464 | tf_op jit(solution)/shard_map/ppermute | solution.py:743
  5.8 4.3 %copy-start.5 = (bf16[1024,16]{0,1:T(8,128)(2,1)S(1)}, bf16[1024,16]{0,1:T(8,128)(2,1)}, u32[]{:S(2)}) copy-start(bf16[1024,16]{0,1:T(8,128)(2,1)} %param.19) | copy-start | bytes 98308
  5.8 4.8 %copy-start.1 = (bf16[1024,1024]{1,0:T(8,128)(2,1)S(1)}, bf16[1024,1024]{1,0:T(8,128)(2,1)}, u32[]{:S(2)}) copy-start(bf16[1024,1024]{1,0:T(8,128)(2,1)} %refs_1_.1) | copy-start | bytes 6291460
  7.5 7.4 %collective-permute-start = (bf16[16,1024]{1,0:T(8,128)(2,1)S(1)}, bf16[16,1024]{1,0:T(8,128)(2,1)S(1)}, u32[]{:S(2)}, u32[]{:S(2)}) collective-permute-start(bf16[16,1024]{1,0:T(8,128)(2,1)S(1)} %get-tuple-element.29), channel_id=1, source_target_pairs={{0,2},{1,0},{2,4},{3,1},{4,6},{5,3},{6,8},{7,5},{8,10},{9,7},{10,1... | collective-permute-start | bytes 98312 | tf_op jit(solution)/shard_map/ppermute | solution.py:537
  10.1 16.8 %collective-permute-start.3 = (f32[8,1024]{1,0:T(8,128)S(1)}, f32[8,1024]{1,0:T(8,128)S(1)}, u32[]{:S(2)}, u32[]{:S(2)}) collective-permute-start(f32[8,1024]{1,0:T(8,128)S(1)} %get-tuple-element.31.refs_7_.refs_8_), channel_id=1, source_target_pairs={{0,1},{1,0},{2,3},{3,2},{4,5},{5,4},{6,7},{7,6},{8,9},{9,8},{10,11... | collective-permute-start | bytes 98312 | tf_op jit(solution)/shard_map/ppermute | solution.py:743
  10.1 18.4 %collective-permute-start.2 = (bf16[16,1024]{1,0:T(8,128)(2,1)S(1)}, bf16[16,1024]{1,0:T(8,128)(2,1)S(1)}, u32[]{:S(2)}, u32[]{:S(2)}) collective-permute-start(bf16[16,1024]{1,0:T(8,128)(2,1)S(1)} %bitcast.8), channel_id=1, source_target_pairs={{0,1},{1,0},{2,3},{3,2},{4,5},{5,4},{6,7},{7,6},{8,9},{9,8},{10,11... | collective-permute-start | bytes 98312 | tf_op jit(solution)/shard_map/ppermute | solution.py:743
  10.6 45.7 %collective-permute-start.10 = (bf16[1024,1024]{1,0:T(8,128)(2,1)S(1)}, bf16[1024,1024]{1,0:T(8,128)(2,1)}, u32[]{:S(2)}, u32[]{:S(2)}) collective-permute-start(bf16[1024,1024]{1,0:T(8,128)(2,1)S(1)} %copy-done.1), channel_id=1, source_target_pairs={{0,1},{1,0},{2,3},{3,2},{4,5},{5,4},{6,7},{7,6},{8,9},{9,8},{10,11... | collective-permute-start | bytes 6291464 | tf_op jit(solution)/shard_map/ppermute | solution.py:743
  10.7 4.7 %copy-start.4 = (bf16[1024,256]{1,0:T(8,128)(2,1)S(1)}, bf16[1024,256]{1,0:T(8,128)(2,1)}, u32[]{:S(2)}) copy-start(bf16[1024,256]{1,0:T(8,128)(2,1)} %refs_3_.3) | copy-start | bytes 1572868
  10.7 4.7 %copy-start.9 = (f32[4,256]{1,0:T(4,128)S(1)}, f32[4,256]{1,0:T(4,128)}, u32[]{:S(2)}) copy-start(f32[4,256]{1,0:T(4,128)} %refs_4_.3) | copy-start | bytes 12292
  14.9 48.8 %collective-permute-start.12 = (bf16[1024,1024]{1,0:T(8,128)(2,1)}, bf16[1024,1024]{1,0:T(8,128)(2,1)S(1)}, u32[]{:S(2)}, u32[]{:S(2)}) collective-permute-start(bf16[1024,1024]{1,0:T(8,128)(2,1)} %refs_9_.1), channel_id=1, source_target_pairs={{0,1},{1,0},{2,3},{3,2},{4,5},{5,4},{6,7},{7,6},{8,9},{9,8},{10,11... | collective-permute-start | bytes 6291464 | tf_op jit(solution)/shard_map/ppermute | solution.py:743
  15.4 1.2 %copy-start.14 = (bf16[512,1024]{1,0:T(8,128)(2,1)S(1)}, bf16[512,1024]{1,0:T(8,128)(2,1)}, u32[]{:S(2)}) copy-start(bf16[512,1024]{1,0:T(8,128)(2,1)} %copy-done.13) | copy-start | bytes 3145732
  17.8 1.6 %copy-start = (bf16[1024,1024]{1,0:T(8,128)(2,1)S(1)}, bf16[1024,1024]{1,0:T(8,128)(2,1)}, u32[]{:S(2)}) copy-start(bf16[1024,1024]{1,0:T(8,128)(2,1)} %refs_5_.1) | copy-start | bytes 6291460
  17.8 1.9 %copy-start.18 = (bf16[512,1024]{1,0:T(8,128)(2,1)S(1)}, bf16[512,1024]{1,0:T(8,128)(2,1)}, u32[]{:S(2)}) copy-start(bf16[512,1024]{1,0:T(8,128)(2,1)} %copy-done.16) | copy-start | bytes 3145732
  26.9 9.6 %collective-permute-start.4 = (bf16[144,512]{1,0:T(8,128)(2,1)S(1)}, bf16[144,512]{1,0:T(8,128)(2,1)S(1)}, u32[]{:S(2)}, u32[]{:S(2)}) collective-permute-start(bf16[144,512]{1,0:T(8,128)(2,1)S(1)} %get-tuple-element.37), channel_id=1, source_target_pairs={{0,2},{2,0},{4,6},{6,4},{8,10},{10,8},{12,14},{14,12},{1,3},{3,1},... | collective-permute-start | bytes 442376 | tf_op jit(solution)/shard_map/ppermute | solution.py:545
  36.6 6.3 %collective-permute-start.5 = (bf16[144,512]{1,0:T(8,128)(2,1)S(1)}, bf16[144,512]{1,0:T(8,128)(2,1)S(1)}, u32[]{:S(2)}, u32[]{:S(2)}) collective-permute-start(bf16[144,512]{1,0:T(8,128)(2,1)S(1)} %pair_own.1.refs_4_.refs_1_), channel_id=1, source_target_pairs={{0,4},{1,0},{2,6},{3,2},{4,8},{5,1},{6,10},{7,3},{8,12},{9,5},{10,... | collective-permute-start | bytes 442376 | tf_op jit(solution)/shard_map/ppermute | solution.py:537
  38.3 7.4 %collective-permute-start.7 = (bf16[144,512]{1,0:T(8,128)(2,1)S(1)}, bf16[144,512]{1,0:T(8,128)(2,1)S(1)}, u32[]{:S(2)}, u32[]{:S(2)}) collective-permute-start(bf16[144,512]{1,0:T(8,128)(2,1)S(1)} %get-tuple-element.42), channel_id=1, source_target_pairs={{0,2},{2,0},{4,6},{6,4},{8,10},{10,8},{12,14},{14,12},{1,3},{3,1},... | collective-permute-start | bytes 442376 | tf_op jit(solution)/shard_map/ppermute | solution.py:545
  43.0 5.4 %collective-permute-start.6 = (bf16[144,512]{1,0:T(8,128)(2,1)S(1)}, bf16[144,512]{1,0:T(8,128)(2,1)S(1)}, u32[]{:S(2)}, u32[]{:S(2)}) collective-permute-start(bf16[144,512]{1,0:T(8,128)(2,1)S(1)} %chain_own.1.refs_3_), channel_id=1, source_target_pairs={{0,8},{1,0},{2,10},{3,2},{4,12},{5,4},{6,14},{7,6},{8,9},{9,1},{10... | collective-permute-start | bytes 442376 | tf_op jit(solution)/shard_map/ppermute | solution.py:537
  45.7 6.0 %collective-permute-start.8 = (bf16[144,512]{1,0:T(8,128)(2,1)S(1)}, bf16[144,512]{1,0:T(8,128)(2,1)S(1)}, u32[]{:S(2)}, u32[]{:S(2)}) collective-permute-start(bf16[144,512]{1,0:T(8,128)(2,1)S(1)} %pair_other.1.refs_5_.refs_1_), channel_id=1, source_target_pairs={{0,4},{1,0},{2,6},{3,2},{4,8},{5,1},{6,10},{7,3},{8,12},{9,5},{10,... | collective-permute-start | bytes 442376 | tf_op jit(solution)/shard_map/ppermute | solution.py:537
  51.8 8.2 %collective-permute-start.9 = (bf16[144,512]{1,0:T(8,128)(2,1)S(1)}, bf16[144,512]{1,0:T(8,128)(2,1)S(1)}, u32[]{:S(2)}, u32[]{:S(2)}) collective-permute-start(bf16[144,512]{1,0:T(8,128)(2,1)S(1)} %chain_other.1.refs_2_), channel_id=1, source_target_pairs={{0,8},{1,0},{2,10},{3,2},{4,12},{5,4},{6,14},{7,6},{8,9},{9,1},{10... | collective-permute-start | bytes 442376 | tf_op jit(solution)/shard_map/ppermute | solution.py:537
  55.5 5.8 %copy-start.2 = (bf16[1024,1024]{1,0:T(8,128)(2,1)S(1)}, bf16[1024,1024]{1,0:T(8,128)(2,1)}, u32[]{:S(2)}) copy-start(bf16[1024,1024]{1,0:T(8,128)(2,1)} %refs_9_.1) | copy-start | bytes 6291460
  55.5 5.8 %copy-start.15 = (bf16[512,1024]{1,0:T(8,128)(2,1)S(1)}, bf16[512,1024]{1,0:T(8,128)(2,1)}, u32[]{:S(2)}) copy-start(bf16[512,1024]{1,0:T(8,128)(2,1)} %copy-done.13) | copy-start | bytes 3145732
  55.5 5.8 %collective-permute-start.13 = (bf16[128,512]{1,0:T(8,128)(2,1)S(1)}, bf16[128,512]{1,0:T(8,128)(2,1)S(1)}, u32[]{:S(2)}, u32[]{:S(2)}) collective-permute-start(bf16[128,512]{1,0:T(8,128)(2,1)S(1)} %get-tuple-element.46), channel_id=1, source_target_pairs={{0,2},{2,0},{4,6},{6,4},{8,10},{10,8},{12,14},{14,12},{1,3},{3,1},... | collective-permute-start | bytes 393224 | tf_op jit(solution)/shard_map/ppermute | solution.py:611
  60.1 5.0 %collective-permute-start.11 = (bf16[128,512]{1,0:T(8,128)(2,1)S(1)}, bf16[128,512]{1,0:T(8,128)(2,1)S(1)}, u32[]{:S(2)}, u32[]{:S(2)}) collective-permute-start(bf16[128,512]{1,0:T(8,128)(2,1)S(1)} %get-tuple-element.45), channel_id=1, source_target_pairs={{0,2},{2,0},{4,6},{6,4},{8,10},{10,8},{12,14},{14,12},{1,3},{3,1},... | collective-permute-start | bytes 393224 | tf_op jit(solution)/shard_map/ppermute | solution.py:611
  67.7 2.0 %collective-permute-start.14 = (bf16[512,512]{1,0:T(8,128)(2,1)S(1)}, bf16[512,512]{1,0:T(8,128)(2,1)S(1)}, u32[]{:S(2)}, u32[]{:S(2)}) collective-permute-start(bf16[512,512]{1,0:T(8,128)(2,1)S(1)} %get-tuple-element.50), channel_id=1, source_target_pairs={{0,1},{1,0},{2,3},{3,2},{4,5},{5,4},{6,7},{7,6},{8,9},{9,8},{10,11... | collective-permute-start | bytes 1572872 | tf_op jit(solution)/shard_map/ppermute | solution.py:743
  (10 other events, 8.6 us)

commit v3 on v2

--- a/solution.py
+++ b/solution.py
@@ -101,19 +101,25 @@
 
 def prepare_kernel(
     back_ref,
+    parity_ref,
+    place_ref,
+    hidden_hbm,
     tokens_hbm,
-    hidden_hbm,
     emb_hbm,
+    conv_hbm,
+    gain_hbm,
+    bias_hbm,
+    rate_hbm,
+    out_ref,
+    tail_ref,
+    small_ref,
+    hidden_ref,
+    tokens_ref,
+    emb_ref,
     conv_ref,
     gain_ref,
     bias_ref,
     rate_ref,
-    out_ref,
-    tail_ref,
-    small_ref,
-    tokens_ref,
-    hidden_ref,
-    emb_ref,
     sems,
 ):
     rows = hidden_ref.shape[0]
@@ -122,26 +128,28 @@
     heads = bias_ref.shape[1]
     count = rows // CHUNK
     back = back_ref[0] == 1
+    whole = [
+        (tokens_hbm, tokens_ref),
+        (emb_hbm, emb_ref),
+        (conv_hbm, conv_ref),
+        (gain_hbm, gain_ref),
+        (bias_hbm, bias_ref),
+        (rate_hbm, rate_ref),
+    ]
+    small_copies = [pltpu.make_async_copy(src, dst, sems.at[count + i]) for i, (src, dst) in enumerate(whole)]
+    parts = [pl.ds(r * CHUNK, CHUNK) for r in range(count)]
     copies = [
-        pltpu.make_async_copy(tokens_hbm, tokens_ref, sems.at[0]),
-        pltpu.make_async_copy(emb_hbm, emb_ref, sems.at[1]),
+        pltpu.make_async_copy(hidden_hbm.at[part, :], hidden_ref.at[part, :], sems.at[r])
+        for r, part in enumerate(parts)
     ]
-    for r in range(count):
-        part = pl.ds(r * CHUNK, CHUNK)
-        copies.append(pltpu.make_async_copy(hidden_hbm.at[part, :], hidden_ref.at[part, :], sems.at[2 + r]))
-    for copy in copies:
+    for copy in small_copies[:2] + copies + small_copies[2:]:
         copy.start()
-    small_ref[:taps, :] = conv_ref[...]
-    small_ref[taps : taps + 1, :] = gain_ref[...]
-    small_ref[taps + 1 :, :] = jnp.zeros((SMALL_ROWS - taps - 1, inner), F32)
-    small_ref[taps + 1 : taps + 2, :heads] = bias_ref[...]
-    small_ref[taps + 2 : taps + 3, :heads] = rate_ref[...]
-    copies[0].wait()
-    copies[1].wait()
+    for copy in small_copies[:2]:
+        copy.wait()
     kind = lax.broadcasted_iota(jnp.int32, (kinds, rows), 0)
     onehot = jnp.where(kind == tokens_ref[...], 1.0, 0.0).astype(BF16)
     for r in range(count):
-        copies[2 + r].wait()
+        copies[r].wait()
         low, high = r * CHUNK, (r + 1) * CHUNK
         base = dot_tn(onehot[:, low:high], emb_ref[...])
         merged = (hidden_ref[low:high, :].astype(F32) + base).astype(BF16).astype(F32)
@@ -161,42 +169,37 @@
             if r == count - 1:
                 tail_ref[...] = normed[CHUNK - HALO :, :]
 
-
-def prepare_call(back, tokens, hidden, embedding, conv, gain, bias, rate):
+    for copy in small_copies[2:]:
+        copy.wait()
+    small_ref[:taps, :] = conv_ref[...]
+    small_ref[taps : taps + 1, :] = gain_ref[...]
+    small_ref[taps + 1 :, :] = jnp.zeros((SMALL_ROWS - taps - 1, inner), F32)
+    small_ref[taps + 1 : taps + 2, :heads] = bias_ref[...]
+    small_ref[taps + 2 : taps + 3, :heads] = rate_ref[...]
+
+
+def prepare_call(scalars, hidden, tokens, embedding, conv, gain, bias, rate):
     rows, width = hidden.shape
     inner = conv.shape[1]
     vmem = pl.BlockSpec(memory_space=pltpu.VMEM)
-    hbm = pl.BlockSpec(memory_space=pltpu.HBM)
+    arrays = [hidden, tokens.reshape(1, -1), embedding, conv]
+    arrays += [a.reshape(1, -1) for a in (gain, bias, rate)]
     return call(
         prepare_kernel,
         "prepare",
         vmem=12,
         cost=micros(1.5),
-        scalars=(back,),
-        grid=(),
-        in_specs=[hbm] * 3 + [vmem] * 4,
+        scalars=scalars,
+        in_specs=[pl.BlockSpec(memory_space=pltpu.HBM)] * len(arrays),
         out_specs=[vmem] * 3,
         out_shape=[
             jax.ShapeDtypeStruct((rows, width), BF16),
             jax.ShapeDtypeStruct((HALO, width), BF16),
             jax.ShapeDtypeStruct((SMALL_ROWS, inner), F32),
         ],
-        scratch=[
-            pltpu.VMEM((1, rows), jnp.int32),
-            pltpu.VMEM((rows, width), BF16),
-            pltpu.VMEM(embedding.shape, BF16),
-            pltpu.SemaphoreType.DMA((2 + rows // CHUNK,)),
-        ],
-    )(
-        back,
-        tokens.reshape(1, rows),
-        hidden,
-        embedding,
-        conv,
-        gain.reshape(1, -1),
-        bias.reshape(1, -1),
-        rate.reshape(1, -1),
-    )
+        scratch=[pltpu.VMEM(a.shape, a.dtype) for a in arrays]
+        + [pltpu.SemaphoreType.DMA((rows // CHUNK + len(arrays) - 1,))],
+    )(*scalars, *(pltpu.with_memory_space_constraint(a, pltpu.HBM) for a in arrays))
 
 
 def gate_kernel(rows_ref, wg_ref, out_ref):
@@ -746,11 +749,11 @@
     index = lax.axis_index("seq").astype(jnp.int32)
     last = lax.axis_size("seq") - 1
     back = core.reshape(1)
-    parity = (index % 2).reshape(1)
+    parity = (index & 1).reshape(1)
     place = (index + core * (last - 2 * index)).reshape(1)
     w_inner_2 = theirs(w_inner)
     normed, tail, small = prepare_call(
-        back, tokens, hidden, embedding, conv_inner, norm_gain, step_bias, decay_rate
+        (back, parity, place), hidden, tokens, embedding, conv_inner, norm_gain, step_bias, decay_rate
     )
     halo = onward(tail, 1)
     small_2 = theirs(small)

time: 71.5 us -> 61.1 us (0.85)
  local copies, waits for them, and re-layouts: 10.7 us -> 0.07 us
    unnamed x38 -> x12, local copies, waits for them, and re-layouts: 10.7 us -> 0.07 us
  transfers between devices with their start and end apart: 15 -> 15, of which waited for: 3 -> 4; matrix products, arithmetic and copies ran while one was open for 0% -> 0% of each run, Pallas kernels for 46% -> 54%
where the time goes in v3:
time: 61.1 us; the launch traced here: 60 us
  Pallas kernels  36.3 us (59%)
  starting transfers between devices  18.1 us (30%)
  waiting for transfers between devices  5.34 us (9%)
    pallas_call x17, Pallas kernels, call(): return lambda *arrays: run(*arrays, *after)  36.3 us
    ppermute x5, starting transfers between devices, onward(): return lax.ppermute(value, ('seq', 'ch'), pairs)  10.8 us
    ppermute x2, starting transfers between devices, __init__(): self.other = lax.ppermute(send, 'seq', self.swap)  3.59 us
    ppermute x5, waiting for transfers between devices, onward(): return lax.ppermute(value, ('seq', 'ch'), pairs)  2.27 us
    ppermute x2, starting transfers between devices, entry(): return (keep, lax.ppermute(out, 'seq', self.swap))  2.09 us
    ppermute x6, waiting for transfers between devices, theirs(): return lax.ppermute(a, 'ch', swap)  1.91 us
    ppermute x6, starting transfers between devices, theirs(): return lax.ppermute(a, 'ch', swap)  1.61 us
  transfers between devices with their start and end apart: 15, of which 4 were waited for; matrix products, arithmetic and copies ran while one was open for 0% of the time, Pallas kernels for 54%

profile of v3, /device:TPU:0, one launch (start us, length us, event | category | flops | bytes accessed | tf_op | source)
XLA Modules:
  0.0 60.0 jit_solution(951291441965667011)
XLA Ops:
  0.5 2.8 %prepare.1 = (bf16[512,1024]{1,0:T(8,128)(2,1)S(1)}, bf16[16,1024]{1,0:T(8,128)(2,1)S(1)}, f32[8,1024]{1,0:T(8,128)S(1)}) custom-call(s32[1]{0:T(128)} %bitcast.refs_0_, s32[1]{0:T(128)} %bitcast.1.refs_1_, s32[1]{0:T(128)} %bitcast.2.refs_2_.refs_0_, bf16[512,1024]{1,0:T(8,128)(2,1)} %refs_3_.2, s32[1,512]{1,0:T(1,128)} %bitcast.11, ...), custom_call_target="tpu_custom_call" | custom-call | flops 1650000000 | bytes 1500000 | tf_op jit(solution)/shard_map/prepare/pallas_call | solution.py:45
  3.2 2.6 %collective-permute-start = (bf16[16,1024]{1,0:T(8,128)(2,1)S(1)}, bf16[16,1024]{1,0:T(8,128)(2,1)S(1)}, u32[]{:S(2)}, u32[]{:S(2)}) collective-permute-start(bf16[16,1024]{1,0:T(8,128)(2,1)S(1)} %get-tuple-element.29), channel_id=1, source_target_pairs={{0,2},{1,0},{2,4},{3,1},{4,6},{5,3},{6,8},{7,5},{8,10},{9,7},{10,1... | collective-permute-start | bytes 98312 | tf_op jit(solution)/shard_map/ppermute | solution.py:540
  5.8 0.5 collective-permute-start.2
  6.4 2.2 %gate_own.1.refs_5_.refs_7_ = bf16[512,1024]{1,0:T(8,128)(2,1)S(1)} custom-call(bf16[512,1024]{1,0:T(8,128)(2,1)S(1)} %get-tuple-element.28.refs_0_.refs_1_.refs_2_, bf16[1024,1024]{1,0:T(8,128)(2,1)S(1)} %copy-done.1), custom_call_target="tpu_custom_call" | custom-call | flops 2640000000 | bytes 2400000 | tf_op jit(solution)/shard_map/gate_own/pallas_call | solution.py:45
  8.7 0.5 collective-permute-start.12
  9.2 1.0 %maps.1 = (bf16[512,256]{1,0:T(8,128)(2,1)S(1)}, bf16[128,512]{1,0:T(8,128)(2,1)S(1)}) custom-call(s32[1]{0:T(128)} %bitcast.2.refs_2_.refs_0_, bf16[512,1024]{1,0:T(8,128)(2,1)S(1)} %get-tuple-element.28.refs_0_.refs_1_.refs_2_, bf16[16,1024]{1,0:T(8,128)(2,1)S(1)} %collective-permute-done.refs_2_.refs_3_, bf16[1024,256]{1,0:T(8,128)(2,1)S(1)} %copy-done.3, ...), custom_call_target="tpu_custom_call" | custom-call | flops 1650000000 | bytes 1500000 | tf_op jit(solution)/shard_map/maps/pallas_call | solution.py:45
  10.2 7.2 %local_own.1 = (bf16[512,1024]{1,0:T(8,128)(2,1)S(1)}, f32[512,16]{1,0:T(8,128)S(1)}, f32[16,512]{1,0:T(8,128)S(1)}, bf16[144,512]{1,0:T(8,128)(2,1)S(1)}, bf16[144,512]{1,0:T(8,128)(2,1)S(1)}) custom-call(s32[1]{0:T(128)} %bitcast.2.refs_2_.refs_0_, s32[1]{0:T(128)} %bitcast.1.refs_1_, bf16[512,1024]{1,0:T(8,128)(2,1)S(1)} %get-tuple-element.28.refs_0_.refs_1_.refs_2_, ...), custom_call_target="tpu_custom_call" | custom-call | flops 5500000256 | bytes 5000000 | tf_op jit(solution)/shard_map/local_own/pallas_call | solution.py:45
  17.5 2.3 %collective-permute-start.4 = (bf16[144,512]{1,0:T(8,128)(2,1)S(1)}, bf16[144,512]{1,0:T(8,128)(2,1)S(1)}, u32[]{:S(2)}, u32[]{:S(2)}) collective-permute-start(bf16[144,512]{1,0:T(8,128)(2,1)S(1)} %get-tuple-element.37), channel_id=1, source_target_pairs={{0,2},{2,0},{4,6},{6,4},{8,10},{10,8},{12,14},{14,12},{1,3},{3,1},... | collective-permute-start | bytes 442376 | tf_op jit(solution)/shard_map/ppermute | solution.py:548
  19.8 7.2 %local_other.1 = (bf16[512,1024]{1,0:T(8,128)(2,1)S(1)}, f32[512,16]{1,0:T(8,128)S(1)}, f32[16,512]{1,0:T(8,128)S(1)}, bf16[144,512]{1,0:T(8,128)(2,1)S(1)}, bf16[144,512]{1,0:T(8,128)(2,1)S(1)}) custom-call(s32[1]{0:T(128)} %bitcast.2.refs_2_.refs_0_, s32[1]{0:T(128)} %bitcast.1.refs_1_, bf16[512,1024]{1,0:T(8,128)(2,1)S(1)} %get-tuple-element.28.refs_0_.refs_1_.refs_2_, ...), custom_call_target="tpu_custom_call" | custom-call | flops 5500000256 | bytes 5000000 | tf_op jit(solution)/shard_map/local_other/pallas_call | solution.py:45
  27.2 1.6 %collective-permute-start.5 = (bf16[144,512]{1,0:T(8,128)(2,1)S(1)}, bf16[144,512]{1,0:T(8,128)(2,1)S(1)}, u32[]{:S(2)}, u32[]{:S(2)}) collective-permute-start(bf16[144,512]{1,0:T(8,128)(2,1)S(1)} %pair_own.1.refs_4_.refs_1_), channel_id=1, source_target_pairs={{0,4},{1,0},{2,6},{3,2},{4,8},{5,1},{6,10},{7,3},{8,12},{9,5},{10,... | collective-permute-start | bytes 442376 | tf_op jit(solution)/shard_map/ppermute | solution.py:540
  28.8 1.3 %collective-permute-start.7 = (bf16[144,512]{1,0:T(8,128)(2,1)S(1)}, bf16[144,512]{1,0:T(8,128)(2,1)S(1)}, u32[]{:S(2)}, u32[]{:S(2)}) collective-permute-start(bf16[144,512]{1,0:T(8,128)(2,1)S(1)} %get-tuple-element.42), channel_id=1, source_target_pairs={{0,2},{2,0},{4,6},{6,4},{8,10},{10,8},{12,14},{14,12},{1,3},{3,1},... | collective-permute-start | bytes 442376 | tf_op jit(solution)/shard_map/ppermute | solution.py:548
  30.0 3.3 %inside_own.1.refs_3_.refs_2_ = bf16[512,1024]{1,0:T(8,128)(2,1)S(1)} custom-call(bf16[512,1024]{1,0:T(8,128)(2,1)S(1)} %get-tuple-element.38.refs_0_, bf16[512,256]{1,0:T(8,128)(2,1)S(1)} %get-tuple-element.34.refs_1_.refs_3_, f32[512,16]{1,0:T(8,128)S(1)} %get-tuple-element.39.refs_2_.refs_4_, f32[16,512]{1,0:T(8,128)S(1)} %get-tuple-element.40.refs_3_, ...), custom_call_target="tpu_custom_call" | custom-call | flops 3520000000 | bytes 3200000 | tf_op jit(solution)/shard_map/inside_own/pallas_call | solution.py:45
  33.5 2.6 %collective-permute-start.6 = (bf16[144,512]{1,0:T(8,128)(2,1)S(1)}, bf16[144,512]{1,0:T(8,128)(2,1)S(1)}, u32[]{:S(2)}, u32[]{:S(2)}) collective-permute-start(bf16[144,512]{1,0:T(8,128)(2,1)S(1)} %chain_own.1.refs_3_), channel_id=1, source_target_pairs={{0,8},{1,0},{2,10},{3,2},{4,12},{5,4},{6,14},{7,6},{8,9},{9,1},{10... | collective-permute-start | bytes 442376 | tf_op jit(solution)/shard_map/ppermute | solution.py:540
  36.5 2.3 %collective-permute-done.6.refs_4_ = bf16[144,512]{1,0:T(8,128)(2,1)S(1)} collective-permute-done((bf16[144,512]{1,0:T(8,128)(2,1)S(1)}, bf16[144,512]{1,0:T(8,128)(2,1)S(1)}, u32[]{:S(2)}, u32[]{:S(2)}) %collective-permute-start.6) | collective-permute-done | bytes 147488 | tf_op jit(solution)/shard_map/ppermute | solution.py:540
  38.9 3.4 %inside_other.1.refs_3_.refs_2_ = bf16[512,1024]{1,0:T(8,128)(2,1)S(1)} custom-call(bf16[512,1024]{1,0:T(8,128)(2,1)S(1)} %get-tuple-element.33.refs_3_.refs_0_, bf16[512,256]{1,0:T(8,128)(2,1)S(1)} %get-tuple-element.34.refs_1_.refs_3_, f32[512,16]{1,0:T(8,128)S(1)} %get-tuple-element.35.refs_2_.refs_4_, f32[16,512]{1,0:T(8,128)S(1)} %get-tuple-element.36.refs_3_, ...), custom_call_target="tpu_custom_call" | custom-call | flops 3520000000 | bytes 3200000 | tf_op jit(solution)/shard_map/inside_other/pallas_call | solution.py:45
  42.4 3.7 %collective-permute-start.9 = (bf16[144,512]{1,0:T(8,128)(2,1)S(1)}, bf16[144,512]{1,0:T(8,128)(2,1)S(1)}, u32[]{:S(2)}, u32[]{:S(2)}) collective-permute-start(bf16[144,512]{1,0:T(8,128)(2,1)S(1)} %chain_other.1.refs_2_), channel_id=1, source_target_pairs={{0,8},{1,0},{2,10},{3,2},{4,12},{5,4},{6,14},{7,6},{8,9},{9,1},{10... | collective-permute-start | bytes 442376 | tf_op jit(solution)/shard_map/ppermute | solution.py:540
  46.1 0.6 %collective-permute-start.13 = (bf16[128,512]{1,0:T(8,128)(2,1)S(1)}, bf16[128,512]{1,0:T(8,128)(2,1)S(1)}, u32[]{:S(2)}, u32[]{:S(2)}) collective-permute-start(bf16[128,512]{1,0:T(8,128)(2,1)S(1)} %get-tuple-element.46), channel_id=1, source_target_pairs={{0,2},{2,0},{4,6},{6,4},{8,10},{10,8},{12,14},{14,12},{1,3},{3,1},... | collective-permute-start | bytes 393224 | tf_op jit(solution)/shard_map/ppermute | solution.py:614
  46.7 2.2 %gate_other.1.refs_5_.refs_7_ = bf16[512,1024]{1,0:T(8,128)(2,1)S(1)} custom-call(bf16[512,1024]{1,0:T(8,128)(2,1)S(1)} %get-tuple-element.28.refs_0_.refs_1_.refs_2_, bf16[1024,1024]{1,0:T(8,128)(2,1)S(1)} %collective-permute-done.10.refs_1_, bf16[144,512]{1,0:T(8,128)(2,1)S(1)} %chain_other.1.refs_2_), custom_call_target="tpu_custom_call" | custom-call | flops 2640000000 | bytes 2400000 | tf_op jit(solution)/shard_map/gate_other/pallas_call | solution.py:45
  49.1 1.5 %collective-permute-start.11 = (bf16[128,512]{1,0:T(8,128)(2,1)S(1)}, bf16[128,512]{1,0:T(8,128)(2,1)S(1)}, u32[]{:S(2)}, u32[]{:S(2)}) collective-permute-start(bf16[128,512]{1,0:T(8,128)(2,1)S(1)} %get-tuple-element.45), channel_id=1, source_target_pairs={{0,2},{2,0},{4,6},{6,4},{8,10},{10,8},{12,14},{14,12},{1,3},{3,1},... | collective-permute-start | bytes 393224 | tf_op jit(solution)/shard_map/ppermute | solution.py:614
  50.6 0.8 %collective-permute-done.13.refs_6_ = bf16[128,512]{1,0:T(8,128)(2,1)S(1)} collective-permute-done((bf16[128,512]{1,0:T(8,128)(2,1)S(1)}, bf16[128,512]{1,0:T(8,128)(2,1)S(1)}, u32[]{:S(2)}, u32[]{:S(2)}) %collective-permute-start.13) | collective-permute-done | bytes 131104 | tf_op jit(solution)/shard_map/ppermute | solution.py:614
  51.4 2.4 %part.1 = (f32[512,1024]{1,0:T(8,128)S(1)}, f32[512,128]{1,0:T(8,128)S(1)}) custom-call(s32[1]{0:T(128)} %bitcast.refs_0_, s32[1]{0:T(128)} %bitcast.1.refs_1_, bf16[512,1024]{1,0:T(8,128)(2,1)S(1)} %inside_own.1.refs_3_.refs_2_, bf16[512,256]{1,0:T(8,128)(2,1)S(1)} %get-tuple-element.34.refs_1_.refs_3_, f32[512,16]{1,0:T(8,128)S(1)} %get-tuple-element.39.refs_2_.refs_4_, ...), custom_call_target="tpu_custom_call" | custom-call | flops 3849999872 | bytes 3500000 | tf_op jit(solution)/shard_map/part/pallas_call | solution.py:45
  54.1 2.5 %finish.1 = (bf16[512,512]{1,0:T(8,128)(2,1)S(1)}, bf16[512,512]{1,0:T(8,128)(2,1)S(1)}) custom-call(s32[1]{0:T(128)} %bitcast.refs_0_, s32[1]{0:T(128)} %bitcast.1.refs_1_, bf16[512,1024]{1,0:T(8,128)(2,1)S(1)} %inside_other.1.refs_3_.refs_2_, bf16[512,256]{1,0:T(8,128)(2,1)S(1)} %get-tuple-element.34.refs_1_.refs_3_, ...), custom_call_target="tpu_custom_call" | custom-call | flops 3849999872 | bytes 3500000 | tf_op jit(solution)/shard_map/finish/pallas_call | solution.py:45
  56.7 1.9 %collective-permute-done.14.refs_1_ = bf16[512,512]{1,0:T(8,128)(2,1)S(1)} collective-permute-done((bf16[512,512]{1,0:T(8,128)(2,1)S(1)}, bf16[512,512]{1,0:T(8,128)(2,1)S(1)}, u32[]{:S(2)}, u32[]{:S(2)}) %collective-permute-start.14) | collective-permute-done | bytes 524320 | tf_op jit(solution)/shard_map/ppermute | solution.py:746
  58.6 1.4 %total.1 = bf16[512,512]{1,0:T(8,128)(2,1)} custom-call(bf16[512,512]{1,0:T(8,128)(2,1)S(1)} %get-tuple-element.49.refs_0_, bf16[512,512]{1,0:T(8,128)(2,1)S(1)} %collective-permute-done.14.refs_1_), custom_call_target="tpu_custom_call" | custom-call | flops 880000000 | bytes 800000 | tf_op jit(solution)/shard_map/total/pallas_call | solution.py:45
  (35 shorter events, 1.9 us)
Async XLA Ops:
  0.0 19.8 %collective-permute-start.1 = (bf16[1024,1024]{1,0:T(8,128)(2,1)}, bf16[1024,1024]{1,0:T(8,128)(2,1)S(1)}, u32[]{:S(2)}, u32[]{:S(2)}) collective-permute-start(bf16[1024,1024]{1,0:T(8,128)(2,1)} %refs_5_.3), channel_id=1, source_target_pairs={{0,1},{1,0},{2,3},{3,2},{4,5},{5,4},{6,7},{7,6},{8,9},{9,8},{10,11... | collective-permute-start | bytes 6291464 | tf_op jit(solution)/shard_map/ppermute | solution.py:746
  0.5 5.4 %copy-start.4 = (bf16[1024,16]{0,1:T(8,128)(2,1)S(1)}, bf16[1024,16]{0,1:T(8,128)(2,1)}, u32[]{:S(2)}) copy-start(bf16[1024,16]{0,1:T(8,128)(2,1)} %param.19) | copy-start | bytes 98308
  0.5 5.9 %copy-start.1 = (bf16[1024,1024]{1,0:T(8,128)(2,1)S(1)}, bf16[1024,1024]{1,0:T(8,128)(2,1)}, u32[]{:S(2)}) copy-start(bf16[1024,1024]{1,0:T(8,128)(2,1)} %refs_1_.1) | copy-start | bytes 6291460
  3.2 5.4 %collective-permute-start = (bf16[16,1024]{1,0:T(8,128)(2,1)S(1)}, bf16[16,1024]{1,0:T(8,128)(2,1)S(1)}, u32[]{:S(2)}, u32[]{:S(2)}) collective-permute-start(bf16[16,1024]{1,0:T(8,128)(2,1)S(1)} %get-tuple-element.29), channel_id=1, source_target_pairs={{0,2},{1,0},{2,4},{3,1},{4,6},{5,3},{6,8},{7,5},{8,10},{9,7},{10,1... | collective-permute-start | bytes 98312 | tf_op jit(solution)/shard_map/ppermute | solution.py:540
  5.8 11.7 %collective-permute-start.3 = (f32[8,1024]{1,0:T(8,128)S(1)}, f32[8,1024]{1,0:T(8,128)S(1)}, u32[]{:S(2)}, u32[]{:S(2)}) collective-permute-start(f32[8,1024]{1,0:T(8,128)S(1)} %get-tuple-element.31.refs_7_.refs_8_), channel_id=1, source_target_pairs={{0,1},{1,0},{2,3},{3,2},{4,5},{5,4},{6,7},{7,6},{8,9},{9,8},{10,11... | collective-permute-start | bytes 98312 | tf_op jit(solution)/shard_map/ppermute | solution.py:746
  5.8 14.0 %collective-permute-start.2 = (bf16[16,1024]{1,0:T(8,128)(2,1)S(1)}, bf16[16,1024]{1,0:T(8,128)(2,1)S(1)}, u32[]{:S(2)}, u32[]{:S(2)}) collective-permute-start(bf16[16,1024]{1,0:T(8,128)(2,1)S(1)} %bitcast.8), channel_id=1, source_target_pairs={{0,1},{1,0},{2,3},{3,2},{4,5},{5,4},{6,7},{7,6},{8,9},{9,8},{10,11... | collective-permute-start | bytes 98312 | tf_op jit(solution)/shard_map/ppermute | solution.py:746
  6.3 40.4 %collective-permute-start.10 = (bf16[1024,1024]{1,0:T(8,128)(2,1)S(1)}, bf16[1024,1024]{1,0:T(8,128)(2,1)S(1)}, u32[]{:S(2)}, u32[]{:S(2)}) collective-permute-start(bf16[1024,1024]{1,0:T(8,128)(2,1)S(1)} %copy-done.1), channel_id=1, source_target_pairs={{0,1},{1,0},{2,3},{3,2},{4,5},{5,4},{6,7},{7,6},{8,9},{9,8},{10,11... | collective-permute-start | bytes 6291464 | tf_op jit(solution)/shard_map/ppermute | solution.py:746
  6.4 2.3 %copy-start.2 = (bf16[1024,1024]{1,0:T(8,128)(2,1)S(1)}, bf16[1024,1024]{1,0:T(8,128)(2,1)}, u32[]{:S(2)}) copy-start(bf16[1024,1024]{1,0:T(8,128)(2,1)} %refs_9_.1) | copy-start | bytes 6291460
  6.4 2.8 %copy-start.3 = (bf16[1024,256]{1,0:T(8,128)(2,1)S(1)}, bf16[1024,256]{1,0:T(8,128)(2,1)}, u32[]{:S(2)}) copy-start(bf16[1024,256]{1,0:T(8,128)(2,1)} %refs_3_.3) | copy-start | bytes 1572868
  6.4 2.8 %copy-start.5 = (f32[4,256]{1,0:T(4,128)S(1)}, f32[4,256]{1,0:T(4,128)}, u32[]{:S(2)}) copy-start(f32[4,256]{1,0:T(4,128)} %refs_4_.1) | copy-start | bytes 12292
  8.6 1.6 %copy-start = (bf16[1024,1024]{1,0:T(8,128)(2,1)S(1)}, bf16[1024,1024]{1,0:T(8,128)(2,1)}, u32[]{:S(2)}) copy-start(bf16[1024,1024]{1,0:T(8,128)(2,1)} %refs_5_.3) | copy-start | bytes 6291460
  8.7 45.1 %collective-permute-start.12 = (bf16[1024,1024]{1,0:T(8,128)(2,1)S(1)}, bf16[1024,1024]{1,0:T(8,128)(2,1)S(1)}, u32[]{:S(2)}, u32[]{:S(2)}) collective-permute-start(bf16[1024,1024]{1,0:T(8,128)(2,1)S(1)} %copy-done.2), channel_id=1, source_target_pairs={{0,1},{1,0},{2,3},{3,2},{4,5},{5,4},{6,7},{7,6},{8,9},{9,8},{10,11... | collective-permute-start | bytes 6291464 | tf_op jit(solution)/shard_map/ppermute | solution.py:746
  17.5 9.6 %collective-permute-start.4 = (bf16[144,512]{1,0:T(8,128)(2,1)S(1)}, bf16[144,512]{1,0:T(8,128)(2,1)S(1)}, u32[]{:S(2)}, u32[]{:S(2)}) collective-permute-start(bf16[144,512]{1,0:T(8,128)(2,1)S(1)} %get-tuple-element.37), channel_id=1, source_target_pairs={{0,2},{2,0},{4,6},{6,4},{8,10},{10,8},{12,14},{14,12},{1,3},{3,1},... | collective-permute-start | bytes 442376 | tf_op jit(solution)/shard_map/ppermute | solution.py:548
  27.2 6.2 %collective-permute-start.5 = (bf16[144,512]{1,0:T(8,128)(2,1)S(1)}, bf16[144,512]{1,0:T(8,128)(2,1)S(1)}, u32[]{:S(2)}, u32[]{:S(2)}) collective-permute-start(bf16[144,512]{1,0:T(8,128)(2,1)S(1)} %pair_own.1.refs_4_.refs_1_), channel_id=1, source_target_pairs={{0,4},{1,0},{2,6},{3,2},{4,8},{5,1},{6,10},{7,3},{8,12},{9,5},{10,... | collective-permute-start | bytes 442376 | tf_op jit(solution)/shard_map/ppermute | solution.py:540
  28.8 7.3 %collective-permute-start.7 = (bf16[144,512]{1,0:T(8,128)(2,1)S(1)}, bf16[144,512]{1,0:T(8,128)(2,1)S(1)}, u32[]{:S(2)}, u32[]{:S(2)}) collective-permute-start(bf16[144,512]{1,0:T(8,128)(2,1)S(1)} %get-tuple-element.42), channel_id=1, source_target_pairs={{0,2},{2,0},{4,6},{6,4},{8,10},{10,8},{12,14},{14,12},{1,3},{3,1},... | collective-permute-start | bytes 442376 | tf_op jit(solution)/shard_map/ppermute | solution.py:548
  33.5 5.3 %collective-permute-start.6 = (bf16[144,512]{1,0:T(8,128)(2,1)S(1)}, bf16[144,512]{1,0:T(8,128)(2,1)S(1)}, u32[]{:S(2)}, u32[]{:S(2)}) collective-permute-start(bf16[144,512]{1,0:T(8,128)(2,1)S(1)} %chain_own.1.refs_3_), channel_id=1, source_target_pairs={{0,8},{1,0},{2,10},{3,2},{4,12},{5,4},{6,14},{7,6},{8,9},{9,1},{10... | collective-permute-start | bytes 442376 | tf_op jit(solution)/shard_map/ppermute | solution.py:540
  36.2 6.1 %collective-permute-start.8 = (bf16[144,512]{1,0:T(8,128)(2,1)S(1)}, bf16[144,512]{1,0:T(8,128)(2,1)S(1)}, u32[]{:S(2)}, u32[]{:S(2)}) collective-permute-start(bf16[144,512]{1,0:T(8,128)(2,1)S(1)} %pair_other.1.refs_5_.refs_1_), channel_id=1, source_target_pairs={{0,4},{1,0},{2,6},{3,2},{4,8},{5,1},{6,10},{7,3},{8,12},{9,5},{10,... | collective-permute-start | bytes 442376 | tf_op jit(solution)/shard_map/ppermute | solution.py:540
  42.4 6.5 %collective-permute-start.9 = (bf16[144,512]{1,0:T(8,128)(2,1)S(1)}, bf16[144,512]{1,0:T(8,128)(2,1)S(1)}, u32[]{:S(2)}, u32[]{:S(2)}) collective-permute-start(bf16[144,512]{1,0:T(8,128)(2,1)S(1)} %chain_other.1.refs_2_), channel_id=1, source_target_pairs={{0,8},{1,0},{2,10},{3,2},{4,12},{5,4},{6,14},{7,6},{8,9},{9,1},{10... | collective-permute-start | bytes 442376 | tf_op jit(solution)/shard_map/ppermute | solution.py:540
  46.1 5.3 %collective-permute-start.13 = (bf16[128,512]{1,0:T(8,128)(2,1)S(1)}, bf16[128,512]{1,0:T(8,128)(2,1)S(1)}, u32[]{:S(2)}, u32[]{:S(2)}) collective-permute-start(bf16[128,512]{1,0:T(8,128)(2,1)S(1)} %get-tuple-element.46), channel_id=1, source_target_pairs={{0,2},{2,0},{4,6},{6,4},{8,10},{10,8},{12,14},{14,12},{1,3},{3,1},... | collective-permute-start | bytes 393224 | tf_op jit(solution)/shard_map/ppermute | solution.py:614
  49.1 5.0 %collective-permute-start.11 = (bf16[128,512]{1,0:T(8,128)(2,1)S(1)}, bf16[128,512]{1,0:T(8,128)(2,1)S(1)}, u32[]{:S(2)}, u32[]{:S(2)}) collective-permute-start(bf16[128,512]{1,0:T(8,128)(2,1)S(1)} %get-tuple-element.45), channel_id=1, source_target_pairs={{0,2},{2,0},{4,6},{6,4},{8,10},{10,8},{12,14},{14,12},{1,3},{3,1},... | collective-permute-start | bytes 393224 | tf_op jit(solution)/shard_map/ppermute | solution.py:614
  56.6 2.0 %collective-permute-start.14 = (bf16[512,512]{1,0:T(8,128)(2,1)S(1)}, bf16[512,512]{1,0:T(8,128)(2,1)S(1)}, u32[]{:S(2)}, u32[]{:S(2)}) collective-permute-start(bf16[512,512]{1,0:T(8,128)(2,1)S(1)} %get-tuple-element.50), channel_id=1, source_target_pairs={{0,1},{1,0},{2,3},{3,2},{4,5},{5,4},{6,7},{7,6},{8,9},{9,8},{10,11... | collective-permute-start | bytes 1572872 | tf_op jit(solution)/shard_map/ppermute | solution.py:746

commit v4 on v3

--- a/solution.py
+++ b/solution.py
@@ -14,6 +14,7 @@
 EXTRA = 16
 CHUNK = 128
 TILE = 256
+BLOCK = 64
 MB = 1024 * 1024
 
 
@@ -90,13 +91,11 @@
     return jnp.concatenate([high, low], axis=1)
 
 
-def spread(value, width, head_size, first_head):
-    heads = value.shape[1]
+def head_matrix(heads, width, head_size, first_head):
     source = lax.broadcasted_iota(jnp.int32, (2 * heads, width), 0)
     source = jnp.where(source >= heads, source - heads, source)
     target = lax.broadcasted_iota(jnp.int32, (2 * heads, width), 1) // head_size + first_head
-    onehot = jnp.where(source == target, 1.0, 0.0).astype(BF16)
-    return dot(two_parts(value), onehot)
+    return jnp.where(source == target, 1.0, 0.0).astype(BF16)
 
 
 def prepare_kernel(
@@ -120,6 +119,8 @@
     gain_ref,
     bias_ref,
     rate_ref,
+    base_ref,
+    normed_ref,
     sems,
 ):
     rows = hidden_ref.shape[0]
@@ -151,24 +152,23 @@
     for r in range(count):
         copies[r].wait()
         low, high = r * CHUNK, (r + 1) * CHUNK
-        base = dot_tn(onehot[:, low:high], emb_ref[...])
-        merged = (hidden_ref[low:high, :].astype(F32) + base).astype(BF16).astype(F32)
-        mean = jnp.mean(merged * merged, axis=-1, keepdims=True)
-        normed = (merged * lax.rsqrt(mean + EPS)).astype(BF16)
+        base_ref[...] = dot_tn(onehot[:, low:high], emb_ref[...])
+        for q in range(low, high, HALO):
+            block = slice(q, q + HALO)
+            merged = hidden_ref[block, :].astype(F32) + base_ref[q - low : q - low + HALO, :]
+            merged = merged.astype(BF16).astype(F32)
+            mean = jnp.mean(merged * merged, axis=-1, keepdims=True)
+            normed_ref[q - low : q - low + HALO, :] = (merged * lax.rsqrt(mean + EPS)).astype(BF16)
 
         @pl.when(back)
         def _():
-            turned = flip_both(normed)
-            out_ref[rows - high : rows - low, :] = turned
-            if r == 0:
-                tail_ref[...] = turned[CHUNK - HALO :, :]
+            out_ref[rows - high : rows - low, :] = flip_both(normed_ref[...])
 
         @pl.when(jnp.logical_not(back))
         def _():
-            out_ref[low:high, :] = normed
-            if r == count - 1:
-                tail_ref[...] = normed[CHUNK - HALO :, :]
-
+            out_ref[low:high, :] = normed_ref[...]
+
+    tail_ref[...] = out_ref[rows - HALO :, :]
     for copy in small_copies[2:]:
         copy.wait()
     small_ref[:taps, :] = conv_ref[...]
@@ -198,13 +198,16 @@
             jax.ShapeDtypeStruct((SMALL_ROWS, inner), F32),
         ],
         scratch=[pltpu.VMEM(a.shape, a.dtype) for a in arrays]
+        + [pltpu.VMEM((CHUNK, width), F32), pltpu.VMEM((CHUNK, width), BF16)]
         + [pltpu.SemaphoreType.DMA((rows // CHUNK + len(arrays) - 1,))],
     )(*scalars, *(pltpu.with_memory_space_constraint(a, pltpu.HBM) for a in arrays))
 
 
-def gate_kernel(rows_ref, wg_ref, out_ref):
-    gate = dot(rows_ref[...], wg_ref[...]).astype(BF16).astype(F32)
-    out_ref[...] = silu(gate).astype(BF16)
+def gate_kernel(rows_ref, wg_ref, out_ref, gate_ref):
+    gate_ref[...] = dot(rows_ref[...], wg_ref[...])
+    for r in range(0, gate_ref.shape[0], BLOCK):
+        gate = gate_ref[r : r + BLOCK, :].astype(BF16).astype(F32)
+        out_ref[r : r + BLOCK, :] = silu(gate).astype(BF16)
 
 
 def gate_call(tag, normed, w_gate, after=()):
@@ -222,16 +225,17 @@
         ],
         out_specs=pl.BlockSpec((rows, TILE), lambda g: (0, g)),
         out_shape=jax.ShapeDtypeStruct((rows, inner), BF16),
+        scratch=[pltpu.VMEM((rows, TILE), F32)],
         after=after,
     )(normed, w_gate)
 
 
-def conv_silu(rows_ref, weights, rows):
+def conv_silu(rows_ref, weights, row):
     taps = weights.shape[0]
     total = None
     for k in range(taps):
-        offset = HALO - (taps - 1) + k
-        term = weights[k : k + 1, :] * rows_ref[offset : offset + rows, :]
+        offset = HALO - (taps - 1) + k + row
+        term = weights[k : k + 1, :] * rows_ref[offset : offset + BLOCK, :]
         total = term if total is None else total + term
     return silu(total).astype(BF16)
 
@@ -242,9 +246,10 @@
     before = dot(halo_ref[...], ws_ref[...]).astype(BF16).astype(F32)
     rows_ref[:HALO, :] = jnp.where(place_ref[0] >= 1, before, 0.0)
     rows_ref[HALO:, :] = dot(normed_ref[...], ws_ref[...]).astype(BF16).astype(F32)
-    state_conv = conv_silu(rows_ref, cs_ref[...], rows)
-    bc_ref[...] = state_conv
-    bt_ref[...] = state_conv[:, :states].astype(F32).T.astype(BF16)
+    weights = cs_ref[...]
+    for r in range(0, rows, BLOCK):
+        bc_ref[r : r + BLOCK, :] = conv_silu(rows_ref, weights, r)
+    bt_ref[...] = bc_ref[:, :states].astype(F32).T.astype(BF16)
 
 
 def maps_call(place, normed, halo, w_state, conv_state, after=()):
@@ -284,7 +289,11 @@
     send_ref,
     mine_ref,
     rows_ref,
+    spread_ref,
+    scaled_ref,
     step_ref,
+    left_ref,
+    whole_ref,
 ):
     rows = normed_ref.shape[0]
     states = bt_ref.shape[0]
@@ -300,34 +309,42 @@
         rate = small_ref[taps + 2 : taps + 3, :heads]
         raw = dot_nt(normed_ref[...], wt_ref[...]) + bias
         step = jnp.maximum(raw, 0.0) + jnp.log1p(jnp.exp(-jnp.abs(raw)))
-        step_ref[...] = step
+        step_ref[...] = two_parts(step)
         logdecay = -step * rate
         high = logdecay.astype(BF16)
         rest = logdecay - high.astype(F32)
         mid = rest.astype(BF16)
         low = (rest - mid.astype(F32)).astype(BF16)
         parts = jnp.concatenate([high, mid, low], axis=1)
-        to = lax.broadcasted_iota(jnp.int32, (rows, rows), 0)
-        frm = lax.broadcasted_iota(jnp.int32, (rows, rows), 1)
-        sums = dot(jnp.where(to >= frm, 1.0, 0.0).astype(BF16), parts)
-        cum = sums[:, :heads] + sums[:, heads : 2 * heads] + sums[:, 2 * heads :]
-        cum_ref[...] = cum
+        to = lax.broadcasted_iota(jnp.int32, (CHUNK, CHUNK), 0)
+        frm = lax.broadcasted_iota(jnp.int32, (CHUNK, CHUNK), 1)
+        lower = jnp.where(to >= frm, 1.0, 0.0).astype(BF16)
+        run = jnp.zeros((1, heads), F32)
+        for r in range(0, rows, CHUNK):
+            sums = dot(lower, parts[r : r + CHUNK, :])
+            sums = sums[:, :heads] + sums[:, heads : 2 * heads] + sums[:, 2 * heads :] + run
+            cum_ref[r : r + CHUNK, :] = sums
+            run = sums[CHUNK - 1 :, :]
+        cum = cum_ref[...]
         cumt_ref[...] = cum.T
+        left_ref[...] = two_parts(jnp.exp(run - cum))
+        whole_ref[...] = two_parts(jnp.exp(run))
 
     weights = wi_ref[...]
     before = dot(halo_ref[...], weights).astype(BF16).astype(F32)
     rows_ref[:HALO, :] = jnp.where(place_ref[0] >= 1, before, 0.0)
     rows_ref[HALO:, :] = dot(normed_ref[...], weights).astype(BF16).astype(F32)
+    onehot = head_matrix(heads, TILE, head_size, tile * (TILE // head_size))
+    spread_ref[0] = dot(step_ref[...], onehot)
+    spread_ref[1] = dot(left_ref[...], onehot)
     columns = pl.ds(pl.multiple_of(tile * TILE, TILE), TILE)
-    x = conv_silu(rows_ref, small_ref[:taps, columns], rows).astype(F32)
-    first = tile * (TILE // head_size)
-    xs = x * spread(step_ref[...], TILE, head_size, first)
-    xs_ref[...] = xs.astype(BF16)
-    cum = cum_ref[...]
-    total = cum[rows - 1 :, :]
-    left = spread(jnp.exp(total - cum), TILE, head_size, first)
-    state = dot(bt_ref[...], (xs * left).astype(BF16))
-    decay = spread(jnp.exp(total), TILE, head_size, first)
+    taps_here = small_ref[:taps, columns]
+    for r in range(0, rows, BLOCK):
+        xs = conv_silu(rows_ref, taps_here, r).astype(F32) * spread_ref[0, r : r + BLOCK, :]
+        xs_ref[r : r + BLOCK, :] = xs.astype(BF16)
+        scaled_ref[r : r + BLOCK, :] = (xs * spread_ref[1, r : r + BLOCK, :]).astype(BF16)
+    state = dot(bt_ref[...], scaled_ref[...])
+    decay = dot(whole_ref[...], onehot)
 
     @pl.when(g < tiles // 2)
     def _():
@@ -383,7 +400,14 @@
             jax.ShapeDtypeStruct((states + EXTRA, inner // 2), BF16),
             jax.ShapeDtypeStruct((states + EXTRA, inner // 2), BF16),
         ],
-        scratch=[pltpu.VMEM((rows + HALO, TILE), F32), pltpu.VMEM((rows, heads), F32)],
+        scratch=[
+            pltpu.VMEM((rows + HALO, TILE), F32),
+            pltpu.VMEM((2, rows, TILE), F32),
+            pltpu.VMEM((rows, TILE), BF16),
+            pltpu.VMEM((rows, 2 * heads), BF16),
+            pltpu.VMEM((rows, 2 * heads), BF16),
+            pltpu.VMEM((1, 2 * heads), BF16),
+        ],
         after=after,
     )(place, parity, normed, halo, bt, w_inner, w_step_t, small)
 
@@ -407,30 +431,32 @@
     cumt = cumt_ref[...]
     last = length - 1
     end = cum[last:, :]
-    since = spread(jnp.exp(cum - prev_ref[...]), inner, head_size, 0)
-    left = spread(jnp.exp(end - cum), inner, head_size, 0)
-    state = state_ref[...]
-    carried = dot(cmat, state.astype(BF16)) * since
-    xs = xs_ref[...]
-    scaled = (xs.astype(F32) * left).astype(BF16)
-    state_ref[...] = state * since[last:, :] + dot_tn(bmat, scaled)
+    since = two_parts(jnp.exp(cum - prev_ref[...]))
+    left = two_parts(jnp.exp(end - cum))
     prev_ref[...] = end
     pair = 2 * head_size
     lane = lax.broadcasted_iota(jnp.int32, (length, pair), 1)
-    for p in range(heads // 2):
-        weights = []
-        for h in (2 * p, 2 * p + 1):
-            apart = jnp.minimum(cum[:, h : h + 1] - cumt[h : h + 1, :], 0.0)
-            weights.append((jnp.exp(apart) * scores).astype(BF16))
-        mine = xs[:, p * pair : (p + 1) * pair]
-        none = jnp.zeros_like(mine)
-        stacked = jnp.concatenate(
-            [jnp.where(lane < head_size, mine, none), jnp.where(lane < head_size, none, mine)], axis=0
-        )
-        inside = dot(jnp.concatenate(weights, axis=1), stacked)
-        y_ref[:, p * pair : (p + 1) * pair] = (
-            inside + carried[:, p * pair : (p + 1) * pair]
-        ).astype(BF16)
+    for first in range(0, heads, TILE // head_size):
+        columns = slice(first * head_size, first * head_size + TILE)
+        onehot = head_matrix(heads, TILE, head_size, first)
+        since_here = dot(since, onehot)
+        state = state_ref[:, columns]
+        carried = dot(cmat, state.astype(BF16)) * since_here
+        scaled = (xs_ref[:, columns].astype(F32) * dot(left, onehot)).astype(BF16)
+        state_ref[:, columns] = state * since_here[last:, :] + dot_tn(bmat, scaled)
+        for start in range(0, TILE, pair):
+            low = first * head_size + start
+            weights = []
+            for h in (low // head_size, low // head_size + 1):
+                apart = jnp.minimum(cum[:, h : h + 1] - cumt[h : h + 1, :], 0.0)
+                weights.append((jnp.exp(apart) * scores).astype(BF16))
+            mine = xs_ref[:, low : low + pair]
+            none = jnp.zeros_like(mine)
+            stacked = jnp.concatenate(
+                [jnp.where(lane < head_size, mine, none), jnp.where(lane < head_size, none, mine)], axis=0
+            )
+            inside = dot(jnp.concatenate(weights, axis=1), stacked)
+            y_ref[:, low : low + pair] = (inside + carried[:, start : start + pair]).astype(BF16)
 
 
 def inside_call(tag, xs, bc, cum, cumt, after=()):
@@ -614,45 +640,60 @@
         return keep, lax.ppermute(out, "seq", self.swap)
 
 
-def gated_part(head_size, swap, y_ref, bc_ref, cum_ref, keep_ref, other_ref, gate_ref, small_ref, wo_ref):
-    inner = y_ref.shape[1]
+def gated_part(
+    head_size, swap, y_ref, bc_ref, cum_ref, keep_ref, other_ref, gate_ref, small_ref, wo_ref, scaled_ref
+):
+    rows, inner = y_ref.shape
     states = bc_ref.shape[1] // 2
+    heads = cum_ref.shape[1]
+    half = inner // 2
     cmat = bc_ref[:, states:]
-    keep = keep_ref[...]
-    other = other_ref[...]
-    entry = jnp.concatenate([jnp.where(swap, other, keep), jnp.where(swap, keep, other)], axis=1)
-    carried = dot(cmat, entry) * spread(jnp.exp(cum_ref[...]), inner, head_size, 0)
-    gated = (y_ref[...].astype(F32) + carried) * gate_ref[...].astype(F32)
-    squares = jnp.sum(gated * gated, axis=-1, keepdims=True)
-    gain = small_ref[SMALL_TAPS : SMALL_TAPS + 1, :]
-    return dot((gated * gain).astype(BF16), wo_ref[...]), squares
+    since = two_parts(jnp.exp(cum_ref[...]))
+    squares = [0.0] * (rows // BLOCK)
+    for low in range(0, inner, TILE):
+        columns = slice(low, low + TILE)
+        here = slice(low % half, low % half + TILE)
+        use_other = swap if low < half else jnp.logical_not(swap)
+        entry = jnp.where(use_other, other_ref[:, here], keep_ref[:, here])
+        onehot = head_matrix(heads, TILE, head_size, low // head_size)
+        gain = small_ref[SMALL_TAPS : SMALL_TAPS + 1, columns]
+        for i, r in enumerate(range(0, rows, BLOCK)):
+            block = slice(r, r + BLOCK)
+            carried = dot(cmat[block, :], entry) * dot(since[block, :], onehot)
+            gated = (y_ref[block, columns].astype(F32) + carried) * gate_ref[block, columns].astype(F32)
+            squares[i] += jnp.sum(gated * gated, axis=-1, keepdims=True)
+            scaled_ref[block, columns] = (gated * gain).astype(BF16)
+    return squares
 
 
 def part_kernel(head_size, back_ref, parity_ref, *refs):
-    *ins, out_ref, sq_ref = refs
-    result, squares = gated_part(head_size, parity_ref[0] == 1, *ins)
-    out_ref[...] = result
-    sq_ref[...] = jnp.broadcast_to(squares, sq_ref.shape)
+    *ins, out_ref, sq_ref, scaled_ref = refs
+    squares = gated_part(head_size, parity_ref[0] == 1, *ins, scaled_ref)
+    for i, square in enumerate(squares):
+        sq_ref[i * BLOCK : (i + 1) * BLOCK, :] = jnp.broadcast_to(square, (BLOCK, sq_ref.shape[1]))
+    out_ref[...] = dot(scaled_ref[...], ins[-1][...])
 
 
 def finish_kernel(head_size, full_width, back_ref, parity_ref, *refs):
-    *ins, part_ref, psq_ref, own_ref, send_ref = refs
-    result, squares = gated_part(head_size, parity_ref[0] == 1, *ins)
-    squares = squares + psq_ref[:, :1]
-    result = (result + part_ref[...]) * lax.rsqrt(squares / full_width + EPS)
-    result = result.astype(BF16)
+    *ins, part_ref, psq_ref, own_ref, send_ref, scaled_ref, sum_ref, out_ref = refs
+    squares = gated_part(head_size, parity_ref[0] == 1, *ins, scaled_ref)
+    sum_ref[...] = dot(scaled_ref[...], ins[-1][...])
     half = own_ref.shape[1]
+    for i, square in enumerate(squares):
+        block = slice(i * BLOCK, (i + 1) * BLOCK)
+        scale = lax.rsqrt((square + psq_ref[block, :1]) / full_width + EPS)
+        out_ref[block, :] = ((sum_ref[block, :] + part_ref[block, :]) * scale).astype(BF16)
 
     @pl.when(back_ref[0] == 1)
     def _():
-        turned = flip_both(result)
+        turned = flip_both(out_ref[...])
         own_ref[...] = turned[:, half:]
         send_ref[...] = turned[:, :half]
 
     @pl.when(back_ref[0] != 1)
     def _():
-        own_ref[...] = result[:, :half]
-        send_ref[...] = result[:, half:]
+        own_ref[...] = out_ref[:, :half]
+        send_ref[...] = out_ref[:, half:]
 
 
 def finish_call(back, parity, y, bc, cum, keep, other, gate, small, w_output, full_width=None, partial=None, after=()):
@@ -683,10 +724,16 @@
     ]
     arrays = [y, bc, cum, keep, other, gate, small, w_output]
     if partial is None:
+        scratch = [pltpu.VMEM((TILE, inner), BF16)]
         kernel = functools.partial(part_kernel, inner // heads)
         out_specs = [block(width), block(128)]
         out_shape = [jax.ShapeDtypeStruct((rows, width), F32), jax.ShapeDtypeStruct((rows, 128), F32)]
     else:
+        scratch = [
+            pltpu.VMEM((TILE, inner), BF16),
+            pltpu.VMEM((TILE, width), F32),
+            pltpu.VMEM((TILE, width), BF16),
+        ]
         kernel = functools.partial(finish_kernel, inner // heads, full_width)
         in_specs += [block(width), block(128)]
         arrays += list(partial)
@@ -702,12 +749,15 @@
         in_specs=in_specs,
         out_specs=out_specs,
         out_shape=out_shape,
+        scratch=scratch,
         after=after,
     )(back, parity, *arrays)
 
 
 def total_kernel(mine_ref, theirs_ref, out_ref):
-    out_ref[...] = (mine_ref[...].astype(F32) + theirs_ref[...].astype(F32)).astype(BF16)
+    for r in range(0, mine_ref.shape[0], BLOCK):
+        block = slice(r, r + BLOCK)
+        out_ref[block, :] = (mine_ref[block, :].astype(F32) + theirs_ref[block, :].astype(F32)).astype(BF16)
 
 
 def total_call(mine, theirs):

time: 61.1 us -> 61.1 us (level)
  no operation moved by 1% of the time
where the time goes in v4:
time: 61.1 us; the launch traced here: 60 us
  Pallas kernels  36.4 us (60%)
  starting transfers between devices  18 us (29%)
  waiting for transfers between devices  5.34 us (9%)
    pallas_call x17, Pallas kernels, call(): return lambda *arrays: run(*arrays, *after)  36.4 us
    ppermute x5, starting transfers between devices, onward(): return lax.ppermute(value, ('seq', 'ch'), pairs)  10.8 us
    ppermute x2, starting transfers between devices, __init__(): self.other = lax.ppermute(send, 'seq', self.swap)  3.49 us
    ppermute x5, waiting for transfers between devices, onward(): return lax.ppermute(value, ('seq', 'ch'), pairs)  2.3 us
    ppermute x2, starting transfers between devices, entry(): return (keep, lax.ppermute(out, 'seq', self.swap))  2.09 us
    ppermute x6, waiting for transfers between devices, theirs(): return lax.ppermute(a, 'ch', swap)  1.91 us
    ppermute x6, starting transfers between devices, theirs(): return lax.ppermute(a, 'ch', swap)  1.61 us
  transfers between devices with their start and end apart: 15, of which 4 were waited for; matrix products, arithmetic and copies ran while one was open for 0% of the time, Pallas kernels for 54%

profile of v4, /device:TPU:0, one launch (start us, length us, event | category | flops | bytes accessed | tf_op | source)
XLA Modules:
  0.0 60.0 jit_solution(64001021678891578)
XLA Ops:
  0.5 2.7 %prepare.1 = (bf16[512,1024]{1,0:T(8,128)(2,1)S(1)}, bf16[16,1024]{1,0:T(8,128)(2,1)S(1)}, f32[8,1024]{1,0:T(8,128)S(1)}) custom-call(s32[1]{0:T(128)} %bitcast.refs_0_, s32[1]{0:T(128)} %bitcast.1.refs_1_, s32[1]{0:T(128)} %bitcast.2.refs_2_.refs_0_, bf16[512,1024]{1,0:T(8,128)(2,1)} %refs_3_.2, s32[1,512]{1,0:T(1,128)} %bitcast.11, ...), custom_call_target="tpu_custom_call" | custom-call | flops 1650000000 | bytes 1500000 | tf_op jit(solution)/shard_map/prepare/pallas_call | solution.py:46
  3.2 2.6 %collective-permute-start = (bf16[16,1024]{1,0:T(8,128)(2,1)S(1)}, bf16[16,1024]{1,0:T(8,128)(2,1)S(1)}, u32[]{:S(2)}, u32[]{:S(2)}) collective-permute-start(bf16[16,1024]{1,0:T(8,128)(2,1)S(1)} %get-tuple-element.29), channel_id=1, source_target_pairs={{0,2},{1,0},{2,4},{3,1},{4,6},{5,3},{6,8},{7,5},{8,10},{9,7},{10,1... | collective-permute-start | bytes 98312 | tf_op jit(solution)/shard_map/ppermute | solution.py:566
  5.8 0.5 collective-permute-start.2
  6.3 2.2 %gate_own.1.refs_5_.refs_7_ = bf16[512,1024]{1,0:T(8,128)(2,1)S(1)} custom-call(bf16[512,1024]{1,0:T(8,128)(2,1)S(1)} %get-tuple-element.28.refs_0_.refs_1_.refs_2_, bf16[1024,1024]{1,0:T(8,128)(2,1)S(1)} %copy-done.1), custom_call_target="tpu_custom_call" | custom-call | flops 2640000000 | bytes 2400000 | tf_op jit(solution)/shard_map/gate_own/pallas_call | solution.py:46
  8.6 0.5 collective-permute-start.12
  9.1 1.1 %maps.1 = (bf16[512,256]{1,0:T(8,128)(2,1)S(1)}, bf16[128,512]{1,0:T(8,128)(2,1)S(1)}) custom-call(s32[1]{0:T(128)} %bitcast.2.refs_2_.refs_0_, bf16[512,1024]{1,0:T(8,128)(2,1)S(1)} %get-tuple-element.28.refs_0_.refs_1_.refs_2_, bf16[16,1024]{1,0:T(8,128)(2,1)S(1)} %collective-permute-done.refs_2_.refs_3_, bf16[1024,256]{1,0:T(8,128)(2,1)S(1)} %copy-done.3, ...), custom_call_target="tpu_custom_call" | custom-call | flops 1650000000 | bytes 1500000 | tf_op jit(solution)/shard_map/maps/pallas_call | solution.py:46
  10.2 7.3 %local_own.1 = (bf16[512,1024]{1,0:T(8,128)(2,1)S(1)}, f32[512,16]{1,0:T(8,128)S(1)}, f32[16,512]{1,0:T(8,128)S(1)}, bf16[144,512]{1,0:T(8,128)(2,1)S(1)}, bf16[144,512]{1,0:T(8,128)(2,1)S(1)}) custom-call(s32[1]{0:T(128)} %bitcast.2.refs_2_.refs_0_, s32[1]{0:T(128)} %bitcast.1.refs_1_, bf16[512,1024]{1,0:T(8,128)(2,1)S(1)} %get-tuple-element.28.refs_0_.refs_1_.refs_2_, ...), custom_call_target="tpu_custom_call" | custom-call | flops 5500000256 | bytes 5000000 | tf_op jit(solution)/shard_map/local_own/pallas_call | solution.py:46
  17.5 2.3 %collective-permute-start.4 = (bf16[144,512]{1,0:T(8,128)(2,1)S(1)}, bf16[144,512]{1,0:T(8,128)(2,1)S(1)}, u32[]{:S(2)}, u32[]{:S(2)}) collective-permute-start(bf16[144,512]{1,0:T(8,128)(2,1)S(1)} %get-tuple-element.37), channel_id=1, source_target_pairs={{0,2},{2,0},{4,6},{6,4},{8,10},{10,8},{12,14},{14,12},{1,3},{3,1},... | collective-permute-start | bytes 442376 | tf_op jit(solution)/shard_map/ppermute | solution.py:574
  19.9 7.3 %local_other.1 = (bf16[512,1024]{1,0:T(8,128)(2,1)S(1)}, f32[512,16]{1,0:T(8,128)S(1)}, f32[16,512]{1,0:T(8,128)S(1)}, bf16[144,512]{1,0:T(8,128)(2,1)S(1)}, bf16[144,512]{1,0:T(8,128)(2,1)S(1)}) custom-call(s32[1]{0:T(128)} %bitcast.2.refs_2_.refs_0_, s32[1]{0:T(128)} %bitcast.1.refs_1_, bf16[512,1024]{1,0:T(8,128)(2,1)S(1)} %get-tuple-element.28.refs_0_.refs_1_.refs_2_, ...), custom_call_target="tpu_custom_call" | custom-call | flops 5500000256 | bytes 5000000 | tf_op jit(solution)/shard_map/local_other/pallas_call | solution.py:46
  27.2 1.6 %collective-permute-start.5 = (bf16[144,512]{1,0:T(8,128)(2,1)S(1)}, bf16[144,512]{1,0:T(8,128)(2,1)S(1)}, u32[]{:S(2)}, u32[]{:S(2)}) collective-permute-start(bf16[144,512]{1,0:T(8,128)(2,1)S(1)} %pair_own.1.refs_4_.refs_1_), channel_id=1, source_target_pairs={{0,4},{1,0},{2,6},{3,2},{4,8},{5,1},{6,10},{7,3},{8,12},{9,5},{10,... | collective-permute-start | bytes 442376 | tf_op jit(solution)/shard_map/ppermute | solution.py:566
  28.8 1.2 %collective-permute-start.7 = (bf16[144,512]{1,0:T(8,128)(2,1)S(1)}, bf16[144,512]{1,0:T(8,128)(2,1)S(1)}, u32[]{:S(2)}, u32[]{:S(2)}) collective-permute-start(bf16[144,512]{1,0:T(8,128)(2,1)S(1)} %get-tuple-element.42), channel_id=1, source_target_pairs={{0,2},{2,0},{4,6},{6,4},{8,10},{10,8},{12,14},{14,12},{1,3},{3,1},... | collective-permute-start | bytes 442376 | tf_op jit(solution)/shard_map/ppermute | solution.py:574
  30.0 3.4 %inside_own.1.refs_3_.refs_2_ = bf16[512,1024]{1,0:T(8,128)(2,1)S(1)} custom-call(bf16[512,1024]{1,0:T(8,128)(2,1)S(1)} %get-tuple-element.38.refs_0_, bf16[512,256]{1,0:T(8,128)(2,1)S(1)} %get-tuple-element.34.refs_1_.refs_3_, f32[512,16]{1,0:T(8,128)S(1)} %get-tuple-element.39.refs_2_.refs_4_, f32[16,512]{1,0:T(8,128)S(1)} %get-tuple-element.40.refs_3_, ...), custom_call_target="tpu_custom_call" | custom-call | flops 3520000000 | bytes 3200000 | tf_op jit(solution)/shard_map/inside_own/pallas_call | solution.py:46
  33.5 2.7 %collective-permute-start.6 = (bf16[144,512]{1,0:T(8,128)(2,1)S(1)}, bf16[144,512]{1,0:T(8,128)(2,1)S(1)}, u32[]{:S(2)}, u32[]{:S(2)}) collective-permute-start(bf16[144,512]{1,0:T(8,128)(2,1)S(1)} %chain_own.1.refs_3_), channel_id=1, source_target_pairs={{0,8},{1,0},{2,10},{3,2},{4,12},{5,4},{6,14},{7,6},{8,9},{9,1},{10... | collective-permute-start | bytes 442376 | tf_op jit(solution)/shard_map/ppermute | solution.py:566
  36.5 2.3 %collective-permute-done.6.refs_4_ = bf16[144,512]{1,0:T(8,128)(2,1)S(1)} collective-permute-done((bf16[144,512]{1,0:T(8,128)(2,1)S(1)}, bf16[144,512]{1,0:T(8,128)(2,1)S(1)}, u32[]{:S(2)}, u32[]{:S(2)}) %collective-permute-start.6) | collective-permute-done | bytes 147488 | tf_op jit(solution)/shard_map/ppermute | solution.py:566
  39.0 3.4 %inside_other.1.refs_3_.refs_2_ = bf16[512,1024]{1,0:T(8,128)(2,1)S(1)} custom-call(bf16[512,1024]{1,0:T(8,128)(2,1)S(1)} %get-tuple-element.33.refs_3_.refs_0_, bf16[512,256]{1,0:T(8,128)(2,1)S(1)} %get-tuple-element.34.refs_1_.refs_3_, f32[512,16]{1,0:T(8,128)S(1)} %get-tuple-element.35.refs_2_.refs_4_, f32[16,512]{1,0:T(8,128)S(1)} %get-tuple-element.36.refs_3_, ...), custom_call_target="tpu_custom_call" | custom-call | flops 3520000000 | bytes 3200000 | tf_op jit(solution)/shard_map/inside_other/pallas_call | solution.py:46
  42.5 3.7 %collective-permute-start.9 = (bf16[144,512]{1,0:T(8,128)(2,1)S(1)}, bf16[144,512]{1,0:T(8,128)(2,1)S(1)}, u32[]{:S(2)}, u32[]{:S(2)}) collective-permute-start(bf16[144,512]{1,0:T(8,128)(2,1)S(1)} %chain_other.1.refs_2_), channel_id=1, source_target_pairs={{0,8},{1,0},{2,10},{3,2},{4,12},{5,4},{6,14},{7,6},{8,9},{9,1},{10... | collective-permute-start | bytes 442376 | tf_op jit(solution)/shard_map/ppermute | solution.py:566
  46.1 0.6 %collective-permute-start.13 = (bf16[128,512]{1,0:T(8,128)(2,1)S(1)}, bf16[128,512]{1,0:T(8,128)(2,1)S(1)}, u32[]{:S(2)}, u32[]{:S(2)}) collective-permute-start(bf16[128,512]{1,0:T(8,128)(2,1)S(1)} %get-tuple-element.46), channel_id=1, source_target_pairs={{0,2},{2,0},{4,6},{6,4},{8,10},{10,8},{12,14},{14,12},{1,3},{3,1},... | collective-permute-start | bytes 393224 | tf_op jit(solution)/shard_map/ppermute | solution.py:640
  46.7 2.2 %gate_other.1.refs_5_.refs_7_ = bf16[512,1024]{1,0:T(8,128)(2,1)S(1)} custom-call(bf16[512,1024]{1,0:T(8,128)(2,1)S(1)} %get-tuple-element.28.refs_0_.refs_1_.refs_2_, bf16[1024,1024]{1,0:T(8,128)(2,1)S(1)} %collective-permute-done.10.refs_1_, bf16[144,512]{1,0:T(8,128)(2,1)S(1)} %chain_other.1.refs_2_), custom_call_target="tpu_custom_call" | custom-call | flops 2640000000 | bytes 2400000 | tf_op jit(solution)/shard_map/gate_other/pallas_call | solution.py:46
  49.1 1.5 %collective-permute-start.11 = (bf16[128,512]{1,0:T(8,128)(2,1)S(1)}, bf16[128,512]{1,0:T(8,128)(2,1)S(1)}, u32[]{:S(2)}, u32[]{:S(2)}) collective-permute-start(bf16[128,512]{1,0:T(8,128)(2,1)S(1)} %get-tuple-element.45), channel_id=1, source_target_pairs={{0,2},{2,0},{4,6},{6,4},{8,10},{10,8},{12,14},{14,12},{1,3},{3,1},... | collective-permute-start | bytes 393224 | tf_op jit(solution)/shard_map/ppermute | solution.py:640
  50.6 0.8 %collective-permute-done.13.refs_6_ = bf16[128,512]{1,0:T(8,128)(2,1)S(1)} collective-permute-done((bf16[128,512]{1,0:T(8,128)(2,1)S(1)}, bf16[128,512]{1,0:T(8,128)(2,1)S(1)}, u32[]{:S(2)}, u32[]{:S(2)}) %collective-permute-start.13) | collective-permute-done | bytes 131104 | tf_op jit(solution)/shard_map/ppermute | solution.py:640
  51.4 2.4 %part.1 = (f32[512,1024]{1,0:T(8,128)S(1)}, f32[512,128]{1,0:T(8,128)S(1)}) custom-call(s32[1]{0:T(128)} %bitcast.refs_0_, s32[1]{0:T(128)} %bitcast.1.refs_1_, bf16[512,1024]{1,0:T(8,128)(2,1)S(1)} %inside_own.1.refs_3_.refs_2_, bf16[512,256]{1,0:T(8,128)(2,1)S(1)} %get-tuple-element.34.refs_1_.refs_3_, f32[512,16]{1,0:T(8,128)S(1)} %get-tuple-element.39.refs_2_.refs_4_, ...), custom_call_target="tpu_custom_call" | custom-call | flops 3849999872 | bytes 3500000 | tf_op jit(solution)/shard_map/part/pallas_call | solution.py:46
  54.2 2.5 %finish.1 = (bf16[512,512]{1,0:T(8,128)(2,1)S(1)}, bf16[512,512]{1,0:T(8,128)(2,1)S(1)}) custom-call(s32[1]{0:T(128)} %bitcast.refs_0_, s32[1]{0:T(128)} %bitcast.1.refs_1_, bf16[512,1024]{1,0:T(8,128)(2,1)S(1)} %inside_other.1.refs_3_.refs_2_, bf16[512,256]{1,0:T(8,128)(2,1)S(1)} %get-tuple-element.34.refs_1_.refs_3_, ...), custom_call_target="tpu_custom_call" | custom-call | flops 3849999872 | bytes 3500000 | tf_op jit(solution)/shard_map/finish/pallas_call | solution.py:46
  56.7 1.9 %collective-permute-done.14.refs_1_ = bf16[512,512]{1,0:T(8,128)(2,1)S(1)} collective-permute-done((bf16[512,512]{1,0:T(8,128)(2,1)S(1)}, bf16[512,512]{1,0:T(8,128)(2,1)S(1)}, u32[]{:S(2)}, u32[]{:S(2)}) %collective-permute-start.14) | collective-permute-done | bytes 524320 | tf_op jit(solution)/shard_map/ppermute | solution.py:796
  58.6 1.4 %total.1 = bf16[512,512]{1,0:T(8,128)(2,1)} custom-call(bf16[512,512]{1,0:T(8,128)(2,1)S(1)} %get-tuple-element.49.refs_0_, bf16[512,512]{1,0:T(8,128)(2,1)S(1)} %collective-permute-done.14.refs_1_), custom_call_target="tpu_custom_call" | custom-call | flops 880000000 | bytes 800000 | tf_op jit(solution)/shard_map/total/pallas_call | solution.py:46
  (35 shorter events, 1.9 us)
Async XLA Ops:
  0.0 19.9 %collective-permute-start.1 = (bf16[1024,1024]{1,0:T(8,128)(2,1)}, bf16[1024,1024]{1,0:T(8,128)(2,1)S(1)}, u32[]{:S(2)}, u32[]{:S(2)}) collective-permute-start(bf16[1024,1024]{1,0:T(8,128)(2,1)} %refs_5_.3), channel_id=1, source_target_pairs={{0,1},{1,0},{2,3},{3,2},{4,5},{5,4},{6,7},{7,6},{8,9},{9,8},{10,11... | collective-permute-start | bytes 6291464 | tf_op jit(solution)/shard_map/ppermute | solution.py:796
  0.5 5.3 %copy-start.4 = (bf16[1024,16]{0,1:T(8,128)(2,1)S(1)}, bf16[1024,16]{0,1:T(8,128)(2,1)}, u32[]{:S(2)}) copy-start(bf16[1024,16]{0,1:T(8,128)(2,1)} %param.19) | copy-start | bytes 98308
  0.5 5.8 %copy-start.1 = (bf16[1024,1024]{1,0:T(8,128)(2,1)S(1)}, bf16[1024,1024]{1,0:T(8,128)(2,1)}, u32[]{:S(2)}) copy-start(bf16[1024,1024]{1,0:T(8,128)(2,1)} %refs_1_.1) | copy-start | bytes 6291460
  3.2 5.4 %collective-permute-start = (bf16[16,1024]{1,0:T(8,128)(2,1)S(1)}, bf16[16,1024]{1,0:T(8,128)(2,1)S(1)}, u32[]{:S(2)}, u32[]{:S(2)}) collective-permute-start(bf16[16,1024]{1,0:T(8,128)(2,1)S(1)} %get-tuple-element.29), channel_id=1, source_target_pairs={{0,2},{1,0},{2,4},{3,1},{4,6},{5,3},{6,8},{7,5},{8,10},{9,7},{10,1... | collective-permute-start | bytes 98312 | tf_op jit(solution)/shard_map/ppermute | solution.py:566
  5.7 11.8 %collective-permute-start.3 = (f32[8,1024]{1,0:T(8,128)S(1)}, f32[8,1024]{1,0:T(8,128)S(1)}, u32[]{:S(2)}, u32[]{:S(2)}) collective-permute-start(f32[8,1024]{1,0:T(8,128)S(1)} %get-tuple-element.31.refs_7_.refs_8_), channel_id=1, source_target_pairs={{0,1},{1,0},{2,3},{3,2},{4,5},{5,4},{6,7},{7,6},{8,9},{9,8},{10,11... | collective-permute-start | bytes 98312 | tf_op jit(solution)/shard_map/ppermute | solution.py:796
  5.8 14.1 %collective-permute-start.2 = (bf16[16,1024]{1,0:T(8,128)(2,1)S(1)}, bf16[16,1024]{1,0:T(8,128)(2,1)S(1)}, u32[]{:S(2)}, u32[]{:S(2)}) collective-permute-start(bf16[16,1024]{1,0:T(8,128)(2,1)S(1)} %bitcast.8), channel_id=1, source_target_pairs={{0,1},{1,0},{2,3},{3,2},{4,5},{5,4},{6,7},{7,6},{8,9},{9,8},{10,11... | collective-permute-start | bytes 98312 | tf_op jit(solution)/shard_map/ppermute | solution.py:796
  6.3 40.5 %collective-permute-start.10 = (bf16[1024,1024]{1,0:T(8,128)(2,1)S(1)}, bf16[1024,1024]{1,0:T(8,128)(2,1)S(1)}, u32[]{:S(2)}, u32[]{:S(2)}) collective-permute-start(bf16[1024,1024]{1,0:T(8,128)(2,1)S(1)} %copy-done.1), channel_id=1, source_target_pairs={{0,1},{1,0},{2,3},{3,2},{4,5},{5,4},{6,7},{7,6},{8,9},{9,8},{10,11... | collective-permute-start | bytes 6291464 | tf_op jit(solution)/shard_map/ppermute | solution.py:796
  6.3 2.3 %copy-start.2 = (bf16[1024,1024]{1,0:T(8,128)(2,1)S(1)}, bf16[1024,1024]{1,0:T(8,128)(2,1)}, u32[]{:S(2)}) copy-start(bf16[1024,1024]{1,0:T(8,128)(2,1)} %refs_9_.1) | copy-start | bytes 6291460
  6.3 2.8 %copy-start.3 = (bf16[1024,256]{1,0:T(8,128)(2,1)S(1)}, bf16[1024,256]{1,0:T(8,128)(2,1)}, u32[]{:S(2)}) copy-start(bf16[1024,256]{1,0:T(8,128)(2,1)} %refs_3_.3) | copy-start | bytes 1572868
  6.3 2.8 %copy-start.5 = (f32[4,256]{1,0:T(4,128)S(1)}, f32[4,256]{1,0:T(4,128)}, u32[]{:S(2)}) copy-start(f32[4,256]{1,0:T(4,128)} %refs_4_.1) | copy-start | bytes 12292
  8.6 1.6 %copy-start = (bf16[1024,1024]{1,0:T(8,128)(2,1)S(1)}, bf16[1024,1024]{1,0:T(8,128)(2,1)}, u32[]{:S(2)}) copy-start(bf16[1024,1024]{1,0:T(8,128)(2,1)} %refs_5_.3) | copy-start | bytes 6291460
  8.6 45.2 %collective-permute-start.12 = (bf16[1024,1024]{1,0:T(8,128)(2,1)S(1)}, bf16[1024,1024]{1,0:T(8,128)(2,1)S(1)}, u32[]{:S(2)}, u32[]{:S(2)}) collective-permute-start(bf16[1024,1024]{1,0:T(8,128)(2,1)S(1)} %copy-done.2), channel_id=1, source_target_pairs={{0,1},{1,0},{2,3},{3,2},{4,5},{5,4},{6,7},{7,6},{8,9},{9,8},{10,11... | collective-permute-start | bytes 6291464 | tf_op jit(solution)/shard_map/ppermute | solution.py:796
  17.5 9.6 %collective-permute-start.4 = (bf16[144,512]{1,0:T(8,128)(2,1)S(1)}, bf16[144,512]{1,0:T(8,128)(2,1)S(1)}, u32[]{:S(2)}, u32[]{:S(2)}) collective-permute-start(bf16[144,512]{1,0:T(8,128)(2,1)S(1)} %get-tuple-element.37), channel_id=1, source_target_pairs={{0,2},{2,0},{4,6},{6,4},{8,10},{10,8},{12,14},{14,12},{1,3},{3,1},... | collective-permute-start | bytes 442376 | tf_op jit(solution)/shard_map/ppermute | solution.py:574
  27.2 6.1 %collective-permute-start.5 = (bf16[144,512]{1,0:T(8,128)(2,1)S(1)}, bf16[144,512]{1,0:T(8,128)(2,1)S(1)}, u32[]{:S(2)}, u32[]{:S(2)}) collective-permute-start(bf16[144,512]{1,0:T(8,128)(2,1)S(1)} %pair_own.1.refs_4_.refs_1_), channel_id=1, source_target_pairs={{0,4},{1,0},{2,6},{3,2},{4,8},{5,1},{6,10},{7,3},{8,12},{9,5},{10,... | collective-permute-start | bytes 442376 | tf_op jit(solution)/shard_map/ppermute | solution.py:566
  28.8 7.3 %collective-permute-start.7 = (bf16[144,512]{1,0:T(8,128)(2,1)S(1)}, bf16[144,512]{1,0:T(8,128)(2,1)S(1)}, u32[]{:S(2)}, u32[]{:S(2)}) collective-permute-start(bf16[144,512]{1,0:T(8,128)(2,1)S(1)} %get-tuple-element.42), channel_id=1, source_target_pairs={{0,2},{2,0},{4,6},{6,4},{8,10},{10,8},{12,14},{14,12},{1,3},{3,1},... | collective-permute-start | bytes 442376 | tf_op jit(solution)/shard_map/ppermute | solution.py:574
  33.5 5.4 %collective-permute-start.6 = (bf16[144,512]{1,0:T(8,128)(2,1)S(1)}, bf16[144,512]{1,0:T(8,128)(2,1)S(1)}, u32[]{:S(2)}, u32[]{:S(2)}) collective-permute-start(bf16[144,512]{1,0:T(8,128)(2,1)S(1)} %chain_own.1.refs_3_), channel_id=1, source_target_pairs={{0,8},{1,0},{2,10},{3,2},{4,12},{5,4},{6,14},{7,6},{8,9},{9,1},{10... | collective-permute-start | bytes 442376 | tf_op jit(solution)/shard_map/ppermute | solution.py:566
  36.2 6.2 %collective-permute-start.8 = (bf16[144,512]{1,0:T(8,128)(2,1)S(1)}, bf16[144,512]{1,0:T(8,128)(2,1)S(1)}, u32[]{:S(2)}, u32[]{:S(2)}) collective-permute-start(bf16[144,512]{1,0:T(8,128)(2,1)S(1)} %pair_other.1.refs_5_.refs_1_), channel_id=1, source_target_pairs={{0,4},{1,0},{2,6},{3,2},{4,8},{5,1},{6,10},{7,3},{8,12},{9,5},{10,... | collective-permute-start | bytes 442376 | tf_op jit(solution)/shard_map/ppermute | solution.py:566
  42.5 6.5 %collective-permute-start.9 = (bf16[144,512]{1,0:T(8,128)(2,1)S(1)}, bf16[144,512]{1,0:T(8,128)(2,1)S(1)}, u32[]{:S(2)}, u32[]{:S(2)}) collective-permute-start(bf16[144,512]{1,0:T(8,128)(2,1)S(1)} %chain_other.1.refs_2_), channel_id=1, source_target_pairs={{0,8},{1,0},{2,10},{3,2},{4,12},{5,4},{6,14},{7,6},{8,9},{9,1},{10... | collective-permute-start | bytes 442376 | tf_op jit(solution)/shard_map/ppermute | solution.py:566
  46.1 5.2 %collective-permute-start.13 = (bf16[128,512]{1,0:T(8,128)(2,1)S(1)}, bf16[128,512]{1,0:T(8,128)(2,1)S(1)}, u32[]{:S(2)}, u32[]{:S(2)}) collective-permute-start(bf16[128,512]{1,0:T(8,128)(2,1)S(1)} %get-tuple-element.46), channel_id=1, source_target_pairs={{0,2},{2,0},{4,6},{6,4},{8,10},{10,8},{12,14},{14,12},{1,3},{3,1},... | collective-permute-start | bytes 393224 | tf_op jit(solution)/shard_map/ppermute | solution.py:640
  49.1 5.0 %collective-permute-start.11 = (bf16[128,512]{1,0:T(8,128)(2,1)S(1)}, bf16[128,512]{1,0:T(8,128)(2,1)S(1)}, u32[]{:S(2)}, u32[]{:S(2)}) collective-permute-start(bf16[128,512]{1,0:T(8,128)(2,1)S(1)} %get-tuple-element.45), channel_id=1, source_target_pairs={{0,2},{2,0},{4,6},{6,4},{8,10},{10,8},{12,14},{14,12},{1,3},{3,1},... | collective-permute-start | bytes 393224 | tf_op jit(solution)/shard_map/ppermute | solution.py:640
  56.6 2.0 %collective-permute-start.14 = (bf16[512,512]{1,0:T(8,128)(2,1)S(1)}, bf16[512,512]{1,0:T(8,128)(2,1)S(1)}, u32[]{:S(2)}, u32[]{:S(2)}) collective-permute-start(bf16[512,512]{1,0:T(8,128)(2,1)S(1)} %get-tuple-element.50), channel_id=1, source_target_pairs={{0,1},{1,0},{2,3},{3,2},{4,5},{5,4},{6,7},{7,6},{8,9},{9,8},{10,11... | collective-permute-start | bytes 1572872 | tf_op jit(solution)/shard_map/ppermute | solution.py:796

commit v5 on v4

--- a/solution.py
+++ b/solution.py
@@ -16,6 +16,8 @@
 TILE = 256
 BLOCK = 64
 MB = 1024 * 1024
+VMEM = pl.BlockSpec(memory_space=pltpu.VMEM)
+HBM = pl.BlockSpec(memory_space=pltpu.HBM)
 
 
 def call(
@@ -181,7 +183,6 @@
 def prepare_call(scalars, hidden, tokens, embedding, conv, gain, bias, rate):
     rows, width = hidden.shape
     inner = conv.shape[1]
-    vmem = pl.BlockSpec(memory_space=pltpu.VMEM)
     arrays = [hidden, tokens.reshape(1, -1), embedding, conv]
     arrays += [a.reshape(1, -1) for a in (gain, bias, rate)]
     return call(
@@ -190,8 +191,8 @@
         vmem=12,
         cost=micros(1.5),
         scalars=scalars,
-        in_specs=[pl.BlockSpec(memory_space=pltpu.HBM)] * len(arrays),
-        out_specs=[vmem] * 3,
+        in_specs=[HBM] * len(arrays),
+        out_specs=[VMEM] * 3,
         out_shape=[
             jax.ShapeDtypeStruct((rows, width), BF16),
             jax.ShapeDtypeStruct((HALO, width), BF16),
@@ -204,26 +205,25 @@
 
 
 def gate_kernel(rows_ref, wg_ref, out_ref, gate_ref):
-    gate_ref[...] = dot(rows_ref[...], wg_ref[...])
-    for r in range(0, gate_ref.shape[0], BLOCK):
-        gate = gate_ref[r : r + BLOCK, :].astype(BF16).astype(F32)
-        out_ref[r : r + BLOCK, :] = silu(gate).astype(BF16)
+    rows, inner = out_ref.shape
+    for low in range(0, inner, TILE):
+        columns = slice(low, low + TILE)
+        gate_ref[...] = dot(rows_ref[...], wg_ref[:, columns])
+        for r in range(0, rows, BLOCK):
+            gate = gate_ref[r : r + BLOCK, :].astype(BF16).astype(F32)
+            out_ref[r : r + BLOCK, columns] = silu(gate).astype(BF16)
 
 
 def gate_call(tag, normed, w_gate, after=()):
-    rows, width = normed.shape
+    rows = normed.shape[0]
     inner = w_gate.shape[1]
     return call(
         gate_kernel,
         "gate_" + tag,
         vmem=8,
         cost=micros(2.4),
-        grid=(inner // TILE,),
-        in_specs=[
-            pl.BlockSpec((rows, width), lambda g: (0, 0)),
-            pl.BlockSpec((width, TILE), lambda g: (0, g)),
-        ],
-        out_specs=pl.BlockSpec((rows, TILE), lambda g: (0, g)),
+        in_specs=[VMEM] * 2,
+        out_specs=VMEM,
         out_shape=jax.ShapeDtypeStruct((rows, inner), BF16),
         scratch=[pltpu.VMEM((rows, TILE), F32)],
         after=after,
@@ -255,15 +255,14 @@
 def maps_call(place, normed, halo, w_state, conv_state, after=()):
     rows = normed.shape[0]
     both = w_state.shape[1]
-    vmem = pl.BlockSpec(memory_space=pltpu.VMEM)
     return call(
         maps_kernel,
         "maps",
         vmem=8,
         cost=micros(1.5),
         scalars=(place,),
-        in_specs=[vmem] * 4,
-        out_specs=[vmem] * 2,
+        in_specs=[VMEM] * 4,
+        out_specs=[VMEM] * 2,
         out_shape=[
             jax.ShapeDtypeStruct((rows, both), BF16),
             jax.ShapeDtypeStruct((both // 2, rows), BF16),
@@ -299,64 +298,59 @@
     states = bt_ref.shape[0]
     heads = wt_ref.shape[0]
     taps = SMALL_TAPS
-    tiles = pl.num_programs(0)
-    g = pl.program_id(0)
-    tile = tile_at(g, tiles, parity_ref)
-
-    @pl.when(g == 0)
-    def _():
-        bias = small_ref[taps + 1 : taps + 2, :heads]
-        rate = small_ref[taps + 2 : taps + 3, :heads]
-        raw = dot_nt(normed_ref[...], wt_ref[...]) + bias
-        step = jnp.maximum(raw, 0.0) + jnp.log1p(jnp.exp(-jnp.abs(raw)))
-        step_ref[...] = two_parts(step)
-        logdecay = -step * rate
-        high = logdecay.astype(BF16)
-        rest = logdecay - high.astype(F32)
-        mid = rest.astype(BF16)
-        low = (rest - mid.astype(F32)).astype(BF16)
-        parts = jnp.concatenate([high, mid, low], axis=1)
-        to = lax.broadcasted_iota(jnp.int32, (CHUNK, CHUNK), 0)
-        frm = lax.broadcasted_iota(jnp.int32, (CHUNK, CHUNK), 1)
-        lower = jnp.where(to >= frm, 1.0, 0.0).astype(BF16)
-        run = jnp.zeros((1, heads), F32)
-        for r in range(0, rows, CHUNK):
-            sums = dot(lower, parts[r : r + CHUNK, :])
-            sums = sums[:, :heads] + sums[:, heads : 2 * heads] + sums[:, 2 * heads :] + run
-            cum_ref[r : r + CHUNK, :] = sums
-            run = sums[CHUNK - 1 :, :]
-        cum = cum_ref[...]
-        cumt_ref[...] = cum.T
-        left_ref[...] = two_parts(jnp.exp(run - cum))
-        whole_ref[...] = two_parts(jnp.exp(run))
-
-    weights = wi_ref[...]
-    before = dot(halo_ref[...], weights).astype(BF16).astype(F32)
-    rows_ref[:HALO, :] = jnp.where(place_ref[0] >= 1, before, 0.0)
-    rows_ref[HALO:, :] = dot(normed_ref[...], weights).astype(BF16).astype(F32)
-    onehot = head_matrix(heads, TILE, head_size, tile * (TILE // head_size))
-    spread_ref[0] = dot(step_ref[...], onehot)
-    spread_ref[1] = dot(left_ref[...], onehot)
-    columns = pl.ds(pl.multiple_of(tile * TILE, TILE), TILE)
-    taps_here = small_ref[:taps, columns]
-    for r in range(0, rows, BLOCK):
-        xs = conv_silu(rows_ref, taps_here, r).astype(F32) * spread_ref[0, r : r + BLOCK, :]
-        xs_ref[r : r + BLOCK, :] = xs.astype(BF16)
-        scaled_ref[r : r + BLOCK, :] = (xs * spread_ref[1, r : r + BLOCK, :]).astype(BF16)
-    state = dot(bt_ref[...], scaled_ref[...])
-    decay = dot(whole_ref[...], onehot)
-
-    @pl.when(g < tiles // 2)
-    def _():
-        write_payload(send_ref, state, decay)
-
-    @pl.when(g >= tiles // 2)
-    def _():
-        write_payload(mine_ref, state, decay)
-
-
-def tile_at(g, tiles, parity_ref):
-    return lax.rem(g + (1 - parity_ref[0]) * (tiles // 2), tiles)
+    bias = small_ref[taps + 1 : taps + 2, :heads]
+    rate = small_ref[taps + 2 : taps + 3, :heads]
+    raw = dot_nt(normed_ref[...], wt_ref[...]) + bias
+    step = jnp.maximum(raw, 0.0) + jnp.log1p(jnp.exp(-jnp.abs(raw)))
+    step_ref[...] = two_parts(step)
+    logdecay = -step * rate
+    high = logdecay.astype(BF16)
+    rest = logdecay - high.astype(F32)
+    mid = rest.astype(BF16)
+    low = (rest - mid.astype(F32)).astype(BF16)
+    parts = jnp.concatenate([high, mid, low], axis=1)
+    to = lax.broadcasted_iota(jnp.int32, (CHUNK, CHUNK), 0)
+    frm = lax.broadcasted_iota(jnp.int32, (CHUNK, CHUNK), 1)
+    lower = jnp.where(to >= frm, 1.0, 0.0).astype(BF16)
+    run = jnp.zeros((1, heads), F32)
+    for r in range(0, rows, CHUNK):
+        sums = dot(lower, parts[r : r + CHUNK, :])
+        sums = sums[:, :heads] + sums[:, heads : 2 * heads] + sums[:, 2 * heads :] + run
+        cum_ref[r : r + CHUNK, :] = sums
+        run = sums[CHUNK - 1 :, :]
+    cum = cum_ref[...]
+    cumt_ref[...] = cum.T
+    left_ref[...] = two_parts(jnp.exp(run - cum))
+    whole_ref[...] = two_parts(jnp.exp(run))
+
+    inner = xs_ref.shape[1]
+    half = inner // 2
+    for low in range(0, inner, TILE):
+        columns = slice(low, low + TILE)
+        weights = wi_ref[:, columns]
+        before = dot(halo_ref[...], weights).astype(BF16).astype(F32)
+        rows_ref[:HALO, :] = jnp.where(place_ref[0] >= 1, before, 0.0)
+        rows_ref[HALO:, :] = dot(normed_ref[...], weights).astype(BF16).astype(F32)
+        onehot = head_matrix(heads, TILE, head_size, low // head_size)
+        spread_ref[0] = dot(step_ref[...], onehot)
+        spread_ref[1] = dot(left_ref[...], onehot)
+        taps_here = small_ref[:taps, columns]
+        for r in range(0, rows, BLOCK):
+            xs = conv_silu(rows_ref, taps_here, r).astype(F32) * spread_ref[0, r : r + BLOCK, :]
+            xs_ref[r : r + BLOCK, columns] = xs.astype(BF16)
+            scaled_ref[r : r + BLOCK, :] = (xs * spread_ref[1, r : r + BLOCK, :]).astype(BF16)
+        state = dot(bt_ref[...], scaled_ref[...])
+        decay = dot(whole_ref[...], onehot)
+        here = slice(low % half, low % half + TILE)
+        is_mine = parity_ref[0] == low // half
+
+        @pl.when(is_mine)
+        def _():
+            write_payload(mine_ref, here, state, decay)
+
+        @pl.when(jnp.logical_not(is_mine))
+        def _():
+            write_payload(send_ref, here, state, decay)
 
 
 SMALL_TAPS = 4
@@ -364,35 +358,18 @@
 
 
 def local_call(tag, place, parity, normed, halo, bt, w_inner, w_step_t, small, after=()):
-    rows, width = normed.shape
+    rows = normed.shape[0]
     inner = w_inner.shape[1]
     heads = w_step_t.shape[0]
     states = bt.shape[0]
-    tiles = inner // TILE
-    half = tiles // 2
-
-    def whole(a):
-        return pl.BlockSpec(a.shape, lambda g, place, parity: (0, 0))
-
-    def tile(count):
-        return pl.BlockSpec((count, TILE), lambda g, place, parity: (0, tile_at(g, tiles, parity)))
-
-    payload = (states + EXTRA, TILE)
     return call(
         functools.partial(local_kernel, inner // heads),
         "local_" + tag,
         vmem=12,
         cost=micros(5.0),
         scalars=(place, parity),
-        grid=(tiles,),
-        in_specs=[whole(normed), whole(halo), whole(bt), tile(width), whole(w_step_t), whole(small)],
-        out_specs=[
-            tile(rows),
-            pl.BlockSpec((rows, heads), lambda g, place, parity: (0, 0)),
-            pl.BlockSpec((heads, rows), lambda g, place, parity: (0, 0)),
-            pl.BlockSpec(payload, lambda g, place, parity: (0, jnp.minimum(g, half - 1))),
-            pl.BlockSpec(payload, lambda g, place, parity: (0, jnp.maximum(g - half, 0))),
-        ],
+        in_specs=[VMEM] * 6,
+        out_specs=[VMEM] * 5,
         out_shape=[
             jax.ShapeDtypeStruct((rows, inner), BF16),
             jax.ShapeDtypeStruct((rows, heads), F32),
@@ -412,76 +389,67 @@
     )(place, parity, normed, halo, bt, w_inner, w_step_t, small)
 
 
-def inside_kernel(head_size, xs_ref, bc_ref, cum_ref, cumt_ref, y_ref, state_ref, prev_ref):
-    length, inner = xs_ref.shape
+def inside_kernel(head_size, xs_ref, bc_ref, cum_ref, cumt_ref, y_ref, state_ref):
+    rows, inner = xs_ref.shape
     states = bc_ref.shape[1] // 2
     heads = cum_ref.shape[1]
-
-    @pl.when(pl.program_id(0) == 0)
-    def _():
-        state_ref[...] = jnp.zeros_like(state_ref)
-        prev_ref[...] = jnp.zeros_like(prev_ref)
-
-    bmat = bc_ref[:, :states]
-    cmat = bc_ref[:, states:]
+    length = CHUNK
+    last = length - 1
+    pair = 2 * head_size
+    lane = lax.broadcasted_iota(jnp.int32, (length, pair), 1)
     to = lax.broadcasted_iota(jnp.int32, (length, length), 0)
     frm = lax.broadcasted_iota(jnp.int32, (length, length), 1)
-    scores = jnp.where(to >= frm, dot_nt(cmat, bmat), 0.0)
-    cum = cum_ref[...]
-    cumt = cumt_ref[...]
-    last = length - 1
-    end = cum[last:, :]
-    since = two_parts(jnp.exp(cum - prev_ref[...]))
-    left = two_parts(jnp.exp(end - cum))
-    prev_ref[...] = end
-    pair = 2 * head_size
-    lane = lax.broadcasted_iota(jnp.int32, (length, pair), 1)
-    for first in range(0, heads, TILE // head_size):
-        columns = slice(first * head_size, first * head_size + TILE)
-        onehot = head_matrix(heads, TILE, head_size, first)
-        since_here = dot(since, onehot)
-        state = state_ref[:, columns]
-        carried = dot(cmat, state.astype(BF16)) * since_here
-        scaled = (xs_ref[:, columns].astype(F32) * dot(left, onehot)).astype(BF16)
-        state_ref[:, columns] = state * since_here[last:, :] + dot_tn(bmat, scaled)
-        for start in range(0, TILE, pair):
-            low = first * head_size + start
-            weights = []
-            for h in (low // head_size, low // head_size + 1):
-                apart = jnp.minimum(cum[:, h : h + 1] - cumt[h : h + 1, :], 0.0)
-                weights.append((jnp.exp(apart) * scores).astype(BF16))
-            mine = xs_ref[:, low : low + pair]
-            none = jnp.zeros_like(mine)
-            stacked = jnp.concatenate(
-                [jnp.where(lane < head_size, mine, none), jnp.where(lane < head_size, none, mine)], axis=0
-            )
-            inside = dot(jnp.concatenate(weights, axis=1), stacked)
-            y_ref[:, low : low + pair] = (inside + carried[:, start : start + pair]).astype(BF16)
+    state_ref[...] = jnp.zeros_like(state_ref)
+
+    def chunk(c, before):
+        at = pl.ds(pl.multiple_of(c * length, length), length)
+        bmat = bc_ref[at, :states]
+        cmat = bc_ref[at, states:]
+        scores = jnp.where(to >= frm, dot_nt(cmat, bmat), 0.0)
+        cum = cum_ref[at, :]
+        cumt = cumt_ref[:, at]
+        end = cum[last:, :]
+        since = two_parts(jnp.exp(cum - before))
+        left = two_parts(jnp.exp(end - cum))
+        for first in range(0, heads, TILE // head_size):
+            columns = slice(first * head_size, first * head_size + TILE)
+            onehot = head_matrix(heads, TILE, head_size, first)
+            since_here = dot(since, onehot)
+            state = state_ref[:, columns]
+            carried = dot(cmat, state.astype(BF16)) * since_here
+            scaled = (xs_ref[at, columns].astype(F32) * dot(left, onehot)).astype(BF16)
+            state_ref[:, columns] = state * since_here[last:, :] + dot_tn(bmat, scaled)
+            for start in range(0, TILE, pair):
+                low = first * head_size + start
+                weights = []
+                for h in (low // head_size, low // head_size + 1):
+                    apart = jnp.minimum(cum[:, h : h + 1] - cumt[h : h + 1, :], 0.0)
+                    weights.append((jnp.exp(apart) * scores).astype(BF16))
+                mine = xs_ref[at, low : low + pair]
+                none = jnp.zeros_like(mine)
+                stacked = jnp.concatenate(
+                    [jnp.where(lane < head_size, mine, none), jnp.where(lane < head_size, none, mine)], axis=0
+                )
+                inside = dot(jnp.concatenate(weights, axis=1), stacked)
+                y_ref[at, low : low + pair] = (inside + carried[:, start : start + pair]).astype(BF16)
+        return end
+
+    lax.fori_loop(0, rows // length, chunk, jnp.zeros((1, heads), F32))
 
 
 def inside_call(tag, xs, bc, cum, cumt, after=()):
     rows, inner = xs.shape
     heads = cum.shape[1]
     both = bc.shape[1]
-
-    def block(width):
-        return pl.BlockSpec((CHUNK, width), lambda c: (c, 0))
-
     return call(
         functools.partial(inside_kernel, inner // heads),
         "inside_" + tag,
         vmem=8,
         cost=micros(3.2),
-        grid=(rows // CHUNK,),
-        in_specs=[
-            block(inner),
-            block(both),
-            block(heads),
-            pl.BlockSpec((heads, CHUNK), lambda c: (0, c)),
-        ],
-        out_specs=block(inner),
+        in_specs=[VMEM] * 4,
+        out_specs=VMEM,
         out_shape=jax.ShapeDtypeStruct((rows, inner), BF16),
-        scratch=[pltpu.VMEM((both // 2, inner), F32), pltpu.VMEM((1, heads), F32)],
+        scratch=[pltpu.VMEM((both // 2, inner), F32)],
         after=after,
     )(xs, bc, cum, cumt)
 
@@ -496,13 +464,16 @@
     return jnp.where(known, state, 0.0), jnp.where(known, decay, 0.0)
 
 
-def write_payload(out_ref, state, decay):
+def write_payload(out_ref, columns, state, decay):
     states = state.shape[0]
-    out_ref[:states, :] = state.astype(BF16)
+    out_ref[:states, columns] = state.astype(BF16)
     decay = jnp.broadcast_to(decay, (EXTRA, decay.shape[1]))
     high = decay.astype(BF16).astype(F32)
     place = lax.broadcasted_iota(jnp.int32, decay.shape, 0)
-    out_ref[states:, :] = jnp.where(place == 0, high, decay - high).astype(BF16)
+    out_ref[states:, columns] = jnp.where(place == 0, high, decay - high).astype(BF16)
+
+
+ALL = slice(None)
 
 
 def pair_kernel(place_ref, mine_ref, other_ref, out_ref):
@@ -512,19 +483,19 @@
     early = jnp.where(is_first, mine, other)
     late = jnp.where(is_first, other, mine)
     late_a = jnp.where(is_first, other_a, mine_a)
-    write_payload(out_ref, late_a * early + late, mine_a * other_a)
+    write_payload(out_ref, ALL, late_a * early + late, mine_a * other_a)
 
 
 def chain_kernel(reach, place_ref, pair_ref, before_ref, out_ref):
     pair, pair_a = parts_of(pair_ref)
     before, before_a = parts_of(before_ref, place_ref[0] >= reach)
-    write_payload(out_ref, pair_a * before + pair, pair_a * before_a)
+    write_payload(out_ref, ALL, pair_a * before + pair, pair_a * before_a)
 
 
 def longer_kernel(reach, farther_reach, place_ref, before_ref, farther_ref, out_ref):
     before, before_a = parts_of(before_ref, place_ref[0] >= reach)
     farther, farther_a = parts_of(farther_ref, place_ref[0] >= farther_reach)
-    write_payload(out_ref, before + before_a * farther, before_a * farther_a)
+    write_payload(out_ref, ALL, before + before_a * farther, before_a * farther_a)
 
 
 def entry_kernel(reach, farther_reach, place_ref, mine_ref, other_ref, before_ref, farther_ref, keep_ref, send_ref):
@@ -542,15 +513,14 @@
 
 
 def small_call(kernel, name, place, arrays, shapes, after=()):
-    vmem = pl.BlockSpec(memory_space=pltpu.VMEM)
     return call(
         kernel,
         name,
         vmem=4,
         cost=micros(0.5),
         scalars=(place,),
-        in_specs=[vmem] * len(arrays),
-        out_specs=[vmem] * len(shapes),
+        in_specs=[VMEM] * len(arrays),
+        out_specs=[VMEM] * len(shapes),
         out_shape=[jax.ShapeDtypeStruct(s, BF16) for s in shapes],
         after=after,
     )(place, *arrays)
@@ -641,13 +611,12 @@
 
 
 def gated_part(
-    head_size, swap, y_ref, bc_ref, cum_ref, keep_ref, other_ref, gate_ref, small_ref, wo_ref, scaled_ref
+    head_size, swap, y_ref, bc_ref, cum_ref, keep_ref, other_ref, gate_ref, small_ref, wo_ref, scaled_ref, tile_ref
 ):
     rows, inner = y_ref.shape
     states = bc_ref.shape[1] // 2
     heads = cum_ref.shape[1]
     half = inner // 2
-    cmat = bc_ref[:, states:]
     since = two_parts(jnp.exp(cum_ref[...]))
     squares = [0.0] * (rows // BLOCK)
     for low in range(0, inner, TILE):
@@ -655,40 +624,53 @@
         here = slice(low % half, low % half + TILE)
         use_other = swap if low < half else jnp.logical_not(swap)
         entry = jnp.where(use_other, other_ref[:, here], keep_ref[:, here])
-        onehot = head_matrix(heads, TILE, head_size, low // head_size)
+        tile_ref[0] = dot(bc_ref[:, states:], entry)
+        tile_ref[1] = dot(since, head_matrix(heads, TILE, head_size, low // head_size))
         gain = small_ref[SMALL_TAPS : SMALL_TAPS + 1, columns]
         for i, r in enumerate(range(0, rows, BLOCK)):
             block = slice(r, r + BLOCK)
-            carried = dot(cmat[block, :], entry) * dot(since[block, :], onehot)
-            gated = (y_ref[block, columns].astype(F32) + carried) * gate_ref[block, columns].astype(F32)
+            gated = y_ref[block, columns].astype(F32) + tile_ref[0, block, :] * tile_ref[1, block, :]
+            gated = gated * gate_ref[block, columns].astype(F32)
             squares[i] += jnp.sum(gated * gated, axis=-1, keepdims=True)
             scaled_ref[block, columns] = (gated * gain).astype(BF16)
     return squares
 
 
-def part_kernel(head_size, back_ref, parity_ref, *refs):
-    *ins, out_ref, sq_ref, scaled_ref = refs
-    squares = gated_part(head_size, parity_ref[0] == 1, *ins, scaled_ref)
+def part_kernel(head_size, parity_ref, *refs):
+    *ins, out_ref, sq_ref, scaled_ref, tile_ref = refs
+    squares = gated_part(head_size, parity_ref[0] == 1, *ins, scaled_ref, tile_ref)
     for i, square in enumerate(squares):
         sq_ref[i * BLOCK : (i + 1) * BLOCK, :] = jnp.broadcast_to(square, (BLOCK, sq_ref.shape[1]))
-    out_ref[...] = dot(scaled_ref[...], ins[-1][...])
+    for low in range(0, out_ref.shape[1], TILE):
+        out_ref[:, low : low + TILE] = dot(scaled_ref[...], ins[-1][:, low : low + TILE])
 
 
 def finish_kernel(head_size, full_width, back_ref, parity_ref, *refs):
-    *ins, part_ref, psq_ref, own_ref, send_ref, scaled_ref, sum_ref, out_ref = refs
-    squares = gated_part(head_size, parity_ref[0] == 1, *ins, scaled_ref)
-    sum_ref[...] = dot(scaled_ref[...], ins[-1][...])
-    half = own_ref.shape[1]
+    *ins, part_ref, psq_ref, own_ref, send_ref, scaled_ref, tile_ref, out_ref = refs
+    squares = gated_part(head_size, parity_ref[0] == 1, *ins, scaled_ref, tile_ref)
+    rows, half = own_ref.shape
+    width = 2 * half
+    scales = []
     for i, square in enumerate(squares):
         block = slice(i * BLOCK, (i + 1) * BLOCK)
-        scale = lax.rsqrt((square + psq_ref[block, :1]) / full_width + EPS)
-        out_ref[block, :] = ((sum_ref[block, :] + part_ref[block, :]) * scale).astype(BF16)
+        scales.append(lax.rsqrt((square + psq_ref[block, :1]) / full_width + EPS))
+    for low in range(0, width, TILE):
+        columns = slice(low, low + TILE)
+        tile_ref[0] = dot(scaled_ref[...], ins[-1][:, columns])
+        for i, scale in enumerate(scales):
+            block = slice(i * BLOCK, (i + 1) * BLOCK)
+            out_ref[block, columns] = ((tile_ref[0, block, :] + part_ref[block, columns]) * scale).astype(BF16)
 
     @pl.when(back_ref[0] == 1)
     def _():
-        turned = flip_both(out_ref[...])
-        own_ref[...] = turned[:, half:]
-        send_ref[...] = turned[:, :half]
+        turn = flip_matrix(TILE)
+        for r in range(0, rows, TILE):
+            for low in range(0, width, TILE):
+                tile = dot(turn, out_ref[r : r + TILE, low : low + TILE]).astype(BF16)
+                tile = dot(tile, turn).astype(BF16)
+                to_row, to = rows - TILE - r, width - TILE - low
+                target, to = (own_ref, to - half) if to >= half else (send_ref, to)
+                target[to_row : to_row + TILE, to : to + TILE] = tile
 
     @pl.when(back_ref[0] != 1)
     def _():
@@ -701,77 +683,56 @@
     width = w_output.shape[1]
     half = width // 2
     heads = cum.shape[1]
-    count = rows // TILE
-
-    def block(columns):
-        return pl.BlockSpec((TILE, columns), lambda r, back, parity: (r, 0))
-
-    def whole(a):
-        return pl.BlockSpec(a.shape, lambda r, back, parity: (0, 0))
-
-    def turned(r, back, parity):
-        return (jnp.where(back[0] == 1, count - 1 - r, r), 0)
-
-    in_specs = [
-        block(inner),
-        block(bc.shape[1]),
-        block(heads),
-        whole(keep),
-        whole(other),
-        block(inner),
-        whole(small),
-        whole(w_output),
-    ]
     arrays = [y, bc, cum, keep, other, gate, small, w_output]
+    scratch = [pltpu.VMEM((rows, inner), BF16), pltpu.VMEM((2, rows, TILE), F32)]
     if partial is None:
-        scratch = [pltpu.VMEM((TILE, inner), BF16)]
+        scalars = (parity,)
         kernel = functools.partial(part_kernel, inner // heads)
-        out_specs = [block(width), block(128)]
         out_shape = [jax.ShapeDtypeStruct((rows, width), F32), jax.ShapeDtypeStruct((rows, 128), F32)]
     else:
-        scratch = [
-            pltpu.VMEM((TILE, inner), BF16),
-            pltpu.VMEM((TILE, width), F32),
-            pltpu.VMEM((TILE, width), BF16),
-        ]
+        scalars = (back, parity)
+        scratch.append(pltpu.VMEM((rows, width), BF16))
         kernel = functools.partial(finish_kernel, inner // heads, full_width)
-        in_specs += [block(width), block(128)]
         arrays += list(partial)
-        out_specs = [pl.BlockSpec((TILE, half), turned)] * 2
         out_shape = [jax.ShapeDtypeStruct((rows, half), BF16)] * 2
     return call(
         kernel,
         "part" if partial is None else "finish",
         vmem=16,
         cost=micros(3.5),
-        scalars=(back, parity),
-        grid=(count,),
-        in_specs=in_specs,
-        out_specs=out_specs,
+        scalars=scalars,
+        in_specs=[VMEM] * len(arrays),
+        out_specs=[VMEM] * 2,
         out_shape=out_shape,
         scratch=scratch,
         after=after,
-    )(back, parity, *arrays)
-
-
-def total_kernel(mine_ref, theirs_ref, out_ref):
-    for r in range(0, mine_ref.shape[0], BLOCK):
-        block = slice(r, r + BLOCK)
-        out_ref[block, :] = (mine_ref[block, :].astype(F32) + theirs_ref[block, :].astype(F32)).astype(BF16)
+    )(*scalars, *arrays)
+
+
+def total_kernel(mine_ref, theirs_ref, out_hbm, out_ref, sems):
+    copies = []
+    for i, r in enumerate(range(0, mine_ref.shape[0], CHUNK)):
+        for q in range(r, r + CHUNK, BLOCK):
+            block = slice(q, q + BLOCK)
+            out_ref[block, :] = (mine_ref[block, :].astype(F32) + theirs_ref[block, :].astype(F32)).astype(BF16)
+        part = pl.ds(r, CHUNK)
+        copies.append(pltpu.make_async_copy(out_ref.at[part, :], out_hbm.at[part, :], sems.at[i]))
+        copies[-1].start()
+    for copy in copies:
+        copy.wait()
 
 
 def total_call(mine, theirs):
     rows, half = mine.shape
-    block = pl.BlockSpec((CHUNK, half), lambda r: (r, 0))
     return call(
         total_kernel,
         "total",
         vmem=4,
         cost=micros(0.8),
-        grid=(rows // CHUNK,),
-        in_specs=[block, block],
-        out_specs=block,
+        in_specs=[VMEM] * 2,
+        out_specs=HBM,
         out_shape=jax.ShapeDtypeStruct((rows, half), BF16),
+        scratch=[pltpu.VMEM((rows, half), BF16), pltpu.SemaphoreType.DMA((rows // CHUNK,))],
     )(mine, theirs)
 
 

time: 61.1 us -> 58.1 us (0.951)
  Pallas kernels: 36.4 us -> 32.1 us
  waiting for transfers between devices: 5.34 us -> 6.99 us
    pallas_call x17, Pallas kernels: 36.4 us -> 32.1 us  [call(): return lambda *arrays: run(*arrays, *after)]
    ppermute x2, waiting for transfers between devices: 1.12 us -> 2.27 us  [entry(): return (keep, lax.ppermute(out, 'seq', self.swap))]
  transfers between devices with their start and end apart: 15 -> 15, of which waited for: 4 -> 5; matrix products, arithmetic and copies ran while one was open for 0% -> 0% of each run, Pallas kernels for 54% -> 51%
where the time goes in v5:
time: 58.1 us; the launch traced here: 57 us
  Pallas kernels  32.1 us (55%)
  starting transfers between devices  17.4 us (30%)
  waiting for transfers between devices  6.99 us (12%)
    pallas_call x17, Pallas kernels, call(): return lambda *arrays: run(*arrays, *after)  32.1 us
    ppermute x5, starting transfers between devices, onward(): return lax.ppermute(value, ('seq', 'ch'), pairs)  10.8 us
    ppermute x2, starting transfers between devices, __init__(): self.other = lax.ppermute(send, 'seq', self.swap)  3.21 us
    ppermute x5, waiting for transfers between devices, onward(): return lax.ppermute(value, ('seq', 'ch'), pairs)  2.81 us
    ppermute x2, waiting for transfers between devices, entry(): return (keep, lax.ppermute(out, 'seq', self.swap))  2.27 us
    ppermute x6, waiting for transfers between devices, theirs(): return lax.ppermute(a, 'ch', swap)  1.91 us
    ppermute x6, starting transfers between devices, theirs(): return lax.ppermute(a, 'ch', swap)  1.91 us
    ppermute x2, starting transfers between devices, entry(): return (keep, lax.ppermute(out, 'seq', self.swap))  1.5 us
  transfers between devices with their start and end apart: 15, of which 5 were waited for; matrix products, arithmetic and copies ran while one was open for 0% of the time, Pallas kernels for 51%

profile of v5, /device:TPU:0, one launch (start us, length us, event | category | flops | bytes accessed | tf_op | source)
XLA Modules:
  0.0 57.0 jit_solution(8133756543144240572)
XLA Ops:
  0.5 2.7 %prepare.1 = (bf16[512,1024]{1,0:T(8,128)(2,1)S(1)}, bf16[16,1024]{1,0:T(8,128)(2,1)S(1)}, f32[8,1024]{1,0:T(8,128)S(1)}) custom-call(s32[1]{0:T(128)} %bitcast.refs_0_, s32[1]{0:T(128)} %bitcast.1.refs_1_.refs_0_, s32[1]{0:T(128)} %bitcast.2.refs_2_.refs_0_, bf16[512,1024]{1,0:T(8,128)(2,1)} %refs_3_.2, s32[1,512]{1,0:T(1,128)} %bitcast.11, ...), custom_call_target="tpu_custom_call" | custom-call | flops 1650000000 | bytes 1500000 | tf_op jit(solution)/shard_map/prepare/pallas_call | solution.py:48
  3.2 2.6 %collective-permute-start = (bf16[16,1024]{1,0:T(8,128)(2,1)S(1)}, bf16[16,1024]{1,0:T(8,128)(2,1)S(1)}, u32[]{:S(2)}, u32[]{:S(2)}) collective-permute-start(bf16[16,1024]{1,0:T(8,128)(2,1)S(1)} %get-tuple-element.29), channel_id=1, source_target_pairs={{0,2},{1,0},{2,4},{3,1},{4,6},{5,3},{6,8},{7,5},{8,10},{9,7},{10,1... | collective-permute-start | bytes 98312 | tf_op jit(solution)/shard_map/ppermute | solution.py:536
  6.3 1.4 %gate_own.1.refs_5_.refs_6_ = bf16[512,1024]{1,0:T(8,128)(2,1)S(1)} custom-call(bf16[512,1024]{1,0:T(8,128)(2,1)S(1)} %get-tuple-element.28.refs_0_.refs_1_.refs_2_, bf16[1024,1024]{1,0:T(8,128)(2,1)S(1)} %copy-done.1), custom_call_target="tpu_custom_call" | custom-call | flops 2640000000 | bytes 2400000 | tf_op jit(solution)/shard_map/gate_own/pallas_call | solution.py:48
  7.9 0.8 %collective-permute-start.12 = (bf16[1024,1024]{1,0:T(8,128)(2,1)S(1)}, bf16[1024,1024]{1,0:T(8,128)(2,1)S(1)}, u32[]{:S(2)}, u32[]{:S(2)}) collective-permute-start(bf16[1024,1024]{1,0:T(8,128)(2,1)S(1)} %copy-done.2), channel_id=1, source_target_pairs={{0,1},{1,0},{2,3},{3,2},{4,5},{5,4},{6,7},{7,6},{8,9},{9,8},{10,11... | collective-permute-start | bytes 6291464 | tf_op jit(solution)/shard_map/ppermute | solution.py:757
  8.7 1.1 %maps.1 = (bf16[512,256]{1,0:T(8,128)(2,1)S(1)}, bf16[128,512]{1,0:T(8,128)(2,1)S(1)}) custom-call(s32[1]{0:T(128)} %bitcast.2.refs_2_.refs_0_, bf16[512,1024]{1,0:T(8,128)(2,1)S(1)} %get-tuple-element.28.refs_0_.refs_1_.refs_2_, bf16[16,1024]{1,0:T(8,128)(2,1)S(1)} %collective-permute-done.refs_2_.refs_3_, bf16[1024,256]{1,0:T(8,128)(2,1)S(1)} %copy-done.3, ...), custom_call_target="tpu_custom_call" | custom-call | flops 1650000000 | bytes 1500000 | tf_op jit(solution)/shard_map/maps/pallas_call | solution.py:48
  9.8 6.6 %local_own.1 = (bf16[512,1024]{1,0:T(8,128)(2,1)S(1)}, f32[512,16]{1,0:T(8,128)S(1)}, f32[16,512]{1,0:T(8,128)S(1)}, bf16[144,512]{1,0:T(8,128)(2,1)S(1)}, bf16[144,512]{1,0:T(8,128)(2,1)S(1)}) custom-call(s32[1]{0:T(128)} %bitcast.2.refs_2_.refs_0_, s32[1]{0:T(128)} %bitcast.1.refs_1_.refs_0_, ...), custom_call_target="tpu_custom_call" | custom-call | flops 5500000256 | bytes 5000000 | tf_op jit(solution)/shard_map/local_own/pallas_call | solution.py:48
  16.5 2.7 %collective-permute-start.4 = (bf16[144,512]{1,0:T(8,128)(2,1)S(1)}, bf16[144,512]{1,0:T(8,128)(2,1)S(1)}, u32[]{:S(2)}, u32[]{:S(2)}) collective-permute-start(bf16[144,512]{1,0:T(8,128)(2,1)S(1)} %get-tuple-element.37), channel_id=1, source_target_pairs={{0,2},{2,0},{4,6},{6,4},{8,10},{10,8},{12,14},{14,12},{1,3},{3,1},... | collective-permute-start | bytes 442376 | tf_op jit(solution)/shard_map/ppermute | solution.py:544
  19.2 6.8 %local_other.1 = (bf16[512,1024]{1,0:T(8,128)(2,1)S(1)}, f32[512,16]{1,0:T(8,128)S(1)}, f32[16,512]{1,0:T(8,128)S(1)}, bf16[144,512]{1,0:T(8,128)(2,1)S(1)}, bf16[144,512]{1,0:T(8,128)(2,1)S(1)}) custom-call(s32[1]{0:T(128)} %bitcast.2.refs_2_.refs_0_, s32[1]{0:T(128)} %bitcast.1.refs_1_.refs_0_, ...), custom_call_target="tpu_custom_call" | custom-call | flops 5500000256 | bytes 5000000 | tf_op jit(solution)/shard_map/local_other/pallas_call | solution.py:48
  26.1 1.6 %collective-permute-start.5 = (bf16[144,512]{1,0:T(8,128)(2,1)S(1)}, bf16[144,512]{1,0:T(8,128)(2,1)S(1)}, u32[]{:S(2)}, u32[]{:S(2)}) collective-permute-start(bf16[144,512]{1,0:T(8,128)(2,1)S(1)} %pair_own.1.refs_4_.refs_1_), channel_id=1, source_target_pairs={{0,4},{1,0},{2,6},{3,2},{4,8},{5,1},{6,10},{7,3},{8,12},{9,5},{10,... | collective-permute-start | bytes 442376 | tf_op jit(solution)/shard_map/ppermute | solution.py:536
  28.2 3.3 %inside_own.1.refs_3_.refs_1_ = bf16[512,1024]{1,0:T(8,128)(2,1)S(1)} custom-call(bf16[512,1024]{1,0:T(8,128)(2,1)S(1)} %get-tuple-element.38.refs_0_, bf16[512,256]{1,0:T(8,128)(2,1)S(1)} %get-tuple-element.34.refs_1_.refs_2_.refs_3_, f32[512,16]{1,0:T(8,128)S(1)} %get-tuple-element.39.refs_2_.refs_3_, f32[16,512]{1,0:T(8,128)S(1)} %get-tuple-element.40.refs_3_, ...), custom_call_target="tpu_custom_call" | custom-call | flops 3520000000 | bytes 3200000 | tf_op jit(solution)/shard_map/inside_own/pallas_call | solution.py:48
  31.6 2.6 %collective-permute-start.6 = (bf16[144,512]{1,0:T(8,128)(2,1)S(1)}, bf16[144,512]{1,0:T(8,128)(2,1)S(1)}, u32[]{:S(2)}, u32[]{:S(2)}) collective-permute-start(bf16[144,512]{1,0:T(8,128)(2,1)S(1)} %chain_own.1.refs_3_), channel_id=1, source_target_pairs={{0,8},{1,0},{2,10},{3,2},{4,12},{5,4},{6,14},{7,6},{8,9},{9,1},{10... | collective-permute-start | bytes 442376 | tf_op jit(solution)/shard_map/ppermute | solution.py:536
  34.7 2.2 %collective-permute-done.6.refs_4_ = bf16[144,512]{1,0:T(8,128)(2,1)S(1)} collective-permute-done((bf16[144,512]{1,0:T(8,128)(2,1)S(1)}, bf16[144,512]{1,0:T(8,128)(2,1)S(1)}, u32[]{:S(2)}, u32[]{:S(2)}) %collective-permute-start.6) | collective-permute-done | bytes 147488 | tf_op jit(solution)/shard_map/ppermute | solution.py:536
  37.1 3.3 %inside_other.1.refs_3_.refs_2_ = bf16[512,1024]{1,0:T(8,128)(2,1)S(1)} custom-call(bf16[512,1024]{1,0:T(8,128)(2,1)S(1)} %get-tuple-element.33.refs_3_.refs_0_, bf16[512,256]{1,0:T(8,128)(2,1)S(1)} %get-tuple-element.34.refs_1_.refs_2_.refs_3_, f32[512,16]{1,0:T(8,128)S(1)} %get-tuple-element.35.refs_2_.refs_4_, f32[16,512]{1,0:T(8,128)S(1)} %get-tuple-element.36.refs_3_, ...), custom_call_target="tpu_custom_call" | custom-call | flops 3520000000 | bytes 3200000 | tf_op jit(solution)/shard_map/inside_other/pallas_call | solution.py:48
  40.4 3.5 %collective-permute-start.9 = (bf16[144,512]{1,0:T(8,128)(2,1)S(1)}, bf16[144,512]{1,0:T(8,128)(2,1)S(1)}, u32[]{:S(2)}, u32[]{:S(2)}) collective-permute-start(bf16[144,512]{1,0:T(8,128)(2,1)S(1)} %chain_other.1.refs_2_), channel_id=1, source_target_pairs={{0,8},{1,0},{2,10},{3,2},{4,12},{5,4},{6,14},{7,6},{8,9},{9,1},{10... | collective-permute-start | bytes 442376 | tf_op jit(solution)/shard_map/ppermute | solution.py:536
  43.9 0.6 %collective-permute-start.13 = (bf16[128,512]{1,0:T(8,128)(2,1)S(1)}, bf16[128,512]{1,0:T(8,128)(2,1)S(1)}, u32[]{:S(2)}, u32[]{:S(2)}) collective-permute-start(bf16[128,512]{1,0:T(8,128)(2,1)S(1)} %get-tuple-element.46), channel_id=1, source_target_pairs={{0,2},{2,0},{4,6},{6,4},{8,10},{10,8},{12,14},{14,12},{1,3},{3,1},... | collective-permute-start | bytes 393224 | tf_op jit(solution)/shard_map/ppermute | solution.py:610
  44.6 1.4 %gate_other.1.refs_5_.refs_7_ = bf16[512,1024]{1,0:T(8,128)(2,1)S(1)} custom-call(bf16[512,1024]{1,0:T(8,128)(2,1)S(1)} %get-tuple-element.28.refs_0_.refs_1_.refs_2_, bf16[1024,1024]{1,0:T(8,128)(2,1)S(1)} %collective-permute-done.10.refs_1_, bf16[144,512]{1,0:T(8,128)(2,1)S(1)} %chain_other.1.refs_2_), custom_call_target="tpu_custom_call" | custom-call | flops 2640000000 | bytes 2400000 | tf_op jit(solution)/shard_map/gate_other/pallas_call | solution.py:48
  46.0 0.6 %collective-permute-done.9.refs_4_ = bf16[144,512]{1,0:T(8,128)(2,1)S(1)} collective-permute-done((bf16[144,512]{1,0:T(8,128)(2,1)S(1)}, bf16[144,512]{1,0:T(8,128)(2,1)S(1)}, u32[]{:S(2)}, u32[]{:S(2)}) %collective-permute-start.9) | collective-permute-done | bytes 147488 | tf_op jit(solution)/shard_map/ppermute | solution.py:536
  46.8 0.9 %collective-permute-start.11 = (bf16[128,512]{1,0:T(8,128)(2,1)S(1)}, bf16[128,512]{1,0:T(8,128)(2,1)S(1)}, u32[]{:S(2)}, u32[]{:S(2)}) collective-permute-start(bf16[128,512]{1,0:T(8,128)(2,1)S(1)} %get-tuple-element.45), channel_id=1, source_target_pairs={{0,2},{2,0},{4,6},{6,4},{8,10},{10,8},{12,14},{14,12},{1,3},{3,1},... | collective-permute-start | bytes 393224 | tf_op jit(solution)/shard_map/ppermute | solution.py:610
  47.6 1.3 %collective-permute-done.13.refs_5_ = bf16[128,512]{1,0:T(8,128)(2,1)S(1)} collective-permute-done((bf16[128,512]{1,0:T(8,128)(2,1)S(1)}, bf16[128,512]{1,0:T(8,128)(2,1)S(1)}, u32[]{:S(2)}, u32[]{:S(2)}) %collective-permute-start.13) | collective-permute-done | bytes 131104 | tf_op jit(solution)/shard_map/ppermute | solution.py:610
  48.9 2.0 %part.1 = (f32[512,1024]{1,0:T(8,128)S(1)}, f32[512,128]{1,0:T(8,128)S(1)}) custom-call(s32[1]{0:T(128)} %bitcast.1.refs_1_.refs_0_, bf16[512,1024]{1,0:T(8,128)(2,1)S(1)} %inside_own.1.refs_3_.refs_1_, bf16[512,256]{1,0:T(8,128)(2,1)S(1)} %get-tuple-element.34.refs_1_.refs_2_.refs_3_, f32[512,16]{1,0:T(8,128)S(1)} %get-tuple-element.39.refs_2_.refs_3_, ...), custom_call_target="tpu_custom_call" | custom-call | flops 3849999872 | bytes 3500000 | tf_op jit(solution)/shard_map/part/pallas_call | solution.py:48
  50.9 1.0 %collective-permute-done.11.refs_6_ = bf16[128,512]{1,0:T(8,128)(2,1)S(1)} collective-permute-done((bf16[128,512]{1,0:T(8,128)(2,1)S(1)}, bf16[128,512]{1,0:T(8,128)(2,1)S(1)}, u32[]{:S(2)}, u32[]{:S(2)}) %collective-permute-start.11) | collective-permute-done | bytes 131104 | tf_op jit(solution)/shard_map/ppermute | solution.py:610
  51.9 2.1 %finish.1 = (bf16[512,512]{1,0:T(8,128)(2,1)S(1)}, bf16[512,512]{1,0:T(8,128)(2,1)S(1)}) custom-call(s32[1]{0:T(128)} %bitcast.refs_0_, s32[1]{0:T(128)} %bitcast.1.refs_1_.refs_0_, bf16[512,1024]{1,0:T(8,128)(2,1)S(1)} %inside_other.1.refs_3_.refs_2_, bf16[512,256]{1,0:T(8,128)(2,1)S(1)} %get-tuple-element.34.refs_1_.refs_2_.refs_3_, ...), custom_call_target="tpu_custom_call" | custom-call | flops 3849999872 | bytes 3500000 | tf_op jit(solution)/shard_map/finish/pallas_call | solution.py:48
  54.1 1.9 %collective-permute-done.14.refs_1_ = bf16[512,512]{1,0:T(8,128)(2,1)S(1)} collective-permute-done((bf16[512,512]{1,0:T(8,128)(2,1)S(1)}, bf16[512,512]{1,0:T(8,128)(2,1)S(1)}, u32[]{:S(2)}, u32[]{:S(2)}) %collective-permute-start.14) | collective-permute-done | bytes 524320 | tf_op jit(solution)/shard_map/ppermute | solution.py:757
  56.0 0.8 %total.1 = bf16[512,512]{1,0:T(8,128)(2,1)} custom-call(bf16[512,512]{1,0:T(8,128)(2,1)S(1)} %get-tuple-element.49.refs_0_, bf16[512,512]{1,0:T(8,128)(2,1)S(1)} %collective-permute-done.14.refs_1_), custom_call_target="tpu_custom_call" | custom-call | flops 880000000 | bytes 800000 | tf_op jit(solution)/shard_map/total/pallas_call | solution.py:48
  (35 shorter events, 2.7 us)
Async XLA Ops:
  0.0 19.2 %collective-permute-start.1 = (bf16[1024,1024]{1,0:T(8,128)(2,1)}, bf16[1024,1024]{1,0:T(8,128)(2,1)S(1)}, u32[]{:S(2)}, u32[]{:S(2)}) collective-permute-start(bf16[1024,1024]{1,0:T(8,128)(2,1)} %refs_5_.3), channel_id=1, source_target_pairs={{0,1},{1,0},{2,3},{3,2},{4,5},{5,4},{6,7},{7,6},{8,9},{9,8},{10,11... | collective-permute-start | bytes 6291464 | tf_op jit(solution)/shard_map/ppermute | solution.py:757
  0.5 5.3 %copy-start.4 = (bf16[1024,16]{0,1:T(8,128)(2,1)S(1)}, bf16[1024,16]{0,1:T(8,128)(2,1)}, u32[]{:S(2)}) copy-start(bf16[1024,16]{0,1:T(8,128)(2,1)} %param.19) | copy-start | bytes 98308
  0.5 5.8 %copy-start.1 = (bf16[1024,1024]{1,0:T(8,128)(2,1)S(1)}, bf16[1024,1024]{1,0:T(8,128)(2,1)}, u32[]{:S(2)}) copy-start(bf16[1024,1024]{1,0:T(8,128)(2,1)} %refs_1_.1) | copy-start | bytes 6291460
  3.2 4.6 %collective-permute-start = (bf16[16,1024]{1,0:T(8,128)(2,1)S(1)}, bf16[16,1024]{1,0:T(8,128)(2,1)S(1)}, u32[]{:S(2)}, u32[]{:S(2)}) collective-permute-start(bf16[16,1024]{1,0:T(8,128)(2,1)S(1)} %get-tuple-element.29), channel_id=1, source_target_pairs={{0,2},{1,0},{2,4},{3,1},{4,6},{5,3},{6,8},{7,5},{8,10},{9,7},{10,1... | collective-permute-start | bytes 98312 | tf_op jit(solution)/shard_map/ppermute | solution.py:536
  5.7 10.7 %collective-permute-start.3 = (f32[8,1024]{1,0:T(8,128)S(1)}, f32[8,1024]{1,0:T(8,128)S(1)}, u32[]{:S(2)}, u32[]{:S(2)}) collective-permute-start(f32[8,1024]{1,0:T(8,128)S(1)} %get-tuple-element.31.refs_7_), channel_id=1, source_target_pairs={{0,1},{1,0},{2,3},{3,2},{4,5},{5,4},{6,7},{7,6},{8,9},{9,8},{10,11... | collective-permute-start | bytes 98312 | tf_op jit(solution)/shard_map/ppermute | solution.py:757
  5.8 13.4 %collective-permute-start.2 = (bf16[16,1024]{1,0:T(8,128)(2,1)S(1)}, bf16[16,1024]{1,0:T(8,128)(2,1)S(1)}, u32[]{:S(2)}, u32[]{:S(2)}) collective-permute-start(bf16[16,1024]{1,0:T(8,128)(2,1)S(1)} %bitcast.8), channel_id=1, source_target_pairs={{0,1},{1,0},{2,3},{3,2},{4,5},{5,4},{6,7},{7,6},{8,9},{9,8},{10,11... | collective-permute-start | bytes 98312 | tf_op jit(solution)/shard_map/ppermute | solution.py:757
  6.3 38.3 %collective-permute-start.10 = (bf16[1024,1024]{1,0:T(8,128)(2,1)S(1)}, bf16[1024,1024]{1,0:T(8,128)(2,1)S(1)}, u32[]{:S(2)}, u32[]{:S(2)}) collective-permute-start(bf16[1024,1024]{1,0:T(8,128)(2,1)S(1)} %copy-done.1), channel_id=1, source_target_pairs={{0,1},{1,0},{2,3},{3,2},{4,5},{5,4},{6,7},{7,6},{8,9},{9,8},{10,11... | collective-permute-start | bytes 6291464 | tf_op jit(solution)/shard_map/ppermute | solution.py:757
  6.3 1.6 %copy-start.2 = (bf16[1024,1024]{1,0:T(8,128)(2,1)S(1)}, bf16[1024,1024]{1,0:T(8,128)(2,1)}, u32[]{:S(2)}) copy-start(bf16[1024,1024]{1,0:T(8,128)(2,1)} %refs_8_.1) | copy-start | bytes 6291460
  6.3 2.4 %copy-start.3 = (bf16[1024,256]{1,0:T(8,128)(2,1)S(1)}, bf16[1024,256]{1,0:T(8,128)(2,1)}, u32[]{:S(2)}) copy-start(bf16[1024,256]{1,0:T(8,128)(2,1)} %refs_3_.3) | copy-start | bytes 1572868
  6.3 2.4 %copy-start.5 = (f32[4,256]{1,0:T(4,128)S(1)}, f32[4,256]{1,0:T(4,128)}, u32[]{:S(2)}) copy-start(f32[4,256]{1,0:T(4,128)} %refs_4_.1) | copy-start | bytes 12292
  7.8 2.0 %copy-start = (bf16[1024,1024]{1,0:T(8,128)(2,1)S(1)}, bf16[1024,1024]{1,0:T(8,128)(2,1)}, u32[]{:S(2)}) copy-start(bf16[1024,1024]{1,0:T(8,128)(2,1)} %refs_5_.3) | copy-start | bytes 6291460
  7.9 43.0 %collective-permute-start.12 = (bf16[1024,1024]{1,0:T(8,128)(2,1)S(1)}, bf16[1024,1024]{1,0:T(8,128)(2,1)S(1)}, u32[]{:S(2)}, u32[]{:S(2)}) collective-permute-start(bf16[1024,1024]{1,0:T(8,128)(2,1)S(1)} %copy-done.2), channel_id=1, source_target_pairs={{0,1},{1,0},{2,3},{3,2},{4,5},{5,4},{6,7},{7,6},{8,9},{9,8},{10,11... | collective-permute-start | bytes 6291464 | tf_op jit(solution)/shard_map/ppermute | solution.py:757
  16.5 9.5 %collective-permute-start.4 = (bf16[144,512]{1,0:T(8,128)(2,1)S(1)}, bf16[144,512]{1,0:T(8,128)(2,1)S(1)}, u32[]{:S(2)}, u32[]{:S(2)}) collective-permute-start(bf16[144,512]{1,0:T(8,128)(2,1)S(1)} %get-tuple-element.37), channel_id=1, source_target_pairs={{0,2},{2,0},{4,6},{6,4},{8,10},{10,8},{12,14},{14,12},{1,3},{3,1},... | collective-permute-start | bytes 442376 | tf_op jit(solution)/shard_map/ppermute | solution.py:544
  26.1 5.4 %collective-permute-start.5 = (bf16[144,512]{1,0:T(8,128)(2,1)S(1)}, bf16[144,512]{1,0:T(8,128)(2,1)S(1)}, u32[]{:S(2)}, u32[]{:S(2)}) collective-permute-start(bf16[144,512]{1,0:T(8,128)(2,1)S(1)} %pair_own.1.refs_4_.refs_1_), channel_id=1, source_target_pairs={{0,4},{1,0},{2,6},{3,2},{4,8},{5,1},{6,10},{7,3},{8,12},{9,5},{10,... | collective-permute-start | bytes 442376 | tf_op jit(solution)/shard_map/ppermute | solution.py:536
  27.7 6.5 %collective-permute-start.7 = (bf16[144,512]{1,0:T(8,128)(2,1)S(1)}, bf16[144,512]{1,0:T(8,128)(2,1)S(1)}, u32[]{:S(2)}, u32[]{:S(2)}) collective-permute-start(bf16[144,512]{1,0:T(8,128)(2,1)S(1)} %get-tuple-element.42), channel_id=1, source_target_pairs={{0,2},{2,0},{4,6},{6,4},{8,10},{10,8},{12,14},{14,12},{1,3},{3,1},... | collective-permute-start | bytes 442376 | tf_op jit(solution)/shard_map/ppermute | solution.py:544
  31.6 5.4 %collective-permute-start.6 = (bf16[144,512]{1,0:T(8,128)(2,1)S(1)}, bf16[144,512]{1,0:T(8,128)(2,1)S(1)}, u32[]{:S(2)}, u32[]{:S(2)}) collective-permute-start(bf16[144,512]{1,0:T(8,128)(2,1)S(1)} %chain_own.1.refs_3_), channel_id=1, source_target_pairs={{0,8},{1,0},{2,10},{3,2},{4,12},{5,4},{6,14},{7,6},{8,9},{9,1},{10... | collective-permute-start | bytes 442376 | tf_op jit(solution)/shard_map/ppermute | solution.py:536
  34.3 6.1 %collective-permute-start.8 = (bf16[144,512]{1,0:T(8,128)(2,1)S(1)}, bf16[144,512]{1,0:T(8,128)(2,1)S(1)}, u32[]{:S(2)}, u32[]{:S(2)}) collective-permute-start(bf16[144,512]{1,0:T(8,128)(2,1)S(1)} %pair_other.1.refs_5_.refs_1_), channel_id=1, source_target_pairs={{0,4},{1,0},{2,6},{3,2},{4,8},{5,1},{6,10},{7,3},{8,12},{9,5},{10,... | collective-permute-start | bytes 442376 | tf_op jit(solution)/shard_map/ppermute | solution.py:536
  40.4 6.2 %collective-permute-start.9 = (bf16[144,512]{1,0:T(8,128)(2,1)S(1)}, bf16[144,512]{1,0:T(8,128)(2,1)S(1)}, u32[]{:S(2)}, u32[]{:S(2)}) collective-permute-start(bf16[144,512]{1,0:T(8,128)(2,1)S(1)} %chain_other.1.refs_2_), channel_id=1, source_target_pairs={{0,8},{1,0},{2,10},{3,2},{4,12},{5,4},{6,14},{7,6},{8,9},{9,1},{10... | collective-permute-start | bytes 442376 | tf_op jit(solution)/shard_map/ppermute | solution.py:536
  43.9 5.0 %collective-permute-start.13 = (bf16[128,512]{1,0:T(8,128)(2,1)S(1)}, bf16[128,512]{1,0:T(8,128)(2,1)S(1)}, u32[]{:S(2)}, u32[]{:S(2)}) collective-permute-start(bf16[128,512]{1,0:T(8,128)(2,1)S(1)} %get-tuple-element.46), channel_id=1, source_target_pairs={{0,2},{2,0},{4,6},{6,4},{8,10},{10,8},{12,14},{14,12},{1,3},{3,1},... | collective-permute-start | bytes 393224 | tf_op jit(solution)/shard_map/ppermute | solution.py:610
  46.8 5.2 %collective-permute-start.11 = (bf16[128,512]{1,0:T(8,128)(2,1)S(1)}, bf16[128,512]{1,0:T(8,128)(2,1)S(1)}, u32[]{:S(2)}, u32[]{:S(2)}) collective-permute-start(bf16[128,512]{1,0:T(8,128)(2,1)S(1)} %get-tuple-element.45), channel_id=1, source_target_pairs={{0,2},{2,0},{4,6},{6,4},{8,10},{10,8},{12,14},{14,12},{1,3},{3,1},... | collective-permute-start | bytes 393224 | tf_op jit(solution)/shard_map/ppermute | solution.py:610
  54.0 2.0 %collective-permute-start.14 = (bf16[512,512]{1,0:T(8,128)(2,1)S(1)}, bf16[512,512]{1,0:T(8,128)(2,1)S(1)}, u32[]{:S(2)}, u32[]{:S(2)}) collective-permute-start(bf16[512,512]{1,0:T(8,128)(2,1)S(1)} %get-tuple-element.50), channel_id=1, source_target_pairs={{0,1},{1,0},{2,3},{3,2},{4,5},{5,4},{6,7},{7,6},{8,9},{9,8},{10,11... | collective-permute-start | bytes 1572872 | tf_op jit(solution)/shard_map/ppermute | solution.py:757

commit v6 on v5

--- a/solution.py
+++ b/solution.py
@@ -93,6 +93,11 @@
     return jnp.concatenate([high, low], axis=1)
 
 
+def two_rows(value):
+    high = value.astype(BF16).astype(F32)
+    return jnp.concatenate([high, value - high], axis=0)
+
+
 def head_matrix(heads, width, head_size, first_head):
     source = lax.broadcasted_iota(jnp.int32, (2 * heads, width), 0)
     source = jnp.where(source >= heads, source - heads, source)
@@ -111,6 +116,7 @@
     gain_hbm,
     bias_hbm,
     rate_hbm,
+    step_hbm,
     out_ref,
     tail_ref,
     small_ref,
@@ -121,6 +127,7 @@
     gain_ref,
     bias_ref,
     rate_ref,
+    step_ref,
     base_ref,
     normed_ref,
     sems,
@@ -138,6 +145,7 @@
         (gain_hbm, gain_ref),
         (bias_hbm, bias_ref),
         (rate_hbm, rate_ref),
+        (step_hbm, step_ref),
     ]
     small_copies = [pltpu.make_async_copy(src, dst, sems.at[count + i]) for i, (src, dst) in enumerate(whole)]
     parts = [pl.ds(r * CHUNK, CHUNK) for r in range(count)]
@@ -175,28 +183,29 @@
         copy.wait()
     small_ref[:taps, :] = conv_ref[...]
     small_ref[taps : taps + 1, :] = gain_ref[...]
-    small_ref[taps + 1 :, :] = jnp.zeros((SMALL_ROWS - taps - 1, inner), F32)
+    small_ref[taps + 1 : SMALL_ROWS, :] = jnp.zeros((SMALL_ROWS - taps - 1, inner), F32)
     small_ref[taps + 1 : taps + 2, :heads] = bias_ref[...]
     small_ref[taps + 2 : taps + 3, :heads] = rate_ref[...]
-
-
-def prepare_call(scalars, hidden, tokens, embedding, conv, gain, bias, rate):
+    small_ref[SMALL_ROWS:, :] = step_ref[...].astype(F32)
+
+
+def prepare_call(scalars, hidden, tokens, embedding, conv, gain, bias, rate, step):
     rows, width = hidden.shape
     inner = conv.shape[1]
     arrays = [hidden, tokens.reshape(1, -1), embedding, conv]
-    arrays += [a.reshape(1, -1) for a in (gain, bias, rate)]
+    arrays += [a.reshape(1, -1) for a in (gain, bias, rate)] + [step]
     return call(
         prepare_kernel,
         "prepare",
         vmem=12,
-        cost=micros(1.5),
+        cost=micros(2.7),
         scalars=scalars,
         in_specs=[HBM] * len(arrays),
         out_specs=[VMEM] * 3,
         out_shape=[
             jax.ShapeDtypeStruct((rows, width), BF16),
             jax.ShapeDtypeStruct((HALO, width), BF16),
-            jax.ShapeDtypeStruct((SMALL_ROWS, inner), F32),
+            jax.ShapeDtypeStruct((SMALL_ROWS + step.shape[0], inner), F32),
         ],
         scratch=[pltpu.VMEM(a.shape, a.dtype) for a in arrays]
         + [pltpu.VMEM((CHUNK, width), F32), pltpu.VMEM((CHUNK, width), BF16)]
@@ -232,11 +241,11 @@
 
 def conv_silu(rows_ref, weights, row):
     taps = weights.shape[0]
-    total = None
-    for k in range(taps):
-        offset = HALO - (taps - 1) + k + row
-        term = weights[k : k + 1, :] * rows_ref[offset : offset + BLOCK, :]
-        total = term if total is None else total + term
+    ahead = 8
+    window = rows_ref[HALO - ahead + row : HALO + row + BLOCK, :]
+    total = weights[taps - 1 :, :] * window[ahead:, :]
+    for back in range(1, taps):
+        total += weights[taps - 1 - back : taps - back, :] * pltpu.roll(window, back, 0)[ahead:, :]
     return silu(total).astype(BF16)
 
 
@@ -280,87 +289,92 @@
     halo_ref,
     bt_ref,
     wi_ref,
-    wt_ref,
     small_ref,
-    xs_ref,
+    x_ref,
     cum_ref,
-    cumt_ref,
+    times_ref,
     send_ref,
     mine_ref,
     rows_ref,
     spread_ref,
     scaled_ref,
-    step_ref,
     left_ref,
     whole_ref,
+    payload_ref,
 ):
     rows = normed_ref.shape[0]
     states = bt_ref.shape[0]
-    heads = wt_ref.shape[0]
+    heads = cum_ref.shape[1]
     taps = SMALL_TAPS
-    bias = small_ref[taps + 1 : taps + 2, :heads]
-    rate = small_ref[taps + 2 : taps + 3, :heads]
-    raw = dot_nt(normed_ref[...], wt_ref[...]) + bias
+    raw = dot_nt(normed_ref[...], small_ref[SMALL_ROWS:, :].astype(BF16))
+    columns = small_ref[:SMALL_ROWS, :CHUNK].T
+    raw = raw.T + columns[:heads, taps + 1 : taps + 2]
     step = jnp.maximum(raw, 0.0) + jnp.log1p(jnp.exp(-jnp.abs(raw)))
-    step_ref[...] = two_parts(step)
-    logdecay = -step * rate
+    logdecay = -step * columns[:heads, taps + 2 : taps + 3]
     high = logdecay.astype(BF16)
     rest = logdecay - high.astype(F32)
     mid = rest.astype(BF16)
     low = (rest - mid.astype(F32)).astype(BF16)
-    parts = jnp.concatenate([high, mid, low], axis=1)
-    to = lax.broadcasted_iota(jnp.int32, (CHUNK, CHUNK), 0)
-    frm = lax.broadcasted_iota(jnp.int32, (CHUNK, CHUNK), 1)
-    lower = jnp.where(to >= frm, 1.0, 0.0).astype(BF16)
-    run = jnp.zeros((1, heads), F32)
-    for r in range(0, rows, CHUNK):
-        sums = dot(lower, parts[r : r + CHUNK, :])
-        sums = sums[:, :heads] + sums[:, heads : 2 * heads] + sums[:, 2 * heads :] + run
-        cum_ref[r : r + CHUNK, :] = sums
-        run = sums[CHUNK - 1 :, :]
-    cum = cum_ref[...]
-    cumt_ref[...] = cum.T
-    left_ref[...] = two_parts(jnp.exp(run - cum))
-    whole_ref[...] = two_parts(jnp.exp(run))
-
-    inner = xs_ref.shape[1]
+    starts = range(0, rows, CHUNK)
+    pieces = [part[:, r : r + CHUNK] for r in starts for part in (high, mid, low)]
+    frm = lax.broadcasted_iota(jnp.int32, (CHUNK, CHUNK), 0)
+    to = lax.broadcasted_iota(jnp.int32, (CHUNK, CHUNK), 1)
+    sums = dot(jnp.concatenate(pieces, axis=0), jnp.where(to >= frm, 1.0, 0.0).astype(BF16))
+    run = jnp.zeros((heads, 1), F32)
+    cums = []
+    for i in range(len(starts)):
+        at = 3 * i * heads
+        cums.append(sums[at : at + heads] + sums[at + heads : at + 2 * heads] + sums[at + 2 * heads : at + 3 * heads] + run)
+        run = cums[-1][:, CHUNK - 1 :]
+    cum = jnp.concatenate(cums, axis=1)
+    times_ref[:heads, :] = cum
+    times_ref[heads:, :] = step
+    cum_ref[...] = cum.T
+    left_ref[...] = two_rows(step * jnp.exp(run - cum)).T.astype(BF16)
+    whole_ref[...] = two_parts(jnp.exp(cum_ref[rows - 1 :, :]))
+
+    inner = x_ref.shape[1]
     half = inner // 2
-    for low in range(0, inner, TILE):
-        columns = slice(low, low + TILE)
-        weights = wi_ref[:, columns]
+    tiles = range(inner // TILE)
+    onehots = [head_matrix(heads, TILE, head_size, t * (TILE // head_size)) for t in tiles]
+    spans = [slice(t * TILE, (t + 1) * TILE) for t in tiles]
+
+    def project(t):
+        weights = wi_ref[:, spans[t]]
         before = dot(halo_ref[...], weights).astype(BF16).astype(F32)
-        rows_ref[:HALO, :] = jnp.where(place_ref[0] >= 1, before, 0.0)
-        rows_ref[HALO:, :] = dot(normed_ref[...], weights).astype(BF16).astype(F32)
-        onehot = head_matrix(heads, TILE, head_size, low // head_size)
-        spread_ref[0] = dot(step_ref[...], onehot)
-        spread_ref[1] = dot(left_ref[...], onehot)
-        taps_here = small_ref[:taps, columns]
+        rows_ref[t % 2, :HALO, :] = jnp.where(place_ref[0] >= 1, before, 0.0)
+        rows_ref[t % 2, HALO:, :] = dot(normed_ref[...], weights).astype(BF16).astype(F32)
+        spread_ref[t % 2] = dot(left_ref[...], onehots[t])
+
+    def combine(t):
+        taps_here = small_ref[:taps, spans[t]]
         for r in range(0, rows, BLOCK):
-            xs = conv_silu(rows_ref, taps_here, r).astype(F32) * spread_ref[0, r : r + BLOCK, :]
-            xs_ref[r : r + BLOCK, columns] = xs.astype(BF16)
-            scaled_ref[r : r + BLOCK, :] = (xs * spread_ref[1, r : r + BLOCK, :]).astype(BF16)
-        state = dot(bt_ref[...], scaled_ref[...])
-        decay = dot(whole_ref[...], onehot)
-        here = slice(low % half, low % half + TILE)
-        is_mine = parity_ref[0] == low // half
-
-        @pl.when(is_mine)
-        def _():
-            write_payload(mine_ref, here, state, decay)
-
-        @pl.when(jnp.logical_not(is_mine))
-        def _():
-            write_payload(send_ref, here, state, decay)
+            block = slice(r, r + BLOCK)
+            x = conv_silu(rows_ref.at[t % 2], taps_here, r)
+            x_ref[block, spans[t]] = x
+            scaled_ref[t % 2, block, :] = (x.astype(F32) * spread_ref[t % 2, block, :]).astype(BF16)
+        state = dot(bt_ref[...], scaled_ref[t % 2])
+        here = slice(t * TILE % half, t * TILE % half + TILE)
+        is_mine = jnp.where(parity_ref[0] == t * TILE // half, 1, 0)
+        write_payload(payload_ref.at[is_mine], here, state, dot(whole_ref[...], onehots[t]))
+
+    project(0)
+    for t in tiles:
+        if t + 1 < len(tiles):
+            project(t + 1)
+        combine(t)
+    send_ref[...] = payload_ref[0]
+    mine_ref[...] = payload_ref[1]
 
 
 SMALL_TAPS = 4
 SMALL_ROWS = 8
 
 
-def local_call(tag, place, parity, normed, halo, bt, w_inner, w_step_t, small, after=()):
+def local_call(tag, place, parity, normed, halo, bt, w_inner, small, after=()):
     rows = normed.shape[0]
     inner = w_inner.shape[1]
-    heads = w_step_t.shape[0]
+    heads = small.shape[0] - SMALL_ROWS
     states = bt.shape[0]
     return call(
         functools.partial(local_kernel, inner // heads),
@@ -368,29 +382,29 @@
         vmem=12,
         cost=micros(5.0),
         scalars=(place, parity),
-        in_specs=[VMEM] * 6,
+        in_specs=[VMEM] * 5,
         out_specs=[VMEM] * 5,
         out_shape=[
             jax.ShapeDtypeStruct((rows, inner), BF16),
             jax.ShapeDtypeStruct((rows, heads), F32),
-            jax.ShapeDtypeStruct((heads, rows), F32),
+            jax.ShapeDtypeStruct((2 * heads, rows), F32),
             jax.ShapeDtypeStruct((states + EXTRA, inner // 2), BF16),
             jax.ShapeDtypeStruct((states + EXTRA, inner // 2), BF16),
         ],
         scratch=[
-            pltpu.VMEM((rows + HALO, TILE), F32),
+            pltpu.VMEM((2, rows + HALO, TILE), F32),
             pltpu.VMEM((2, rows, TILE), F32),
-            pltpu.VMEM((rows, TILE), BF16),
-            pltpu.VMEM((rows, 2 * heads), BF16),
+            pltpu.VMEM((2, rows, TILE), BF16),
             pltpu.VMEM((rows, 2 * heads), BF16),
             pltpu.VMEM((1, 2 * heads), BF16),
+            pltpu.VMEM((2, states + EXTRA, inner // 2), BF16),
         ],
         after=after,
-    )(place, parity, normed, halo, bt, w_inner, w_step_t, small)
-
-
-def inside_kernel(head_size, xs_ref, bc_ref, cum_ref, cumt_ref, y_ref, state_ref):
-    rows, inner = xs_ref.shape
+    )(place, parity, normed, halo, bt, w_inner, small)
+
+
+def inside_kernel(head_size, x_ref, bc_ref, bt_ref, cum_ref, times_ref, y_ref, state_ref):
+    rows, inner = x_ref.shape
     states = bc_ref.shape[1] // 2
     heads = cum_ref.shape[1]
     length = CHUNK
@@ -402,30 +416,31 @@
     state_ref[...] = jnp.zeros_like(state_ref)
 
     def chunk(c, before):
-        at = pl.ds(pl.multiple_of(c * length, length), length)
-        bmat = bc_ref[at, :states]
+        at = slice(c * length, (c + 1) * length)
+        bmat = bt_ref[:, at]
         cmat = bc_ref[at, states:]
-        scores = jnp.where(to >= frm, dot_nt(cmat, bmat), 0.0)
+        scores = jnp.where(to >= frm, dot(cmat, bmat), 0.0)
         cum = cum_ref[at, :]
-        cumt = cumt_ref[:, at]
-        end = cum[last:, :]
-        since = two_parts(jnp.exp(cum - before))
-        left = two_parts(jnp.exp(end - cum))
+        cumt = times_ref[:heads, at]
+        step = times_ref[heads:, at]
+        end = cumt[:, last:]
+        since = two_rows(jnp.exp(cumt - before)).T.astype(BF16)
+        left = two_rows(step * jnp.exp(end - cumt)).T.astype(BF16)
         for first in range(0, heads, TILE // head_size):
             columns = slice(first * head_size, first * head_size + TILE)
             onehot = head_matrix(heads, TILE, head_size, first)
             since_here = dot(since, onehot)
             state = state_ref[:, columns]
             carried = dot(cmat, state.astype(BF16)) * since_here
-            scaled = (xs_ref[at, columns].astype(F32) * dot(left, onehot)).astype(BF16)
-            state_ref[:, columns] = state * since_here[last:, :] + dot_tn(bmat, scaled)
+            scaled = (x_ref[at, columns].astype(F32) * dot(left, onehot)).astype(BF16)
+            state_ref[:, columns] = state * since_here[last:, :] + dot(bmat, scaled)
             for start in range(0, TILE, pair):
                 low = first * head_size + start
                 weights = []
                 for h in (low // head_size, low // head_size + 1):
                     apart = jnp.minimum(cum[:, h : h + 1] - cumt[h : h + 1, :], 0.0)
-                    weights.append((jnp.exp(apart) * scores).astype(BF16))
-                mine = xs_ref[at, low : low + pair]
+                    weights.append((jnp.exp(apart) * (scores * step[h : h + 1, :])).astype(BF16))
+                mine = x_ref[at, low : low + pair]
                 none = jnp.zeros_like(mine)
                 stacked = jnp.concatenate(
                     [jnp.where(lane < head_size, mine, none), jnp.where(lane < head_size, none, mine)], axis=0
@@ -434,11 +449,13 @@
                 y_ref[at, low : low + pair] = (inside + carried[:, start : start + pair]).astype(BF16)
         return end
 
-    lax.fori_loop(0, rows // length, chunk, jnp.zeros((1, heads), F32))
-
-
-def inside_call(tag, xs, bc, cum, cumt, after=()):
-    rows, inner = xs.shape
+    before = jnp.zeros((heads, 1), F32)
+    for c in range(rows // length):
+        before = chunk(c, before)
+
+
+def inside_call(tag, x, bc, bt, cum, times, after=()):
+    rows, inner = x.shape
     heads = cum.shape[1]
     both = bc.shape[1]
     return call(
@@ -446,12 +463,12 @@
         "inside_" + tag,
         vmem=8,
         cost=micros(3.2),
-        in_specs=[VMEM] * 4,
+        in_specs=[VMEM] * 5,
         out_specs=VMEM,
         out_shape=jax.ShapeDtypeStruct((rows, inner), BF16),
         scratch=[pltpu.VMEM((both // 2, inner), F32)],
         after=after,
-    )(xs, bc, cum, cumt)
+    )(x, bc, bt, cum, times)
 
 
 def parts_of(ref, known=None):
@@ -645,37 +662,60 @@
         out_ref[:, low : low + TILE] = dot(scaled_ref[...], ins[-1][:, low : low + TILE])
 
 
-def finish_kernel(head_size, full_width, back_ref, parity_ref, *refs):
-    *ins, part_ref, psq_ref, own_ref, send_ref, scaled_ref, tile_ref, out_ref = refs
-    squares = gated_part(head_size, parity_ref[0] == 1, *ins, scaled_ref, tile_ref)
-    rows, half = own_ref.shape
-    width = 2 * half
-    scales = []
-    for i, square in enumerate(squares):
-        block = slice(i * BLOCK, (i + 1) * BLOCK)
-        scales.append(lax.rsqrt((square + psq_ref[block, :1]) / full_width + EPS))
-    for low in range(0, width, TILE):
-        columns = slice(low, low + TILE)
-        tile_ref[0] = dot(scaled_ref[...], ins[-1][:, columns])
-        for i, scale in enumerate(scales):
-            block = slice(i * BLOCK, (i + 1) * BLOCK)
-            out_ref[block, columns] = ((tile_ref[0, block, :] + part_ref[block, columns]) * scale).astype(BF16)
-
-    @pl.when(back_ref[0] == 1)
+def product(back, scaled_ref, weights_ref, part_ref, scale_ref, tile_ref, half_ref, out_ref, first):
+    rows, half = out_ref.shape
+    for low in range(0, half, TILE):
+        columns = slice(first + low, first + low + TILE)
+        tile_ref[...] = dot(scaled_ref[...], weights_ref[:, columns])
+        for r in range(0, rows, BLOCK):
+            block = slice(r, r + BLOCK)
+            value = (tile_ref[block, :] + part_ref[block, columns]) * scale_ref[block, :1]
+            half_ref[block, low : low + TILE] = value.astype(BF16)
+
+    @pl.when(back == 1)
     def _():
         turn = flip_matrix(TILE)
         for r in range(0, rows, TILE):
-            for low in range(0, width, TILE):
-                tile = dot(turn, out_ref[r : r + TILE, low : low + TILE]).astype(BF16)
+            for low in range(0, half, TILE):
+                tile = dot(turn, half_ref[r : r + TILE, low : low + TILE]).astype(BF16)
                 tile = dot(tile, turn).astype(BF16)
-                to_row, to = rows - TILE - r, width - TILE - low
-                target, to = (own_ref, to - half) if to >= half else (send_ref, to)
-                target[to_row : to_row + TILE, to : to + TILE] = tile
-
-    @pl.when(back_ref[0] != 1)
+                to_row, to = rows - TILE - r, half - TILE - low
+                out_ref[to_row : to_row + TILE, to : to + TILE] = tile
+
+    @pl.when(back != 1)
     def _():
-        own_ref[...] = out_ref[:, :half]
-        send_ref[...] = out_ref[:, half:]
+        out_ref[...] = half_ref[...]
+
+
+def finish_kernel(head_size, full_width, back_ref, parity_ref, *refs):
+    *ins, part_ref, psq_ref, send_ref, scaled_ref, scale_ref, tile_ref, half_ref = refs
+    squares = gated_part(head_size, parity_ref[0] == 1, *ins, scaled_ref, tile_ref)
+    for i, square in enumerate(squares):
+        block = slice(i * BLOCK, (i + 1) * BLOCK)
+        scale = lax.rsqrt((square + psq_ref[block, :1]) / full_width + EPS)
+        scale_ref[block, :] = jnp.broadcast_to(scale, (BLOCK, scale_ref.shape[1]))
+    product(back_ref[0], scaled_ref, ins[-1], part_ref, scale_ref, tile_ref.at[0], half_ref, send_ref, send_ref.shape[1])
+
+
+def own_kernel(back_ref, scaled_ref, weights_ref, part_ref, scale_ref, own_ref, tile_ref, half_ref):
+    product(back_ref[0], scaled_ref, weights_ref, part_ref, scale_ref, tile_ref, half_ref, own_ref, 0)
+
+
+def own_call(back, scaled, w_output, part, scale, after):
+    rows, width = part.shape
+    half = width // 2
+    return call(
+        own_kernel,
+        "own_half",
+        vmem=8,
+        cost=micros(0.7),
+        scalars=(back,),
+        in_specs=[VMEM] * 4,
+        out_specs=VMEM,
+        out_shape=jax.ShapeDtypeStruct((rows, half), BF16),
+        scratch=[pltpu.VMEM((rows, TILE), F32), pltpu.VMEM((rows, half), BF16)],
+        after=after,
+    )(back, scaled, w_output, part, scale)
 
 
 def finish_call(back, parity, y, bc, cum, keep, other, gate, small, w_output, full_width=None, partial=None, after=()):
@@ -684,17 +724,22 @@
     half = width // 2
     heads = cum.shape[1]
     arrays = [y, bc, cum, keep, other, gate, small, w_output]
-    scratch = [pltpu.VMEM((rows, inner), BF16), pltpu.VMEM((2, rows, TILE), F32)]
+    tiles = pltpu.VMEM((2, rows, TILE), F32)
     if partial is None:
+        scratch = [pltpu.VMEM((rows, inner), BF16), tiles]
         scalars = (parity,)
         kernel = functools.partial(part_kernel, inner // heads)
         out_shape = [jax.ShapeDtypeStruct((rows, width), F32), jax.ShapeDtypeStruct((rows, 128), F32)]
     else:
         scalars = (back, parity)
-        scratch.append(pltpu.VMEM((rows, width), BF16))
+        scratch = [tiles, pltpu.VMEM((rows, half), BF16)]
         kernel = functools.partial(finish_kernel, inner // heads, full_width)
         arrays += list(partial)
-        out_shape = [jax.ShapeDtypeStruct((rows, half), BF16)] * 2
+        out_shape = [
+            jax.ShapeDtypeStruct((rows, half), BF16),
+            jax.ShapeDtypeStruct((rows, inner), BF16),
+            jax.ShapeDtypeStruct((rows, 128), F32),
+        ]
     return call(
         kernel,
         "part" if partial is None else "finish",
@@ -702,7 +747,7 @@
         cost=micros(3.5),
         scalars=scalars,
         in_specs=[VMEM] * len(arrays),
-        out_specs=[VMEM] * 2,
+        out_specs=[VMEM] * len(out_shape),
         out_shape=out_shape,
         scratch=scratch,
         after=after,
@@ -764,30 +809,28 @@
     place = (index + core * (last - 2 * index)).reshape(1)
     w_inner_2 = theirs(w_inner)
     normed, tail, small = prepare_call(
-        (back, parity, place), hidden, tokens, embedding, conv_inner, norm_gain, step_bias, decay_rate
+        (back, parity, place), hidden, tokens, embedding, conv_inner, norm_gain, step_bias, decay_rate, w_step.T
     )
     halo = onward(tail, 1)
     small_2 = theirs(small)
-    w_step_t = w_step.T
-    w_step_2 = theirs(w_step_t)
     w_gate_2 = theirs(w_gate)
     w_output_2 = theirs(w_output)
     gate_1 = gate_call("own", normed, w_gate)
     bc, bt = maps_call(place, normed, halo, w_state, conv_state, after=[gate_1])
-    xs_1, cum_1, cumt_1, send_1, mine_1 = local_call(
-        "own", place, parity, normed, halo, bt, w_inner, w_step_t, small
+    x_1, cum_1, times_1, send_1, mine_1 = local_call(
+        "own", place, parity, normed, halo, bt, w_inner, small
     )
     chain_1 = Chain("own", place, send_1, mine_1)
-    xs_2, cum_2, cumt_2, send_2, mine_2 = local_call(
-        "other", place, parity, normed, halo, bt, w_inner_2, w_step_2, small_2, after=[mine_1]
+    x_2, cum_2, times_2, send_2, mine_2 = local_call(
+        "other", place, parity, normed, halo, bt, w_inner_2, small_2, after=[mine_1]
     )
     chain_2 = Chain("other", place, send_2, mine_2)
-    done = chain_1.pair(after=[xs_2])
-    y_1 = inside_call("own", xs_1, bc, cum_1, cumt_1, after=[done])
+    done = chain_1.pair(after=[x_2])
+    y_1 = inside_call("own", x_1, bc, bt, cum_1, times_1, after=[done])
     done = chain_1.middle(after=[y_1])
     done = chain_2.pair(after=[done])
     entry_1 = chain_1.entry(after=[done])
-    y_2 = inside_call("other", xs_2, bc, cum_2, cumt_2, after=[entry_1[0]])
+    y_2 = inside_call("other", x_2, bc, bt, cum_2, times_2, after=[entry_1[0]])
     done = chain_2.middle(after=[y_2])
     gate_2 = gate_call("other", normed, w_gate_2, after=[done])
     entry_2 = chain_2.entry(after=[gate_2])
@@ -795,10 +838,12 @@
         back, parity, y_1, bc, cum_1, *entry_1, gate_1, small, w_output, after=[entry_2[0]]
     )
     full_width = float(w_inner.shape[1] * lax.axis_size("ch"))
-    mine, send = finish_call(
+    send, scaled, scale = finish_call(
         back, parity, y_2, bc, cum_2, *entry_2, gate_2, small_2, w_output_2, full_width, partial
     )
-    return total_call(mine, theirs(send))
+    arriving = theirs(send)
+    mine = own_call(back, scaled, w_output_2, partial[0], scale, after=[send])
+    return total_call(mine, arriving)
 
 
 def solution(mesh):

time: 58.1 us -> 52.8 us (0.909)
  Pallas kernels: 32.1 us -> 27.3 us
  waiting for transfers between devices: 6.99 us -> 5.27 us
  starting transfers between devices: 17.4 us -> 18.5 us
    pallas_call x17 -> x18, Pallas kernels: 32.1 us -> 27.3 us  [call(): return lambda *arrays: run(*arrays, *after)]
    ppermute x5, waiting for transfers between devices: 2.81 us -> 1.68 us  [onward(): return lax.ppermute(value, ('seq', 'ch'), pairs)]
    ppermute x2, starting transfers between devices: 1.5 us -> 2.46 us  [entry(): return (keep, lax.ppermute(out, 'seq', self.swap))]
    ppermute x5, starting transfers between devices: 10.8 us -> 11.6 us  [onward(): return lax.ppermute(value, ('seq', 'ch'), pairs)]
    ppermute x6 -> x5, starting transfers between devices: 1.91 us -> 1.1 us  [theirs(): return lax.ppermute(a, 'ch', swap)]
    ppermute x6 -> x5, waiting for transfers between devices: 1.91 us -> 1.15 us  [theirs(): return lax.ppermute(a, 'ch', swap)]
  transfers between devices with their start and end apart: 15 -> 14, of which waited for: 5 -> 5; matrix products, arithmetic and copies ran while one was open for 0% -> 0% of each run, Pallas kernels for 51% -> 48%
where the time goes in v6:
time: 52.8 us; the launch traced here: 52.1 us
  Pallas kernels  27.3 us (52%)
  starting transfers between devices  18.5 us (35%)
  waiting for transfers between devices  5.27 us (10%)
  local copies, waits for them, and re-layouts  0.65 us (1%)
    pallas_call x18, Pallas kernels, call(): return lambda *arrays: run(*arrays, *after)  27.3 us
    ppermute x5, starting transfers between devices, onward(): return lax.ppermute(value, ('seq', 'ch'), pairs)  11.6 us
    ppermute x2, starting transfers between devices, __init__(): self.other = lax.ppermute(send, 'seq', self.swap)  3.38 us
    ppermute x2, starting transfers between devices, entry(): return (keep, lax.ppermute(out, 'seq', self.swap))  2.46 us
    ppermute x2, waiting for transfers between devices, entry(): return (keep, lax.ppermute(out, 'seq', self.swap))  2.21 us
    ppermute x5, waiting for transfers between devices, onward(): return lax.ppermute(value, ('seq', 'ch'), pairs)  1.68 us
    ppermute x5, waiting for transfers between devices, theirs(): return lax.ppermute(a, 'ch', swap)  1.15 us
    ppermute x5, starting transfers between devices, theirs(): return lax.ppermute(a, 'ch', swap)  1.1 us
  transfers between devices with their start and end apart: 14, of which 5 were waited for; matrix products, arithmetic and copies ran while one was open for 0% of the time, Pallas kernels for 48%

profile of v6, /device:TPU:0, one launch (start us, length us, event | category | flops | bytes accessed | tf_op | source)
XLA Modules:
  0.0 52.1 jit_solution(3521904527452673545)
XLA Ops:
  0.5 2.7 %prepare.1 = (bf16[512,1024]{1,0:T(8,128)(2,1)S(1)}, bf16[16,1024]{1,0:T(8,128)(2,1)S(1)}, f32[24,1024]{1,0:T(8,128)S(1)}) custom-call(s32[1]{0:T(128)} %bitcast.refs_0_, s32[1]{0:T(128)} %bitcast.1.refs_1_.refs_0_, s32[1]{0:T(128)} %bitcast.2.refs_2_.refs_0_, bf16[512,1024]{1,0:T(8,128)(2,1)} %refs_3_.2, s32[1,512]{1,0:T(1,128)} %bitcast.10, ...), custom_call_target="tpu_custom_call" | custom-call | flops 2969999872 | bytes 2700000 | tf_op jit(solution)/shard_map/prepare/pallas_call | solution.py:48
  3.2 2.6 %collective-permute-start = (bf16[16,1024]{1,0:T(8,128)(2,1)S(1)}, bf16[16,1024]{1,0:T(8,128)(2,1)S(1)}, u32[]{:S(2)}, u32[]{:S(2)}) collective-permute-start(bf16[16,1024]{1,0:T(8,128)(2,1)S(1)} %get-tuple-element.30), channel_id=1, source_target_pairs={{0,2},{1,0},{2,4},{3,1},{4,6},{5,3},{6,8},{7,5},{8,10},{9,7},{10,1... | collective-permute-start | bytes 98312 | tf_op jit(solution)/shard_map/ppermute | solution.py:553
  6.4 1.4 %gate_own.1.refs_5_.refs_6_ = bf16[512,1024]{1,0:T(8,128)(2,1)S(1)} custom-call(bf16[512,1024]{1,0:T(8,128)(2,1)S(1)} %get-tuple-element.29.refs_0_.refs_1_.refs_2_, bf16[1024,1024]{1,0:T(8,128)(2,1)S(1)} %copy-done.1), custom_call_target="tpu_custom_call" | custom-call | flops 2640000000 | bytes 2400000 | tf_op jit(solution)/shard_map/gate_own/pallas_call | solution.py:48
  7.8 0.9 %maps.1 = (bf16[512,256]{1,0:T(8,128)(2,1)S(1)}, bf16[128,512]{1,0:T(8,128)(2,1)S(1)}) custom-call(s32[1]{0:T(128)} %bitcast.2.refs_2_.refs_0_, bf16[512,1024]{1,0:T(8,128)(2,1)S(1)} %get-tuple-element.29.refs_0_.refs_1_.refs_2_, bf16[16,1024]{1,0:T(8,128)(2,1)S(1)} %collective-permute-done.refs_2_.refs_3_, bf16[1024,256]{1,0:T(8,128)(2,1)S(1)} %copy-done.3, ...), custom_call_target="tpu_custom_call" | custom-call | flops 1650000000 | bytes 1500000 | tf_op jit(solution)/shard_map/maps/pallas_call | solution.py:48
  9.4 4.3 %local_own.1 = (bf16[512,1024]{1,0:T(8,128)(2,1)S(1)}, f32[512,16]{1,0:T(8,128)S(1)}, f32[32,512]{1,0:T(8,128)S(1)}, bf16[144,512]{1,0:T(8,128)(2,1)S(1)}, bf16[144,512]{1,0:T(8,128)(2,1)S(1)}) custom-call(s32[1]{0:T(128)} %bitcast.2.refs_2_.refs_0_, s32[1]{0:T(128)} %bitcast.1.refs_1_.refs_0_, ...), custom_call_target="tpu_custom_call" | custom-call | flops 5500000256 | bytes 5000000 | tf_op jit(solution)/shard_map/local_own/pallas_call | solution.py:48
  13.7 2.0 %collective-permute-start.3 = (bf16[144,512]{1,0:T(8,128)(2,1)S(1)}, bf16[144,512]{1,0:T(8,128)(2,1)S(1)}, u32[]{:S(2)}, u32[]{:S(2)}) collective-permute-start(bf16[144,512]{1,0:T(8,128)(2,1)S(1)} %get-tuple-element.38), channel_id=1, source_target_pairs={{0,2},{2,0},{4,6},{6,4},{8,10},{10,8},{12,14},{14,12},{1,3},{3,1},... | collective-permute-start | bytes 442376 | tf_op jit(solution)/shard_map/ppermute | solution.py:561
  15.7 4.3 %local_other.1 = (bf16[512,1024]{1,0:T(8,128)(2,1)S(1)}, f32[512,16]{1,0:T(8,128)S(1)}, f32[32,512]{1,0:T(8,128)S(1)}, bf16[144,512]{1,0:T(8,128)(2,1)S(1)}, bf16[144,512]{1,0:T(8,128)(2,1)S(1)}) custom-call(s32[1]{0:T(128)} %bitcast.2.refs_2_.refs_0_, s32[1]{0:T(128)} %bitcast.1.refs_1_.refs_0_, ...), custom_call_target="tpu_custom_call" | custom-call | flops 5500000256 | bytes 5000000 | tf_op jit(solution)/shard_map/local_other/pallas_call | solution.py:48
  20.4 2.4 %collective-permute-start.4 = (bf16[144,512]{1,0:T(8,128)(2,1)S(1)}, bf16[144,512]{1,0:T(8,128)(2,1)S(1)}, u32[]{:S(2)}, u32[]{:S(2)}) collective-permute-start(bf16[144,512]{1,0:T(8,128)(2,1)S(1)} %pair_own.1.refs_5_.refs_1_), channel_id=1, source_target_pairs={{0,4},{1,0},{2,6},{3,2},{4,8},{5,1},{6,10},{7,3},{8,12},{9,5},{10,... | collective-permute-start | bytes 442376 | tf_op jit(solution)/shard_map/ppermute | solution.py:553
  22.8 1.4 %collective-permute-start.6 = (bf16[144,512]{1,0:T(8,128)(2,1)S(1)}, bf16[144,512]{1,0:T(8,128)(2,1)S(1)}, u32[]{:S(2)}, u32[]{:S(2)}) collective-permute-start(bf16[144,512]{1,0:T(8,128)(2,1)S(1)} %get-tuple-element.43), channel_id=1, source_target_pairs={{0,2},{2,0},{4,6},{6,4},{8,10},{10,8},{12,14},{14,12},{1,3},{3,1},... | collective-permute-start | bytes 442376 | tf_op jit(solution)/shard_map/ppermute | solution.py:561
  24.1 3.3 %inside_own.1.refs_3_.refs_1_ = bf16[512,1024]{1,0:T(8,128)(2,1)S(1)} custom-call(bf16[512,1024]{1,0:T(8,128)(2,1)S(1)} %get-tuple-element.39.refs_0_, bf16[512,256]{1,0:T(8,128)(2,1)S(1)} %get-tuple-element.35.refs_1_.refs_2_.refs_3_, bf16[128,512]{1,0:T(8,128)(2,1)S(1)} %get-tuple-element.31.refs_4_.refs_2_, f32[512,16]{1,0:T(8,128)S(1)} %get-tuple-element.40.refs_3_, ...), custom_call_target="tpu_custom_call" | custom-call | flops 3520000000 | bytes 3200000 | tf_op jit(solution)/shard_map/inside_own/pallas_call | solution.py:48
  27.5 2.1 %collective-permute-start.5 = (bf16[144,512]{1,0:T(8,128)(2,1)S(1)}, bf16[144,512]{1,0:T(8,128)(2,1)S(1)}, u32[]{:S(2)}, u32[]{:S(2)}) collective-permute-start(bf16[144,512]{1,0:T(8,128)(2,1)S(1)} %chain_own.1.refs_3_), channel_id=1, source_target_pairs={{0,8},{1,0},{2,10},{3,2},{4,12},{5,4},{6,14},{7,6},{8,9},{9,1},{10... | collective-permute-start | bytes 442376 | tf_op jit(solution)/shard_map/ppermute | solution.py:553
  29.7 1.0 %collective-permute-start.7 = (bf16[144,512]{1,0:T(8,128)(2,1)S(1)}, bf16[144,512]{1,0:T(8,128)(2,1)S(1)}, u32[]{:S(2)}, u32[]{:S(2)}) collective-permute-start(bf16[144,512]{1,0:T(8,128)(2,1)S(1)} %pair_other.1.refs_5_.refs_1_), channel_id=1, source_target_pairs={{0,4},{1,0},{2,6},{3,2},{4,8},{5,1},{6,10},{7,3},{8,12},{9,5},{10,... | collective-permute-start | bytes 442376 | tf_op jit(solution)/shard_map/ppermute | solution.py:553
  30.7 1.6 %collective-permute-done.5.refs_4_ = bf16[144,512]{1,0:T(8,128)(2,1)S(1)} collective-permute-done((bf16[144,512]{1,0:T(8,128)(2,1)S(1)}, bf16[144,512]{1,0:T(8,128)(2,1)S(1)}, u32[]{:S(2)}, u32[]{:S(2)}) %collective-permute-start.5) | collective-permute-done | bytes 147488 | tf_op jit(solution)/shard_map/ppermute | solution.py:553
  32.5 3.2 %inside_other.1.refs_3_.refs_2_ = bf16[512,1024]{1,0:T(8,128)(2,1)S(1)} custom-call(bf16[512,1024]{1,0:T(8,128)(2,1)S(1)} %get-tuple-element.34.refs_3_.refs_0_, bf16[512,256]{1,0:T(8,128)(2,1)S(1)} %get-tuple-element.35.refs_1_.refs_2_.refs_3_, bf16[128,512]{1,0:T(8,128)(2,1)S(1)} %get-tuple-element.31.refs_4_.refs_2_, ...), custom_call_target="tpu_custom_call" | custom-call | flops 3520000000 | bytes 3200000 | tf_op jit(solution)/shard_map/inside_other/pallas_call | solution.py:48
  35.8 3.5 %collective-permute-start.8 = (bf16[144,512]{1,0:T(8,128)(2,1)S(1)}, bf16[144,512]{1,0:T(8,128)(2,1)S(1)}, u32[]{:S(2)}, u32[]{:S(2)}) collective-permute-start(bf16[144,512]{1,0:T(8,128)(2,1)S(1)} %chain_other.1.refs_2_), channel_id=1, source_target_pairs={{0,8},{1,0},{2,10},{3,2},{4,12},{5,4},{6,14},{7,6},{8,9},{9,1},{10... | collective-permute-start | bytes 442376 | tf_op jit(solution)/shard_map/ppermute | solution.py:553
  39.3 1.2 %collective-permute-start.12 = (bf16[128,512]{1,0:T(8,128)(2,1)S(1)}, bf16[128,512]{1,0:T(8,128)(2,1)S(1)}, u32[]{:S(2)}, u32[]{:S(2)}) collective-permute-start(bf16[128,512]{1,0:T(8,128)(2,1)S(1)} %get-tuple-element.47), channel_id=1, source_target_pairs={{0,2},{2,0},{4,6},{6,4},{8,10},{10,8},{12,14},{14,12},{1,3},{3,1},... | collective-permute-start | bytes 393224 | tf_op jit(solution)/shard_map/ppermute | solution.py:627
  40.5 1.4 %gate_other.1.refs_5_.refs_7_ = bf16[512,1024]{1,0:T(8,128)(2,1)S(1)} custom-call(bf16[512,1024]{1,0:T(8,128)(2,1)S(1)} %get-tuple-element.29.refs_0_.refs_1_.refs_2_, bf16[1024,1024]{1,0:T(8,128)(2,1)S(1)} %collective-permute-done.9.refs_1_, bf16[144,512]{1,0:T(8,128)(2,1)S(1)} %chain_other.1.refs_2_), custom_call_target="tpu_custom_call" | custom-call | flops 2640000000 | bytes 2400000 | tf_op jit(solution)/shard_map/gate_other/pallas_call | solution.py:48
  42.1 1.3 %collective-permute-start.10 = (bf16[128,512]{1,0:T(8,128)(2,1)S(1)}, bf16[128,512]{1,0:T(8,128)(2,1)S(1)}, u32[]{:S(2)}, u32[]{:S(2)}) collective-permute-start(bf16[128,512]{1,0:T(8,128)(2,1)S(1)} %get-tuple-element.46), channel_id=1, source_target_pairs={{0,2},{2,0},{4,6},{6,4},{8,10},{10,8},{12,14},{14,12},{1,3},{3,1},... | collective-permute-start | bytes 393224 | tf_op jit(solution)/shard_map/ppermute | solution.py:627
  43.3 0.9 %collective-permute-done.12.refs_5_ = bf16[128,512]{1,0:T(8,128)(2,1)S(1)} collective-permute-done((bf16[128,512]{1,0:T(8,128)(2,1)S(1)}, bf16[128,512]{1,0:T(8,128)(2,1)S(1)}, u32[]{:S(2)}, u32[]{:S(2)}) %collective-permute-start.12) | collective-permute-done | bytes 131104 | tf_op jit(solution)/shard_map/ppermute | solution.py:627
  44.2 2.0 %part.1 = (f32[512,1024]{1,0:T(8,128)S(1)}, f32[512,128]{1,0:T(8,128)S(1)}) custom-call(s32[1]{0:T(128)} %bitcast.1.refs_1_.refs_0_, bf16[512,1024]{1,0:T(8,128)(2,1)S(1)} %inside_own.1.refs_3_.refs_1_, bf16[512,256]{1,0:T(8,128)(2,1)S(1)} %get-tuple-element.35.refs_1_.refs_2_.refs_3_, f32[512,16]{1,0:T(8,128)S(1)} %get-tuple-element.40.refs_3_, ...), custom_call_target="tpu_custom_call" | custom-call | flops 3849999872 | bytes 3500000 | tf_op jit(solution)/shard_map/part/pallas_call | solution.py:48
  46.3 1.3 %collective-permute-done.10.refs_6_ = bf16[128,512]{1,0:T(8,128)(2,1)S(1)} collective-permute-done((bf16[128,512]{1,0:T(8,128)(2,1)S(1)}, bf16[128,512]{1,0:T(8,128)(2,1)S(1)}, u32[]{:S(2)}, u32[]{:S(2)}) %collective-permute-start.10) | collective-permute-done | bytes 131104 | tf_op jit(solution)/shard_map/ppermute | solution.py:627
  47.6 1.5 %finish.1 = (bf16[512,512]{1,0:T(8,128)(2,1)S(1)}, bf16[512,1024]{1,0:T(8,128)(2,1)S(1)}, f32[512,128]{1,0:T(8,128)S(1)}) custom-call(s32[1]{0:T(128)} %bitcast.refs_0_, s32[1]{0:T(128)} %bitcast.1.refs_1_.refs_0_, bf16[512,1024]{1,0:T(8,128)(2,1)S(1)} %inside_other.1.refs_3_.refs_2_, bf16[512,256]{1,0:T(8,128)(2,1)S(1)} %get-tuple-element.35.refs_1_.refs_2_.refs_3_, ...), custom_call_target="tpu_custom_call" | custom-call | flops 3849999872 | bytes 3500000 | tf_op jit(solution)/shard_map/finish/pallas_call | solution.py:48
  49.9 1.1 %collective-permute-done.13.refs_1_ = bf16[512,512]{1,0:T(8,128)(2,1)S(1)} collective-permute-done((bf16[512,512]{1,0:T(8,128)(2,1)S(1)}, bf16[512,512]{1,0:T(8,128)(2,1)S(1)}, u32[]{:S(2)}, u32[]{:S(2)}) %collective-permute-start.13) | collective-permute-done | bytes 524320 | tf_op jit(solution)/shard_map/ppermute | solution.py:802
  51.0 0.8 %total.1 = bf16[512,512]{1,0:T(8,128)(2,1)} custom-call(bf16[512,512]{1,0:T(8,128)(2,1)S(1)} %own_half.1.refs_0_, bf16[512,512]{1,0:T(8,128)(2,1)S(1)} %collective-permute-done.13.refs_1_), custom_call_target="tpu_custom_call" | custom-call | flops 880000000 | bytes 800000 | tf_op jit(solution)/shard_map/total/pallas_call | solution.py:48
  (32 shorter events, 3.3 us)
Async XLA Ops:
  0.0 15.7 %collective-permute-start.1 = (bf16[1024,1024]{1,0:T(8,128)(2,1)}, bf16[1024,1024]{1,0:T(8,128)(2,1)S(1)}, u32[]{:S(2)}, u32[]{:S(2)}) collective-permute-start(bf16[1024,1024]{1,0:T(8,128)(2,1)} %refs_5_.3), channel_id=1, source_target_pairs={{0,1},{1,0},{2,3},{3,2},{4,5},{5,4},{6,7},{7,6},{8,9},{9,8},{10,11... | collective-permute-start | bytes 6291464 | tf_op jit(solution)/shard_map/ppermute | solution.py:802
  0.5 5.3 %copy-start.1 = (bf16[1024,1024]{1,0:T(8,128)(2,1)S(1)}, bf16[1024,1024]{1,0:T(8,128)(2,1)}, u32[]{:S(2)}) copy-start(bf16[1024,1024]{1,0:T(8,128)(2,1)} %refs_1_.1) | copy-start | bytes 6291460
  0.5 5.8 %copy-start.2 = (bf16[1024,1024]{1,0:T(8,128)(2,1)S(1)}, bf16[1024,1024]{1,0:T(8,128)(2,1)}, u32[]{:S(2)}) copy-start(bf16[1024,1024]{1,0:T(8,128)(2,1)} %refs_8_.1) | copy-start | bytes 6291460
  3.2 4.6 %collective-permute-start = (bf16[16,1024]{1,0:T(8,128)(2,1)S(1)}, bf16[16,1024]{1,0:T(8,128)(2,1)S(1)}, u32[]{:S(2)}, u32[]{:S(2)}) collective-permute-start(bf16[16,1024]{1,0:T(8,128)(2,1)S(1)} %get-tuple-element.30), channel_id=1, source_target_pairs={{0,2},{1,0},{2,4},{3,1},{4,6},{5,3},{6,8},{7,5},{8,10},{9,7},{10,1... | collective-permute-start | bytes 98312 | tf_op jit(solution)/shard_map/ppermute | solution.py:553
  5.8 10.0 %collective-permute-start.2 = (f32[24,1024]{1,0:T(8,128)S(1)}, f32[24,1024]{1,0:T(8,128)S(1)}, u32[]{:S(2)}, u32[]{:S(2)}) collective-permute-start(f32[24,1024]{1,0:T(8,128)S(1)} %get-tuple-element.32.refs_6_.refs_7_), channel_id=1, source_target_pairs={{0,1},{1,0},{2,3},{3,2},{4,5},{5,4},{6,7},{7,6},{8,9},{9,8},{10,11... | collective-permute-start | bytes 294920 | tf_op jit(solution)/shard_map/ppermute | solution.py:802
  5.8 34.7 %collective-permute-start.9 = (bf16[1024,1024]{1,0:T(8,128)(2,1)S(1)}, bf16[1024,1024]{1,0:T(8,128)(2,1)S(1)}, u32[]{:S(2)}, u32[]{:S(2)}) collective-permute-start(bf16[1024,1024]{1,0:T(8,128)(2,1)S(1)} %copy-done.1), channel_id=1, source_target_pairs={{0,1},{1,0},{2,3},{3,2},{4,5},{5,4},{6,7},{7,6},{8,9},{9,8},{10,11... | collective-permute-start | bytes 6291464 | tf_op jit(solution)/shard_map/ppermute | solution.py:802
  6.3 40.0 %collective-permute-start.11 = (bf16[1024,1024]{1,0:T(8,128)(2,1)S(1)}, bf16[1024,1024]{1,0:T(8,128)(2,1)S(1)}, u32[]{:S(2)}, u32[]{:S(2)}) collective-permute-start(bf16[1024,1024]{1,0:T(8,128)(2,1)S(1)} %copy-done.2), channel_id=1, source_target_pairs={{0,1},{1,0},{2,3},{3,2},{4,5},{5,4},{6,7},{7,6},{8,9},{9,8},{10,11... | collective-permute-start | bytes 6291464 | tf_op jit(solution)/shard_map/ppermute | solution.py:802
  6.4 1.5 %copy-start.3 = (bf16[1024,256]{1,0:T(8,128)(2,1)S(1)}, bf16[1024,256]{1,0:T(8,128)(2,1)}, u32[]{:S(2)}) copy-start(bf16[1024,256]{1,0:T(8,128)(2,1)} %refs_3_.3) | copy-start | bytes 1572868
  6.4 1.5 %copy-start.4 = (f32[4,256]{1,0:T(4,128)S(1)}, f32[4,256]{1,0:T(4,128)}, u32[]{:S(2)}) copy-start(f32[4,256]{1,0:T(4,128)} %refs_4_.1) | copy-start | bytes 12292
  7.8 1.6 %copy-start = (bf16[1024,1024]{1,0:T(8,128)(2,1)S(1)}, bf16[1024,1024]{1,0:T(8,128)(2,1)}, u32[]{:S(2)}) copy-start(bf16[1024,1024]{1,0:T(8,128)(2,1)} %refs_5_.3) | copy-start | bytes 6291460
  13.7 6.6 %collective-permute-start.3 = (bf16[144,512]{1,0:T(8,128)(2,1)S(1)}, bf16[144,512]{1,0:T(8,128)(2,1)S(1)}, u32[]{:S(2)}, u32[]{:S(2)}) collective-permute-start(bf16[144,512]{1,0:T(8,128)(2,1)S(1)} %get-tuple-element.38), channel_id=1, source_target_pairs={{0,2},{2,0},{4,6},{6,4},{8,10},{10,8},{12,14},{14,12},{1,3},{3,1},... | collective-permute-start | bytes 442376 | tf_op jit(solution)/shard_map/ppermute | solution.py:561
  20.4 7.1 %collective-permute-start.4 = (bf16[144,512]{1,0:T(8,128)(2,1)S(1)}, bf16[144,512]{1,0:T(8,128)(2,1)S(1)}, u32[]{:S(2)}, u32[]{:S(2)}) collective-permute-start(bf16[144,512]{1,0:T(8,128)(2,1)S(1)} %pair_own.1.refs_5_.refs_1_), channel_id=1, source_target_pairs={{0,4},{1,0},{2,6},{3,2},{4,8},{5,1},{6,10},{7,3},{8,12},{9,5},{10,... | collective-permute-start | bytes 442376 | tf_op jit(solution)/shard_map/ppermute | solution.py:553
  22.8 6.9 %collective-permute-start.6 = (bf16[144,512]{1,0:T(8,128)(2,1)S(1)}, bf16[144,512]{1,0:T(8,128)(2,1)S(1)}, u32[]{:S(2)}, u32[]{:S(2)}) collective-permute-start(bf16[144,512]{1,0:T(8,128)(2,1)S(1)} %get-tuple-element.43), channel_id=1, source_target_pairs={{0,2},{2,0},{4,6},{6,4},{8,10},{10,8},{12,14},{14,12},{1,3},{3,1},... | collective-permute-start | bytes 442376 | tf_op jit(solution)/shard_map/ppermute | solution.py:561
  27.5 4.8 %collective-permute-start.5 = (bf16[144,512]{1,0:T(8,128)(2,1)S(1)}, bf16[144,512]{1,0:T(8,128)(2,1)S(1)}, u32[]{:S(2)}, u32[]{:S(2)}) collective-permute-start(bf16[144,512]{1,0:T(8,128)(2,1)S(1)} %chain_own.1.refs_3_), channel_id=1, source_target_pairs={{0,8},{1,0},{2,10},{3,2},{4,12},{5,4},{6,14},{7,6},{8,9},{9,1},{10... | collective-permute-start | bytes 442376 | tf_op jit(solution)/shard_map/ppermute | solution.py:553
  29.7 5.9 %collective-permute-start.7 = (bf16[144,512]{1,0:T(8,128)(2,1)S(1)}, bf16[144,512]{1,0:T(8,128)(2,1)S(1)}, u32[]{:S(2)}, u32[]{:S(2)}) collective-permute-start(bf16[144,512]{1,0:T(8,128)(2,1)S(1)} %pair_other.1.refs_5_.refs_1_), channel_id=1, source_target_pairs={{0,4},{1,0},{2,6},{3,2},{4,8},{5,1},{6,10},{7,3},{8,12},{9,5},{10,... | collective-permute-start | bytes 442376 | tf_op jit(solution)/shard_map/ppermute | solution.py:553
  35.8 6.2 %collective-permute-start.8 = (bf16[144,512]{1,0:T(8,128)(2,1)S(1)}, bf16[144,512]{1,0:T(8,128)(2,1)S(1)}, u32[]{:S(2)}, u32[]{:S(2)}) collective-permute-start(bf16[144,512]{1,0:T(8,128)(2,1)S(1)} %chain_other.1.refs_2_), channel_id=1, source_target_pairs={{0,8},{1,0},{2,10},{3,2},{4,12},{5,4},{6,14},{7,6},{8,9},{9,1},{10... | collective-permute-start | bytes 442376 | tf_op jit(solution)/shard_map/ppermute | solution.py:553
  39.3 5.0 %collective-permute-start.12 = (bf16[128,512]{1,0:T(8,128)(2,1)S(1)}, bf16[128,512]{1,0:T(8,128)(2,1)S(1)}, u32[]{:S(2)}, u32[]{:S(2)}) collective-permute-start(bf16[128,512]{1,0:T(8,128)(2,1)S(1)} %get-tuple-element.47), channel_id=1, source_target_pairs={{0,2},{2,0},{4,6},{6,4},{8,10},{10,8},{12,14},{14,12},{1,3},{3,1},... | collective-permute-start | bytes 393224 | tf_op jit(solution)/shard_map/ppermute | solution.py:627
  42.1 5.5 %collective-permute-start.10 = (bf16[128,512]{1,0:T(8,128)(2,1)S(1)}, bf16[128,512]{1,0:T(8,128)(2,1)S(1)}, u32[]{:S(2)}, u32[]{:S(2)}) collective-permute-start(bf16[128,512]{1,0:T(8,128)(2,1)S(1)} %get-tuple-element.46), channel_id=1, source_target_pairs={{0,2},{2,0},{4,6},{6,4},{8,10},{10,8},{12,14},{14,12},{1,3},{3,1},... | collective-permute-start | bytes 393224 | tf_op jit(solution)/shard_map/ppermute | solution.py:627
  49.1 2.0 %collective-permute-start.13 = (bf16[512,512]{1,0:T(8,128)(2,1)S(1)}, bf16[512,512]{1,0:T(8,128)(2,1)S(1)}, u32[]{:S(2)}, u32[]{:S(2)}) collective-permute-start(bf16[512,512]{1,0:T(8,128)(2,1)S(1)} %get-tuple-element.52.refs_5_), channel_id=1, source_target_pairs={{0,1},{1,0},{2,3},{3,2},{4,5},{5,4},{6,7},{7,6},{8,9},{9,8},{10,11... | collective-permute-start | bytes 1572872 | tf_op jit(solution)/shard_map/ppermute | solution.py:802

commit v7 on v6

--- a/solution.py
+++ b/solution.py
@@ -807,33 +807,34 @@
     back = core.reshape(1)
     parity = (index & 1).reshape(1)
     place = (index + core * (last - 2 * index)).reshape(1)
-    w_inner_2 = theirs(w_inner)
+    place, parity, w_inner_3, w_gate_3, w_output_3 = lax.optimization_barrier(
+        (place, parity, w_inner, w_gate, w_output)
+    )
+    w_inner_2 = theirs(w_inner_3)
     normed, tail, small = prepare_call(
         (back, parity, place), hidden, tokens, embedding, conv_inner, norm_gain, step_bias, decay_rate, w_step.T
     )
     halo = onward(tail, 1)
     small_2 = theirs(small)
-    w_gate_2 = theirs(w_gate)
-    w_output_2 = theirs(w_output)
-    gate_1 = gate_call("own", normed, w_gate)
-    bc, bt = maps_call(place, normed, halo, w_state, conv_state, after=[gate_1])
-    x_1, cum_1, times_1, send_1, mine_1 = local_call(
-        "own", place, parity, normed, halo, bt, w_inner, small
-    )
+    w_gate_2 = theirs(w_gate_3)
+    w_output_2 = theirs(w_output_3)
+    bc, bt = maps_call(place, normed, halo, w_state, conv_state)
+    x_1, cum_1, times_1, send_1, mine_1 = local_call("own", place, parity, normed, halo, bt, w_inner, small)
     chain_1 = Chain("own", place, send_1, mine_1)
     x_2, cum_2, times_2, send_2, mine_2 = local_call(
         "other", place, parity, normed, halo, bt, w_inner_2, small_2, after=[mine_1]
     )
     chain_2 = Chain("other", place, send_2, mine_2)
-    done = chain_1.pair(after=[x_2])
+    gate_2 = gate_call("other", normed, w_gate_2, after=[x_2])
+    done = chain_1.pair(after=[gate_2])
     y_1 = inside_call("own", x_1, bc, bt, cum_1, times_1, after=[done])
     done = chain_1.middle(after=[y_1])
     done = chain_2.pair(after=[done])
-    entry_1 = chain_1.entry(after=[done])
-    y_2 = inside_call("other", x_2, bc, bt, cum_2, times_2, after=[entry_1[0]])
-    done = chain_2.middle(after=[y_2])
-    gate_2 = gate_call("other", normed, w_gate_2, after=[done])
-    entry_2 = chain_2.entry(after=[gate_2])
+    y_2 = inside_call("other", x_2, bc, bt, cum_2, times_2, after=[done])
+    entry_1 = chain_1.entry(after=[y_2])
+    done = chain_2.middle(after=[entry_1[0]])
+    gate_1 = gate_call("own", normed, w_gate, after=[done])
+    entry_2 = chain_2.entry(after=[gate_1])
     partial = finish_call(
         back, parity, y_1, bc, cum_1, *entry_1, gate_1, small, w_output, after=[entry_2[0]]
     )

time: 52.8 us -> 53.5 us (1.013)
  waiting for transfers between devices: 5.27 us -> 5.84 us
    ppermute x5, starting transfers between devices: 11.6 us -> 14 us  [onward(): return lax.ppermute(value, ('seq', 'ch'), pairs)]
    ppermute x2, starting transfers between devices: 2.46 us -> 1.34 us  [entry(): return (keep, lax.ppermute(out, 'seq', self.swap))]
    ppermute x2, starting transfers between devices: 3.38 us -> 2.46 us  [__init__(): self.other = lax.ppermute(send, 'seq', self.swap)]
    ppermute x5, waiting for transfers between devices: 1.68 us -> 2.34 us  [onward(): return lax.ppermute(value, ('seq', 'ch'), pairs)]
  transfers between devices with their start and end apart: 14 -> 14, of which waited for: 5 -> 4; matrix products, arithmetic and copies ran while one was open for 0% -> 0% of each run, Pallas kernels for 48% -> 47%
where the time goes in v7:
time: 53.5 us; the launch traced here: 53.1 us
  Pallas kernels  27.3 us (51%)
  starting transfers between devices  18.9 us (35%)
  waiting for transfers between devices  5.84 us (11%)
  local copies, waits for them, and re-layouts  0.69 us (1%)
    pallas_call x18, Pallas kernels, call(): return lambda *arrays: run(*arrays, *after)  27.3 us
    ppermute x5, starting transfers between devices, onward(): return lax.ppermute(value, ('seq', 'ch'), pairs)  14 us
    ppermute x2, starting transfers between devices, __init__(): self.other = lax.ppermute(send, 'seq', self.swap)  2.46 us
    ppermute x2, waiting for transfers between devices, entry(): return (keep, lax.ppermute(out, 'seq', self.swap))  2.35 us
    ppermute x5, waiting for transfers between devices, onward(): return lax.ppermute(value, ('seq', 'ch'), pairs)  2.34 us
    ppermute x2, starting transfers between devices, entry(): return (keep, lax.ppermute(out, 'seq', self.swap))  1.34 us
    ppermute x5, waiting for transfers between devices, theirs(): return lax.ppermute(a, 'ch', swap)  1.15 us
    ppermute x5, starting transfers between devices, theirs(): return lax.ppermute(a, 'ch', swap)  1.09 us
  transfers between devices with their start and end apart: 14, of which 4 were waited for; matrix products, arithmetic and copies ran while one was open for 0% of the time, Pallas kernels for 47%

profile of v7, /device:TPU:0, one launch (start us, length us, event | category | flops | bytes accessed | tf_op | source)
XLA Modules:
  0.0 53.1 jit_solution(10201338336332139819)
XLA Ops:
  0.5 2.7 %prepare.1 = (bf16[512,1024]{1,0:T(8,128)(2,1)S(1)}, bf16[16,1024]{1,0:T(8,128)(2,1)S(1)}, f32[24,1024]{1,0:T(8,128)S(1)}) custom-call(s32[1]{0:T(128)} %bitcast.refs_0_, s32[1]{0:T(128)} %bitcast.2.refs_1_.refs_0_, s32[1]{0:T(128)} %bitcast.1.refs_2_.refs_0_, bf16[512,1024]{1,0:T(8,128)(2,1)} %refs_3_.2, s32[1,512]{1,0:T(1,128)} %bitcast.10, ...), custom_call_target="tpu_custom_call" | custom-call | flops 2969999872 | bytes 2700000 | tf_op jit(solution)/shard_map/prepare/pallas_call | solution.py:48
  3.2 3.0 %collective-permute-start = (bf16[16,1024]{1,0:T(8,128)(2,1)S(1)}, bf16[16,1024]{1,0:T(8,128)(2,1)S(1)}, u32[]{:S(2)}, u32[]{:S(2)}) collective-permute-start(bf16[16,1024]{1,0:T(8,128)(2,1)S(1)} %get-tuple-element.37), channel_id=1, source_target_pairs={{0,2},{1,0},{2,4},{3,1},{4,6},{5,3},{6,8},{7,5},{8,10},{9,7},{10,1... | collective-permute-start | bytes 98312 | tf_op jit(solution)/shard_map/ppermute | solution.py:553
  6.8 1.1 %collective-permute-done.refs_2_.refs_3_ = bf16[16,1024]{1,0:T(8,128)(2,1)S(1)} collective-permute-done((bf16[16,1024]{1,0:T(8,128)(2,1)S(1)}, bf16[16,1024]{1,0:T(8,128)(2,1)S(1)}, u32[]{:S(2)}, u32[]{:S(2)}) %collective-permute-start) | collective-permute-done | bytes 32800 | tf_op jit(solution)/shard_map/ppermute | solution.py:553
  7.9 0.9 %maps.1 = (bf16[512,256]{1,0:T(8,128)(2,1)S(1)}, bf16[128,512]{1,0:T(8,128)(2,1)S(1)}) custom-call(s32[1]{0:T(128)} %bitcast.1.refs_2_.refs_0_, bf16[512,1024]{1,0:T(8,128)(2,1)S(1)} %get-tuple-element.36.refs_1_.refs_2_.refs_0_, bf16[16,1024]{1,0:T(8,128)(2,1)S(1)} %collective-permute-done.refs_2_.refs_3_, bf16[1024,256]{1,0:T(8,128)(2,1)S(1)} %copy-done.3, ...), custom_call_target="tpu_custom_call" | custom-call | flops 1650000000 | bytes 1500000 | tf_op jit(solution)/shard_map/maps/pallas_call | solution.py:48
  8.8 0.7 %copy-done = bf16[1024,1024]{1,0:T(8,128)(2,1)S(1)} copy-done((bf16[1024,1024]{1,0:T(8,128)(2,1)S(1)}, bf16[1024,1024]{1,0:T(8,128)(2,1)}, u32[]{:S(2)}) %copy-start) | copy-done | bytes 2097176
  9.5 4.3 %local_own.1 = (bf16[512,1024]{1,0:T(8,128)(2,1)S(1)}, f32[512,16]{1,0:T(8,128)S(1)}, f32[32,512]{1,0:T(8,128)S(1)}, bf16[144,512]{1,0:T(8,128)(2,1)S(1)}, bf16[144,512]{1,0:T(8,128)(2,1)S(1)}) custom-call(s32[1]{0:T(128)} %bitcast.1.refs_2_.refs_0_, s32[1]{0:T(128)} %bitcast.2.refs_1_.refs_0_, ...), custom_call_target="tpu_custom_call" | custom-call | flops 5500000256 | bytes 5000000 | tf_op jit(solution)/shard_map/local_own/pallas_call | solution.py:48
  13.8 2.4 %collective-permute-start.4 = (bf16[144,512]{1,0:T(8,128)(2,1)S(1)}, bf16[144,512]{1,0:T(8,128)(2,1)S(1)}, u32[]{:S(2)}, u32[]{:S(2)}) collective-permute-start(bf16[144,512]{1,0:T(8,128)(2,1)S(1)} %get-tuple-element.48), channel_id=1, source_target_pairs={{0,2},{2,0},{4,6},{6,4},{8,10},{10,8},{12,14},{14,12},{1,3},{3,1},... | collective-permute-start | bytes 442376 | tf_op jit(solution)/shard_map/ppermute | solution.py:561
  16.2 4.3 %local_other.1 = (bf16[512,1024]{1,0:T(8,128)(2,1)S(1)}, f32[512,16]{1,0:T(8,128)S(1)}, f32[32,512]{1,0:T(8,128)S(1)}, bf16[144,512]{1,0:T(8,128)(2,1)S(1)}, bf16[144,512]{1,0:T(8,128)(2,1)S(1)}) custom-call(s32[1]{0:T(128)} %bitcast.1.refs_2_.refs_0_, s32[1]{0:T(128)} %bitcast.2.refs_1_.refs_0_, ...), custom_call_target="tpu_custom_call" | custom-call | flops 5500000256 | bytes 5000000 | tf_op jit(solution)/shard_map/local_other/pallas_call | solution.py:48
  20.6 1.4 %gate_other.1.refs_3_.refs_7_ = bf16[512,1024]{1,0:T(8,128)(2,1)S(1)} custom-call(bf16[512,1024]{1,0:T(8,128)(2,1)S(1)} %get-tuple-element.36.refs_1_.refs_2_.refs_0_, bf16[1024,1024]{1,0:T(8,128)(2,1)S(1)} %collective-permute-done.5.refs_1_, bf16[512,1024]{1,0:T(8,128)(2,1)S(1)} %get-tuple-element.42.refs_2_.refs_0_), custom_call_target="tpu_custom_call" | custom-call | flops 2640000000 | bytes 2400000 | tf_op jit(solution)/shard_map/gate_other/pallas_call | solution.py:48
  22.1 3.0 %collective-permute-start.6 = (bf16[144,512]{1,0:T(8,128)(2,1)S(1)}, bf16[144,512]{1,0:T(8,128)(2,1)S(1)}, u32[]{:S(2)}, u32[]{:S(2)}) collective-permute-start(bf16[144,512]{1,0:T(8,128)(2,1)S(1)} %pair_own.1.refs_5_.refs_1_), channel_id=1, source_target_pairs={{0,4},{1,0},{2,6},{3,2},{4,8},{5,1},{6,10},{7,3},{8,12},{9,5},{10,... | collective-permute-start | bytes 442376 | tf_op jit(solution)/shard_map/ppermute | solution.py:553
  25.1 3.3 %inside_own.1.refs_3_.refs_1_ = bf16[512,1024]{1,0:T(8,128)(2,1)S(1)} custom-call(bf16[512,1024]{1,0:T(8,128)(2,1)S(1)} %get-tuple-element.50.refs_0_, bf16[512,256]{1,0:T(8,128)(2,1)S(1)} %get-tuple-element.43.refs_1_.refs_2_.refs_3_, bf16[128,512]{1,0:T(8,128)(2,1)S(1)} %get-tuple-element.38.refs_4_.refs_2_, f32[512,16]{1,0:T(8,128)S(1)} %get-tuple-element.51.refs_3_, ...), custom_call_target="tpu_custom_call" | custom-call | flops 3520000000 | bytes 3200000 | tf_op jit(solution)/shard_map/inside_own/pallas_call | solution.py:48
  28.5 2.9 %collective-permute-start.8 = (bf16[144,512]{1,0:T(8,128)(2,1)S(1)}, bf16[144,512]{1,0:T(8,128)(2,1)S(1)}, u32[]{:S(2)}, u32[]{:S(2)}) collective-permute-start(bf16[144,512]{1,0:T(8,128)(2,1)S(1)} %chain_own.1.refs_3_), channel_id=1, source_target_pairs={{0,8},{1,0},{2,10},{3,2},{4,12},{5,4},{6,14},{7,6},{8,9},{9,1},{10... | collective-permute-start | bytes 442376 | tf_op jit(solution)/shard_map/ppermute | solution.py:553
  31.4 1.6 %collective-permute-start.7 = (bf16[144,512]{1,0:T(8,128)(2,1)S(1)}, bf16[144,512]{1,0:T(8,128)(2,1)S(1)}, u32[]{:S(2)}, u32[]{:S(2)}) collective-permute-start(bf16[144,512]{1,0:T(8,128)(2,1)S(1)} %pair_other.1.refs_5_.refs_1_), channel_id=1, source_target_pairs={{0,4},{1,0},{2,6},{3,2},{4,8},{5,1},{6,10},{7,3},{8,12},{9,5},{10,... | collective-permute-start | bytes 442376 | tf_op jit(solution)/shard_map/ppermute | solution.py:553
  33.0 3.2 %inside_other.1.refs_5_.refs_2_ = bf16[512,1024]{1,0:T(8,128)(2,1)S(1)} custom-call(bf16[512,1024]{1,0:T(8,128)(2,1)S(1)} %get-tuple-element.42.refs_2_.refs_0_, bf16[512,256]{1,0:T(8,128)(2,1)S(1)} %get-tuple-element.43.refs_1_.refs_2_.refs_3_, bf16[128,512]{1,0:T(8,128)(2,1)S(1)} %get-tuple-element.38.refs_4_.refs_2_, ...), custom_call_target="tpu_custom_call" | custom-call | flops 3520000000 | bytes 3200000 | tf_op jit(solution)/shard_map/inside_other/pallas_call | solution.py:48
  36.4 0.7 %collective-permute-start.12 = (bf16[128,512]{1,0:T(8,128)(2,1)S(1)}, bf16[128,512]{1,0:T(8,128)(2,1)S(1)}, u32[]{:S(2)}, u32[]{:S(2)}) collective-permute-start(bf16[128,512]{1,0:T(8,128)(2,1)S(1)} %get-tuple-element.57), channel_id=1, source_target_pairs={{0,2},{2,0},{4,6},{6,4},{8,10},{10,8},{12,14},{14,12},{1,3},{3,1},... | collective-permute-start | bytes 393224 | tf_op jit(solution)/shard_map/ppermute | solution.py:627
  37.1 3.6 %collective-permute-start.9 = (bf16[144,512]{1,0:T(8,128)(2,1)S(1)}, bf16[144,512]{1,0:T(8,128)(2,1)S(1)}, u32[]{:S(2)}, u32[]{:S(2)}) collective-permute-start(bf16[144,512]{1,0:T(8,128)(2,1)S(1)} %chain_other.1.refs_2_), channel_id=1, source_target_pairs={{0,8},{1,0},{2,10},{3,2},{4,12},{5,4},{6,14},{7,6},{8,9},{9,1},{10... | collective-permute-start | bytes 442376 | tf_op jit(solution)/shard_map/ppermute | solution.py:553
  40.7 1.4 %gate_own.1.refs_5_.refs_6_ = bf16[512,1024]{1,0:T(8,128)(2,1)S(1)} custom-call(bf16[512,1024]{1,0:T(8,128)(2,1)S(1)} %get-tuple-element.36.refs_1_.refs_2_.refs_0_, bf16[1024,1024]{1,0:T(8,128)(2,1)S(1)} %copy-done.1, bf16[144,512]{1,0:T(8,128)(2,1)S(1)} %chain_other.1.refs_2_), custom_call_target="tpu_custom_call" | custom-call | flops 2640000000 | bytes 2400000 | tf_op jit(solution)/shard_map/gate_own/pallas_call | solution.py:48
  42.1 1.2 %collective-permute-done.9.refs_4_ = bf16[144,512]{1,0:T(8,128)(2,1)S(1)} collective-permute-done((bf16[144,512]{1,0:T(8,128)(2,1)S(1)}, bf16[144,512]{1,0:T(8,128)(2,1)S(1)}, u32[]{:S(2)}, u32[]{:S(2)}) %collective-permute-start.9) | collective-permute-done | bytes 147488 | tf_op jit(solution)/shard_map/ppermute | solution.py:553
  44.2 2.0 %part.1 = (f32[512,1024]{1,0:T(8,128)S(1)}, f32[512,128]{1,0:T(8,128)S(1)}) custom-call(s32[1]{0:T(128)} %bitcast.2.refs_1_.refs_0_, bf16[512,1024]{1,0:T(8,128)(2,1)S(1)} %inside_own.1.refs_3_.refs_1_, bf16[512,256]{1,0:T(8,128)(2,1)S(1)} %get-tuple-element.43.refs_1_.refs_2_.refs_3_, f32[512,16]{1,0:T(8,128)S(1)} %get-tuple-element.51.refs_3_, ...), custom_call_target="tpu_custom_call" | custom-call | flops 3849999872 | bytes 3500000 | tf_op jit(solution)/shard_map/part/pallas_call | solution.py:48
  46.2 2.3 %collective-permute-done.10.refs_6_ = bf16[128,512]{1,0:T(8,128)(2,1)S(1)} collective-permute-done((bf16[128,512]{1,0:T(8,128)(2,1)S(1)}, bf16[128,512]{1,0:T(8,128)(2,1)S(1)}, u32[]{:S(2)}, u32[]{:S(2)}) %collective-permute-start.10) | collective-permute-done | bytes 131104 | tf_op jit(solution)/shard_map/ppermute | solution.py:627
  48.6 1.5 %finish.1 = (bf16[512,512]{1,0:T(8,128)(2,1)S(1)}, bf16[512,1024]{1,0:T(8,128)(2,1)S(1)}, f32[512,128]{1,0:T(8,128)S(1)}) custom-call(s32[1]{0:T(128)} %bitcast.refs_0_, s32[1]{0:T(128)} %bitcast.2.refs_1_.refs_0_, bf16[512,1024]{1,0:T(8,128)(2,1)S(1)} %inside_other.1.refs_5_.refs_2_, bf16[512,256]{1,0:T(8,128)(2,1)S(1)} %get-tuple-element.43.refs_1_.refs_2_.refs_3_, ...), custom_call_target="tpu_custom_call" | custom-call | flops 3849999872 | bytes 3500000 | tf_op jit(solution)/shard_map/finish/pallas_call | solution.py:48
  50.2 0.7 %own_half.1.refs_0_ = bf16[512,512]{1,0:T(8,128)(2,1)S(1)} custom-call(s32[1]{0:T(128)} %bitcast.refs_0_, bf16[512,1024]{1,0:T(8,128)(2,1)S(1)} %get-tuple-element.60.refs_1_, bf16[1024,1024]{1,0:T(8,128)(2,1)S(1)} %collective-permute-done.11.refs_9_.refs_2_, f32[512,1024]{1,0:T(8,128)S(1)} %get-tuple-element.58.refs_10_.refs_3_, ...), custom_call_target="tpu_custom_call" | custom-call | flops 770000000 | bytes 700000 | tf_op jit(solution)/shard_map/own_half/pallas_call | solution.py:48
  50.9 1.1 %collective-permute-done.13.refs_1_ = bf16[512,512]{1,0:T(8,128)(2,1)S(1)} collective-permute-done((bf16[512,512]{1,0:T(8,128)(2,1)S(1)}, bf16[512,512]{1,0:T(8,128)(2,1)S(1)}, u32[]{:S(2)}, u32[]{:S(2)}) %collective-permute-start.13) | collective-permute-done | bytes 524320 | tf_op jit(solution)/shard_map/ppermute | solution.py:802
  52.1 0.8 %total.1 = bf16[512,512]{1,0:T(8,128)(2,1)} custom-call(bf16[512,512]{1,0:T(8,128)(2,1)S(1)} %own_half.1.refs_0_, bf16[512,512]{1,0:T(8,128)(2,1)S(1)} %collective-permute-done.13.refs_1_), custom_call_target="tpu_custom_call" | custom-call | flops 880000000 | bytes 800000 | tf_op jit(solution)/shard_map/total/pallas_call | solution.py:48
  (32 shorter events, 2.4 us)
Async XLA Ops:
  0.0 16.2 %collective-permute-start.1 = (bf16[1024,1024]{1,0:T(8,128)(2,1)}, bf16[1024,1024]{1,0:T(8,128)(2,1)S(1)}, u32[]{:S(2)}, u32[]{:S(2)}) collective-permute-start(bf16[1024,1024]{1,0:T(8,128)(2,1)} %refs_5_.3), channel_id=1, source_target_pairs={{0,1},{1,0},{2,3},{3,2},{4,5},{5,4},{6,7},{7,6},{8,9},{9,8},{10,11... | collective-permute-start | bytes 6291464 | tf_op jit(solution)/shard_map/ppermute | solution.py:802
  0.5 20.1 %collective-permute-start.5 = (bf16[1024,1024]{1,0:T(8,128)(2,1)}, bf16[1024,1024]{1,0:T(8,128)(2,1)S(1)}, u32[]{:S(2)}, u32[]{:S(2)}) collective-permute-start(bf16[1024,1024]{1,0:T(8,128)(2,1)} %refs_1_.1), channel_id=1, source_target_pairs={{0,1},{1,0},{2,3},{3,2},{4,5},{5,4},{6,7},{7,6},{8,9},{9,8},{10,11... | collective-permute-start | bytes 6291464 | tf_op jit(solution)/shard_map/ppermute | solution.py:802
  0.5 5.8 %copy-start.2 = (bf16[1024,1024]{1,0:T(8,128)(2,1)S(1)}, bf16[1024,1024]{1,0:T(8,128)(2,1)}, u32[]{:S(2)}) copy-start(bf16[1024,1024]{1,0:T(8,128)(2,1)} %refs_8_.1) | copy-start | bytes 6291460
  0.5 7.4 %copy-start.3 = (bf16[1024,256]{1,0:T(8,128)(2,1)S(1)}, bf16[1024,256]{1,0:T(8,128)(2,1)}, u32[]{:S(2)}) copy-start(bf16[1024,256]{1,0:T(8,128)(2,1)} %refs_3_.3) | copy-start | bytes 1572868
  0.5 7.4 %copy-start.4 = (f32[4,256]{1,0:T(4,128)S(1)}, f32[4,256]{1,0:T(4,128)}, u32[]{:S(2)}) copy-start(f32[4,256]{1,0:T(4,128)} %refs_4_.1) | copy-start | bytes 12292
  3.2 4.6 %collective-permute-start = (bf16[16,1024]{1,0:T(8,128)(2,1)S(1)}, bf16[16,1024]{1,0:T(8,128)(2,1)S(1)}, u32[]{:S(2)}, u32[]{:S(2)}) collective-permute-start(bf16[16,1024]{1,0:T(8,128)(2,1)S(1)} %get-tuple-element.37), channel_id=1, source_target_pairs={{0,2},{1,0},{2,4},{3,1},{4,6},{5,3},{6,8},{7,5},{8,10},{9,7},{10,1... | collective-permute-start | bytes 98312 | tf_op jit(solution)/shard_map/ppermute | solution.py:553
  6.3 9.9 %collective-permute-start.2 = (f32[24,1024]{1,0:T(8,128)S(1)}, f32[24,1024]{1,0:T(8,128)S(1)}, u32[]{:S(2)}, u32[]{:S(2)}) collective-permute-start(f32[24,1024]{1,0:T(8,128)S(1)} %get-tuple-element.40.refs_6_.refs_7_), channel_id=1, source_target_pairs={{0,1},{1,0},{2,3},{3,2},{4,5},{5,4},{6,7},{7,6},{8,9},{9,8},{10,11... | collective-permute-start | bytes 294920 | tf_op jit(solution)/shard_map/ppermute | solution.py:802
  6.3 39.9 %collective-permute-start.11 = (bf16[1024,1024]{1,0:T(8,128)(2,1)S(1)}, bf16[1024,1024]{1,0:T(8,128)(2,1)S(1)}, u32[]{:S(2)}, u32[]{:S(2)}) collective-permute-start(bf16[1024,1024]{1,0:T(8,128)(2,1)S(1)} %copy-done.2), channel_id=1, source_target_pairs={{0,1},{1,0},{2,3},{3,2},{4,5},{5,4},{6,7},{7,6},{8,9},{9,8},{10,11... | collective-permute-start | bytes 6291464 | tf_op jit(solution)/shard_map/ppermute | solution.py:802
  7.9 1.6 %copy-start = (bf16[1024,1024]{1,0:T(8,128)(2,1)S(1)}, bf16[1024,1024]{1,0:T(8,128)(2,1)}, u32[]{:S(2)}) copy-start(bf16[1024,1024]{1,0:T(8,128)(2,1)} %refs_5_.3) | copy-start | bytes 6291460
  13.8 8.2 %collective-permute-start.4 = (bf16[144,512]{1,0:T(8,128)(2,1)S(1)}, bf16[144,512]{1,0:T(8,128)(2,1)S(1)}, u32[]{:S(2)}, u32[]{:S(2)}) collective-permute-start(bf16[144,512]{1,0:T(8,128)(2,1)S(1)} %get-tuple-element.48), channel_id=1, source_target_pairs={{0,2},{2,0},{4,6},{6,4},{8,10},{10,8},{12,14},{14,12},{1,3},{3,1},... | collective-permute-start | bytes 442376 | tf_op jit(solution)/shard_map/ppermute | solution.py:561
  20.5 10.9 %collective-permute-start.3 = (bf16[144,512]{1,0:T(8,128)(2,1)S(1)}, bf16[144,512]{1,0:T(8,128)(2,1)S(1)}, u32[]{:S(2)}, u32[]{:S(2)}) collective-permute-start(bf16[144,512]{1,0:T(8,128)(2,1)S(1)} %get-tuple-element.47), channel_id=1, source_target_pairs={{0,2},{2,0},{4,6},{6,4},{8,10},{10,8},{12,14},{14,12},{1,3},{3,1},... | collective-permute-start | bytes 442376 | tf_op jit(solution)/shard_map/ppermute | solution.py:561
  22.1 6.3 %collective-permute-start.6 = (bf16[144,512]{1,0:T(8,128)(2,1)S(1)}, bf16[144,512]{1,0:T(8,128)(2,1)S(1)}, u32[]{:S(2)}, u32[]{:S(2)}) collective-permute-start(bf16[144,512]{1,0:T(8,128)(2,1)S(1)} %pair_own.1.refs_5_.refs_1_), channel_id=1, source_target_pairs={{0,4},{1,0},{2,6},{3,2},{4,8},{5,1},{6,10},{7,3},{8,12},{9,5},{10,... | collective-permute-start | bytes 442376 | tf_op jit(solution)/shard_map/ppermute | solution.py:553
  28.5 7.7 %collective-permute-start.8 = (bf16[144,512]{1,0:T(8,128)(2,1)S(1)}, bf16[144,512]{1,0:T(8,128)(2,1)S(1)}, u32[]{:S(2)}, u32[]{:S(2)}) collective-permute-start(bf16[144,512]{1,0:T(8,128)(2,1)S(1)} %chain_own.1.refs_3_), channel_id=1, source_target_pairs={{0,8},{1,0},{2,10},{3,2},{4,12},{5,4},{6,14},{7,6},{8,9},{9,1},{10... | collective-permute-start | bytes 442376 | tf_op jit(solution)/shard_map/ppermute | solution.py:553
  31.4 5.6 %collective-permute-start.7 = (bf16[144,512]{1,0:T(8,128)(2,1)S(1)}, bf16[144,512]{1,0:T(8,128)(2,1)S(1)}, u32[]{:S(2)}, u32[]{:S(2)}) collective-permute-start(bf16[144,512]{1,0:T(8,128)(2,1)S(1)} %pair_other.1.refs_5_.refs_1_), channel_id=1, source_target_pairs={{0,4},{1,0},{2,6},{3,2},{4,8},{5,1},{6,10},{7,3},{8,12},{9,5},{10,... | collective-permute-start | bytes 442376 | tf_op jit(solution)/shard_map/ppermute | solution.py:553
  36.2 4.5 %copy-start.1 = (bf16[1024,1024]{1,0:T(8,128)(2,1)S(1)}, bf16[1024,1024]{1,0:T(8,128)(2,1)}, u32[]{:S(2)}) copy-start(bf16[1024,1024]{1,0:T(8,128)(2,1)} %refs_1_.1) | copy-start | bytes 6291460
  36.4 7.8 %collective-permute-start.12 = (bf16[128,512]{1,0:T(8,128)(2,1)S(1)}, bf16[128,512]{1,0:T(8,128)(2,1)S(1)}, u32[]{:S(2)}, u32[]{:S(2)}) collective-permute-start(bf16[128,512]{1,0:T(8,128)(2,1)S(1)} %get-tuple-element.57), channel_id=1, source_target_pairs={{0,2},{2,0},{4,6},{6,4},{8,10},{10,8},{12,14},{14,12},{1,3},{3,1},... | collective-permute-start | bytes 393224 | tf_op jit(solution)/shard_map/ppermute | solution.py:627
  37.1 6.3 %collective-permute-start.9 = (bf16[144,512]{1,0:T(8,128)(2,1)S(1)}, bf16[144,512]{1,0:T(8,128)(2,1)S(1)}, u32[]{:S(2)}, u32[]{:S(2)}) collective-permute-start(bf16[144,512]{1,0:T(8,128)(2,1)S(1)} %chain_other.1.refs_2_), channel_id=1, source_target_pairs={{0,8},{1,0},{2,10},{3,2},{4,12},{5,4},{6,14},{7,6},{8,9},{9,1},{10... | collective-permute-start | bytes 442376 | tf_op jit(solution)/shard_map/ppermute | solution.py:553
  43.5 5.0 %collective-permute-start.10 = (bf16[128,512]{1,0:T(8,128)(2,1)S(1)}, bf16[128,512]{1,0:T(8,128)(2,1)S(1)}, u32[]{:S(2)}, u32[]{:S(2)}) collective-permute-start(bf16[128,512]{1,0:T(8,128)(2,1)S(1)} %get-tuple-element.55), channel_id=1, source_target_pairs={{0,2},{2,0},{4,6},{6,4},{8,10},{10,8},{12,14},{14,12},{1,3},{3,1},... | collective-permute-start | bytes 393224 | tf_op jit(solution)/shard_map/ppermute | solution.py:627
  50.1 2.0 %collective-permute-start.13 = (bf16[512,512]{1,0:T(8,128)(2,1)S(1)}, bf16[512,512]{1,0:T(8,128)(2,1)S(1)}, u32[]{:S(2)}, u32[]{:S(2)}) collective-permute-start(bf16[512,512]{1,0:T(8,128)(2,1)S(1)} %get-tuple-element.62.refs_5_), channel_id=1, source_target_pairs={{0,1},{1,0},{2,3},{3,2},{4,5},{5,4},{6,7},{7,6},{8,9},{9,8},{10,11... | collective-permute-start | bytes 1572872 | tf_op jit(solution)/shard_map/ppermute | solution.py:802

commit v8 on v7

--- a/solution.py
+++ b/solution.py
@@ -818,7 +818,8 @@
     small_2 = theirs(small)
     w_gate_2 = theirs(w_gate_3)
     w_output_2 = theirs(w_output_3)
-    bc, bt = maps_call(place, normed, halo, w_state, conv_state)
+    gate_1 = gate_call("own", normed, w_gate)
+    bc, bt = maps_call(place, normed, halo, w_state, conv_state, after=[gate_1])
     x_1, cum_1, times_1, send_1, mine_1 = local_call("own", place, parity, normed, halo, bt, w_inner, small)
     chain_1 = Chain("own", place, send_1, mine_1)
     x_2, cum_2, times_2, send_2, mine_2 = local_call(
@@ -830,13 +831,12 @@
     y_1 = inside_call("own", x_1, bc, bt, cum_1, times_1, after=[done])
     done = chain_1.middle(after=[y_1])
     done = chain_2.pair(after=[done])
-    y_2 = inside_call("other", x_2, bc, bt, cum_2, times_2, after=[done])
-    entry_1 = chain_1.entry(after=[y_2])
+    entry_1 = chain_1.entry(after=[done])
     done = chain_2.middle(after=[entry_1[0]])
-    gate_1 = gate_call("own", normed, w_gate, after=[done])
-    entry_2 = chain_2.entry(after=[gate_1])
+    entry_2 = chain_2.entry(after=[done])
+    y_2 = inside_call("other", x_2, bc, bt, cum_2, times_2, after=[entry_2[0]])
     partial = finish_call(
-        back, parity, y_1, bc, cum_1, *entry_1, gate_1, small, w_output, after=[entry_2[0]]
+        back, parity, y_1, bc, cum_1, *entry_1, gate_1, small, w_output, after=[y_2]
     )
     full_width = float(w_inner.shape[1] * lax.axis_size("ch"))
     send, scaled, scale = finish_call(

time: 53.5 us -> 53.7 us (level)
  starting transfers between devices: 18.9 us -> 19.6 us
    ppermute x2, waiting for transfers between devices: 2.35 us -> 0.01 us  [entry(): return (keep, lax.ppermute(out, 'seq', self.swap))]
    ppermute x5, waiting for transfers between devices: 2.34 us -> 4.45 us  [onward(): return lax.ppermute(value, ('seq', 'ch'), pairs)]
    ppermute x5, starting transfers between devices: 14 us -> 14.7 us  [onward(): return lax.ppermute(value, ('seq', 'ch'), pairs)]
where the time goes in v8:
time: 53.7 us; the launch traced here: 53.5 us
  Pallas kernels  27.4 us (51%)
  starting transfers between devices  19.6 us (36%)
  waiting for transfers between devices  5.61 us (10%)
  local copies, waits for them, and re-layouts  0.65 us (1%)
    pallas_call x18, Pallas kernels, call(): return lambda *arrays: run(*arrays, *after)  27.4 us
    ppermute x5, starting transfers between devices, onward(): return lax.ppermute(value, ('seq', 'ch'), pairs)  14.7 us
    ppermute x5, waiting for transfers between devices, onward(): return lax.ppermute(value, ('seq', 'ch'), pairs)  4.45 us
    ppermute x2, starting transfers between devices, __init__(): self.other = lax.ppermute(send, 'seq', self.swap)  2.14 us
    ppermute x2, starting transfers between devices, entry(): return (keep, lax.ppermute(out, 'seq', self.swap))  1.68 us
    ppermute x5, waiting for transfers between devices, theirs(): return lax.ppermute(a, 'ch', swap)  1.15 us
    ppermute x5, starting transfers between devices, theirs(): return lax.ppermute(a, 'ch', swap)  1.09 us
  transfers between devices with their start and end apart: 14, of which 4 were waited for; matrix products, arithmetic and copies ran while one was open for 0% of the time, Pallas kernels for 47%

profile of v8, /device:TPU:0, one launch (start us, length us, event | category | flops | bytes accessed | tf_op | source)
XLA Modules:
  0.0 53.5 jit_solution(4428494000518298111)
XLA Ops:
  0.5 2.7 %prepare.1 = (bf16[512,1024]{1,0:T(8,128)(2,1)S(1)}, bf16[16,1024]{1,0:T(8,128)(2,1)S(1)}, f32[24,1024]{1,0:T(8,128)S(1)}) custom-call(s32[1]{0:T(128)} %bitcast.refs_0_, s32[1]{0:T(128)} %bitcast.2.refs_1_.refs_0_, s32[1]{0:T(128)} %bitcast.1.refs_2_.refs_0_, bf16[512,1024]{1,0:T(8,128)(2,1)} %refs_3_.2, s32[1,512]{1,0:T(1,128)} %bitcast.10, ...), custom_call_target="tpu_custom_call" | custom-call | flops 2969999872 | bytes 2700000 | tf_op jit(solution)/shard_map/prepare/pallas_call | solution.py:48
  3.2 3.0 %collective-permute-start = (bf16[16,1024]{1,0:T(8,128)(2,1)S(1)}, bf16[16,1024]{1,0:T(8,128)(2,1)S(1)}, u32[]{:S(2)}, u32[]{:S(2)}) collective-permute-start(bf16[16,1024]{1,0:T(8,128)(2,1)S(1)} %get-tuple-element.37), channel_id=1, source_target_pairs={{0,2},{1,0},{2,4},{3,1},{4,6},{5,3},{6,8},{7,5},{8,10},{9,7},{10,1... | collective-permute-start | bytes 98312 | tf_op jit(solution)/shard_map/ppermute | solution.py:553
  6.8 1.4 %gate_own.1.refs_5_.refs_6_ = bf16[512,1024]{1,0:T(8,128)(2,1)S(1)} custom-call(bf16[512,1024]{1,0:T(8,128)(2,1)S(1)} %get-tuple-element.36.refs_0_.refs_1_.refs_2_, bf16[1024,1024]{1,0:T(8,128)(2,1)S(1)} %copy-done.1), custom_call_target="tpu_custom_call" | custom-call | flops 2640000000 | bytes 2400000 | tf_op jit(solution)/shard_map/gate_own/pallas_call | solution.py:48
  8.3 0.9 %maps.1 = (bf16[512,256]{1,0:T(8,128)(2,1)S(1)}, bf16[128,512]{1,0:T(8,128)(2,1)S(1)}) custom-call(s32[1]{0:T(128)} %bitcast.1.refs_2_.refs_0_, bf16[512,1024]{1,0:T(8,128)(2,1)S(1)} %get-tuple-element.36.refs_0_.refs_1_.refs_2_, bf16[16,1024]{1,0:T(8,128)(2,1)S(1)} %collective-permute-done.refs_2_.refs_3_, bf16[1024,256]{1,0:T(8,128)(2,1)S(1)} %copy-done.3, ...), custom_call_target="tpu_custom_call" | custom-call | flops 1650000000 | bytes 1500000 | tf_op jit(solution)/shard_map/maps/pallas_call | solution.py:48
  9.8 4.3 %local_own.1 = (bf16[512,1024]{1,0:T(8,128)(2,1)S(1)}, f32[512,16]{1,0:T(8,128)S(1)}, f32[32,512]{1,0:T(8,128)S(1)}, bf16[144,512]{1,0:T(8,128)(2,1)S(1)}, bf16[144,512]{1,0:T(8,128)(2,1)S(1)}) custom-call(s32[1]{0:T(128)} %bitcast.1.refs_2_.refs_0_, s32[1]{0:T(128)} %bitcast.2.refs_1_.refs_0_, ...), custom_call_target="tpu_custom_call" | custom-call | flops 5500000256 | bytes 5000000 | tf_op jit(solution)/shard_map/local_own/pallas_call | solution.py:48
  14.2 1.6 %collective-permute-start.4 = (bf16[144,512]{1,0:T(8,128)(2,1)S(1)}, bf16[144,512]{1,0:T(8,128)(2,1)S(1)}, u32[]{:S(2)}, u32[]{:S(2)}) collective-permute-start(bf16[144,512]{1,0:T(8,128)(2,1)S(1)} %get-tuple-element.48), channel_id=1, source_target_pairs={{0,2},{2,0},{4,6},{6,4},{8,10},{10,8},{12,14},{14,12},{1,3},{3,1},... | collective-permute-start | bytes 442376 | tf_op jit(solution)/shard_map/ppermute | solution.py:561
  15.7 4.3 %local_other.1 = (bf16[512,1024]{1,0:T(8,128)(2,1)S(1)}, f32[512,16]{1,0:T(8,128)S(1)}, f32[32,512]{1,0:T(8,128)S(1)}, bf16[144,512]{1,0:T(8,128)(2,1)S(1)}, bf16[144,512]{1,0:T(8,128)(2,1)S(1)}) custom-call(s32[1]{0:T(128)} %bitcast.1.refs_2_.refs_0_, s32[1]{0:T(128)} %bitcast.2.refs_1_.refs_0_, ...), custom_call_target="tpu_custom_call" | custom-call | flops 5500000256 | bytes 5000000 | tf_op jit(solution)/shard_map/local_other/pallas_call | solution.py:48
  20.6 1.4 %gate_other.1.refs_3_.refs_7_ = bf16[512,1024]{1,0:T(8,128)(2,1)S(1)} custom-call(bf16[512,1024]{1,0:T(8,128)(2,1)S(1)} %get-tuple-element.36.refs_0_.refs_1_.refs_2_, bf16[1024,1024]{1,0:T(8,128)(2,1)S(1)} %collective-permute-done.5.refs_1_, bf16[512,1024]{1,0:T(8,128)(2,1)S(1)} %get-tuple-element.42.refs_2_.refs_0_), custom_call_target="tpu_custom_call" | custom-call | flops 2640000000 | bytes 2400000 | tf_op jit(solution)/shard_map/gate_other/pallas_call | solution.py:48
  22.2 2.3 %collective-permute-start.6 = (bf16[144,512]{1,0:T(8,128)(2,1)S(1)}, bf16[144,512]{1,0:T(8,128)(2,1)S(1)}, u32[]{:S(2)}, u32[]{:S(2)}) collective-permute-start(bf16[144,512]{1,0:T(8,128)(2,1)S(1)} %pair_own.1.refs_5_.refs_1_), channel_id=1, source_target_pairs={{0,4},{1,0},{2,6},{3,2},{4,8},{5,1},{6,10},{7,3},{8,12},{9,5},{10,... | collective-permute-start | bytes 442376 | tf_op jit(solution)/shard_map/ppermute | solution.py:553
  24.5 3.4 %inside_own.1.refs_3_.refs_1_ = bf16[512,1024]{1,0:T(8,128)(2,1)S(1)} custom-call(bf16[512,1024]{1,0:T(8,128)(2,1)S(1)} %get-tuple-element.50.refs_0_, bf16[512,256]{1,0:T(8,128)(2,1)S(1)} %get-tuple-element.43.refs_1_.refs_2_.refs_3_, bf16[128,512]{1,0:T(8,128)(2,1)S(1)} %get-tuple-element.38.refs_4_.refs_2_, f32[512,16]{1,0:T(8,128)S(1)} %get-tuple-element.51.refs_3_, ...), custom_call_target="tpu_custom_call" | custom-call | flops 3520000000 | bytes 3200000 | tf_op jit(solution)/shard_map/inside_own/pallas_call | solution.py:48
  28.0 2.8 %collective-permute-start.8 = (bf16[144,512]{1,0:T(8,128)(2,1)S(1)}, bf16[144,512]{1,0:T(8,128)(2,1)S(1)}, u32[]{:S(2)}, u32[]{:S(2)}) collective-permute-start(bf16[144,512]{1,0:T(8,128)(2,1)S(1)} %chain_own.1.refs_3_), channel_id=1, source_target_pairs={{0,8},{1,0},{2,10},{3,2},{4,12},{5,4},{6,14},{7,6},{8,9},{9,1},{10... | collective-permute-start | bytes 442376 | tf_op jit(solution)/shard_map/ppermute | solution.py:553
  30.9 1.6 %collective-permute-start.7 = (bf16[144,512]{1,0:T(8,128)(2,1)S(1)}, bf16[144,512]{1,0:T(8,128)(2,1)S(1)}, u32[]{:S(2)}, u32[]{:S(2)}) collective-permute-start(bf16[144,512]{1,0:T(8,128)(2,1)S(1)} %pair_other.1.refs_5_.refs_1_), channel_id=1, source_target_pairs={{0,4},{1,0},{2,6},{3,2},{4,8},{5,1},{6,10},{7,3},{8,12},{9,5},{10,... | collective-permute-start | bytes 442376 | tf_op jit(solution)/shard_map/ppermute | solution.py:553
  32.4 1.0 %collective-permute-done.8.refs_4_ = bf16[144,512]{1,0:T(8,128)(2,1)S(1)} collective-permute-done((bf16[144,512]{1,0:T(8,128)(2,1)S(1)}, bf16[144,512]{1,0:T(8,128)(2,1)S(1)}, u32[]{:S(2)}, u32[]{:S(2)}) %collective-permute-start.8) | collective-permute-done | bytes 147488 | tf_op jit(solution)/shard_map/ppermute | solution.py:553
  33.6 1.5 %collective-permute-done.7.refs_2_.refs_3_ = bf16[144,512]{1,0:T(8,128)(2,1)S(1)} collective-permute-done((bf16[144,512]{1,0:T(8,128)(2,1)S(1)}, bf16[144,512]{1,0:T(8,128)(2,1)S(1)}, u32[]{:S(2)}, u32[]{:S(2)}) %collective-permute-start.7) | collective-permute-done | bytes 147488 | tf_op jit(solution)/shard_map/ppermute | solution.py:553
  35.2 4.9 %collective-permute-start.9 = (bf16[144,512]{1,0:T(8,128)(2,1)S(1)}, bf16[144,512]{1,0:T(8,128)(2,1)S(1)}, u32[]{:S(2)}, u32[]{:S(2)}) collective-permute-start(bf16[144,512]{1,0:T(8,128)(2,1)S(1)} %chain_other.1.refs_5_), channel_id=1, source_target_pairs={{0,8},{1,0},{2,10},{3,2},{4,12},{5,4},{6,14},{7,6},{8,9},{9,1},{10... | collective-permute-start | bytes 442376 | tf_op jit(solution)/shard_map/ppermute | solution.py:553
  40.1 0.8 %collective-permute-start.12 = (bf16[128,512]{1,0:T(8,128)(2,1)S(1)}, bf16[128,512]{1,0:T(8,128)(2,1)S(1)}, u32[]{:S(2)}, u32[]{:S(2)}) collective-permute-start(bf16[128,512]{1,0:T(8,128)(2,1)S(1)} %get-tuple-element.57), channel_id=1, source_target_pairs={{0,2},{2,0},{4,6},{6,4},{8,10},{10,8},{12,14},{14,12},{1,3},{3,1},... | collective-permute-start | bytes 393224 | tf_op jit(solution)/shard_map/ppermute | solution.py:627
  40.9 1.9 %collective-permute-done.9.refs_4_ = bf16[144,512]{1,0:T(8,128)(2,1)S(1)} collective-permute-done((bf16[144,512]{1,0:T(8,128)(2,1)S(1)}, bf16[144,512]{1,0:T(8,128)(2,1)S(1)}, u32[]{:S(2)}, u32[]{:S(2)}) %collective-permute-start.9) | collective-permute-done | bytes 147488 | tf_op jit(solution)/shard_map/ppermute | solution.py:553
  43.0 0.9 %collective-permute-start.10 = (bf16[128,512]{1,0:T(8,128)(2,1)S(1)}, bf16[128,512]{1,0:T(8,128)(2,1)S(1)}, u32[]{:S(2)}, u32[]{:S(2)}) collective-permute-start(bf16[128,512]{1,0:T(8,128)(2,1)S(1)} %get-tuple-element.55), channel_id=1, source_target_pairs={{0,2},{2,0},{4,6},{6,4},{8,10},{10,8},{12,14},{14,12},{1,3},{3,1},... | collective-permute-start | bytes 393224 | tf_op jit(solution)/shard_map/ppermute | solution.py:627
  43.8 3.2 %inside_other.1.refs_9_.refs_2_ = bf16[512,1024]{1,0:T(8,128)(2,1)S(1)} custom-call(bf16[512,1024]{1,0:T(8,128)(2,1)S(1)} %get-tuple-element.42.refs_2_.refs_0_, bf16[512,256]{1,0:T(8,128)(2,1)S(1)} %get-tuple-element.43.refs_1_.refs_2_.refs_3_, bf16[128,512]{1,0:T(8,128)(2,1)S(1)} %get-tuple-element.38.refs_4_.refs_2_, ...), custom_call_target="tpu_custom_call" | custom-call | flops 3520000000 | bytes 3200000 | tf_op jit(solution)/shard_map/inside_other/pallas_call | solution.py:48
  47.0 2.0 %part.1 = (f32[512,1024]{1,0:T(8,128)S(1)}, f32[512,128]{1,0:T(8,128)S(1)}) custom-call(s32[1]{0:T(128)} %bitcast.2.refs_1_.refs_0_, bf16[512,1024]{1,0:T(8,128)(2,1)S(1)} %inside_own.1.refs_3_.refs_1_, bf16[512,256]{1,0:T(8,128)(2,1)S(1)} %get-tuple-element.43.refs_1_.refs_2_.refs_3_, f32[512,16]{1,0:T(8,128)S(1)} %get-tuple-element.51.refs_3_, ...), custom_call_target="tpu_custom_call" | custom-call | flops 3849999872 | bytes 3500000 | tf_op jit(solution)/shard_map/part/pallas_call | solution.py:48
  49.1 1.5 %finish.1 = (bf16[512,512]{1,0:T(8,128)(2,1)S(1)}, bf16[512,1024]{1,0:T(8,128)(2,1)S(1)}, f32[512,128]{1,0:T(8,128)S(1)}) custom-call(s32[1]{0:T(128)} %bitcast.refs_0_, s32[1]{0:T(128)} %bitcast.2.refs_1_.refs_0_, bf16[512,1024]{1,0:T(8,128)(2,1)S(1)} %inside_other.1.refs_9_.refs_2_, bf16[512,256]{1,0:T(8,128)(2,1)S(1)} %get-tuple-element.43.refs_1_.refs_2_.refs_3_, ...), custom_call_target="tpu_custom_call" | custom-call | flops 3849999872 | bytes 3500000 | tf_op jit(solution)/shard_map/finish/pallas_call | solution.py:48
  50.6 0.7 %own_half.1.refs_0_ = bf16[512,512]{1,0:T(8,128)(2,1)S(1)} custom-call(s32[1]{0:T(128)} %bitcast.refs_0_, bf16[512,1024]{1,0:T(8,128)(2,1)S(1)} %get-tuple-element.60.refs_1_, bf16[1024,1024]{1,0:T(8,128)(2,1)S(1)} %collective-permute-done.11.refs_9_.refs_2_, f32[512,1024]{1,0:T(8,128)S(1)} %get-tuple-element.58.refs_10_.refs_3_, ...), custom_call_target="tpu_custom_call" | custom-call | flops 770000000 | bytes 700000 | tf_op jit(solution)/shard_map/own_half/pallas_call | solution.py:48
  51.4 1.1 %collective-permute-done.13.refs_1_ = bf16[512,512]{1,0:T(8,128)(2,1)S(1)} collective-permute-done((bf16[512,512]{1,0:T(8,128)(2,1)S(1)}, bf16[512,512]{1,0:T(8,128)(2,1)S(1)}, u32[]{:S(2)}, u32[]{:S(2)}) %collective-permute-start.13) | collective-permute-done | bytes 524320 | tf_op jit(solution)/shard_map/ppermute | solution.py:802
  52.5 0.8 %total.1 = bf16[512,512]{1,0:T(8,128)(2,1)} custom-call(bf16[512,512]{1,0:T(8,128)(2,1)S(1)} %own_half.1.refs_0_, bf16[512,512]{1,0:T(8,128)(2,1)S(1)} %collective-permute-done.13.refs_1_), custom_call_target="tpu_custom_call" | custom-call | flops 880000000 | bytes 800000 | tf_op jit(solution)/shard_map/total/pallas_call | solution.py:48
  (32 shorter events, 2.8 us)
Async XLA Ops:
  0.0 15.7 %collective-permute-start.1 = (bf16[1024,1024]{1,0:T(8,128)(2,1)}, bf16[1024,1024]{1,0:T(8,128)(2,1)S(1)}, u32[]{:S(2)}, u32[]{:S(2)}) collective-permute-start(bf16[1024,1024]{1,0:T(8,128)(2,1)} %refs_5_.3), channel_id=1, source_target_pairs={{0,1},{1,0},{2,3},{3,2},{4,5},{5,4},{6,7},{7,6},{8,9},{9,8},{10,11... | collective-permute-start | bytes 6291464 | tf_op jit(solution)/shard_map/ppermute | solution.py:802
  0.5 20.2 %collective-permute-start.5 = (bf16[1024,1024]{1,0:T(8,128)(2,1)}, bf16[1024,1024]{1,0:T(8,128)(2,1)S(1)}, u32[]{:S(2)}, u32[]{:S(2)}) collective-permute-start(bf16[1024,1024]{1,0:T(8,128)(2,1)} %refs_1_.1), channel_id=1, source_target_pairs={{0,1},{1,0},{2,3},{3,2},{4,5},{5,4},{6,7},{7,6},{8,9},{9,8},{10,11... | collective-permute-start | bytes 6291464 | tf_op jit(solution)/shard_map/ppermute | solution.py:802
  0.5 5.8 %copy-start.2 = (bf16[1024,1024]{1,0:T(8,128)(2,1)S(1)}, bf16[1024,1024]{1,0:T(8,128)(2,1)}, u32[]{:S(2)}) copy-start(bf16[1024,1024]{1,0:T(8,128)(2,1)} %refs_8_.1) | copy-start | bytes 6291460
  0.5 6.3 %copy-start.1 = (bf16[1024,1024]{1,0:T(8,128)(2,1)S(1)}, bf16[1024,1024]{1,0:T(8,128)(2,1)}, u32[]{:S(2)}) copy-start(bf16[1024,1024]{1,0:T(8,128)(2,1)} %refs_1_.1) | copy-start | bytes 6291460
  3.2 5.0 %collective-permute-start = (bf16[16,1024]{1,0:T(8,128)(2,1)S(1)}, bf16[16,1024]{1,0:T(8,128)(2,1)S(1)}, u32[]{:S(2)}, u32[]{:S(2)}) collective-permute-start(bf16[16,1024]{1,0:T(8,128)(2,1)S(1)} %get-tuple-element.37), channel_id=1, source_target_pairs={{0,2},{1,0},{2,4},{3,1},{4,6},{5,3},{6,8},{7,5},{8,10},{9,7},{10,1... | collective-permute-start | bytes 98312 | tf_op jit(solution)/shard_map/ppermute | solution.py:553
  6.3 9.5 %collective-permute-start.2 = (f32[24,1024]{1,0:T(8,128)S(1)}, f32[24,1024]{1,0:T(8,128)S(1)}, u32[]{:S(2)}, u32[]{:S(2)}) collective-permute-start(f32[24,1024]{1,0:T(8,128)S(1)} %get-tuple-element.40.refs_6_.refs_7_), channel_id=1, source_target_pairs={{0,1},{1,0},{2,3},{3,2},{4,5},{5,4},{6,7},{7,6},{8,9},{9,8},{10,11... | collective-permute-start | bytes 294920 | tf_op jit(solution)/shard_map/ppermute | solution.py:802
  6.3 42.8 %collective-permute-start.11 = (bf16[1024,1024]{1,0:T(8,128)(2,1)S(1)}, bf16[1024,1024]{1,0:T(8,128)(2,1)S(1)}, u32[]{:S(2)}, u32[]{:S(2)}) collective-permute-start(bf16[1024,1024]{1,0:T(8,128)(2,1)S(1)} %copy-done.2), channel_id=1, source_target_pairs={{0,1},{1,0},{2,3},{3,2},{4,5},{5,4},{6,7},{7,6},{8,9},{9,8},{10,11... | collective-permute-start | bytes 6291464 | tf_op jit(solution)/shard_map/ppermute | solution.py:802
  6.8 1.5 %copy-start.3 = (bf16[1024,256]{1,0:T(8,128)(2,1)S(1)}, bf16[1024,256]{1,0:T(8,128)(2,1)}, u32[]{:S(2)}) copy-start(bf16[1024,256]{1,0:T(8,128)(2,1)} %refs_3_.3) | copy-start | bytes 1572868
  6.8 1.5 %copy-start.4 = (f32[4,256]{1,0:T(4,128)S(1)}, f32[4,256]{1,0:T(4,128)}, u32[]{:S(2)}) copy-start(f32[4,256]{1,0:T(4,128)} %refs_4_.1) | copy-start | bytes 12292
  8.2 1.6 %copy-start = (bf16[1024,1024]{1,0:T(8,128)(2,1)S(1)}, bf16[1024,1024]{1,0:T(8,128)(2,1)}, u32[]{:S(2)}) copy-start(bf16[1024,1024]{1,0:T(8,128)(2,1)} %refs_5_.3) | copy-start | bytes 6291460
  14.2 7.9 %collective-permute-start.4 = (bf16[144,512]{1,0:T(8,128)(2,1)S(1)}, bf16[144,512]{1,0:T(8,128)(2,1)S(1)}, u32[]{:S(2)}, u32[]{:S(2)}) collective-permute-start(bf16[144,512]{1,0:T(8,128)(2,1)S(1)} %get-tuple-element.48), channel_id=1, source_target_pairs={{0,2},{2,0},{4,6},{6,4},{8,10},{10,8},{12,14},{14,12},{1,3},{3,1},... | collective-permute-start | bytes 442376 | tf_op jit(solution)/shard_map/ppermute | solution.py:561
  20.1 10.7 %collective-permute-start.3 = (bf16[144,512]{1,0:T(8,128)(2,1)S(1)}, bf16[144,512]{1,0:T(8,128)(2,1)S(1)}, u32[]{:S(2)}, u32[]{:S(2)}) collective-permute-start(bf16[144,512]{1,0:T(8,128)(2,1)S(1)} %get-tuple-element.47), channel_id=1, source_target_pairs={{0,2},{2,0},{4,6},{6,4},{8,10},{10,8},{12,14},{14,12},{1,3},{3,1},... | collective-permute-start | bytes 442376 | tf_op jit(solution)/shard_map/ppermute | solution.py:561
  22.2 5.7 %collective-permute-start.6 = (bf16[144,512]{1,0:T(8,128)(2,1)S(1)}, bf16[144,512]{1,0:T(8,128)(2,1)S(1)}, u32[]{:S(2)}, u32[]{:S(2)}) collective-permute-start(bf16[144,512]{1,0:T(8,128)(2,1)S(1)} %pair_own.1.refs_5_.refs_1_), channel_id=1, source_target_pairs={{0,4},{1,0},{2,6},{3,2},{4,8},{5,1},{6,10},{7,3},{8,12},{9,5},{10,... | collective-permute-start | bytes 442376 | tf_op jit(solution)/shard_map/ppermute | solution.py:553
  28.0 5.5 %collective-permute-start.8 = (bf16[144,512]{1,0:T(8,128)(2,1)S(1)}, bf16[144,512]{1,0:T(8,128)(2,1)S(1)}, u32[]{:S(2)}, u32[]{:S(2)}) collective-permute-start(bf16[144,512]{1,0:T(8,128)(2,1)S(1)} %chain_own.1.refs_3_), channel_id=1, source_target_pairs={{0,8},{1,0},{2,10},{3,2},{4,12},{5,4},{6,14},{7,6},{8,9},{9,1},{10... | collective-permute-start | bytes 442376 | tf_op jit(solution)/shard_map/ppermute | solution.py:553
  30.9 4.3 %collective-permute-start.7 = (bf16[144,512]{1,0:T(8,128)(2,1)S(1)}, bf16[144,512]{1,0:T(8,128)(2,1)S(1)}, u32[]{:S(2)}, u32[]{:S(2)}) collective-permute-start(bf16[144,512]{1,0:T(8,128)(2,1)S(1)} %pair_other.1.refs_5_.refs_1_), channel_id=1, source_target_pairs={{0,4},{1,0},{2,6},{3,2},{4,8},{5,1},{6,10},{7,3},{8,12},{9,5},{10,... | collective-permute-start | bytes 442376 | tf_op jit(solution)/shard_map/ppermute | solution.py:553
  35.2 7.6 %collective-permute-start.9 = (bf16[144,512]{1,0:T(8,128)(2,1)S(1)}, bf16[144,512]{1,0:T(8,128)(2,1)S(1)}, u32[]{:S(2)}, u32[]{:S(2)}) collective-permute-start(bf16[144,512]{1,0:T(8,128)(2,1)S(1)} %chain_other.1.refs_5_), channel_id=1, source_target_pairs={{0,8},{1,0},{2,10},{3,2},{4,12},{5,4},{6,14},{7,6},{8,9},{9,1},{10... | collective-permute-start | bytes 442376 | tf_op jit(solution)/shard_map/ppermute | solution.py:553
  40.1 6.9 %collective-permute-start.12 = (bf16[128,512]{1,0:T(8,128)(2,1)S(1)}, bf16[128,512]{1,0:T(8,128)(2,1)S(1)}, u32[]{:S(2)}, u32[]{:S(2)}) collective-permute-start(bf16[128,512]{1,0:T(8,128)(2,1)S(1)} %get-tuple-element.57), channel_id=1, source_target_pairs={{0,2},{2,0},{4,6},{6,4},{8,10},{10,8},{12,14},{14,12},{1,3},{3,1},... | collective-permute-start | bytes 393224 | tf_op jit(solution)/shard_map/ppermute | solution.py:627
  43.0 6.1 %collective-permute-start.10 = (bf16[128,512]{1,0:T(8,128)(2,1)S(1)}, bf16[128,512]{1,0:T(8,128)(2,1)S(1)}, u32[]{:S(2)}, u32[]{:S(2)}) collective-permute-start(bf16[128,512]{1,0:T(8,128)(2,1)S(1)} %get-tuple-element.55), channel_id=1, source_target_pairs={{0,2},{2,0},{4,6},{6,4},{8,10},{10,8},{12,14},{14,12},{1,3},{3,1},... | collective-permute-start | bytes 393224 | tf_op jit(solution)/shard_map/ppermute | solution.py:627
  50.6 2.0 %collective-permute-start.13 = (bf16[512,512]{1,0:T(8,128)(2,1)S(1)}, bf16[512,512]{1,0:T(8,128)(2,1)S(1)}, u32[]{:S(2)}, u32[]{:S(2)}) collective-permute-start(bf16[512,512]{1,0:T(8,128)(2,1)S(1)} %get-tuple-element.62.refs_5_), channel_id=1, source_target_pairs={{0,1},{1,0},{2,3},{3,2},{4,5},{5,4},{6,7},{7,6},{8,9},{9,8},{10,11... | collective-permute-start | bytes 1572872 | tf_op jit(solution)/shard_map/ppermute | solution.py:802

commit v9 on v8

--- a/solution.py
+++ b/solution.py
@@ -493,14 +493,19 @@
 ALL = slice(None)
 
 
-def pair_kernel(place_ref, mine_ref, other_ref, out_ref):
-    mine, mine_a = parts_of(mine_ref)
-    other, other_a = parts_of(other_ref)
+def pair_kernel(place_ref, *refs):
+    *ins, out_ref = refs
     is_first = lax.rem(place_ref[0], 2) == 0
-    early = jnp.where(is_first, mine, other)
-    late = jnp.where(is_first, other, mine)
-    late_a = jnp.where(is_first, other_a, mine_a)
-    write_payload(out_ref, ALL, late_a * early + late, mine_a * other_a)
+    for group in range(len(ins) // 2):
+        mine_ref, other_ref = ins[2 * group : 2 * group + 2]
+        mine, mine_a = parts_of(mine_ref)
+        other, other_a = parts_of(other_ref)
+        early = jnp.where(is_first, mine, other)
+        late = jnp.where(is_first, other, mine)
+        late_a = jnp.where(is_first, other_a, mine_a)
+        width = mine_ref.shape[1]
+        here = slice(group * width, (group + 1) * width)
+        write_payload(out_ref, here, late_a * early + late, mine_a * other_a)
 
 
 def chain_kernel(reach, place_ref, pair_ref, before_ref, out_ref):
@@ -515,18 +520,25 @@
     write_payload(out_ref, ALL, before + before_a * farther, before_a * farther_a)
 
 
-def entry_kernel(reach, farther_reach, place_ref, mine_ref, other_ref, before_ref, farther_ref, keep_ref, send_ref):
-    mine, mine_a = parts_of(mine_ref)
-    other, other_a = parts_of(other_ref)
+def entry_kernel(reach, farther_reach, place_ref, *refs):
+    groups = (len(refs) - 2) // 4
+    before_ref, farther_ref = refs[2 * groups : 2 * groups + 2]
+    is_first = lax.rem(place_ref[0], 2) == 0
     before, before_a = parts_of(before_ref, place_ref[0] >= reach)
     farther, _ = parts_of(farther_ref, place_ref[0] >= farther_reach)
-    is_first = lax.rem(place_ref[0], 2) == 0
-    entry_first = before + before_a * farther
-    early = jnp.where(is_first, mine, other)
-    early_a = jnp.where(is_first, mine_a, other_a)
-    entry_second = early_a * entry_first + early
-    keep_ref[...] = jnp.where(is_first, entry_first, entry_second).astype(BF16)
-    send_ref[...] = jnp.where(is_first, entry_second, entry_first).astype(BF16)
+    entries = before + before_a * farther
+    for group in range(groups):
+        mine_ref, other_ref = refs[2 * group : 2 * group + 2]
+        keep_ref, send_ref = refs[2 * groups + 2 + 2 * group : 2 * groups + 4 + 2 * group]
+        mine, mine_a = parts_of(mine_ref)
+        other, other_a = parts_of(other_ref)
+        width = mine_ref.shape[1]
+        entry_first = entries[:, group * width : (group + 1) * width]
+        early = jnp.where(is_first, mine, other)
+        early_a = jnp.where(is_first, mine_a, other_a)
+        entry_second = early_a * entry_first + early
+        keep_ref[...] = jnp.where(is_first, entry_first, entry_second).astype(BF16)
+        send_ref[...] = jnp.where(is_first, entry_second, entry_first).astype(BF16)
 
 
 def small_call(kernel, name, place, arrays, shapes, after=()):
@@ -553,20 +565,24 @@
     return lax.ppermute(value, ("seq", "ch"), pairs)
 
 
+def in_pairs(value):
+    count = lax.axis_size("seq")
+    return lax.ppermute(value, "seq", [(i, i ^ 1) for i in range(count)])
+
+
 class Chain:
-    def __init__(self, tag, place, send, mine):
-        self.tag, self.place, self.mine = tag, place, mine
+    def __init__(self, place, halves):
+        self.place, self.halves = place, halves
+        self.flat = [a for pair in halves for a in pair]
+        height, width = self.flat[0].shape
+        self.shape = (height, width * len(halves))
         self.count = lax.axis_size("seq")
-        self.swap = [(i, i ^ 1) for i in range(self.count)]
-        self.other = lax.ppermute(send, "seq", self.swap)
         self.before = self.farther = None
         self.reach = self.farther_reach = 0
         self.apart = 2
 
     def pair(self, after):
-        (self.pair_state,) = small_call(
-            pair_kernel, "pair_" + self.tag, self.place, [self.mine, self.other], [self.mine.shape], after
-        )
+        (self.pair_state,) = small_call(pair_kernel, "pair", self.place, self.flat, [self.shape], after)
         self.running = self.pair_state
         self.hop()
         return self.pair_state
@@ -580,10 +596,10 @@
             self.take(after)
             (self.running,) = small_call(
                 functools.partial(chain_kernel, self.reach),
-                "chain_" + self.tag,
+                "chain",
                 self.place,
                 [self.pair_state, self.before],
-                [self.mine.shape],
+                [self.shape],
                 after,
             )
             self.apart *= 2
@@ -596,16 +612,15 @@
         else:
             (self.before,) = small_call(
                 functools.partial(longer_kernel, self.reach, self.apart),
-                "longer_" + self.tag,
+                "longer",
                 self.place,
                 [self.before, self.arrived],
-                [self.mine.shape],
+                [self.shape],
                 after,
             )
             self.reach = 0
 
     def entry(self, after):
-        shape = self.mine.shape
         if self.apart < self.count:
             if self.before is None:
                 self.before, self.reach = self.arrived, self.apart
@@ -613,18 +628,18 @@
             else:
                 self.farther, self.farther_reach = self.arrived, self.apart
         else:
-            self.before = self.farther = self.mine
+            self.before = self.farther = self.pair_state
             self.reach = self.farther_reach = self.count
-        half = (shape[0] - EXTRA, shape[1])
-        keep, out = small_call(
+        half = (self.shape[0] - EXTRA, self.flat[0].shape[1])
+        outs = small_call(
             functools.partial(entry_kernel, self.reach, self.farther_reach),
-            "entry_" + self.tag,
+            "entry",
             self.place,
-            [self.mine, self.other, self.before, self.farther],
-            [half, half],
+            self.flat + [self.before, self.farther],
+            [half, half] * len(self.halves),
             after,
         )
-        return keep, lax.ppermute(out, "seq", self.swap)
+        return [(outs[2 * i], in_pairs(outs[2 * i + 1])) for i in range(len(self.halves))]
 
 
 def gated_part(
@@ -821,22 +836,20 @@
     gate_1 = gate_call("own", normed, w_gate)
     bc, bt = maps_call(place, normed, halo, w_state, conv_state, after=[gate_1])
     x_1, cum_1, times_1, send_1, mine_1 = local_call("own", place, parity, normed, halo, bt, w_inner, small)
-    chain_1 = Chain("own", place, send_1, mine_1)
+    other_1 = in_pairs(send_1)
     x_2, cum_2, times_2, send_2, mine_2 = local_call(
         "other", place, parity, normed, halo, bt, w_inner_2, small_2, after=[mine_1]
     )
-    chain_2 = Chain("other", place, send_2, mine_2)
+    other_2 = in_pairs(send_2)
     gate_2 = gate_call("other", normed, w_gate_2, after=[x_2])
-    done = chain_1.pair(after=[gate_2])
-    y_1 = inside_call("own", x_1, bc, bt, cum_1, times_1, after=[done])
-    done = chain_1.middle(after=[y_1])
-    done = chain_2.pair(after=[done])
-    entry_1 = chain_1.entry(after=[done])
-    done = chain_2.middle(after=[entry_1[0]])
-    entry_2 = chain_2.entry(after=[done])
-    y_2 = inside_call("other", x_2, bc, bt, cum_2, times_2, after=[entry_2[0]])
+    y_1 = inside_call("own", x_1, bc, bt, cum_1, times_1, after=[gate_2])
+    chain = Chain(place, [(mine_1, other_1), (mine_2, other_2)])
+    done = chain.pair(after=[y_1])
+    y_2 = inside_call("other", x_2, bc, bt, cum_2, times_2, after=[done])
+    done = chain.middle(after=[y_2])
+    entry_1, entry_2 = chain.entry(after=[done])
     partial = finish_call(
-        back, parity, y_1, bc, cum_1, *entry_1, gate_1, small, w_output, after=[y_2]
+        back, parity, y_1, bc, cum_1, *entry_1, gate_1, small, w_output
     )
     full_width = float(w_inner.shape[1] * lax.axis_size("ch"))
     send, scaled, scale = finish_call(

time: 53.7 us -> 54.8 us (1.020)
  waiting for transfers between devices: 5.61 us -> 11.7 us
  starting transfers between devices: 19.6 us -> 14.7 us
    ppermute x5 -> x3, starting transfers between devices: 14.7 us -> 8.17 us  [onward(): return lax.ppermute(value, ('seq', 'ch'), pairs)]
    ppermute x4, waiting for transfers between devices: 0.01 us -> 5.55 us  [in_pairs(): return lax.ppermute(value, 'seq', [(i, i ^ 1) for i in range(count)])]
    ppermute x5, starting transfers between devices: 1.09 us -> 2.33 us  [theirs(): return lax.ppermute(a, 'ch', swap)]
    ppermute x5 -> x3, waiting for transfers between devices: 4.45 us -> 5.36 us  [onward(): return lax.ppermute(value, ('seq', 'ch'), pairs)]
    pallas_call x18 -> x15, Pallas kernels: 27.4 us -> 27.3 us  [call(): return lambda *arrays: run(*arrays, *after)]
  transfers between devices with their start and end apart: 14 -> 12, of which waited for: 4 -> 6; matrix products, arithmetic and copies ran while one was open for 0% -> 0% of each run, Pallas kernels for 47% -> 46%
where the time goes in v9:
time: 54.8 us; the launch traced here: 54.7 us
  Pallas kernels  27.3 us (50%)
  starting transfers between devices  14.7 us (27%)
  waiting for transfers between devices  11.7 us (21%)
  local copies, waits for them, and re-layouts  0.65 us (1%)
    pallas_call x15, Pallas kernels, call(): return lambda *arrays: run(*arrays, *after)  27.3 us
    ppermute x3, starting transfers between devices, onward(): return lax.ppermute(value, ('seq', 'ch'), pairs)  8.17 us
    ppermute x4, waiting for transfers between devices, in_pairs(): return lax.ppermute(value, 'seq', [(i, i ^ 1) for i in range(count)])  5.55 us
    ppermute x3, waiting for transfers between devices, onward(): return lax.ppermute(value, ('seq', 'ch'), pairs)  5.36 us
    ppermute x4, starting transfers between devices, in_pairs(): return lax.ppermute(value, 'seq', [(i, i ^ 1) for i in range(count)])  4.23 us
    ppermute x5, starting transfers between devices, theirs(): return lax.ppermute(a, 'ch', swap)  2.33 us
  transfers between devices with their start and end apart: 12, of which 6 were waited for; matrix products, arithmetic and copies ran while one was open for 0% of the time, Pallas kernels for 46%

profile of v9, /device:TPU:0, one launch (start us, length us, event | category | flops | bytes accessed | tf_op | source)
XLA Modules:
  0.0 54.7 jit_solution(2988074305813281603)
XLA Ops:
  0.5 2.7 %prepare.1 = (bf16[512,1024]{1,0:T(8,128)(2,1)S(1)}, bf16[16,1024]{1,0:T(8,128)(2,1)S(1)}, f32[24,1024]{1,0:T(8,128)S(1)}) custom-call(s32[1]{0:T(128)} %bitcast.refs_0_, s32[1]{0:T(128)} %bitcast.2.refs_1_.refs_0_, s32[1]{0:T(128)} %bitcast.1.refs_2_.refs_0_, bf16[512,1024]{1,0:T(8,128)(2,1)} %refs_3_.2, s32[1,512]{1,0:T(1,128)} %bitcast.10, ...), custom_call_target="tpu_custom_call" | custom-call | flops 2969999872 | bytes 2700000 | tf_op jit(solution)/shard_map/prepare/pallas_call | solution.py:48
  3.2 3.0 %collective-permute-start = (bf16[16,1024]{1,0:T(8,128)(2,1)S(1)}, bf16[16,1024]{1,0:T(8,128)(2,1)S(1)}, u32[]{:S(2)}, u32[]{:S(2)}) collective-permute-start(bf16[16,1024]{1,0:T(8,128)(2,1)S(1)} %get-tuple-element.37), channel_id=1, source_target_pairs={{0,2},{1,0},{2,4},{3,1},{4,6},{5,3},{6,8},{7,5},{8,10},{9,7},{10,1... | collective-permute-start | bytes 98312 | tf_op jit(solution)/shard_map/ppermute | solution.py:565
  6.8 1.4 %gate_own.1.refs_5_.refs_6_ = bf16[512,1024]{1,0:T(8,128)(2,1)S(1)} custom-call(bf16[512,1024]{1,0:T(8,128)(2,1)S(1)} %get-tuple-element.36.refs_0_.refs_1_.refs_2_, bf16[1024,1024]{1,0:T(8,128)(2,1)S(1)} %copy-done.1), custom_call_target="tpu_custom_call" | custom-call | flops 2640000000 | bytes 2400000 | tf_op jit(solution)/shard_map/gate_own/pallas_call | solution.py:48
  8.3 0.9 %maps.1 = (bf16[512,256]{1,0:T(8,128)(2,1)S(1)}, bf16[128,512]{1,0:T(8,128)(2,1)S(1)}) custom-call(s32[1]{0:T(128)} %bitcast.1.refs_2_.refs_0_, bf16[512,1024]{1,0:T(8,128)(2,1)S(1)} %get-tuple-element.36.refs_0_.refs_1_.refs_2_, bf16[16,1024]{1,0:T(8,128)(2,1)S(1)} %collective-permute-done.refs_2_.refs_3_, bf16[1024,256]{1,0:T(8,128)(2,1)S(1)} %copy-done.3, ...), custom_call_target="tpu_custom_call" | custom-call | flops 1650000000 | bytes 1500000 | tf_op jit(solution)/shard_map/maps/pallas_call | solution.py:48
  9.8 4.3 %local_own.1 = (bf16[512,1024]{1,0:T(8,128)(2,1)S(1)}, f32[512,16]{1,0:T(8,128)S(1)}, f32[32,512]{1,0:T(8,128)S(1)}, bf16[144,512]{1,0:T(8,128)(2,1)S(1)}, bf16[144,512]{1,0:T(8,128)(2,1)S(1)}) custom-call(s32[1]{0:T(128)} %bitcast.1.refs_2_.refs_0_, s32[1]{0:T(128)} %bitcast.2.refs_1_.refs_0_, ...), custom_call_target="tpu_custom_call" | custom-call | flops 5500000256 | bytes 5000000 | tf_op jit(solution)/shard_map/local_own/pallas_call | solution.py:48
  14.1 1.6 %collective-permute-start.3 = (bf16[144,512]{1,0:T(8,128)(2,1)S(1)}, bf16[144,512]{1,0:T(8,128)(2,1)S(1)}, u32[]{:S(2)}, u32[]{:S(2)}) collective-permute-start(bf16[144,512]{1,0:T(8,128)(2,1)S(1)} %get-tuple-element.46), channel_id=1, source_target_pairs={{0,2},{2,0},{4,6},{6,4},{8,10},{10,8},{12,14},{14,12},{1,3},{3,1},... | collective-permute-start | bytes 442376 | tf_op jit(solution)/shard_map/ppermute | solution.py:570
  15.7 4.3 %local_other.1 = (bf16[512,1024]{1,0:T(8,128)(2,1)S(1)}, f32[512,16]{1,0:T(8,128)S(1)}, f32[32,512]{1,0:T(8,128)S(1)}, bf16[144,512]{1,0:T(8,128)(2,1)S(1)}, bf16[144,512]{1,0:T(8,128)(2,1)S(1)}) custom-call(s32[1]{0:T(128)} %bitcast.1.refs_2_.refs_0_, s32[1]{0:T(128)} %bitcast.2.refs_1_.refs_0_, ...), custom_call_target="tpu_custom_call" | custom-call | flops 5500000256 | bytes 5000000 | tf_op jit(solution)/shard_map/local_other/pallas_call | solution.py:48
  20.6 1.5 %gate_other.1.refs_5_.refs_7_ = bf16[512,1024]{1,0:T(8,128)(2,1)S(1)} custom-call(bf16[512,1024]{1,0:T(8,128)(2,1)S(1)} %get-tuple-element.36.refs_0_.refs_1_.refs_2_, bf16[1024,1024]{1,0:T(8,128)(2,1)S(1)} %collective-permute-done.5.refs_1_, bf16[512,1024]{1,0:T(8,128)(2,1)S(1)} %get-tuple-element.42.refs_2_.refs_0_), custom_call_target="tpu_custom_call" | custom-call | flops 2640000000 | bytes 2400000 | tf_op jit(solution)/shard_map/gate_other/pallas_call | solution.py:48
  22.1 3.4 %inside_own.1.refs_5_.refs_1_ = bf16[512,1024]{1,0:T(8,128)(2,1)S(1)} custom-call(bf16[512,1024]{1,0:T(8,128)(2,1)S(1)} %get-tuple-element.49.refs_0_, bf16[512,256]{1,0:T(8,128)(2,1)S(1)} %get-tuple-element.43.refs_1_.refs_2_.refs_3_, bf16[128,512]{1,0:T(8,128)(2,1)S(1)} %get-tuple-element.38.refs_4_.refs_2_, f32[512,16]{1,0:T(8,128)S(1)} %get-tuple-element.50.refs_3_, ...), custom_call_target="tpu_custom_call" | custom-call | flops 3520000000 | bytes 3200000 | tf_op jit(solution)/shard_map/inside_own/pallas_call | solution.py:48
  25.4 1.1 %collective-permute-done.4.refs_4_ = bf16[144,512]{1,0:T(8,128)(2,1)S(1)} collective-permute-done((bf16[144,512]{1,0:T(8,128)(2,1)S(1)}, bf16[144,512]{1,0:T(8,128)(2,1)S(1)}, u32[]{:S(2)}, u32[]{:S(2)}) %collective-permute-start.4) | collective-permute-done | bytes 147488 | tf_op jit(solution)/shard_map/ppermute | solution.py:570
  26.7 1.6 %collective-permute-start.6 = (bf16[144,1024]{1,0:T(8,128)(2,1)S(1)}, bf16[144,1024]{1,0:T(8,128)(2,1)S(1)}, u32[]{:S(2)}, u32[]{:S(2)}) collective-permute-start(bf16[144,1024]{1,0:T(8,128)(2,1)S(1)} %pair.1.refs_5_.refs_1_), channel_id=1, source_target_pairs={{0,4},{1,0},{2,6},{3,2},{4,8},{5,1},{6,10},{7,3},{8,12},{9,5},{10,... | collective-permute-start | bytes 884744 | tf_op jit(solution)/shard_map/ppermute | solution.py:565
  28.3 3.2 %inside_other.1.refs_3_.refs_2_ = bf16[512,1024]{1,0:T(8,128)(2,1)S(1)} custom-call(bf16[512,1024]{1,0:T(8,128)(2,1)S(1)} %get-tuple-element.42.refs_2_.refs_0_, bf16[512,256]{1,0:T(8,128)(2,1)S(1)} %get-tuple-element.43.refs_1_.refs_2_.refs_3_, bf16[128,512]{1,0:T(8,128)(2,1)S(1)} %get-tuple-element.38.refs_4_.refs_2_, ...), custom_call_target="tpu_custom_call" | custom-call | flops 3520000000 | bytes 3200000 | tf_op jit(solution)/shard_map/inside_other/pallas_call | solution.py:48
  31.5 1.1 %collective-permute-done.6.refs_2_.refs_5_ = bf16[144,1024]{1,0:T(8,128)(2,1)S(1)} collective-permute-done((bf16[144,1024]{1,0:T(8,128)(2,1)S(1)}, bf16[144,1024]{1,0:T(8,128)(2,1)S(1)}, u32[]{:S(2)}, u32[]{:S(2)}) %collective-permute-start.6) | collective-permute-done | bytes 294944 | tf_op jit(solution)/shard_map/ppermute | solution.py:565
  32.7 3.6 %collective-permute-start.7 = (bf16[144,1024]{1,0:T(8,128)(2,1)S(1)}, bf16[144,1024]{1,0:T(8,128)(2,1)S(1)}, u32[]{:S(2)}, u32[]{:S(2)}) collective-permute-start(bf16[144,1024]{1,0:T(8,128)(2,1)S(1)} %chain.1.refs_7_), channel_id=1, source_target_pairs={{0,8},{1,0},{2,10},{3,2},{4,12},{5,4},{6,14},{7,6},{8,9},{9,1},{10... | collective-permute-start | bytes 884744 | tf_op jit(solution)/shard_map/ppermute | solution.py:565
  36.2 4.3 %collective-permute-done.7.refs_6_ = bf16[144,1024]{1,0:T(8,128)(2,1)S(1)} collective-permute-done((bf16[144,1024]{1,0:T(8,128)(2,1)S(1)}, bf16[144,1024]{1,0:T(8,128)(2,1)S(1)}, u32[]{:S(2)}, u32[]{:S(2)}) %collective-permute-start.7) | collective-permute-done | bytes 294944 | tf_op jit(solution)/shard_map/ppermute | solution.py:565
  41.4 1.4 %collective-permute-start.8 = (bf16[128,512]{1,0:T(8,128)(2,1)S(1)}, bf16[128,512]{1,0:T(8,128)(2,1)S(1)}, u32[]{:S(2)}, u32[]{:S(2)}) collective-permute-start(bf16[128,512]{1,0:T(8,128)(2,1)S(1)} %get-tuple-element.54), channel_id=1, source_target_pairs={{0,2},{2,0},{4,6},{6,4},{8,10},{10,8},{12,14},{14,12},{1,3},{3,1},... | collective-permute-start | bytes 393224 | tf_op jit(solution)/shard_map/ppermute | solution.py:570
  42.9 3.6 %collective-permute-done.10.refs_5_ = bf16[128,512]{1,0:T(8,128)(2,1)S(1)} collective-permute-done((bf16[128,512]{1,0:T(8,128)(2,1)S(1)}, bf16[128,512]{1,0:T(8,128)(2,1)S(1)}, u32[]{:S(2)}, u32[]{:S(2)}) %collective-permute-start.10) | collective-permute-done | bytes 131104 | tf_op jit(solution)/shard_map/ppermute | solution.py:570
  46.5 2.0 %part.1 = (f32[512,1024]{1,0:T(8,128)S(1)}, f32[512,128]{1,0:T(8,128)S(1)}) custom-call(s32[1]{0:T(128)} %bitcast.2.refs_1_.refs_0_, bf16[512,1024]{1,0:T(8,128)(2,1)S(1)} %inside_own.1.refs_5_.refs_1_, bf16[512,256]{1,0:T(8,128)(2,1)S(1)} %get-tuple-element.43.refs_1_.refs_2_.refs_3_, f32[512,16]{1,0:T(8,128)S(1)} %get-tuple-element.50.refs_3_, ...), custom_call_target="tpu_custom_call" | custom-call | flops 3849999872 | bytes 3500000 | tf_op jit(solution)/shard_map/part/pallas_call | solution.py:48
  48.5 0.8 %collective-permute-done.8.refs_6_ = bf16[128,512]{1,0:T(8,128)(2,1)S(1)} collective-permute-done((bf16[128,512]{1,0:T(8,128)(2,1)S(1)}, bf16[128,512]{1,0:T(8,128)(2,1)S(1)}, u32[]{:S(2)}, u32[]{:S(2)}) %collective-permute-start.8) | collective-permute-done | bytes 131104 | tf_op jit(solution)/shard_map/ppermute | solution.py:570
  49.3 1.5 %finish.1 = (bf16[512,512]{1,0:T(8,128)(2,1)S(1)}, bf16[512,1024]{1,0:T(8,128)(2,1)S(1)}, f32[512,128]{1,0:T(8,128)S(1)}) custom-call(s32[1]{0:T(128)} %bitcast.refs_0_, s32[1]{0:T(128)} %bitcast.2.refs_1_.refs_0_, bf16[512,1024]{1,0:T(8,128)(2,1)S(1)} %inside_other.1.refs_3_.refs_2_, bf16[512,256]{1,0:T(8,128)(2,1)S(1)} %get-tuple-element.43.refs_1_.refs_2_.refs_3_, ...), custom_call_target="tpu_custom_call" | custom-call | flops 3849999872 | bytes 3500000 | tf_op jit(solution)/shard_map/finish/pallas_call | solution.py:48
  50.8 1.3 %collective-permute-start.11 = (bf16[512,512]{1,0:T(8,128)(2,1)S(1)}, bf16[512,512]{1,0:T(8,128)(2,1)S(1)}, u32[]{:S(2)}, u32[]{:S(2)}) collective-permute-start(bf16[512,512]{1,0:T(8,128)(2,1)S(1)} %get-tuple-element.62.refs_5_), channel_id=1, source_target_pairs={{0,1},{1,0},{2,3},{3,2},{4,5},{5,4},{6,7},{7,6},{8,9},{9,8},{10,11... | collective-permute-start | bytes 1572872 | tf_op jit(solution)/shard_map/ppermute | solution.py:817
  52.1 0.7 %own_half.1.refs_0_ = bf16[512,512]{1,0:T(8,128)(2,1)S(1)} custom-call(s32[1]{0:T(128)} %bitcast.refs_0_, bf16[512,1024]{1,0:T(8,128)(2,1)S(1)} %get-tuple-element.60.refs_1_, bf16[1024,1024]{1,0:T(8,128)(2,1)S(1)} %collective-permute-done.9.refs_9_.refs_2_, f32[512,1024]{1,0:T(8,128)S(1)} %get-tuple-element.58.refs_10_.refs_3_, ...), custom_call_target="tpu_custom_call" | custom-call | flops 770000000 | bytes 700000 | tf_op jit(solution)/shard_map/own_half/pallas_call | solution.py:48
  52.9 0.8 %collective-permute-done.11.refs_1_ = bf16[512,512]{1,0:T(8,128)(2,1)S(1)} collective-permute-done((bf16[512,512]{1,0:T(8,128)(2,1)S(1)}, bf16[512,512]{1,0:T(8,128)(2,1)S(1)}, u32[]{:S(2)}, u32[]{:S(2)}) %collective-permute-start.11) | collective-permute-done | bytes 524320 | tf_op jit(solution)/shard_map/ppermute | solution.py:817
  53.7 0.8 %total.1 = bf16[512,512]{1,0:T(8,128)(2,1)} custom-call(bf16[512,512]{1,0:T(8,128)(2,1)S(1)} %own_half.1.refs_0_, bf16[512,512]{1,0:T(8,128)(2,1)S(1)} %collective-permute-done.11.refs_1_), custom_call_target="tpu_custom_call" | custom-call | flops 880000000 | bytes 800000 | tf_op jit(solution)/shard_map/total/pallas_call | solution.py:48
  (25 shorter events, 3.4 us)
Async XLA Ops:
  0.0 15.7 %collective-permute-start.1 = (bf16[1024,1024]{1,0:T(8,128)(2,1)}, bf16[1024,1024]{1,0:T(8,128)(2,1)S(1)}, u32[]{:S(2)}, u32[]{:S(2)}) collective-permute-start(bf16[1024,1024]{1,0:T(8,128)(2,1)} %refs_5_.3), channel_id=1, source_target_pairs={{0,1},{1,0},{2,3},{3,2},{4,5},{5,4},{6,7},{7,6},{8,9},{9,8},{10,11... | collective-permute-start | bytes 6291464 | tf_op jit(solution)/shard_map/ppermute | solution.py:817
  0.5 20.2 %collective-permute-start.5 = (bf16[1024,1024]{1,0:T(8,128)(2,1)}, bf16[1024,1024]{1,0:T(8,128)(2,1)S(1)}, u32[]{:S(2)}, u32[]{:S(2)}) collective-permute-start(bf16[1024,1024]{1,0:T(8,128)(2,1)} %refs_1_.1), channel_id=1, source_target_pairs={{0,1},{1,0},{2,3},{3,2},{4,5},{5,4},{6,7},{7,6},{8,9},{9,8},{10,11... | collective-permute-start | bytes 6291464 | tf_op jit(solution)/shard_map/ppermute | solution.py:817
  0.5 5.8 %copy-start.2 = (bf16[1024,1024]{1,0:T(8,128)(2,1)S(1)}, bf16[1024,1024]{1,0:T(8,128)(2,1)}, u32[]{:S(2)}) copy-start(bf16[1024,1024]{1,0:T(8,128)(2,1)} %refs_8_.1) | copy-start | bytes 6291460
  0.5 6.3 %copy-start.1 = (bf16[1024,1024]{1,0:T(8,128)(2,1)S(1)}, bf16[1024,1024]{1,0:T(8,128)(2,1)}, u32[]{:S(2)}) copy-start(bf16[1024,1024]{1,0:T(8,128)(2,1)} %refs_1_.1) | copy-start | bytes 6291460
  3.2 5.0 %collective-permute-start = (bf16[16,1024]{1,0:T(8,128)(2,1)S(1)}, bf16[16,1024]{1,0:T(8,128)(2,1)S(1)}, u32[]{:S(2)}, u32[]{:S(2)}) collective-permute-start(bf16[16,1024]{1,0:T(8,128)(2,1)S(1)} %get-tuple-element.37), channel_id=1, source_target_pairs={{0,2},{1,0},{2,4},{3,1},{4,6},{5,3},{6,8},{7,5},{8,10},{9,7},{10,1... | collective-permute-start | bytes 98312 | tf_op jit(solution)/shard_map/ppermute | solution.py:565
  6.3 9.5 %collective-permute-start.2 = (f32[24,1024]{1,0:T(8,128)S(1)}, f32[24,1024]{1,0:T(8,128)S(1)}, u32[]{:S(2)}, u32[]{:S(2)}) collective-permute-start(f32[24,1024]{1,0:T(8,128)S(1)} %get-tuple-element.40.refs_6_.refs_7_), channel_id=1, source_target_pairs={{0,1},{1,0},{2,3},{3,2},{4,5},{5,4},{6,7},{7,6},{8,9},{9,8},{10,11... | collective-permute-start | bytes 294920 | tf_op jit(solution)/shard_map/ppermute | solution.py:817
  6.3 42.3 %collective-permute-start.9 = (bf16[1024,1024]{1,0:T(8,128)(2,1)S(1)}, bf16[1024,1024]{1,0:T(8,128)(2,1)S(1)}, u32[]{:S(2)}, u32[]{:S(2)}) collective-permute-start(bf16[1024,1024]{1,0:T(8,128)(2,1)S(1)} %copy-done.2), channel_id=1, source_target_pairs={{0,1},{1,0},{2,3},{3,2},{4,5},{5,4},{6,7},{7,6},{8,9},{9,8},{10,11... | collective-permute-start | bytes 6291464 | tf_op jit(solution)/shard_map/ppermute | solution.py:817
  6.8 1.5 %copy-start.3 = (bf16[1024,256]{1,0:T(8,128)(2,1)S(1)}, bf16[1024,256]{1,0:T(8,128)(2,1)}, u32[]{:S(2)}) copy-start(bf16[1024,256]{1,0:T(8,128)(2,1)} %refs_3_.3) | copy-start | bytes 1572868
  6.8 1.5 %copy-start.4 = (f32[4,256]{1,0:T(4,128)S(1)}, f32[4,256]{1,0:T(4,128)}, u32[]{:S(2)}) copy-start(f32[4,256]{1,0:T(4,128)} %refs_4_.1) | copy-start | bytes 12292
  8.2 1.6 %copy-start = (bf16[1024,1024]{1,0:T(8,128)(2,1)S(1)}, bf16[1024,1024]{1,0:T(8,128)(2,1)}, u32[]{:S(2)}) copy-start(bf16[1024,1024]{1,0:T(8,128)(2,1)} %refs_5_.3) | copy-start | bytes 6291460
  14.1 11.3 %collective-permute-start.3 = (bf16[144,512]{1,0:T(8,128)(2,1)S(1)}, bf16[144,512]{1,0:T(8,128)(2,1)S(1)}, u32[]{:S(2)}, u32[]{:S(2)}) collective-permute-start(bf16[144,512]{1,0:T(8,128)(2,1)S(1)} %get-tuple-element.46), channel_id=1, source_target_pairs={{0,2},{2,0},{4,6},{6,4},{8,10},{10,8},{12,14},{14,12},{1,3},{3,1},... | collective-permute-start | bytes 442376 | tf_op jit(solution)/shard_map/ppermute | solution.py:570
  20.1 6.5 %collective-permute-start.4 = (bf16[144,512]{1,0:T(8,128)(2,1)S(1)}, bf16[144,512]{1,0:T(8,128)(2,1)S(1)}, u32[]{:S(2)}, u32[]{:S(2)}) collective-permute-start(bf16[144,512]{1,0:T(8,128)(2,1)S(1)} %get-tuple-element.48), channel_id=1, source_target_pairs={{0,2},{2,0},{4,6},{6,4},{8,10},{10,8},{12,14},{14,12},{1,3},{3,1},... | collective-permute-start | bytes 442376 | tf_op jit(solution)/shard_map/ppermute | solution.py:570
  26.7 5.8 %collective-permute-start.6 = (bf16[144,1024]{1,0:T(8,128)(2,1)S(1)}, bf16[144,1024]{1,0:T(8,128)(2,1)S(1)}, u32[]{:S(2)}, u32[]{:S(2)}) collective-permute-start(bf16[144,1024]{1,0:T(8,128)(2,1)S(1)} %pair.1.refs_5_.refs_1_), channel_id=1, source_target_pairs={{0,4},{1,0},{2,6},{3,2},{4,8},{5,1},{6,10},{7,3},{8,12},{9,5},{10,... | collective-permute-start | bytes 884744 | tf_op jit(solution)/shard_map/ppermute | solution.py:565
  32.7 7.8 %collective-permute-start.7 = (bf16[144,1024]{1,0:T(8,128)(2,1)S(1)}, bf16[144,1024]{1,0:T(8,128)(2,1)S(1)}, u32[]{:S(2)}, u32[]{:S(2)}) collective-permute-start(bf16[144,1024]{1,0:T(8,128)(2,1)S(1)} %chain.1.refs_7_), channel_id=1, source_target_pairs={{0,8},{1,0},{2,10},{3,2},{4,12},{5,4},{6,14},{7,6},{8,9},{9,1},{10... | collective-permute-start | bytes 884744 | tf_op jit(solution)/shard_map/ppermute | solution.py:565
  40.8 5.7 %collective-permute-start.10 = (bf16[128,512]{1,0:T(8,128)(2,1)S(1)}, bf16[128,512]{1,0:T(8,128)(2,1)S(1)}, u32[]{:S(2)}, u32[]{:S(2)}) collective-permute-start(bf16[128,512]{1,0:T(8,128)(2,1)S(1)} %get-tuple-element.57), channel_id=1, source_target_pairs={{0,2},{2,0},{4,6},{6,4},{8,10},{10,8},{12,14},{14,12},{1,3},{3,1},... | collective-permute-start | bytes 393224 | tf_op jit(solution)/shard_map/ppermute | solution.py:570
  41.4 7.9 %collective-permute-start.8 = (bf16[128,512]{1,0:T(8,128)(2,1)S(1)}, bf16[128,512]{1,0:T(8,128)(2,1)S(1)}, u32[]{:S(2)}, u32[]{:S(2)}) collective-permute-start(bf16[128,512]{1,0:T(8,128)(2,1)S(1)} %get-tuple-element.54), channel_id=1, source_target_pairs={{0,2},{2,0},{4,6},{6,4},{8,10},{10,8},{12,14},{14,12},{1,3},{3,1},... | collective-permute-start | bytes 393224 | tf_op jit(solution)/shard_map/ppermute | solution.py:570
  50.8 2.8 %collective-permute-start.11 = (bf16[512,512]{1,0:T(8,128)(2,1)S(1)}, bf16[512,512]{1,0:T(8,128)(2,1)S(1)}, u32[]{:S(2)}, u32[]{:S(2)}) collective-permute-start(bf16[512,512]{1,0:T(8,128)(2,1)S(1)} %get-tuple-element.62.refs_5_), channel_id=1, source_target_pairs={{0,1},{1,0},{2,3},{3,2},{4,5},{5,4},{6,7},{7,6},{8,9},{9,8},{10,11... | collective-permute-start | bytes 1572872 | tf_op jit(solution)/shard_map/ppermute | solution.py:817

commit v10 on v8

--- a/solution.py
+++ b/solution.py
@@ -829,11 +829,11 @@
     gate_2 = gate_call("other", normed, w_gate_2, after=[x_2])
     done = chain_1.pair(after=[gate_2])
     y_1 = inside_call("own", x_1, bc, bt, cum_1, times_1, after=[done])
-    done = chain_1.middle(after=[y_1])
-    done = chain_2.pair(after=[done])
+    done = chain_2.pair(after=[y_1])
+    done = chain_1.middle(after=[done])
+    done = chain_2.middle(after=[done])
     entry_1 = chain_1.entry(after=[done])
-    done = chain_2.middle(after=[entry_1[0]])
-    entry_2 = chain_2.entry(after=[done])
+    entry_2 = chain_2.entry(after=[entry_1[0]])
     y_2 = inside_call("other", x_2, bc, bt, cum_2, times_2, after=[entry_2[0]])
     partial = finish_call(
         back, parity, y_1, bc, cum_1, *entry_1, gate_1, small, w_output, after=[y_2]

time: 53.7 us -> 50.5 us (0.940)
  starting transfers between devices: 19.6 us -> 16.6 us
    ppermute x2, starting transfers between devices: 1.68 us -> 0.14 us  [entry(): return (keep, lax.ppermute(out, 'seq', self.swap))]
    ppermute x5, starting transfers between devices: 14.7 us -> 13.2 us  [onward(): return lax.ppermute(value, ('seq', 'ch'), pairs)]
  transfers between devices with their start and end apart: 14 -> 14, of which waited for: 4 -> 4; matrix products, arithmetic and copies ran while one was open for 0% -> 0% of each run, Pallas kernels for 47% -> 50%
where the time goes in v10:
time: 50.5 us; the launch traced here: 50.4 us
  Pallas kernels  27.4 us (54%)
  starting transfers between devices  16.6 us (33%)
  waiting for transfers between devices  5.45 us (11%)
  local copies, waits for them, and re-layouts  0.65 us (1%)
    pallas_call x18, Pallas kernels, call(): return lambda *arrays: run(*arrays, *after)  27.4 us
    ppermute x5, starting transfers between devices, onward(): return lax.ppermute(value, ('seq', 'ch'), pairs)  13.2 us
    ppermute x5, waiting for transfers between devices, onward(): return lax.ppermute(value, ('seq', 'ch'), pairs)  3.93 us
    ppermute x2, starting transfers between devices, __init__(): self.other = lax.ppermute(send, 'seq', self.swap)  2.14 us
    ppermute x5, waiting for transfers between devices, theirs(): return lax.ppermute(a, 'ch', swap)  1.15 us
    ppermute x5, starting transfers between devices, theirs(): return lax.ppermute(a, 'ch', swap)  1.09 us
  transfers between devices with their start and end apart: 14, of which 4 were waited for; matrix products, arithmetic and copies ran while one was open for 0% of the time, Pallas kernels for 50%

profile of v10, /device:TPU:0, one launch (start us, length us, event | category | flops | bytes accessed | tf_op | source)
XLA Modules:
  0.0 50.4 jit_solution(6022333227830349869)
XLA Ops:
  0.5 2.7 %prepare.1 = (bf16[512,1024]{1,0:T(8,128)(2,1)S(1)}, bf16[16,1024]{1,0:T(8,128)(2,1)S(1)}, f32[24,1024]{1,0:T(8,128)S(1)}) custom-call(s32[1]{0:T(128)} %bitcast.refs_0_, s32[1]{0:T(128)} %bitcast.2.refs_1_.refs_0_, s32[1]{0:T(128)} %bitcast.1.refs_2_.refs_0_, bf16[512,1024]{1,0:T(8,128)(2,1)} %refs_3_.2, s32[1,512]{1,0:T(1,128)} %bitcast.10, ...), custom_call_target="tpu_custom_call" | custom-call | flops 2969999872 | bytes 2700000 | tf_op jit(solution)/shard_map/prepare/pallas_call | solution.py:48
  3.2 3.0 %collective-permute-start = (bf16[16,1024]{1,0:T(8,128)(2,1)S(1)}, bf16[16,1024]{1,0:T(8,128)(2,1)S(1)}, u32[]{:S(2)}, u32[]{:S(2)}) collective-permute-start(bf16[16,1024]{1,0:T(8,128)(2,1)S(1)} %get-tuple-element.37), channel_id=1, source_target_pairs={{0,2},{1,0},{2,4},{3,1},{4,6},{5,3},{6,8},{7,5},{8,10},{9,7},{10,1... | collective-permute-start | bytes 98312 | tf_op jit(solution)/shard_map/ppermute | solution.py:553
  6.3 0.5 %collective-permute-start.11 = (bf16[1024,1024]{1,0:T(8,128)(2,1)S(1)}, bf16[1024,1024]{1,0:T(8,128)(2,1)S(1)}, u32[]{:S(2)}, u32[]{:S(2)}) collective-permute-start(bf16[1024,1024]{1,0:T(8,128)(2,1)S(1)} %copy-done.2), channel_id=1, source_target_pairs={{0,1},{1,0},{2,3},{3,2},{4,5},{5,4},{6,7},{7,6},{8,9},{9,8},{10,11... | collective-permute-start | bytes 6291464 | tf_op jit(solution)/shard_map/ppermute | solution.py:802
  6.8 1.4 %gate_own.1.refs_5_.refs_6_ = bf16[512,1024]{1,0:T(8,128)(2,1)S(1)} custom-call(bf16[512,1024]{1,0:T(8,128)(2,1)S(1)} %get-tuple-element.36.refs_0_.refs_1_.refs_2_, bf16[1024,1024]{1,0:T(8,128)(2,1)S(1)} %copy-done.1), custom_call_target="tpu_custom_call" | custom-call | flops 2640000000 | bytes 2400000 | tf_op jit(solution)/shard_map/gate_own/pallas_call | solution.py:48
  8.3 0.9 %maps.1 = (bf16[512,256]{1,0:T(8,128)(2,1)S(1)}, bf16[128,512]{1,0:T(8,128)(2,1)S(1)}) custom-call(s32[1]{0:T(128)} %bitcast.1.refs_2_.refs_0_, bf16[512,1024]{1,0:T(8,128)(2,1)S(1)} %get-tuple-element.36.refs_0_.refs_1_.refs_2_, bf16[16,1024]{1,0:T(8,128)(2,1)S(1)} %collective-permute-done.refs_2_.refs_3_, bf16[1024,256]{1,0:T(8,128)(2,1)S(1)} %copy-done.3, ...), custom_call_target="tpu_custom_call" | custom-call | flops 1650000000 | bytes 1500000 | tf_op jit(solution)/shard_map/maps/pallas_call | solution.py:48
  9.2 0.6 %copy-done = bf16[1024,1024]{1,0:T(8,128)(2,1)S(1)} copy-done((bf16[1024,1024]{1,0:T(8,128)(2,1)S(1)}, bf16[1024,1024]{1,0:T(8,128)(2,1)}, u32[]{:S(2)}) %copy-start) | copy-done | bytes 2097176
  9.8 4.3 %local_own.1 = (bf16[512,1024]{1,0:T(8,128)(2,1)S(1)}, f32[512,16]{1,0:T(8,128)S(1)}, f32[32,512]{1,0:T(8,128)S(1)}, bf16[144,512]{1,0:T(8,128)(2,1)S(1)}, bf16[144,512]{1,0:T(8,128)(2,1)S(1)}) custom-call(s32[1]{0:T(128)} %bitcast.1.refs_2_.refs_0_, s32[1]{0:T(128)} %bitcast.2.refs_1_.refs_0_, ...), custom_call_target="tpu_custom_call" | custom-call | flops 5500000256 | bytes 5000000 | tf_op jit(solution)/shard_map/local_own/pallas_call | solution.py:48
  14.2 1.6 %collective-permute-start.4 = (bf16[144,512]{1,0:T(8,128)(2,1)S(1)}, bf16[144,512]{1,0:T(8,128)(2,1)S(1)}, u32[]{:S(2)}, u32[]{:S(2)}) collective-permute-start(bf16[144,512]{1,0:T(8,128)(2,1)S(1)} %get-tuple-element.51), channel_id=1, source_target_pairs={{0,2},{2,0},{4,6},{6,4},{8,10},{10,8},{12,14},{14,12},{1,3},{3,1},... | collective-permute-start | bytes 442376 | tf_op jit(solution)/shard_map/ppermute | solution.py:561
  15.8 4.3 %local_other.1 = (bf16[512,1024]{1,0:T(8,128)(2,1)S(1)}, f32[512,16]{1,0:T(8,128)S(1)}, f32[32,512]{1,0:T(8,128)S(1)}, bf16[144,512]{1,0:T(8,128)(2,1)S(1)}, bf16[144,512]{1,0:T(8,128)(2,1)S(1)}) custom-call(s32[1]{0:T(128)} %bitcast.1.refs_2_.refs_0_, s32[1]{0:T(128)} %bitcast.2.refs_1_.refs_0_, ...), custom_call_target="tpu_custom_call" | custom-call | flops 5500000256 | bytes 5000000 | tf_op jit(solution)/shard_map/local_other/pallas_call | solution.py:48
  20.1 0.6 %collective-permute-start.3 = (bf16[144,512]{1,0:T(8,128)(2,1)S(1)}, bf16[144,512]{1,0:T(8,128)(2,1)S(1)}, u32[]{:S(2)}, u32[]{:S(2)}) collective-permute-start(bf16[144,512]{1,0:T(8,128)(2,1)S(1)} %get-tuple-element.47), channel_id=1, source_target_pairs={{0,2},{2,0},{4,6},{6,4},{8,10},{10,8},{12,14},{14,12},{1,3},{3,1},... | collective-permute-start | bytes 442376 | tf_op jit(solution)/shard_map/ppermute | solution.py:561
  20.6 1.4 %gate_other.1.refs_3_.refs_7_ = bf16[512,1024]{1,0:T(8,128)(2,1)S(1)} custom-call(bf16[512,1024]{1,0:T(8,128)(2,1)S(1)} %get-tuple-element.36.refs_0_.refs_1_.refs_2_, bf16[1024,1024]{1,0:T(8,128)(2,1)S(1)} %collective-permute-done.5.refs_1_, bf16[512,1024]{1,0:T(8,128)(2,1)S(1)} %get-tuple-element.42.refs_2_.refs_0_), custom_call_target="tpu_custom_call" | custom-call | flops 2640000000 | bytes 2400000 | tf_op jit(solution)/shard_map/gate_other/pallas_call | solution.py:48
  22.2 2.3 %collective-permute-start.7 = (bf16[144,512]{1,0:T(8,128)(2,1)S(1)}, bf16[144,512]{1,0:T(8,128)(2,1)S(1)}, u32[]{:S(2)}, u32[]{:S(2)}) collective-permute-start(bf16[144,512]{1,0:T(8,128)(2,1)S(1)} %pair_own.1.refs_5_.refs_1_), channel_id=1, source_target_pairs={{0,4},{1,0},{2,6},{3,2},{4,8},{5,1},{6,10},{7,3},{8,12},{9,5},{10,... | collective-permute-start | bytes 442376 | tf_op jit(solution)/shard_map/ppermute | solution.py:553
  24.5 3.4 %inside_own.1.refs_3_.refs_1_ = bf16[512,1024]{1,0:T(8,128)(2,1)S(1)} custom-call(bf16[512,1024]{1,0:T(8,128)(2,1)S(1)} %get-tuple-element.48.refs_0_, bf16[512,256]{1,0:T(8,128)(2,1)S(1)} %get-tuple-element.43.refs_1_.refs_2_.refs_3_, bf16[128,512]{1,0:T(8,128)(2,1)S(1)} %get-tuple-element.38.refs_4_.refs_2_, f32[512,16]{1,0:T(8,128)S(1)} %get-tuple-element.49.refs_3_, ...), custom_call_target="tpu_custom_call" | custom-call | flops 3520000000 | bytes 3200000 | tf_op jit(solution)/shard_map/inside_own/pallas_call | solution.py:48
  28.0 1.6 %collective-permute-start.6 = (bf16[144,512]{1,0:T(8,128)(2,1)S(1)}, bf16[144,512]{1,0:T(8,128)(2,1)S(1)}, u32[]{:S(2)}, u32[]{:S(2)}) collective-permute-start(bf16[144,512]{1,0:T(8,128)(2,1)S(1)} %pair_other.1.refs_3_.refs_1_), channel_id=1, source_target_pairs={{0,4},{1,0},{2,6},{3,2},{4,8},{5,1},{6,10},{7,3},{8,12},{9,5},{10,... | collective-permute-start | bytes 442376 | tf_op jit(solution)/shard_map/ppermute | solution.py:553
  29.6 1.1 %collective-permute-start.9 = (bf16[144,512]{1,0:T(8,128)(2,1)S(1)}, bf16[144,512]{1,0:T(8,128)(2,1)S(1)}, u32[]{:S(2)}, u32[]{:S(2)}) collective-permute-start(bf16[144,512]{1,0:T(8,128)(2,1)S(1)} %chain_own.1.refs_3_), channel_id=1, source_target_pairs={{0,8},{1,0},{2,10},{3,2},{4,12},{5,4},{6,14},{7,6},{8,9},{9,1},{10... | collective-permute-start | bytes 442376 | tf_op jit(solution)/shard_map/ppermute | solution.py:553
  30.8 1.5 %collective-permute-done.6.refs_2_.refs_3_ = bf16[144,512]{1,0:T(8,128)(2,1)S(1)} collective-permute-done((bf16[144,512]{1,0:T(8,128)(2,1)S(1)}, bf16[144,512]{1,0:T(8,128)(2,1)S(1)}, u32[]{:S(2)}, u32[]{:S(2)}) %collective-permute-start.6) | collective-permute-done | bytes 147488 | tf_op jit(solution)/shard_map/ppermute | solution.py:553
  32.3 5.1 %collective-permute-start.8 = (bf16[144,512]{1,0:T(8,128)(2,1)S(1)}, bf16[144,512]{1,0:T(8,128)(2,1)S(1)}, u32[]{:S(2)}, u32[]{:S(2)}) collective-permute-start(bf16[144,512]{1,0:T(8,128)(2,1)S(1)} %chain_other.1.refs_5_), channel_id=1, source_target_pairs={{0,8},{1,0},{2,10},{3,2},{4,12},{5,4},{6,14},{7,6},{8,9},{9,1},{10... | collective-permute-start | bytes 442376 | tf_op jit(solution)/shard_map/ppermute | solution.py:553
  37.6 2.5 %collective-permute-done.8.refs_4_ = bf16[144,512]{1,0:T(8,128)(2,1)S(1)} collective-permute-done((bf16[144,512]{1,0:T(8,128)(2,1)S(1)}, bf16[144,512]{1,0:T(8,128)(2,1)S(1)}, u32[]{:S(2)}, u32[]{:S(2)}) %collective-permute-start.8) | collective-permute-done | bytes 147488 | tf_op jit(solution)/shard_map/ppermute | solution.py:553
  40.3 3.2 %inside_other.1.refs_9_.refs_2_ = bf16[512,1024]{1,0:T(8,128)(2,1)S(1)} custom-call(bf16[512,1024]{1,0:T(8,128)(2,1)S(1)} %get-tuple-element.42.refs_2_.refs_0_, bf16[512,256]{1,0:T(8,128)(2,1)S(1)} %get-tuple-element.43.refs_1_.refs_2_.refs_3_, bf16[128,512]{1,0:T(8,128)(2,1)S(1)} %get-tuple-element.38.refs_4_.refs_2_, ...), custom_call_target="tpu_custom_call" | custom-call | flops 3520000000 | bytes 3200000 | tf_op jit(solution)/shard_map/inside_other/pallas_call | solution.py:48
  43.9 2.0 %part.1 = (f32[512,1024]{1,0:T(8,128)S(1)}, f32[512,128]{1,0:T(8,128)S(1)}) custom-call(s32[1]{0:T(128)} %bitcast.2.refs_1_.refs_0_, bf16[512,1024]{1,0:T(8,128)(2,1)S(1)} %inside_own.1.refs_3_.refs_1_, bf16[512,256]{1,0:T(8,128)(2,1)S(1)} %get-tuple-element.43.refs_1_.refs_2_.refs_3_, f32[512,16]{1,0:T(8,128)S(1)} %get-tuple-element.49.refs_3_, ...), custom_call_target="tpu_custom_call" | custom-call | flops 3849999872 | bytes 3500000 | tf_op jit(solution)/shard_map/part/pallas_call | solution.py:48
  45.9 1.5 %finish.1 = (bf16[512,512]{1,0:T(8,128)(2,1)S(1)}, bf16[512,1024]{1,0:T(8,128)(2,1)S(1)}, f32[512,128]{1,0:T(8,128)S(1)}) custom-call(s32[1]{0:T(128)} %bitcast.refs_0_, s32[1]{0:T(128)} %bitcast.2.refs_1_.refs_0_, bf16[512,1024]{1,0:T(8,128)(2,1)S(1)} %inside_other.1.refs_9_.refs_2_, bf16[512,256]{1,0:T(8,128)(2,1)S(1)} %get-tuple-element.43.refs_1_.refs_2_.refs_3_, ...), custom_call_target="tpu_custom_call" | custom-call | flops 3849999872 | bytes 3500000 | tf_op jit(solution)/shard_map/finish/pallas_call | solution.py:48
  47.5 0.7 %own_half.1.refs_0_ = bf16[512,512]{1,0:T(8,128)(2,1)S(1)} custom-call(s32[1]{0:T(128)} %bitcast.refs_0_, bf16[512,1024]{1,0:T(8,128)(2,1)S(1)} %get-tuple-element.60.refs_1_, bf16[1024,1024]{1,0:T(8,128)(2,1)S(1)} %collective-permute-done.11.refs_9_.refs_2_, f32[512,1024]{1,0:T(8,128)S(1)} %get-tuple-element.58.refs_10_.refs_3_, ...), custom_call_target="tpu_custom_call" | custom-call | flops 770000000 | bytes 700000 | tf_op jit(solution)/shard_map/own_half/pallas_call | solution.py:48
  48.2 1.1 %collective-permute-done.13.refs_1_ = bf16[512,512]{1,0:T(8,128)(2,1)S(1)} collective-permute-done((bf16[512,512]{1,0:T(8,128)(2,1)S(1)}, bf16[512,512]{1,0:T(8,128)(2,1)S(1)}, u32[]{:S(2)}, u32[]{:S(2)}) %collective-permute-start.13) | collective-permute-done | bytes 524320 | tf_op jit(solution)/shard_map/ppermute | solution.py:802
  49.4 0.8 %total.1 = bf16[512,512]{1,0:T(8,128)(2,1)} custom-call(bf16[512,512]{1,0:T(8,128)(2,1)S(1)} %own_half.1.refs_0_, bf16[512,512]{1,0:T(8,128)(2,1)S(1)} %collective-permute-done.13.refs_1_), custom_call_target="tpu_custom_call" | custom-call | flops 880000000 | bytes 800000 | tf_op jit(solution)/shard_map/total/pallas_call | solution.py:48
  (32 shorter events, 1.7 us)
Async XLA Ops:
  0.0 15.8 %collective-permute-start.1 = (bf16[1024,1024]{1,0:T(8,128)(2,1)}, bf16[1024,1024]{1,0:T(8,128)(2,1)S(1)}, u32[]{:S(2)}, u32[]{:S(2)}) collective-permute-start(bf16[1024,1024]{1,0:T(8,128)(2,1)} %refs_5_.3), channel_id=1, source_target_pairs={{0,1},{1,0},{2,3},{3,2},{4,5},{5,4},{6,7},{7,6},{8,9},{9,8},{10,11... | collective-permute-start | bytes 6291464 | tf_op jit(solution)/shard_map/ppermute | solution.py:802
  0.5 20.2 %collective-permute-start.5 = (bf16[1024,1024]{1,0:T(8,128)(2,1)}, bf16[1024,1024]{1,0:T(8,128)(2,1)S(1)}, u32[]{:S(2)}, u32[]{:S(2)}) collective-permute-start(bf16[1024,1024]{1,0:T(8,128)(2,1)} %refs_1_.1), channel_id=1, source_target_pairs={{0,1},{1,0},{2,3},{3,2},{4,5},{5,4},{6,7},{7,6},{8,9},{9,8},{10,11... | collective-permute-start | bytes 6291464 | tf_op jit(solution)/shard_map/ppermute | solution.py:802
  0.5 5.8 %copy-start.2 = (bf16[1024,1024]{1,0:T(8,128)(2,1)S(1)}, bf16[1024,1024]{1,0:T(8,128)(2,1)}, u32[]{:S(2)}) copy-start(bf16[1024,1024]{1,0:T(8,128)(2,1)} %refs_8_.1) | copy-start | bytes 6291460
  0.5 6.3 %copy-start.1 = (bf16[1024,1024]{1,0:T(8,128)(2,1)S(1)}, bf16[1024,1024]{1,0:T(8,128)(2,1)}, u32[]{:S(2)}) copy-start(bf16[1024,1024]{1,0:T(8,128)(2,1)} %refs_1_.1) | copy-start | bytes 6291460
  3.2 5.0 %collective-permute-start = (bf16[16,1024]{1,0:T(8,128)(2,1)S(1)}, bf16[16,1024]{1,0:T(8,128)(2,1)S(1)}, u32[]{:S(2)}, u32[]{:S(2)}) collective-permute-start(bf16[16,1024]{1,0:T(8,128)(2,1)S(1)} %get-tuple-element.37), channel_id=1, source_target_pairs={{0,2},{1,0},{2,4},{3,1},{4,6},{5,3},{6,8},{7,5},{8,10},{9,7},{10,1... | collective-permute-start | bytes 98312 | tf_op jit(solution)/shard_map/ppermute | solution.py:553
  6.3 9.5 %collective-permute-start.2 = (f32[24,1024]{1,0:T(8,128)S(1)}, f32[24,1024]{1,0:T(8,128)S(1)}, u32[]{:S(2)}, u32[]{:S(2)}) collective-permute-start(f32[24,1024]{1,0:T(8,128)S(1)} %get-tuple-element.40.refs_6_.refs_7_), channel_id=1, source_target_pairs={{0,1},{1,0},{2,3},{3,2},{4,5},{5,4},{6,7},{7,6},{8,9},{9,8},{10,11... | collective-permute-start | bytes 294920 | tf_op jit(solution)/shard_map/ppermute | solution.py:802
  6.3 39.6 %collective-permute-start.11 = (bf16[1024,1024]{1,0:T(8,128)(2,1)S(1)}, bf16[1024,1024]{1,0:T(8,128)(2,1)S(1)}, u32[]{:S(2)}, u32[]{:S(2)}) collective-permute-start(bf16[1024,1024]{1,0:T(8,128)(2,1)S(1)} %copy-done.2), channel_id=1, source_target_pairs={{0,1},{1,0},{2,3},{3,2},{4,5},{5,4},{6,7},{7,6},{8,9},{9,8},{10,11... | collective-permute-start | bytes 6291464 | tf_op jit(solution)/shard_map/ppermute | solution.py:802
  6.8 1.5 %copy-start.3 = (bf16[1024,256]{1,0:T(8,128)(2,1)S(1)}, bf16[1024,256]{1,0:T(8,128)(2,1)}, u32[]{:S(2)}) copy-start(bf16[1024,256]{1,0:T(8,128)(2,1)} %refs_3_.3) | copy-start | bytes 1572868
  6.8 1.5 %copy-start.4 = (f32[4,256]{1,0:T(4,128)S(1)}, f32[4,256]{1,0:T(4,128)}, u32[]{:S(2)}) copy-start(f32[4,256]{1,0:T(4,128)} %refs_4_.1) | copy-start | bytes 12292
  8.2 1.6 %copy-start = (bf16[1024,1024]{1,0:T(8,128)(2,1)S(1)}, bf16[1024,1024]{1,0:T(8,128)(2,1)}, u32[]{:S(2)}) copy-start(bf16[1024,1024]{1,0:T(8,128)(2,1)} %refs_5_.3) | copy-start | bytes 6291460
  14.2 7.9 %collective-permute-start.4 = (bf16[144,512]{1,0:T(8,128)(2,1)S(1)}, bf16[144,512]{1,0:T(8,128)(2,1)S(1)}, u32[]{:S(2)}, u32[]{:S(2)}) collective-permute-start(bf16[144,512]{1,0:T(8,128)(2,1)S(1)} %get-tuple-element.51), channel_id=1, source_target_pairs={{0,2},{2,0},{4,6},{6,4},{8,10},{10,8},{12,14},{14,12},{1,3},{3,1},... | collective-permute-start | bytes 442376 | tf_op jit(solution)/shard_map/ppermute | solution.py:561
  20.1 7.8 %collective-permute-start.3 = (bf16[144,512]{1,0:T(8,128)(2,1)S(1)}, bf16[144,512]{1,0:T(8,128)(2,1)S(1)}, u32[]{:S(2)}, u32[]{:S(2)}) collective-permute-start(bf16[144,512]{1,0:T(8,128)(2,1)S(1)} %get-tuple-element.47), channel_id=1, source_target_pairs={{0,2},{2,0},{4,6},{6,4},{8,10},{10,8},{12,14},{14,12},{1,3},{3,1},... | collective-permute-start | bytes 442376 | tf_op jit(solution)/shard_map/ppermute | solution.py:561
  22.2 7.4 %collective-permute-start.7 = (bf16[144,512]{1,0:T(8,128)(2,1)S(1)}, bf16[144,512]{1,0:T(8,128)(2,1)S(1)}, u32[]{:S(2)}, u32[]{:S(2)}) collective-permute-start(bf16[144,512]{1,0:T(8,128)(2,1)S(1)} %pair_own.1.refs_5_.refs_1_), channel_id=1, source_target_pairs={{0,4},{1,0},{2,6},{3,2},{4,8},{5,1},{6,10},{7,3},{8,12},{9,5},{10,... | collective-permute-start | bytes 442376 | tf_op jit(solution)/shard_map/ppermute | solution.py:553
  28.0 4.3 %collective-permute-start.6 = (bf16[144,512]{1,0:T(8,128)(2,1)S(1)}, bf16[144,512]{1,0:T(8,128)(2,1)S(1)}, u32[]{:S(2)}, u32[]{:S(2)}) collective-permute-start(bf16[144,512]{1,0:T(8,128)(2,1)S(1)} %pair_other.1.refs_3_.refs_1_), channel_id=1, source_target_pairs={{0,4},{1,0},{2,6},{3,2},{4,8},{5,1},{6,10},{7,3},{8,12},{9,5},{10,... | collective-permute-start | bytes 442376 | tf_op jit(solution)/shard_map/ppermute | solution.py:553
  29.6 7.8 %collective-permute-start.9 = (bf16[144,512]{1,0:T(8,128)(2,1)S(1)}, bf16[144,512]{1,0:T(8,128)(2,1)S(1)}, u32[]{:S(2)}, u32[]{:S(2)}) collective-permute-start(bf16[144,512]{1,0:T(8,128)(2,1)S(1)} %chain_own.1.refs_3_), channel_id=1, source_target_pairs={{0,8},{1,0},{2,10},{3,2},{4,12},{5,4},{6,14},{7,6},{8,9},{9,1},{10... | collective-permute-start | bytes 442376 | tf_op jit(solution)/shard_map/ppermute | solution.py:553
  32.3 7.8 %collective-permute-start.8 = (bf16[144,512]{1,0:T(8,128)(2,1)S(1)}, bf16[144,512]{1,0:T(8,128)(2,1)S(1)}, u32[]{:S(2)}, u32[]{:S(2)}) collective-permute-start(bf16[144,512]{1,0:T(8,128)(2,1)S(1)} %chain_other.1.refs_5_), channel_id=1, source_target_pairs={{0,8},{1,0},{2,10},{3,2},{4,12},{5,4},{6,14},{7,6},{8,9},{9,1},{10... | collective-permute-start | bytes 442376 | tf_op jit(solution)/shard_map/ppermute | solution.py:553
  37.6 6.3 %collective-permute-start.12 = (bf16[128,512]{1,0:T(8,128)(2,1)S(1)}, bf16[128,512]{1,0:T(8,128)(2,1)S(1)}, u32[]{:S(2)}, u32[]{:S(2)}) collective-permute-start(bf16[128,512]{1,0:T(8,128)(2,1)S(1)} %get-tuple-element.57), channel_id=1, source_target_pairs={{0,2},{2,0},{4,6},{6,4},{8,10},{10,8},{12,14},{14,12},{1,3},{3,1},... | collective-permute-start | bytes 393224 | tf_op jit(solution)/shard_map/ppermute | solution.py:627
  40.2 5.6 %collective-permute-start.10 = (bf16[128,512]{1,0:T(8,128)(2,1)S(1)}, bf16[128,512]{1,0:T(8,128)(2,1)S(1)}, u32[]{:S(2)}, u32[]{:S(2)}) collective-permute-start(bf16[128,512]{1,0:T(8,128)(2,1)S(1)} %get-tuple-element.55), channel_id=1, source_target_pairs={{0,2},{2,0},{4,6},{6,4},{8,10},{10,8},{12,14},{14,12},{1,3},{3,1},... | collective-permute-start | bytes 393224 | tf_op jit(solution)/shard_map/ppermute | solution.py:627
  47.4 2.0 %collective-permute-start.13 = (bf16[512,512]{1,0:T(8,128)(2,1)S(1)}, bf16[512,512]{1,0:T(8,128)(2,1)S(1)}, u32[]{:S(2)}, u32[]{:S(2)}) collective-permute-start(bf16[512,512]{1,0:T(8,128)(2,1)S(1)} %get-tuple-element.62.refs_5_), channel_id=1, source_target_pairs={{0,1},{1,0},{2,3},{3,2},{4,5},{5,4},{6,7},{7,6},{8,9},{9,8},{10,11... | collective-permute-start | bytes 1572872 | tf_op jit(solution)/shard_map/ppermute | solution.py:802

commit v11 on v10

--- a/solution.py
+++ b/solution.py
@@ -403,8 +403,8 @@
     )(place, parity, normed, halo, bt, w_inner, small)
 
 
-def inside_kernel(head_size, x_ref, bc_ref, bt_ref, cum_ref, times_ref, y_ref, state_ref):
-    rows, inner = x_ref.shape
+def inside_kernel(head_size, head, x_ref, bc_ref, bt_ref, cum_ref, times_ref, y_ref, state_ref):
+    rows, width = y_ref.shape
     states = bc_ref.shape[1] // 2
     heads = cum_ref.shape[1]
     length = CHUNK
@@ -426,14 +426,16 @@
         end = cumt[:, last:]
         since = two_rows(jnp.exp(cumt - before)).T.astype(BF16)
         left = two_rows(step * jnp.exp(end - cumt)).T.astype(BF16)
-        for first in range(0, heads, TILE // head_size):
+        for offset in range(0, width, TILE):
+            first = head + offset // head_size
             columns = slice(first * head_size, first * head_size + TILE)
+            here = slice(offset, offset + TILE)
             onehot = head_matrix(heads, TILE, head_size, first)
             since_here = dot(since, onehot)
-            state = state_ref[:, columns]
+            state = state_ref[:, here]
             carried = dot(cmat, state.astype(BF16)) * since_here
             scaled = (x_ref[at, columns].astype(F32) * dot(left, onehot)).astype(BF16)
-            state_ref[:, columns] = state * since_here[last:, :] + dot(bmat, scaled)
+            state_ref[:, here] = state * since_here[last:, :] + dot(bmat, scaled)
             for start in range(0, TILE, pair):
                 low = first * head_size + start
                 weights = []
@@ -446,7 +448,9 @@
                     [jnp.where(lane < head_size, mine, none), jnp.where(lane < head_size, none, mine)], axis=0
                 )
                 inside = dot(jnp.concatenate(weights, axis=1), stacked)
-                y_ref[at, low : low + pair] = (inside + carried[:, start : start + pair]).astype(BF16)
+                y_ref[at, offset + start : offset + start + pair] = (
+                    inside + carried[:, start : start + pair]
+                ).astype(BF16)
         return end
 
     before = jnp.zeros((heads, 1), F32)
@@ -454,21 +458,39 @@
         before = chunk(c, before)
 
 
-def inside_call(tag, x, bc, bt, cum, times, after=()):
+def inside_call(tag, x, bc, bt, cum, times, after=(), part=0, parts=1):
     rows, inner = x.shape
     heads = cum.shape[1]
     both = bc.shape[1]
+    width = inner // parts
     return call(
-        functools.partial(inside_kernel, inner // heads),
+        functools.partial(inside_kernel, inner // heads, part * heads // parts),
         "inside_" + tag,
         vmem=8,
-        cost=micros(3.2),
+        cost=micros(3.2 / parts),
         in_specs=[VMEM] * 5,
         out_specs=VMEM,
-        out_shape=jax.ShapeDtypeStruct((rows, inner), BF16),
-        scratch=[pltpu.VMEM((both // 2, inner), F32)],
+        out_shape=jax.ShapeDtypeStruct((rows, width), BF16),
+        scratch=[pltpu.VMEM((both // 2, width), F32)],
         after=after,
     )(x, bc, bt, cum, times)
+
+
+def mark_kernel(rows_ref, out_ref):
+    out_ref[...] = rows_ref[: out_ref.shape[0], : out_ref.shape[1]]
+
+
+def mark_call(value, after):
+    return call(
+        mark_kernel,
+        "mark",
+        vmem=4,
+        cost=micros(2.4),
+        in_specs=[VMEM],
+        out_specs=VMEM,
+        out_shape=jax.ShapeDtypeStruct((HALO, 128), value.dtype),
+        after=after,
+    )(value)
 
 
 def parts_of(ref, known=None):
@@ -628,9 +650,10 @@
 
 
 def gated_part(
-    head_size, swap, y_ref, bc_ref, cum_ref, keep_ref, other_ref, gate_ref, small_ref, wo_ref, scaled_ref, tile_ref
+    head_size, swap, y_refs, bc_ref, cum_ref, keep_ref, other_ref, gate_ref, small_ref, wo_ref, scaled_ref, tile_ref
 ):
-    rows, inner = y_ref.shape
+    rows, share = y_refs[0].shape
+    inner = share * len(y_refs)
     states = bc_ref.shape[1] // 2
     heads = cum_ref.shape[1]
     half = inner // 2
@@ -638,6 +661,8 @@
     squares = [0.0] * (rows // BLOCK)
     for low in range(0, inner, TILE):
         columns = slice(low, low + TILE)
+        y_ref = y_refs[low // share]
+        of_share = slice(low % share, low % share + TILE)
         here = slice(low % half, low % half + TILE)
         use_other = swap if low < half else jnp.logical_not(swap)
         entry = jnp.where(use_other, other_ref[:, here], keep_ref[:, here])
@@ -646,16 +671,16 @@
         gain = small_ref[SMALL_TAPS : SMALL_TAPS + 1, columns]
         for i, r in enumerate(range(0, rows, BLOCK)):
             block = slice(r, r + BLOCK)
-            gated = y_ref[block, columns].astype(F32) + tile_ref[0, block, :] * tile_ref[1, block, :]
+            gated = y_ref[block, of_share].astype(F32) + tile_ref[0, block, :] * tile_ref[1, block, :]
             gated = gated * gate_ref[block, columns].astype(F32)
             squares[i] += jnp.sum(gated * gated, axis=-1, keepdims=True)
             scaled_ref[block, columns] = (gated * gain).astype(BF16)
     return squares
 
 
-def part_kernel(head_size, parity_ref, *refs):
+def part_kernel(head_size, shares, parity_ref, *refs):
     *ins, out_ref, sq_ref, scaled_ref, tile_ref = refs
-    squares = gated_part(head_size, parity_ref[0] == 1, *ins, scaled_ref, tile_ref)
+    squares = gated_part(head_size, parity_ref[0] == 1, ins[:shares], *ins[shares:], scaled_ref, tile_ref)
     for i, square in enumerate(squares):
         sq_ref[i * BLOCK : (i + 1) * BLOCK, :] = jnp.broadcast_to(square, (BLOCK, sq_ref.shape[1]))
     for low in range(0, out_ref.shape[1], TILE):
@@ -687,9 +712,9 @@
         out_ref[...] = half_ref[...]
 
 
-def finish_kernel(head_size, full_width, back_ref, parity_ref, *refs):
+def finish_kernel(head_size, shares, full_width, back_ref, parity_ref, *refs):
     *ins, part_ref, psq_ref, send_ref, scaled_ref, scale_ref, tile_ref, half_ref = refs
-    squares = gated_part(head_size, parity_ref[0] == 1, *ins, scaled_ref, tile_ref)
+    squares = gated_part(head_size, parity_ref[0] == 1, ins[:shares], *ins[shares:], scaled_ref, tile_ref)
     for i, square in enumerate(squares):
         block = slice(i * BLOCK, (i + 1) * BLOCK)
         scale = lax.rsqrt((square + psq_ref[block, :1]) / full_width + EPS)
@@ -718,22 +743,23 @@
     )(back, scaled, w_output, part, scale)
 
 
-def finish_call(back, parity, y, bc, cum, keep, other, gate, small, w_output, full_width=None, partial=None, after=()):
-    rows, inner = y.shape
+def finish_call(back, parity, ys, bc, cum, keep, other, gate, small, w_output, full_width=None, partial=None, after=()):
+    rows = ys[0].shape[0]
+    inner = ys[0].shape[1] * len(ys)
     width = w_output.shape[1]
     half = width // 2
     heads = cum.shape[1]
-    arrays = [y, bc, cum, keep, other, gate, small, w_output]
+    arrays = [*ys, bc, cum, keep, other, gate, small, w_output]
     tiles = pltpu.VMEM((2, rows, TILE), F32)
     if partial is None:
         scratch = [pltpu.VMEM((rows, inner), BF16), tiles]
         scalars = (parity,)
-        kernel = functools.partial(part_kernel, inner // heads)
+        kernel = functools.partial(part_kernel, inner // heads, len(ys))
         out_shape = [jax.ShapeDtypeStruct((rows, width), F32), jax.ShapeDtypeStruct((rows, 128), F32)]
     else:
         scalars = (back, parity)
         scratch = [tiles, pltpu.VMEM((rows, half), BF16)]
-        kernel = functools.partial(finish_kernel, inner // heads, full_width)
+        kernel = functools.partial(finish_kernel, inner // heads, len(ys), full_width)
         arrays += list(partial)
         out_shape = [
             jax.ShapeDtypeStruct((rows, half), BF16),
@@ -826,17 +852,20 @@
         "other", place, parity, normed, halo, bt, w_inner_2, small_2, after=[mine_1]
     )
     chain_2 = Chain("other", place, send_2, mine_2)
-    gate_2 = gate_call("other", normed, w_gate_2, after=[x_2])
-    done = chain_1.pair(after=[gate_2])
+    done = mark_call(normed, after=[x_2])
+    done = chain_1.pair(after=[done])
     y_1 = inside_call("own", x_1, bc, bt, cum_1, times_1, after=[done])
     done = chain_2.pair(after=[y_1])
     done = chain_1.middle(after=[done])
-    done = chain_2.middle(after=[done])
+    gate_2 = gate_call("other", normed, w_gate_2, after=[done])
+    done = chain_2.middle(after=[gate_2])
     entry_1 = chain_1.entry(after=[done])
-    entry_2 = chain_2.entry(after=[entry_1[0]])
-    y_2 = inside_call("other", x_2, bc, bt, cum_2, times_2, after=[entry_2[0]])
+    scan_2 = ("other", x_2, bc, bt, cum_2, times_2)
+    y_2 = [inside_call(*scan_2, after=[entry_1[0]], part=0, parts=2)]
+    entry_2 = chain_2.entry(after=y_2)
+    y_2.append(inside_call(*scan_2, after=[entry_2[0]], part=1, parts=2))
     partial = finish_call(
-        back, parity, y_1, bc, cum_1, *entry_1, gate_1, small, w_output, after=[y_2]
+        back, parity, [y_1], bc, cum_1, *entry_1, gate_1, small, w_output, after=y_2
     )
     full_width = float(w_inner.shape[1] * lax.axis_size("ch"))
     send, scaled, scale = finish_call(

time: 50.5 us -> 48 us (0.950)
  waiting for transfers between devices: 5.45 us -> 1.5 us
  Pallas kernels: 27.4 us -> 28.1 us
  starting transfers between devices: 16.6 us -> 17.3 us
    ppermute x5, waiting for transfers between devices: 3.93 us -> 0.01 us  [onward(): return lax.ppermute(value, ('seq', 'ch'), pairs)]
    ppermute x2, starting transfers between devices: 0.14 us -> 2.16 us  [entry(): return (keep, lax.ppermute(out, 'seq', self.swap))]
    ppermute x5, starting transfers between devices: 13.2 us -> 11.8 us  [onward(): return lax.ppermute(value, ('seq', 'ch'), pairs)]
    pallas_call x18 -> x20, Pallas kernels: 27.4 us -> 28.1 us  [call(): return lambda *arrays: run(*arrays, *after)]
  transfers between devices with their start and end apart: 14 -> 14, of which waited for: 4 -> 3; matrix products, arithmetic and copies ran while one was open for 0% -> 0% of each run, Pallas kernels for 50% -> 54%
where the time goes in v11:
time: 48 us; the launch traced here: 47.9 us
  Pallas kernels  28.1 us (59%)
  starting transfers between devices  17.3 us (36%)
  waiting for transfers between devices  1.5 us (3%)
  local copies, waits for them, and re-layouts  0.65 us (1%)
    pallas_call x20, Pallas kernels, call(): return lambda *arrays: run(*arrays, *after)  28.1 us
    ppermute x5, starting transfers between devices, onward(): return lax.ppermute(value, ('seq', 'ch'), pairs)  11.8 us
    ppermute x2, starting transfers between devices, entry(): return (keep, lax.ppermute(out, 'seq', self.swap))  2.16 us
    ppermute x2, starting transfers between devices, __init__(): self.other = lax.ppermute(send, 'seq', self.swap)  2.14 us
    ppermute x5, waiting for transfers between devices, theirs(): return lax.ppermute(a, 'ch', swap)  1.15 us
    ppermute x5, starting transfers between devices, theirs(): return lax.ppermute(a, 'ch', swap)  1.1 us
  transfers between devices with their start and end apart: 14, of which 3 were waited for; matrix products, arithmetic and copies ran while one was open for 0% of the time, Pallas kernels for 54%

profile of v11, /device:TPU:0, one launch (start us, length us, event | category | flops | bytes accessed | tf_op | source)
XLA Modules:
  0.0 47.9 jit_solution(9058209400401154221)
XLA Ops:
  0.5 2.7 %prepare.1 = (bf16[512,1024]{1,0:T(8,128)(2,1)S(1)}, bf16[16,1024]{1,0:T(8,128)(2,1)S(1)}, f32[24,1024]{1,0:T(8,128)S(1)}) custom-call(s32[1]{0:T(128)} %bitcast.refs_0_, s32[1]{0:T(128)} %bitcast.2.refs_1_.refs_0_, s32[1]{0:T(128)} %bitcast.1.refs_2_.refs_0_, bf16[512,1024]{1,0:T(8,128)(2,1)} %refs_3_.2, s32[1,512]{1,0:T(1,128)} %bitcast.10, ...), custom_call_target="tpu_custom_call" | custom-call | flops 2969999872 | bytes 2700000 | tf_op jit(solution)/shard_map/prepare/pallas_call | solution.py:48
  3.2 2.6 %collective-permute-start = (bf16[16,1024]{1,0:T(8,128)(2,1)S(1)}, bf16[16,1024]{1,0:T(8,128)(2,1)S(1)}, u32[]{:S(2)}, u32[]{:S(2)}) collective-permute-start(bf16[16,1024]{1,0:T(8,128)(2,1)S(1)} %get-tuple-element.37), channel_id=1, source_target_pairs={{0,2},{1,0},{2,4},{3,1},{4,6},{5,3},{6,8},{7,5},{8,10},{9,7},{10,1... | collective-permute-start | bytes 98312 | tf_op jit(solution)/shard_map/ppermute | solution.py:575
  5.8 0.5 %collective-permute-start.8 = (bf16[1024,1024]{1,0:T(8,128)(2,1)S(1)}, bf16[1024,1024]{1,0:T(8,128)(2,1)S(1)}, u32[]{:S(2)}, u32[]{:S(2)}) collective-permute-start(bf16[1024,1024]{1,0:T(8,128)(2,1)S(1)} %copy-done.1), channel_id=1, source_target_pairs={{0,1},{1,0},{2,3},{3,2},{4,5},{5,4},{6,7},{7,6},{8,9},{9,8},{10,11... | collective-permute-start | bytes 6291464 | tf_op jit(solution)/shard_map/ppermute | solution.py:828
  6.4 1.4 %gate_own.1.refs_5_.refs_6_ = bf16[512,1024]{1,0:T(8,128)(2,1)S(1)} custom-call(bf16[512,1024]{1,0:T(8,128)(2,1)S(1)} %get-tuple-element.36.refs_0_.refs_1_.refs_2_, bf16[1024,1024]{1,0:T(8,128)(2,1)S(1)} %copy-done.1), custom_call_target="tpu_custom_call" | custom-call | flops 2640000000 | bytes 2400000 | tf_op jit(solution)/shard_map/gate_own/pallas_call | solution.py:48
  7.9 0.9 %maps.1 = (bf16[512,256]{1,0:T(8,128)(2,1)S(1)}, bf16[128,512]{1,0:T(8,128)(2,1)S(1)}) custom-call(s32[1]{0:T(128)} %bitcast.1.refs_2_.refs_0_, bf16[512,1024]{1,0:T(8,128)(2,1)S(1)} %get-tuple-element.36.refs_0_.refs_1_.refs_2_, bf16[16,1024]{1,0:T(8,128)(2,1)S(1)} %collective-permute-done.refs_2_.refs_3_, bf16[1024,256]{1,0:T(8,128)(2,1)S(1)} %copy-done.3, ...), custom_call_target="tpu_custom_call" | custom-call | flops 1650000000 | bytes 1500000 | tf_op jit(solution)/shard_map/maps/pallas_call | solution.py:48
  8.8 0.6 %copy-done = bf16[1024,1024]{1,0:T(8,128)(2,1)S(1)} copy-done((bf16[1024,1024]{1,0:T(8,128)(2,1)S(1)}, bf16[1024,1024]{1,0:T(8,128)(2,1)}, u32[]{:S(2)}) %copy-start) | copy-done | bytes 2097176
  9.4 4.3 %local_own.1 = (bf16[512,1024]{1,0:T(8,128)(2,1)S(1)}, f32[512,16]{1,0:T(8,128)S(1)}, f32[32,512]{1,0:T(8,128)S(1)}, bf16[144,512]{1,0:T(8,128)(2,1)S(1)}, bf16[144,512]{1,0:T(8,128)(2,1)S(1)}) custom-call(s32[1]{0:T(128)} %bitcast.1.refs_2_.refs_0_, s32[1]{0:T(128)} %bitcast.2.refs_1_.refs_0_, ...), custom_call_target="tpu_custom_call" | custom-call | flops 5500000256 | bytes 5000000 | tf_op jit(solution)/shard_map/local_own/pallas_call | solution.py:48
  13.7 2.0 %collective-permute-start.3 = (bf16[144,512]{1,0:T(8,128)(2,1)S(1)}, bf16[144,512]{1,0:T(8,128)(2,1)S(1)}, u32[]{:S(2)}, u32[]{:S(2)}) collective-permute-start(bf16[144,512]{1,0:T(8,128)(2,1)S(1)} %get-tuple-element.46), channel_id=1, source_target_pairs={{0,2},{2,0},{4,6},{6,4},{8,10},{10,8},{12,14},{14,12},{1,3},{3,1},... | collective-permute-start | bytes 442376 | tf_op jit(solution)/shard_map/ppermute | solution.py:583
  15.8 4.3 %local_other.1 = (bf16[512,1024]{1,0:T(8,128)(2,1)S(1)}, f32[512,16]{1,0:T(8,128)S(1)}, f32[32,512]{1,0:T(8,128)S(1)}, bf16[144,512]{1,0:T(8,128)(2,1)S(1)}, bf16[144,512]{1,0:T(8,128)(2,1)S(1)}) custom-call(s32[1]{0:T(128)} %bitcast.1.refs_2_.refs_0_, s32[1]{0:T(128)} %bitcast.2.refs_1_.refs_0_, ...), custom_call_target="tpu_custom_call" | custom-call | flops 5500000256 | bytes 5000000 | tf_op jit(solution)/shard_map/local_other/pallas_call | solution.py:48
  20.4 3.0 %collective-permute-start.4 = (bf16[144,512]{1,0:T(8,128)(2,1)S(1)}, bf16[144,512]{1,0:T(8,128)(2,1)S(1)}, u32[]{:S(2)}, u32[]{:S(2)}) collective-permute-start(bf16[144,512]{1,0:T(8,128)(2,1)S(1)} %pair_own.1.refs_5_.refs_1_), channel_id=1, source_target_pairs={{0,4},{1,0},{2,6},{3,2},{4,8},{5,1},{6,10},{7,3},{8,12},{9,5},{10,... | collective-permute-start | bytes 442376 | tf_op jit(solution)/shard_map/ppermute | solution.py:575
  23.4 3.4 %inside_own.1.refs_3_.refs_1_ = bf16[512,1024]{1,0:T(8,128)(2,1)S(1)} custom-call(bf16[512,1024]{1,0:T(8,128)(2,1)S(1)} %get-tuple-element.49.refs_0_, bf16[512,256]{1,0:T(8,128)(2,1)S(1)} %get-tuple-element.43.refs_1_.refs_2_.refs_4_, bf16[128,512]{1,0:T(8,128)(2,1)S(1)} %get-tuple-element.38.refs_4_.refs_2_, f32[512,16]{1,0:T(8,128)S(1)} %get-tuple-element.50.refs_3_, ...), custom_call_target="tpu_custom_call" | custom-call | flops 3520000000 | bytes 3200000 | tf_op jit(solution)/shard_map/inside_own/pallas_call | solution.py:48
  26.8 1.6 %collective-permute-start.7 = (bf16[144,512]{1,0:T(8,128)(2,1)S(1)}, bf16[144,512]{1,0:T(8,128)(2,1)S(1)}, u32[]{:S(2)}, u32[]{:S(2)}) collective-permute-start(bf16[144,512]{1,0:T(8,128)(2,1)S(1)} %pair_other.1.refs_3_.refs_1_), channel_id=1, source_target_pairs={{0,4},{1,0},{2,6},{3,2},{4,8},{5,1},{6,10},{7,3},{8,12},{9,5},{10,... | collective-permute-start | bytes 442376 | tf_op jit(solution)/shard_map/ppermute | solution.py:575
  28.5 1.9 %collective-permute-start.6 = (bf16[144,512]{1,0:T(8,128)(2,1)S(1)}, bf16[144,512]{1,0:T(8,128)(2,1)S(1)}, u32[]{:S(2)}, u32[]{:S(2)}) collective-permute-start(bf16[144,512]{1,0:T(8,128)(2,1)S(1)} %chain_own.1.refs_2_), channel_id=1, source_target_pairs={{0,8},{1,0},{2,10},{3,2},{4,12},{5,4},{6,14},{7,6},{8,9},{9,1},{10... | collective-permute-start | bytes 442376 | tf_op jit(solution)/shard_map/ppermute | solution.py:575
  30.5 1.4 %gate_other.1.refs_3_.refs_8_ = bf16[512,1024]{1,0:T(8,128)(2,1)S(1)} custom-call(bf16[512,1024]{1,0:T(8,128)(2,1)S(1)} %get-tuple-element.36.refs_0_.refs_1_.refs_2_, bf16[1024,1024]{1,0:T(8,128)(2,1)S(1)} %collective-permute-done.8.refs_1_, bf16[144,512]{1,0:T(8,128)(2,1)S(1)} %chain_own.1.refs_2_), custom_call_target="tpu_custom_call" | custom-call | flops 2640000000 | bytes 2400000 | tf_op jit(solution)/shard_map/gate_other/pallas_call | solution.py:48
  32.0 2.7 %collective-permute-start.9 = (bf16[144,512]{1,0:T(8,128)(2,1)S(1)}, bf16[144,512]{1,0:T(8,128)(2,1)S(1)}, u32[]{:S(2)}, u32[]{:S(2)}) collective-permute-start(bf16[144,512]{1,0:T(8,128)(2,1)S(1)} %chain_other.1.refs_5_), channel_id=1, source_target_pairs={{0,8},{1,0},{2,10},{3,2},{4,12},{5,4},{6,14},{7,6},{8,9},{9,1},{10... | collective-permute-start | bytes 442376 | tf_op jit(solution)/shard_map/ppermute | solution.py:575
  34.9 0.7 %collective-permute-start.12 = (bf16[128,512]{1,0:T(8,128)(2,1)S(1)}, bf16[128,512]{1,0:T(8,128)(2,1)S(1)}, u32[]{:S(2)}, u32[]{:S(2)}) collective-permute-start(bf16[128,512]{1,0:T(8,128)(2,1)S(1)} %get-tuple-element.57), channel_id=1, source_target_pairs={{0,2},{2,0},{4,6},{6,4},{8,10},{10,8},{12,14},{14,12},{1,3},{3,1},... | collective-permute-start | bytes 393224 | tf_op jit(solution)/shard_map/ppermute | solution.py:649
  35.5 2.0 %inside_other.2.refs_5_.refs_9_.refs_2_ = bf16[512,512]{1,0:T(8,128)(2,1)S(1)} custom-call(bf16[512,1024]{1,0:T(8,128)(2,1)S(1)} %get-tuple-element.42.refs_1_.refs_0_, bf16[512,256]{1,0:T(8,128)(2,1)S(1)} %get-tuple-element.43.refs_1_.refs_2_.refs_4_, bf16[128,512]{1,0:T(8,128)(2,1)S(1)} %get-tuple-element.38.refs_4_.refs_2_, ...), custom_call_target="tpu_custom_call" | custom-call | flops 1760000000 | bytes 1600000 | tf_op jit(solution)/shard_map/inside_other/pallas_call | solution.py:48
  37.7 1.5 %collective-permute-start.10 = (bf16[128,512]{1,0:T(8,128)(2,1)S(1)}, bf16[128,512]{1,0:T(8,128)(2,1)S(1)}, u32[]{:S(2)}, u32[]{:S(2)}) collective-permute-start(bf16[128,512]{1,0:T(8,128)(2,1)S(1)} %get-tuple-element.55), channel_id=1, source_target_pairs={{0,2},{2,0},{4,6},{6,4},{8,10},{10,8},{12,14},{14,12},{1,3},{3,1},... | collective-permute-start | bytes 393224 | tf_op jit(solution)/shard_map/ppermute | solution.py:649
  39.1 2.0 %inside_other.3.refs_10_.refs_3_ = bf16[512,512]{1,0:T(8,128)(2,1)S(1)} custom-call(bf16[512,1024]{1,0:T(8,128)(2,1)S(1)} %get-tuple-element.42.refs_1_.refs_0_, bf16[512,256]{1,0:T(8,128)(2,1)S(1)} %get-tuple-element.43.refs_1_.refs_2_.refs_4_, bf16[128,512]{1,0:T(8,128)(2,1)S(1)} %get-tuple-element.38.refs_4_.refs_2_, ...), custom_call_target="tpu_custom_call" | custom-call | flops 1760000000 | bytes 1600000 | tf_op jit(solution)/shard_map/inside_other/pallas_call | solution.py:48
  41.1 2.0 %part.1 = (f32[512,1024]{1,0:T(8,128)S(1)}, f32[512,128]{1,0:T(8,128)S(1)}) custom-call(s32[1]{0:T(128)} %bitcast.2.refs_1_.refs_0_, bf16[512,1024]{1,0:T(8,128)(2,1)S(1)} %inside_own.1.refs_3_.refs_1_, bf16[512,256]{1,0:T(8,128)(2,1)S(1)} %get-tuple-element.43.refs_1_.refs_2_.refs_4_, f32[512,16]{1,0:T(8,128)S(1)} %get-tuple-element.50.refs_3_, ...), custom_call_target="tpu_custom_call" | custom-call | flops 3849999872 | bytes 3500000 | tf_op jit(solution)/shard_map/part/pallas_call | solution.py:48
  43.4 1.5 %finish.1 = (bf16[512,512]{1,0:T(8,128)(2,1)S(1)}, bf16[512,1024]{1,0:T(8,128)(2,1)S(1)}, f32[512,128]{1,0:T(8,128)S(1)}) custom-call(s32[1]{0:T(128)} %bitcast.refs_0_, s32[1]{0:T(128)} %bitcast.2.refs_1_.refs_0_, bf16[512,512]{1,0:T(8,128)(2,1)S(1)} %inside_other.2.refs_5_.refs_9_.refs_2_, bf16[512,512]{1,0:T(8,128)(2,1)S(1)} %inside_other.3.refs_10_.refs_3_, ...), custom_call_target="tpu_custom_call" | custom-call | flops 3849999872 | bytes 3500000 | tf_op jit(solution)/shard_map/finish/pallas_call | solution.py:48
  45.0 0.7 %own_half.1.refs_0_ = bf16[512,512]{1,0:T(8,128)(2,1)S(1)} custom-call(s32[1]{0:T(128)} %bitcast.refs_0_, bf16[512,1024]{1,0:T(8,128)(2,1)S(1)} %get-tuple-element.60.refs_1_, bf16[1024,1024]{1,0:T(8,128)(2,1)S(1)} %collective-permute-done.11.refs_10_.refs_2_, f32[512,1024]{1,0:T(8,128)S(1)} %get-tuple-element.58.refs_11_.refs_3_, ...), custom_call_target="tpu_custom_call" | custom-call | flops 770000000 | bytes 700000 | tf_op jit(solution)/shard_map/own_half/pallas_call | solution.py:48
  45.7 1.1 %collective-permute-done.13.refs_1_ = bf16[512,512]{1,0:T(8,128)(2,1)S(1)} collective-permute-done((bf16[512,512]{1,0:T(8,128)(2,1)S(1)}, bf16[512,512]{1,0:T(8,128)(2,1)S(1)}, u32[]{:S(2)}, u32[]{:S(2)}) %collective-permute-start.13) | collective-permute-done | bytes 524320 | tf_op jit(solution)/shard_map/ppermute | solution.py:828
  46.9 0.8 %total.1 = bf16[512,512]{1,0:T(8,128)(2,1)} custom-call(bf16[512,512]{1,0:T(8,128)(2,1)S(1)} %own_half.1.refs_0_, bf16[512,512]{1,0:T(8,128)(2,1)S(1)} %collective-permute-done.13.refs_1_), custom_call_target="tpu_custom_call" | custom-call | flops 880000000 | bytes 800000 | tf_op jit(solution)/shard_map/total/pallas_call | solution.py:48
  (34 shorter events, 1.7 us)
Async XLA Ops:
  0.0 15.8 %collective-permute-start.1 = (bf16[1024,1024]{1,0:T(8,128)(2,1)}, bf16[1024,1024]{1,0:T(8,128)(2,1)S(1)}, u32[]{:S(2)}, u32[]{:S(2)}) collective-permute-start(bf16[1024,1024]{1,0:T(8,128)(2,1)} %refs_5_.3), channel_id=1, source_target_pairs={{0,1},{1,0},{2,3},{3,2},{4,5},{5,4},{6,7},{7,6},{8,9},{9,8},{10,11... | collective-permute-start | bytes 6291464 | tf_op jit(solution)/shard_map/ppermute | solution.py:828
  0.5 5.3 %copy-start.1 = (bf16[1024,1024]{1,0:T(8,128)(2,1)S(1)}, bf16[1024,1024]{1,0:T(8,128)(2,1)}, u32[]{:S(2)}) copy-start(bf16[1024,1024]{1,0:T(8,128)(2,1)} %refs_1_.1) | copy-start | bytes 6291460
  0.5 5.8 %copy-start.2 = (bf16[1024,1024]{1,0:T(8,128)(2,1)S(1)}, bf16[1024,1024]{1,0:T(8,128)(2,1)}, u32[]{:S(2)}) copy-start(bf16[1024,1024]{1,0:T(8,128)(2,1)} %refs_8_.1) | copy-start | bytes 6291460
  3.2 4.6 %collective-permute-start = (bf16[16,1024]{1,0:T(8,128)(2,1)S(1)}, bf16[16,1024]{1,0:T(8,128)(2,1)S(1)}, u32[]{:S(2)}, u32[]{:S(2)}) collective-permute-start(bf16[16,1024]{1,0:T(8,128)(2,1)S(1)} %get-tuple-element.37), channel_id=1, source_target_pairs={{0,2},{1,0},{2,4},{3,1},{4,6},{5,3},{6,8},{7,5},{8,10},{9,7},{10,1... | collective-permute-start | bytes 98312 | tf_op jit(solution)/shard_map/ppermute | solution.py:575
  5.8 10.0 %collective-permute-start.2 = (f32[24,1024]{1,0:T(8,128)S(1)}, f32[24,1024]{1,0:T(8,128)S(1)}, u32[]{:S(2)}, u32[]{:S(2)}) collective-permute-start(f32[24,1024]{1,0:T(8,128)S(1)} %get-tuple-element.40.refs_6_.refs_7_), channel_id=1, source_target_pairs={{0,1},{1,0},{2,3},{3,2},{4,5},{5,4},{6,7},{7,6},{8,9},{9,8},{10,11... | collective-permute-start | bytes 294920 | tf_op jit(solution)/shard_map/ppermute | solution.py:828
  5.8 24.7 %collective-permute-start.8 = (bf16[1024,1024]{1,0:T(8,128)(2,1)S(1)}, bf16[1024,1024]{1,0:T(8,128)(2,1)S(1)}, u32[]{:S(2)}, u32[]{:S(2)}) collective-permute-start(bf16[1024,1024]{1,0:T(8,128)(2,1)S(1)} %copy-done.1), channel_id=1, source_target_pairs={{0,1},{1,0},{2,3},{3,2},{4,5},{5,4},{6,7},{7,6},{8,9},{9,8},{10,11... | collective-permute-start | bytes 6291464 | tf_op jit(solution)/shard_map/ppermute | solution.py:828
  6.3 36.8 %collective-permute-start.11 = (bf16[1024,1024]{1,0:T(8,128)(2,1)S(1)}, bf16[1024,1024]{1,0:T(8,128)(2,1)S(1)}, u32[]{:S(2)}, u32[]{:S(2)}) collective-permute-start(bf16[1024,1024]{1,0:T(8,128)(2,1)S(1)} %copy-done.2), channel_id=1, source_target_pairs={{0,1},{1,0},{2,3},{3,2},{4,5},{5,4},{6,7},{7,6},{8,9},{9,8},{10,11... | collective-permute-start | bytes 6291464 | tf_op jit(solution)/shard_map/ppermute | solution.py:828
  6.4 1.5 %copy-start.3 = (bf16[1024,256]{1,0:T(8,128)(2,1)S(1)}, bf16[1024,256]{1,0:T(8,128)(2,1)}, u32[]{:S(2)}) copy-start(bf16[1024,256]{1,0:T(8,128)(2,1)} %refs_3_.3) | copy-start | bytes 1572868
  6.4 1.5 %copy-start.4 = (f32[4,256]{1,0:T(4,128)S(1)}, f32[4,256]{1,0:T(4,128)}, u32[]{:S(2)}) copy-start(f32[4,256]{1,0:T(4,128)} %refs_4_.1) | copy-start | bytes 12292
  7.8 1.6 %copy-start = (bf16[1024,1024]{1,0:T(8,128)(2,1)S(1)}, bf16[1024,1024]{1,0:T(8,128)(2,1)}, u32[]{:S(2)}) copy-start(bf16[1024,1024]{1,0:T(8,128)(2,1)} %refs_5_.3) | copy-start | bytes 6291460
  13.7 6.6 %collective-permute-start.3 = (bf16[144,512]{1,0:T(8,128)(2,1)S(1)}, bf16[144,512]{1,0:T(8,128)(2,1)S(1)}, u32[]{:S(2)}, u32[]{:S(2)}) collective-permute-start(bf16[144,512]{1,0:T(8,128)(2,1)S(1)} %get-tuple-element.46), channel_id=1, source_target_pairs={{0,2},{2,0},{4,6},{6,4},{8,10},{10,8},{12,14},{14,12},{1,3},{3,1},... | collective-permute-start | bytes 442376 | tf_op jit(solution)/shard_map/ppermute | solution.py:583
  20.1 6.7 %collective-permute-start.5 = (bf16[144,512]{1,0:T(8,128)(2,1)S(1)}, bf16[144,512]{1,0:T(8,128)(2,1)S(1)}, u32[]{:S(2)}, u32[]{:S(2)}) collective-permute-start(bf16[144,512]{1,0:T(8,128)(2,1)S(1)} %get-tuple-element.48), channel_id=1, source_target_pairs={{0,2},{2,0},{4,6},{6,4},{8,10},{10,8},{12,14},{14,12},{1,3},{3,1},... | collective-permute-start | bytes 442376 | tf_op jit(solution)/shard_map/ppermute | solution.py:583
  20.4 8.0 %collective-permute-start.4 = (bf16[144,512]{1,0:T(8,128)(2,1)S(1)}, bf16[144,512]{1,0:T(8,128)(2,1)S(1)}, u32[]{:S(2)}, u32[]{:S(2)}) collective-permute-start(bf16[144,512]{1,0:T(8,128)(2,1)S(1)} %pair_own.1.refs_5_.refs_1_), channel_id=1, source_target_pairs={{0,4},{1,0},{2,6},{3,2},{4,8},{5,1},{6,10},{7,3},{8,12},{9,5},{10,... | collective-permute-start | bytes 442376 | tf_op jit(solution)/shard_map/ppermute | solution.py:575
  26.8 5.1 %collective-permute-start.7 = (bf16[144,512]{1,0:T(8,128)(2,1)S(1)}, bf16[144,512]{1,0:T(8,128)(2,1)S(1)}, u32[]{:S(2)}, u32[]{:S(2)}) collective-permute-start(bf16[144,512]{1,0:T(8,128)(2,1)S(1)} %pair_other.1.refs_3_.refs_1_), channel_id=1, source_target_pairs={{0,4},{1,0},{2,6},{3,2},{4,8},{5,1},{6,10},{7,3},{8,12},{9,5},{10,... | collective-permute-start | bytes 442376 | tf_op jit(solution)/shard_map/ppermute | solution.py:575
  28.5 6.2 %collective-permute-start.6 = (bf16[144,512]{1,0:T(8,128)(2,1)S(1)}, bf16[144,512]{1,0:T(8,128)(2,1)S(1)}, u32[]{:S(2)}, u32[]{:S(2)}) collective-permute-start(bf16[144,512]{1,0:T(8,128)(2,1)S(1)} %chain_own.1.refs_2_), channel_id=1, source_target_pairs={{0,8},{1,0},{2,10},{3,2},{4,12},{5,4},{6,14},{7,6},{8,9},{9,1},{10... | collective-permute-start | bytes 442376 | tf_op jit(solution)/shard_map/ppermute | solution.py:575
  32.0 5.5 %collective-permute-start.9 = (bf16[144,512]{1,0:T(8,128)(2,1)S(1)}, bf16[144,512]{1,0:T(8,128)(2,1)S(1)}, u32[]{:S(2)}, u32[]{:S(2)}) collective-permute-start(bf16[144,512]{1,0:T(8,128)(2,1)S(1)} %chain_other.1.refs_5_), channel_id=1, source_target_pairs={{0,8},{1,0},{2,10},{3,2},{4,12},{5,4},{6,14},{7,6},{8,9},{9,1},{10... | collective-permute-start | bytes 442376 | tf_op jit(solution)/shard_map/ppermute | solution.py:575
  34.9 6.2 %collective-permute-start.12 = (bf16[128,512]{1,0:T(8,128)(2,1)S(1)}, bf16[128,512]{1,0:T(8,128)(2,1)S(1)}, u32[]{:S(2)}, u32[]{:S(2)}) collective-permute-start(bf16[128,512]{1,0:T(8,128)(2,1)S(1)} %get-tuple-element.57), channel_id=1, source_target_pairs={{0,2},{2,0},{4,6},{6,4},{8,10},{10,8},{12,14},{14,12},{1,3},{3,1},... | collective-permute-start | bytes 393224 | tf_op jit(solution)/shard_map/ppermute | solution.py:649
  37.7 5.7 %collective-permute-start.10 = (bf16[128,512]{1,0:T(8,128)(2,1)S(1)}, bf16[128,512]{1,0:T(8,128)(2,1)S(1)}, u32[]{:S(2)}, u32[]{:S(2)}) collective-permute-start(bf16[128,512]{1,0:T(8,128)(2,1)S(1)} %get-tuple-element.55), channel_id=1, source_target_pairs={{0,2},{2,0},{4,6},{6,4},{8,10},{10,8},{12,14},{14,12},{1,3},{3,1},... | collective-permute-start | bytes 393224 | tf_op jit(solution)/shard_map/ppermute | solution.py:649
  44.9 2.0 %collective-permute-start.13 = (bf16[512,512]{1,0:T(8,128)(2,1)S(1)}, bf16[512,512]{1,0:T(8,128)(2,1)S(1)}, u32[]{:S(2)}, u32[]{:S(2)}) collective-permute-start(bf16[512,512]{1,0:T(8,128)(2,1)S(1)} %get-tuple-element.62.refs_5_), channel_id=1, source_target_pairs={{0,1},{1,0},{2,3},{3,2},{4,5},{5,4},{6,7},{7,6},{8,9},{9,8},{10,11... | collective-permute-start | bytes 1572872 | tf_op jit(solution)/shard_map/ppermute | solution.py:828

commit v12 on v11

--- a/solution.py
+++ b/solution.py
@@ -268,7 +268,7 @@
         maps_kernel,
         "maps",
         vmem=8,
-        cost=micros(1.5),
+        cost=micros(0.3),
         scalars=(place,),
         in_specs=[VMEM] * 4,
         out_specs=[VMEM] * 2,
@@ -413,7 +413,6 @@
     lane = lax.broadcasted_iota(jnp.int32, (length, pair), 1)
     to = lax.broadcasted_iota(jnp.int32, (length, length), 0)
     frm = lax.broadcasted_iota(jnp.int32, (length, length), 1)
-    state_ref[...] = jnp.zeros_like(state_ref)
 
     def chunk(c, before):
         at = slice(c * length, (c + 1) * length)
@@ -424,18 +423,25 @@
         cumt = times_ref[:heads, at]
         step = times_ref[heads:, at]
         end = cumt[:, last:]
-        since = two_rows(jnp.exp(cumt - before)).T.astype(BF16)
-        left = two_rows(step * jnp.exp(end - cumt)).T.astype(BF16)
+        entered = c > 0
+        leaves = (c + 1) * length < rows
+        if entered:
+            since = two_rows(jnp.exp(cumt - before)).T.astype(BF16)
+        if leaves:
+            left = two_rows(step * jnp.exp(end - cumt)).T.astype(BF16)
         for offset in range(0, width, TILE):
             first = head + offset // head_size
             columns = slice(first * head_size, first * head_size + TILE)
             here = slice(offset, offset + TILE)
             onehot = head_matrix(heads, TILE, head_size, first)
-            since_here = dot(since, onehot)
-            state = state_ref[:, here]
-            carried = dot(cmat, state.astype(BF16)) * since_here
-            scaled = (x_ref[at, columns].astype(F32) * dot(left, onehot)).astype(BF16)
-            state_ref[:, here] = state * since_here[last:, :] + dot(bmat, scaled)
+            if entered:
+                since_here = dot(since, onehot)
+                state = state_ref[:, here]
+                carried = dot(cmat, state.astype(BF16)) * since_here
+            if leaves:
+                scaled = (x_ref[at, columns].astype(F32) * dot(left, onehot)).astype(BF16)
+                added = dot(bmat, scaled)
+                state_ref[:, here] = state * since_here[last:, :] + added if entered else added
             for start in range(0, TILE, pair):
                 low = first * head_size + start
                 weights = []
@@ -448,9 +454,9 @@
                     [jnp.where(lane < head_size, mine, none), jnp.where(lane < head_size, none, mine)], axis=0
                 )
                 inside = dot(jnp.concatenate(weights, axis=1), stacked)
-                y_ref[at, offset + start : offset + start + pair] = (
-                    inside + carried[:, start : start + pair]
-                ).astype(BF16)
+                if entered:
+                    inside += carried[:, start : start + pair]
+                y_ref[at, offset + start : offset + start + pair] = inside.astype(BF16)
         return end
 
     before = jnp.zeros((heads, 1), F32)

time: 48 us -> 48 us (level)
  waiting for transfers between devices: 1.5 us -> 3.75 us
  Pallas kernels: 28.1 us -> 26.4 us
  starting transfers between devices: 17.3 us -> 16.8 us
    pallas_call x20, Pallas kernels: 28.1 us -> 26.4 us  [call(): return lambda *arrays: run(*arrays, *after)]
    ppermute x2, waiting for transfers between devices: 0.25 us -> 1.39 us  [entry(): return (keep, lax.ppermute(out, 'seq', self.swap))]
    ppermute x2, waiting for transfers between devices: 0.08 us -> 1.13 us  [__init__(): self.other = lax.ppermute(send, 'seq', self.swap)]
  transfers between devices with their start and end apart: 14 -> 14, of which waited for: 3 -> 6; matrix products, arithmetic and copies ran while one was open for 0% -> 0% of each run, Pallas kernels for 54% -> 50%
where the time goes in v12:
time: 48 us; the launch traced here: 47.9 us
  Pallas kernels  26.4 us (55%)
  starting transfers between devices  16.8 us (35%)
  waiting for transfers between devices  3.75 us (8%)
  local copies, waits for them, and re-layouts  0.65 us (1%)
    pallas_call x20, Pallas kernels, call(): return lambda *arrays: run(*arrays, *after)  26.4 us
    ppermute x5, starting transfers between devices, onward(): return lax.ppermute(value, ('seq', 'ch'), pairs)  11.5 us
    ppermute x2, starting transfers between devices, __init__(): self.other = lax.ppermute(send, 'seq', self.swap)  2.14 us
    ppermute x2, starting transfers between devices, entry(): return (keep, lax.ppermute(out, 'seq', self.swap))  1.81 us
    ppermute x5, starting transfers between devices, theirs(): return lax.ppermute(a, 'ch', swap)  1.4 us
    ppermute x2, waiting for transfers between devices, entry(): return (keep, lax.ppermute(out, 'seq', self.swap))  1.39 us
    ppermute x2, waiting for transfers between devices, __init__(): self.other = lax.ppermute(send, 'seq', self.swap)  1.13 us
  transfers between devices with their start and end apart: 14, of which 6 were waited for; matrix products, arithmetic and copies ran while one was open for 0% of the time, Pallas kernels for 50%

profile of v12, /device:TPU:0, one launch (start us, length us, event | category | flops | bytes accessed | tf_op | source)
XLA Modules:
  0.0 47.9 jit_solution(12225427813741536821)
XLA Ops:
  0.5 2.7 %prepare.1 = (bf16[512,1024]{1,0:T(8,128)(2,1)S(1)}, bf16[16,1024]{1,0:T(8,128)(2,1)S(1)}, f32[24,1024]{1,0:T(8,128)S(1)}) custom-call(s32[1]{0:T(128)} %bitcast.refs_0_, s32[1]{0:T(128)} %bitcast.2.refs_1_.refs_0_, s32[1]{0:T(128)} %bitcast.1.refs_2_.refs_0_, bf16[512,1024]{1,0:T(8,128)(2,1)} %refs_3_.2, s32[1,512]{1,0:T(1,128)} %bitcast.10, ...), custom_call_target="tpu_custom_call" | custom-call | flops 2969999872 | bytes 2700000 | tf_op jit(solution)/shard_map/prepare/pallas_call | solution.py:48
  3.2 3.0 %collective-permute-start = (bf16[16,1024]{1,0:T(8,128)(2,1)S(1)}, bf16[16,1024]{1,0:T(8,128)(2,1)S(1)}, u32[]{:S(2)}, u32[]{:S(2)}) collective-permute-start(bf16[16,1024]{1,0:T(8,128)(2,1)S(1)} %get-tuple-element.37), channel_id=1, source_target_pairs={{0,2},{1,0},{2,4},{3,1},{4,6},{5,3},{6,8},{7,5},{8,10},{9,7},{10,1... | collective-permute-start | bytes 98312 | tf_op jit(solution)/shard_map/ppermute | solution.py:581
  6.8 1.5 %gate_own.1.refs_5_.refs_6_ = bf16[512,1024]{1,0:T(8,128)(2,1)S(1)} custom-call(bf16[512,1024]{1,0:T(8,128)(2,1)S(1)} %get-tuple-element.36.refs_0_.refs_1_.refs_2_, bf16[1024,1024]{1,0:T(8,128)(2,1)S(1)} %copy-done.3), custom_call_target="tpu_custom_call" | custom-call | flops 2640000000 | bytes 2400000 | tf_op jit(solution)/shard_map/gate_own/pallas_call | solution.py:48
  8.3 0.9 %maps.1 = (bf16[512,256]{1,0:T(8,128)(2,1)S(1)}, bf16[128,512]{1,0:T(8,128)(2,1)S(1)}) custom-call(s32[1]{0:T(128)} %bitcast.1.refs_2_.refs_0_, bf16[512,1024]{1,0:T(8,128)(2,1)S(1)} %get-tuple-element.36.refs_0_.refs_1_.refs_2_, bf16[16,1024]{1,0:T(8,128)(2,1)S(1)} %collective-permute-done.refs_2_.refs_3_, bf16[1024,256]{1,0:T(8,128)(2,1)S(1)} %copy-done, ...), custom_call_target="tpu_custom_call" | custom-call | flops 330000000 | bytes 300000 | tf_op jit(solution)/shard_map/maps/pallas_call | solution.py:48
  9.8 4.3 %local_own.1 = (bf16[512,1024]{1,0:T(8,128)(2,1)S(1)}, f32[512,16]{1,0:T(8,128)S(1)}, f32[32,512]{1,0:T(8,128)S(1)}, bf16[144,512]{1,0:T(8,128)(2,1)S(1)}, bf16[144,512]{1,0:T(8,128)(2,1)S(1)}) custom-call(s32[1]{0:T(128)} %bitcast.1.refs_2_.refs_0_, s32[1]{0:T(128)} %bitcast.2.refs_1_.refs_0_, ...), custom_call_target="tpu_custom_call" | custom-call | flops 5500000256 | bytes 5000000 | tf_op jit(solution)/shard_map/local_own/pallas_call | solution.py:48
  14.2 1.6 %collective-permute-start.3 = (bf16[144,512]{1,0:T(8,128)(2,1)S(1)}, bf16[144,512]{1,0:T(8,128)(2,1)S(1)}, u32[]{:S(2)}, u32[]{:S(2)}) collective-permute-start(bf16[144,512]{1,0:T(8,128)(2,1)S(1)} %get-tuple-element.46), channel_id=1, source_target_pairs={{0,2},{2,0},{4,6},{6,4},{8,10},{10,8},{12,14},{14,12},{1,3},{3,1},... | collective-permute-start | bytes 442376 | tf_op jit(solution)/shard_map/ppermute | solution.py:589
  15.7 4.3 %local_other.1 = (bf16[512,1024]{1,0:T(8,128)(2,1)S(1)}, f32[512,16]{1,0:T(8,128)S(1)}, f32[32,512]{1,0:T(8,128)S(1)}, bf16[144,512]{1,0:T(8,128)(2,1)S(1)}, bf16[144,512]{1,0:T(8,128)(2,1)S(1)}) custom-call(s32[1]{0:T(128)} %bitcast.1.refs_2_.refs_0_, s32[1]{0:T(128)} %bitcast.2.refs_1_.refs_0_, ...), custom_call_target="tpu_custom_call" | custom-call | flops 5500000256 | bytes 5000000 | tf_op jit(solution)/shard_map/local_other/pallas_call | solution.py:48
  20.8 2.2 %collective-permute-start.4 = (bf16[144,512]{1,0:T(8,128)(2,1)S(1)}, bf16[144,512]{1,0:T(8,128)(2,1)S(1)}, u32[]{:S(2)}, u32[]{:S(2)}) collective-permute-start(bf16[144,512]{1,0:T(8,128)(2,1)S(1)} %pair_own.1.refs_5_.refs_1_), channel_id=1, source_target_pairs={{0,4},{1,0},{2,6},{3,2},{4,8},{5,1},{6,10},{7,3},{8,12},{9,5},{10,... | collective-permute-start | bytes 442376 | tf_op jit(solution)/shard_map/ppermute | solution.py:581
  23.0 2.5 %inside_own.1.refs_3_.refs_1_ = bf16[512,1024]{1,0:T(8,128)(2,1)S(1)} custom-call(bf16[512,1024]{1,0:T(8,128)(2,1)S(1)} %get-tuple-element.49.refs_0_, bf16[512,256]{1,0:T(8,128)(2,1)S(1)} %get-tuple-element.43.refs_1_.refs_2_.refs_4_, bf16[128,512]{1,0:T(8,128)(2,1)S(1)} %get-tuple-element.38.refs_4_.refs_2_, f32[512,16]{1,0:T(8,128)S(1)} %get-tuple-element.50.refs_3_, ...), custom_call_target="tpu_custom_call" | custom-call | flops 3520000000 | bytes 3200000 | tf_op jit(solution)/shard_map/inside_own/pallas_call | solution.py:48
  25.5 1.1 %collective-permute-done.5.refs_2_ = bf16[144,512]{1,0:T(8,128)(2,1)S(1)} collective-permute-done((bf16[144,512]{1,0:T(8,128)(2,1)S(1)}, bf16[144,512]{1,0:T(8,128)(2,1)S(1)}, u32[]{:S(2)}, u32[]{:S(2)}) %collective-permute-start.5) | collective-permute-done | bytes 147488 | tf_op jit(solution)/shard_map/ppermute | solution.py:589
  26.6 1.6 %collective-permute-start.7 = (bf16[144,512]{1,0:T(8,128)(2,1)S(1)}, bf16[144,512]{1,0:T(8,128)(2,1)S(1)}, u32[]{:S(2)}, u32[]{:S(2)}) collective-permute-start(bf16[144,512]{1,0:T(8,128)(2,1)S(1)} %pair_other.1.refs_3_.refs_1_), channel_id=1, source_target_pairs={{0,4},{1,0},{2,6},{3,2},{4,8},{5,1},{6,10},{7,3},{8,12},{9,5},{10,... | collective-permute-start | bytes 442376 | tf_op jit(solution)/shard_map/ppermute | solution.py:581
  28.3 2.0 %collective-permute-start.6 = (bf16[144,512]{1,0:T(8,128)(2,1)S(1)}, bf16[144,512]{1,0:T(8,128)(2,1)S(1)}, u32[]{:S(2)}, u32[]{:S(2)}) collective-permute-start(bf16[144,512]{1,0:T(8,128)(2,1)S(1)} %chain_own.1.refs_2_), channel_id=1, source_target_pairs={{0,8},{1,0},{2,10},{3,2},{4,12},{5,4},{6,14},{7,6},{8,9},{9,1},{10... | collective-permute-start | bytes 442376 | tf_op jit(solution)/shard_map/ppermute | solution.py:581
  30.3 1.5 %gate_other.1.refs_3_.refs_8_ = bf16[512,1024]{1,0:T(8,128)(2,1)S(1)} custom-call(bf16[512,1024]{1,0:T(8,128)(2,1)S(1)} %get-tuple-element.36.refs_0_.refs_1_.refs_2_, bf16[1024,1024]{1,0:T(8,128)(2,1)S(1)} %collective-permute-done.8.refs_1_, bf16[144,512]{1,0:T(8,128)(2,1)S(1)} %chain_own.1.refs_2_), custom_call_target="tpu_custom_call" | custom-call | flops 2640000000 | bytes 2400000 | tf_op jit(solution)/shard_map/gate_other/pallas_call | solution.py:48
  31.9 2.6 %collective-permute-start.9 = (bf16[144,512]{1,0:T(8,128)(2,1)S(1)}, bf16[144,512]{1,0:T(8,128)(2,1)S(1)}, u32[]{:S(2)}, u32[]{:S(2)}) collective-permute-start(bf16[144,512]{1,0:T(8,128)(2,1)S(1)} %chain_other.1.refs_5_), channel_id=1, source_target_pairs={{0,8},{1,0},{2,10},{3,2},{4,12},{5,4},{6,14},{7,6},{8,9},{9,1},{10... | collective-permute-start | bytes 442376 | tf_op jit(solution)/shard_map/ppermute | solution.py:581
  34.7 0.7 %collective-permute-start.12 = (bf16[128,512]{1,0:T(8,128)(2,1)S(1)}, bf16[128,512]{1,0:T(8,128)(2,1)S(1)}, u32[]{:S(2)}, u32[]{:S(2)}) collective-permute-start(bf16[128,512]{1,0:T(8,128)(2,1)S(1)} %get-tuple-element.57), channel_id=1, source_target_pairs={{0,2},{2,0},{4,6},{6,4},{8,10},{10,8},{12,14},{14,12},{1,3},{3,1},... | collective-permute-start | bytes 393224 | tf_op jit(solution)/shard_map/ppermute | solution.py:655
  35.3 1.5 %inside_other.2.refs_5_.refs_9_.refs_2_ = bf16[512,512]{1,0:T(8,128)(2,1)S(1)} custom-call(bf16[512,1024]{1,0:T(8,128)(2,1)S(1)} %get-tuple-element.42.refs_1_.refs_0_, bf16[512,256]{1,0:T(8,128)(2,1)S(1)} %get-tuple-element.43.refs_1_.refs_2_.refs_4_, bf16[128,512]{1,0:T(8,128)(2,1)S(1)} %get-tuple-element.38.refs_4_.refs_2_, ...), custom_call_target="tpu_custom_call" | custom-call | flops 1760000000 | bytes 1600000 | tf_op jit(solution)/shard_map/inside_other/pallas_call | solution.py:48
  37.4 1.1 %collective-permute-start.10 = (bf16[128,512]{1,0:T(8,128)(2,1)S(1)}, bf16[128,512]{1,0:T(8,128)(2,1)S(1)}, u32[]{:S(2)}, u32[]{:S(2)}) collective-permute-start(bf16[128,512]{1,0:T(8,128)(2,1)S(1)} %get-tuple-element.55), channel_id=1, source_target_pairs={{0,2},{2,0},{4,6},{6,4},{8,10},{10,8},{12,14},{14,12},{1,3},{3,1},... | collective-permute-start | bytes 393224 | tf_op jit(solution)/shard_map/ppermute | solution.py:655
  38.5 1.5 %inside_other.3.refs_10_.refs_3_ = bf16[512,512]{1,0:T(8,128)(2,1)S(1)} custom-call(bf16[512,1024]{1,0:T(8,128)(2,1)S(1)} %get-tuple-element.42.refs_1_.refs_0_, bf16[512,256]{1,0:T(8,128)(2,1)S(1)} %get-tuple-element.43.refs_1_.refs_2_.refs_4_, bf16[128,512]{1,0:T(8,128)(2,1)S(1)} %get-tuple-element.38.refs_4_.refs_2_, ...), custom_call_target="tpu_custom_call" | custom-call | flops 1760000000 | bytes 1600000 | tf_op jit(solution)/shard_map/inside_other/pallas_call | solution.py:48
  40.2 2.0 %part.1 = (f32[512,1024]{1,0:T(8,128)S(1)}, f32[512,128]{1,0:T(8,128)S(1)}) custom-call(s32[1]{0:T(128)} %bitcast.2.refs_1_.refs_0_, bf16[512,1024]{1,0:T(8,128)(2,1)S(1)} %inside_own.1.refs_3_.refs_1_, bf16[512,256]{1,0:T(8,128)(2,1)S(1)} %get-tuple-element.43.refs_1_.refs_2_.refs_4_, f32[512,16]{1,0:T(8,128)S(1)} %get-tuple-element.50.refs_3_, ...), custom_call_target="tpu_custom_call" | custom-call | flops 3849999872 | bytes 3500000 | tf_op jit(solution)/shard_map/part/pallas_call | solution.py:48
  42.3 1.1 %collective-permute-done.10.refs_7_ = bf16[128,512]{1,0:T(8,128)(2,1)S(1)} collective-permute-done((bf16[128,512]{1,0:T(8,128)(2,1)S(1)}, bf16[128,512]{1,0:T(8,128)(2,1)S(1)}, u32[]{:S(2)}, u32[]{:S(2)}) %collective-permute-start.10) | collective-permute-done | bytes 131104 | tf_op jit(solution)/shard_map/ppermute | solution.py:655
  43.4 1.5 %finish.1 = (bf16[512,512]{1,0:T(8,128)(2,1)S(1)}, bf16[512,1024]{1,0:T(8,128)(2,1)S(1)}, f32[512,128]{1,0:T(8,128)S(1)}) custom-call(s32[1]{0:T(128)} %bitcast.refs_0_, s32[1]{0:T(128)} %bitcast.2.refs_1_.refs_0_, bf16[512,512]{1,0:T(8,128)(2,1)S(1)} %inside_other.2.refs_5_.refs_9_.refs_2_, bf16[512,512]{1,0:T(8,128)(2,1)S(1)} %inside_other.3.refs_10_.refs_3_, ...), custom_call_target="tpu_custom_call" | custom-call | flops 3849999872 | bytes 3500000 | tf_op jit(solution)/shard_map/finish/pallas_call | solution.py:48
  45.3 0.7 %own_half.1.refs_0_ = bf16[512,512]{1,0:T(8,128)(2,1)S(1)} custom-call(s32[1]{0:T(128)} %bitcast.refs_0_, bf16[512,1024]{1,0:T(8,128)(2,1)S(1)} %get-tuple-element.60.refs_1_, bf16[1024,1024]{1,0:T(8,128)(2,1)S(1)} %collective-permute-done.11.refs_10_.refs_2_, f32[512,1024]{1,0:T(8,128)S(1)} %get-tuple-element.58.refs_11_.refs_3_, ...), custom_call_target="tpu_custom_call" | custom-call | flops 770000000 | bytes 700000 | tf_op jit(solution)/shard_map/own_half/pallas_call | solution.py:48
  46.0 0.8 %collective-permute-done.13.refs_1_ = bf16[512,512]{1,0:T(8,128)(2,1)S(1)} collective-permute-done((bf16[512,512]{1,0:T(8,128)(2,1)S(1)}, bf16[512,512]{1,0:T(8,128)(2,1)S(1)}, u32[]{:S(2)}, u32[]{:S(2)}) %collective-permute-start.13) | collective-permute-done | bytes 524320 | tf_op jit(solution)/shard_map/ppermute | solution.py:834
  46.9 0.8 %total.1 = bf16[512,512]{1,0:T(8,128)(2,1)} custom-call(bf16[512,512]{1,0:T(8,128)(2,1)S(1)} %own_half.1.refs_0_, bf16[512,512]{1,0:T(8,128)(2,1)S(1)} %collective-permute-done.13.refs_1_), custom_call_target="tpu_custom_call" | custom-call | flops 880000000 | bytes 800000 | tf_op jit(solution)/shard_map/total/pallas_call | solution.py:48
  (34 shorter events, 3.9 us)
Async XLA Ops:
  0.0 15.7 %collective-permute-start.1 = (bf16[1024,1024]{1,0:T(8,128)(2,1)}, bf16[1024,1024]{1,0:T(8,128)(2,1)S(1)}, u32[]{:S(2)}, u32[]{:S(2)}) collective-permute-start(bf16[1024,1024]{1,0:T(8,128)(2,1)} %refs_5_.3), channel_id=1, source_target_pairs={{0,1},{1,0},{2,3},{3,2},{4,5},{5,4},{6,7},{7,6},{8,9},{9,8},{10,11... | collective-permute-start | bytes 6291464 | tf_op jit(solution)/shard_map/ppermute | solution.py:834
  0.5 29.9 %collective-permute-start.8 = (bf16[1024,1024]{1,0:T(8,128)(2,1)}, bf16[1024,1024]{1,0:T(8,128)(2,1)S(1)}, u32[]{:S(2)}, u32[]{:S(2)}) collective-permute-start(bf16[1024,1024]{1,0:T(8,128)(2,1)} %refs_1_.1), channel_id=1, source_target_pairs={{0,1},{1,0},{2,3},{3,2},{4,5},{5,4},{6,7},{7,6},{8,9},{9,8},{10,11... | collective-permute-start | bytes 6291464 | tf_op jit(solution)/shard_map/ppermute | solution.py:834
  0.5 5.8 %copy-start.4 = (bf16[1024,1024]{1,0:T(8,128)(2,1)S(1)}, bf16[1024,1024]{1,0:T(8,128)(2,1)}, u32[]{:S(2)}) copy-start(bf16[1024,1024]{1,0:T(8,128)(2,1)} %refs_8_.1) | copy-start | bytes 6291460
  0.5 6.3 %copy-start.3 = (bf16[1024,1024]{1,0:T(8,128)(2,1)S(1)}, bf16[1024,1024]{1,0:T(8,128)(2,1)}, u32[]{:S(2)}) copy-start(bf16[1024,1024]{1,0:T(8,128)(2,1)} %refs_1_.1) | copy-start | bytes 6291460
  3.2 5.0 %collective-permute-start = (bf16[16,1024]{1,0:T(8,128)(2,1)S(1)}, bf16[16,1024]{1,0:T(8,128)(2,1)S(1)}, u32[]{:S(2)}, u32[]{:S(2)}) collective-permute-start(bf16[16,1024]{1,0:T(8,128)(2,1)S(1)} %get-tuple-element.37), channel_id=1, source_target_pairs={{0,2},{1,0},{2,4},{3,1},{4,6},{5,3},{6,8},{7,5},{8,10},{9,7},{10,1... | collective-permute-start | bytes 98312 | tf_op jit(solution)/shard_map/ppermute | solution.py:581
  6.3 9.5 %collective-permute-start.2 = (f32[24,1024]{1,0:T(8,128)S(1)}, f32[24,1024]{1,0:T(8,128)S(1)}, u32[]{:S(2)}, u32[]{:S(2)}) collective-permute-start(f32[24,1024]{1,0:T(8,128)S(1)} %get-tuple-element.40.refs_6_.refs_7_), channel_id=1, source_target_pairs={{0,1},{1,0},{2,3},{3,2},{4,5},{5,4},{6,7},{7,6},{8,9},{9,8},{10,11... | collective-permute-start | bytes 294920 | tf_op jit(solution)/shard_map/ppermute | solution.py:834
  6.3 36.0 %collective-permute-start.11 = (bf16[1024,1024]{1,0:T(8,128)(2,1)S(1)}, bf16[1024,1024]{1,0:T(8,128)(2,1)S(1)}, u32[]{:S(2)}, u32[]{:S(2)}) collective-permute-start(bf16[1024,1024]{1,0:T(8,128)(2,1)S(1)} %copy-done.4), channel_id=1, source_target_pairs={{0,1},{1,0},{2,3},{3,2},{4,5},{5,4},{6,7},{7,6},{8,9},{9,8},{10,11... | collective-permute-start | bytes 6291464 | tf_op jit(solution)/shard_map/ppermute | solution.py:834
  6.8 1.5 %copy-start = (bf16[1024,256]{1,0:T(8,128)(2,1)S(1)}, bf16[1024,256]{1,0:T(8,128)(2,1)}, u32[]{:S(2)}) copy-start(bf16[1024,256]{1,0:T(8,128)(2,1)} %refs_3_.3) | copy-start | bytes 1572868
  6.8 1.5 %copy-start.1 = (f32[4,256]{1,0:T(4,128)S(1)}, f32[4,256]{1,0:T(4,128)}, u32[]{:S(2)}) copy-start(f32[4,256]{1,0:T(4,128)} %refs_4_.1) | copy-start | bytes 12292
  8.2 1.6 %copy-start.2 = (bf16[1024,1024]{1,0:T(8,128)(2,1)S(1)}, bf16[1024,1024]{1,0:T(8,128)(2,1)}, u32[]{:S(2)}) copy-start(bf16[1024,1024]{1,0:T(8,128)(2,1)} %refs_5_.3) | copy-start | bytes 6291460
  14.2 6.5 %collective-permute-start.3 = (bf16[144,512]{1,0:T(8,128)(2,1)S(1)}, bf16[144,512]{1,0:T(8,128)(2,1)S(1)}, u32[]{:S(2)}, u32[]{:S(2)}) collective-permute-start(bf16[144,512]{1,0:T(8,128)(2,1)S(1)} %get-tuple-element.46), channel_id=1, source_target_pairs={{0,2},{2,0},{4,6},{6,4},{8,10},{10,8},{12,14},{14,12},{1,3},{3,1},... | collective-permute-start | bytes 442376 | tf_op jit(solution)/shard_map/ppermute | solution.py:589
  20.1 6.5 %collective-permute-start.5 = (bf16[144,512]{1,0:T(8,128)(2,1)S(1)}, bf16[144,512]{1,0:T(8,128)(2,1)S(1)}, u32[]{:S(2)}, u32[]{:S(2)}) collective-permute-start(bf16[144,512]{1,0:T(8,128)(2,1)S(1)} %get-tuple-element.48), channel_id=1, source_target_pairs={{0,2},{2,0},{4,6},{6,4},{8,10},{10,8},{12,14},{14,12},{1,3},{3,1},... | collective-permute-start | bytes 442376 | tf_op jit(solution)/shard_map/ppermute | solution.py:589
  20.8 7.4 %collective-permute-start.4 = (bf16[144,512]{1,0:T(8,128)(2,1)S(1)}, bf16[144,512]{1,0:T(8,128)(2,1)S(1)}, u32[]{:S(2)}, u32[]{:S(2)}) collective-permute-start(bf16[144,512]{1,0:T(8,128)(2,1)S(1)} %pair_own.1.refs_5_.refs_1_), channel_id=1, source_target_pairs={{0,4},{1,0},{2,6},{3,2},{4,8},{5,1},{6,10},{7,3},{8,12},{9,5},{10,... | collective-permute-start | bytes 442376 | tf_op jit(solution)/shard_map/ppermute | solution.py:581
  26.6 5.2 %collective-permute-start.7 = (bf16[144,512]{1,0:T(8,128)(2,1)S(1)}, bf16[144,512]{1,0:T(8,128)(2,1)S(1)}, u32[]{:S(2)}, u32[]{:S(2)}) collective-permute-start(bf16[144,512]{1,0:T(8,128)(2,1)S(1)} %pair_other.1.refs_3_.refs_1_), channel_id=1, source_target_pairs={{0,4},{1,0},{2,6},{3,2},{4,8},{5,1},{6,10},{7,3},{8,12},{9,5},{10,... | collective-permute-start | bytes 442376 | tf_op jit(solution)/shard_map/ppermute | solution.py:581
  28.3 6.2 %collective-permute-start.6 = (bf16[144,512]{1,0:T(8,128)(2,1)S(1)}, bf16[144,512]{1,0:T(8,128)(2,1)S(1)}, u32[]{:S(2)}, u32[]{:S(2)}) collective-permute-start(bf16[144,512]{1,0:T(8,128)(2,1)S(1)} %chain_own.1.refs_2_), channel_id=1, source_target_pairs={{0,8},{1,0},{2,10},{3,2},{4,12},{5,4},{6,14},{7,6},{8,9},{9,1},{10... | collective-permute-start | bytes 442376 | tf_op jit(solution)/shard_map/ppermute | solution.py:581
  31.9 5.3 %collective-permute-start.9 = (bf16[144,512]{1,0:T(8,128)(2,1)S(1)}, bf16[144,512]{1,0:T(8,128)(2,1)S(1)}, u32[]{:S(2)}, u32[]{:S(2)}) collective-permute-start(bf16[144,512]{1,0:T(8,128)(2,1)S(1)} %chain_other.1.refs_5_), channel_id=1, source_target_pairs={{0,8},{1,0},{2,10},{3,2},{4,12},{5,4},{6,14},{7,6},{8,9},{9,1},{10... | collective-permute-start | bytes 442376 | tf_op jit(solution)/shard_map/ppermute | solution.py:581
  34.7 5.6 %collective-permute-start.12 = (bf16[128,512]{1,0:T(8,128)(2,1)S(1)}, bf16[128,512]{1,0:T(8,128)(2,1)S(1)}, u32[]{:S(2)}, u32[]{:S(2)}) collective-permute-start(bf16[128,512]{1,0:T(8,128)(2,1)S(1)} %get-tuple-element.57), channel_id=1, source_target_pairs={{0,2},{2,0},{4,6},{6,4},{8,10},{10,8},{12,14},{14,12},{1,3},{3,1},... | collective-permute-start | bytes 393224 | tf_op jit(solution)/shard_map/ppermute | solution.py:655
  37.4 6.0 %collective-permute-start.10 = (bf16[128,512]{1,0:T(8,128)(2,1)S(1)}, bf16[128,512]{1,0:T(8,128)(2,1)S(1)}, u32[]{:S(2)}, u32[]{:S(2)}) collective-permute-start(bf16[128,512]{1,0:T(8,128)(2,1)S(1)} %get-tuple-element.55), channel_id=1, source_target_pairs={{0,2},{2,0},{4,6},{6,4},{8,10},{10,8},{12,14},{14,12},{1,3},{3,1},... | collective-permute-start | bytes 393224 | tf_op jit(solution)/shard_map/ppermute | solution.py:655
  44.9 2.0 %collective-permute-start.13 = (bf16[512,512]{1,0:T(8,128)(2,1)S(1)}, bf16[512,512]{1,0:T(8,128)(2,1)S(1)}, u32[]{:S(2)}, u32[]{:S(2)}) collective-permute-start(bf16[512,512]{1,0:T(8,128)(2,1)S(1)} %get-tuple-element.62.refs_5_), channel_id=1, source_target_pairs={{0,1},{1,0},{2,3},{3,2},{4,5},{5,4},{6,7},{7,6},{8,9},{9,8},{10,11... | collective-permute-start | bytes 1572872 | tf_op jit(solution)/shard_map/ppermute | solution.py:834

commit v13 on v12

--- a/solution.py
+++ b/solution.py
@@ -130,6 +130,7 @@
     step_ref,
     base_ref,
     normed_ref,
+    turned_ref,
     sems,
 ):
     rows = hidden_ref.shape[0]
@@ -168,15 +169,24 @@
             merged = hidden_ref[block, :].astype(F32) + base_ref[q - low : q - low + HALO, :]
             merged = merged.astype(BF16).astype(F32)
             mean = jnp.mean(merged * merged, axis=-1, keepdims=True)
-            normed_ref[q - low : q - low + HALO, :] = (merged * lax.rsqrt(mean + EPS)).astype(BF16)
-
-        @pl.when(back)
-        def _():
-            out_ref[rows - high : rows - low, :] = flip_both(normed_ref[...])
-
-        @pl.when(jnp.logical_not(back))
-        def _():
-            out_ref[low:high, :] = normed_ref[...]
+            normed_ref[block, :] = (merged * lax.rsqrt(mean + EPS)).astype(BF16)
+
+    @pl.when(back)
+    def _():
+        turn = flip_matrix(TILE)
+        for c in range(0, hidden_ref.shape[1], TILE):
+            to = hidden_ref.shape[1] - TILE - c
+            for r in range(0, rows, TILE):
+                turned = dot(turn, normed_ref[r : r + TILE, c : c + TILE]).astype(BF16)
+                turned_ref[r : r + TILE, c : c + TILE] = turned
+            for r in range(0, rows, TILE):
+                out_ref[rows - TILE - r : rows - r, to : to + TILE] = dot(
+                    turned_ref[r : r + TILE, c : c + TILE], turn
+                ).astype(BF16)
+
+    @pl.when(jnp.logical_not(back))
+    def _():
+        out_ref[...] = normed_ref[...]
 
     tail_ref[...] = out_ref[rows - HALO :, :]
     for copy in small_copies[2:]:
@@ -208,7 +218,8 @@
             jax.ShapeDtypeStruct((SMALL_ROWS + step.shape[0], inner), F32),
         ],
         scratch=[pltpu.VMEM(a.shape, a.dtype) for a in arrays]
-        + [pltpu.VMEM((CHUNK, width), F32), pltpu.VMEM((CHUNK, width), BF16)]
+        + [pltpu.VMEM((CHUNK, width), F32)]
+        + [pltpu.VMEM((rows, width), BF16)] * 2
         + [pltpu.SemaphoreType.DMA((rows // CHUNK + len(arrays) - 1,))],
     )(*scalars, *(pltpu.with_memory_space_constraint(a, pltpu.HBM) for a in arrays))
 
@@ -306,6 +317,13 @@
     states = bt_ref.shape[0]
     heads = cum_ref.shape[1]
     taps = SMALL_TAPS
+
+    def project_rows(t):
+        weights = wi_ref[:, t * TILE : (t + 1) * TILE]
+        before = dot(halo_ref[...], weights).astype(BF16).astype(F32)
+        rows_ref[t % 2, :HALO, :] = jnp.where(place_ref[0] >= 1, before, 0.0)
+        rows_ref[t % 2, HALO:, :] = dot(normed_ref[...], weights).astype(BF16).astype(F32)
+
     raw = dot_nt(normed_ref[...], small_ref[SMALL_ROWS:, :].astype(BF16))
     columns = small_ref[:SMALL_ROWS, :CHUNK].T
     raw = raw.T + columns[:heads, taps + 1 : taps + 2]
@@ -317,6 +335,7 @@
     low = (rest - mid.astype(F32)).astype(BF16)
     starts = range(0, rows, CHUNK)
     pieces = [part[:, r : r + CHUNK] for r in starts for part in (high, mid, low)]
+    project_rows(0)
     frm = lax.broadcasted_iota(jnp.int32, (CHUNK, CHUNK), 0)
     to = lax.broadcasted_iota(jnp.int32, (CHUNK, CHUNK), 1)
     sums = dot(jnp.concatenate(pieces, axis=0), jnp.where(to >= frm, 1.0, 0.0).astype(BF16))
@@ -340,10 +359,7 @@
     spans = [slice(t * TILE, (t + 1) * TILE) for t in tiles]
 
     def project(t):
-        weights = wi_ref[:, spans[t]]
-        before = dot(halo_ref[...], weights).astype(BF16).astype(F32)
-        rows_ref[t % 2, :HALO, :] = jnp.where(place_ref[0] >= 1, before, 0.0)
-        rows_ref[t % 2, HALO:, :] = dot(normed_ref[...], weights).astype(BF16).astype(F32)
+        project_rows(t)
         spread_ref[t % 2] = dot(left_ref[...], onehots[t])
 
     def combine(t):
@@ -358,7 +374,7 @@
         is_mine = jnp.where(parity_ref[0] == t * TILE // half, 1, 0)
         write_payload(payload_ref.at[is_mine], here, state, dot(whole_ref[...], onehots[t]))
 
-    project(0)
+    spread_ref[0] = dot(left_ref[...], onehots[0])
     for t in tiles:
         if t + 1 < len(tiles):
             project(t + 1)
@@ -861,10 +877,10 @@
     done = mark_call(normed, after=[x_2])
     done = chain_1.pair(after=[done])
     y_1 = inside_call("own", x_1, bc, bt, cum_1, times_1, after=[done])
-    done = chain_2.pair(after=[y_1])
+    gate_2 = gate_call("other", normed, w_gate_2, after=[y_1])
+    done = chain_2.pair(after=[gate_2])
     done = chain_1.middle(after=[done])
-    gate_2 = gate_call("other", normed, w_gate_2, after=[done])
-    done = chain_2.middle(after=[gate_2])
+    done = chain_2.middle(after=[done])
     entry_1 = chain_1.entry(after=[done])
     scan_2 = ("other", x_2, bc, bt, cum_2, times_2)
     y_2 = [inside_call(*scan_2, after=[entry_1[0]], part=0, parts=2)]

time: 48 us -> 48.3 us (level)
  Pallas kernels: 26.4 us -> 25.5 us
  starting transfers between devices: 16.8 us -> 17.5 us
    ppermute x5, waiting for transfers between devices: 0.37 us -> 2.46 us  [onward(): return lax.ppermute(value, ('seq', 'ch'), pairs)]
    ppermute x5, starting transfers between devices: 11.5 us -> 13 us  [onward(): return lax.ppermute(value, ('seq', 'ch'), pairs)]
    ppermute x2, waiting for transfers between devices: 1.13 us -> 0.06 us  [__init__(): self.other = lax.ppermute(send, 'seq', self.swap)]
    ppermute x2, waiting for transfers between devices: 1.39 us -> 0.49 us  [entry(): return (keep, lax.ppermute(out, 'seq', self.swap))]
    pallas_call x20, Pallas kernels: 26.4 us -> 25.5 us  [call(): return lambda *arrays: run(*arrays, *after)]
    ppermute x2, starting transfers between devices: 1.81 us -> 1.22 us  [entry(): return (keep, lax.ppermute(out, 'seq', self.swap))]
  transfers between devices with their start and end apart: 14 -> 14, of which waited for: 6 -> 6; matrix products, arithmetic and copies ran while one was open for 0% -> 0% of each run, Pallas kernels for 50% -> 48%
where the time goes in v13:
time: 48.3 us; the launch traced here: 48.2 us
  Pallas kernels  25.5 us (53%)
  starting transfers between devices  17.5 us (36%)
  waiting for transfers between devices  4.16 us (9%)
  local copies, waits for them, and re-layouts  0.65 us (1%)
    pallas_call x20, Pallas kernels, call(): return lambda *arrays: run(*arrays, *after)  25.5 us
    ppermute x5, starting transfers between devices, onward(): return lax.ppermute(value, ('seq', 'ch'), pairs)  13 us
    ppermute x5, waiting for transfers between devices, onward(): return lax.ppermute(value, ('seq', 'ch'), pairs)  2.46 us
    ppermute x2, starting transfers between devices, __init__(): self.other = lax.ppermute(send, 'seq', self.swap)  2.14 us
    ppermute x2, starting transfers between devices, entry(): return (keep, lax.ppermute(out, 'seq', self.swap))  1.22 us
    ppermute x5, waiting for transfers between devices, theirs(): return lax.ppermute(a, 'ch', swap)  1.15 us
    ppermute x5, starting transfers between devices, theirs(): return lax.ppermute(a, 'ch', swap)  1.09 us
  transfers between devices with their start and end apart: 14, of which 6 were waited for; matrix products, arithmetic and copies ran while one was open for 0% of the time, Pallas kernels for 48%

profile of v13, /device:TPU:0, one launch (start us, length us, event | category | flops | bytes accessed | tf_op | source)
XLA Modules:
  0.0 48.2 jit_solution(17553287676916328022)
XLA Ops:
  0.5 2.7 %prepare.1 = (bf16[512,1024]{1,0:T(8,128)(2,1)S(1)}, bf16[16,1024]{1,0:T(8,128)(2,1)S(1)}, f32[24,1024]{1,0:T(8,128)S(1)}) custom-call(s32[1]{0:T(128)} %bitcast.refs_0_, s32[1]{0:T(128)} %bitcast.2.refs_1_.refs_0_, s32[1]{0:T(128)} %bitcast.1.refs_2_.refs_0_, bf16[512,1024]{1,0:T(8,128)(2,1)} %refs_3_.2, s32[1,512]{1,0:T(1,128)} %bitcast.10, ...), custom_call_target="tpu_custom_call" | custom-call | flops 2969999872 | bytes 2700000 | tf_op jit(solution)/shard_map/prepare/pallas_call | solution.py:48
  3.2 3.0 %collective-permute-start = (bf16[16,1024]{1,0:T(8,128)(2,1)S(1)}, bf16[16,1024]{1,0:T(8,128)(2,1)S(1)}, u32[]{:S(2)}, u32[]{:S(2)}) collective-permute-start(bf16[16,1024]{1,0:T(8,128)(2,1)S(1)} %get-tuple-element.37), channel_id=1, source_target_pairs={{0,2},{1,0},{2,4},{3,1},{4,6},{5,3},{6,8},{7,5},{8,10},{9,7},{10,1... | collective-permute-start | bytes 98312 | tf_op jit(solution)/shard_map/ppermute | solution.py:597
  6.8 1.5 %gate_own.1.refs_5_.refs_6_ = bf16[512,1024]{1,0:T(8,128)(2,1)S(1)} custom-call(bf16[512,1024]{1,0:T(8,128)(2,1)S(1)} %get-tuple-element.36.refs_0_.refs_1_.refs_2_, bf16[1024,1024]{1,0:T(8,128)(2,1)S(1)} %copy-done.3), custom_call_target="tpu_custom_call" | custom-call | flops 2640000000 | bytes 2400000 | tf_op jit(solution)/shard_map/gate_own/pallas_call | solution.py:48
  8.3 0.9 %maps.1 = (bf16[512,256]{1,0:T(8,128)(2,1)S(1)}, bf16[128,512]{1,0:T(8,128)(2,1)S(1)}) custom-call(s32[1]{0:T(128)} %bitcast.1.refs_2_.refs_0_, bf16[512,1024]{1,0:T(8,128)(2,1)S(1)} %get-tuple-element.36.refs_0_.refs_1_.refs_2_, bf16[16,1024]{1,0:T(8,128)(2,1)S(1)} %collective-permute-done.refs_2_.refs_3_, bf16[1024,256]{1,0:T(8,128)(2,1)S(1)} %copy-done, ...), custom_call_target="tpu_custom_call" | custom-call | flops 330000000 | bytes 300000 | tf_op jit(solution)/shard_map/maps/pallas_call | solution.py:48
  9.2 0.6 %copy-done.2 = bf16[1024,1024]{1,0:T(8,128)(2,1)S(1)} copy-done((bf16[1024,1024]{1,0:T(8,128)(2,1)S(1)}, bf16[1024,1024]{1,0:T(8,128)(2,1)}, u32[]{:S(2)}) %copy-start.2) | copy-done | bytes 2097176
  9.8 3.8 %local_own.1 = (bf16[512,1024]{1,0:T(8,128)(2,1)S(1)}, f32[512,16]{1,0:T(8,128)S(1)}, f32[32,512]{1,0:T(8,128)S(1)}, bf16[144,512]{1,0:T(8,128)(2,1)S(1)}, bf16[144,512]{1,0:T(8,128)(2,1)S(1)}) custom-call(s32[1]{0:T(128)} %bitcast.1.refs_2_.refs_0_, s32[1]{0:T(128)} %bitcast.2.refs_1_.refs_0_, ...), custom_call_target="tpu_custom_call" | custom-call | flops 5500000256 | bytes 5000000 | tf_op jit(solution)/shard_map/local_own/pallas_call | solution.py:48
  13.6 1.6 %collective-permute-start.3 = (bf16[144,512]{1,0:T(8,128)(2,1)S(1)}, bf16[144,512]{1,0:T(8,128)(2,1)S(1)}, u32[]{:S(2)}, u32[]{:S(2)}) collective-permute-start(bf16[144,512]{1,0:T(8,128)(2,1)S(1)} %get-tuple-element.46), channel_id=1, source_target_pairs={{0,2},{2,0},{4,6},{6,4},{8,10},{10,8},{12,14},{14,12},{1,3},{3,1},... | collective-permute-start | bytes 442376 | tf_op jit(solution)/shard_map/ppermute | solution.py:605
  15.2 3.8 %local_other.1 = (bf16[512,1024]{1,0:T(8,128)(2,1)S(1)}, f32[512,16]{1,0:T(8,128)S(1)}, f32[32,512]{1,0:T(8,128)S(1)}, bf16[144,512]{1,0:T(8,128)(2,1)S(1)}, bf16[144,512]{1,0:T(8,128)(2,1)S(1)}) custom-call(s32[1]{0:T(128)} %bitcast.1.refs_2_.refs_0_, s32[1]{0:T(128)} %bitcast.2.refs_1_.refs_0_, ...), custom_call_target="tpu_custom_call" | custom-call | flops 5500000256 | bytes 5000000 | tf_op jit(solution)/shard_map/local_other/pallas_call | solution.py:48
  19.7 2.2 %collective-permute-start.4 = (bf16[144,512]{1,0:T(8,128)(2,1)S(1)}, bf16[144,512]{1,0:T(8,128)(2,1)S(1)}, u32[]{:S(2)}, u32[]{:S(2)}) collective-permute-start(bf16[144,512]{1,0:T(8,128)(2,1)S(1)} %pair_own.1.refs_5_.refs_1_), channel_id=1, source_target_pairs={{0,4},{1,0},{2,6},{3,2},{4,8},{5,1},{6,10},{7,3},{8,12},{9,5},{10,... | collective-permute-start | bytes 442376 | tf_op jit(solution)/shard_map/ppermute | solution.py:597
  21.9 2.5 %inside_own.1.refs_2_.refs_1_ = bf16[512,1024]{1,0:T(8,128)(2,1)S(1)} custom-call(bf16[512,1024]{1,0:T(8,128)(2,1)S(1)} %get-tuple-element.50.refs_0_, bf16[512,256]{1,0:T(8,128)(2,1)S(1)} %get-tuple-element.43.refs_1_.refs_2_.refs_4_, bf16[128,512]{1,0:T(8,128)(2,1)S(1)} %get-tuple-element.38.refs_4_.refs_2_, f32[512,16]{1,0:T(8,128)S(1)} %get-tuple-element.51.refs_3_, ...), custom_call_target="tpu_custom_call" | custom-call | flops 3520000000 | bytes 3200000 | tf_op jit(solution)/shard_map/inside_own/pallas_call | solution.py:48
  24.5 1.5 %gate_other.1.refs_3_.refs_8_ = bf16[512,1024]{1,0:T(8,128)(2,1)S(1)} custom-call(bf16[512,1024]{1,0:T(8,128)(2,1)S(1)} %get-tuple-element.36.refs_0_.refs_1_.refs_2_, bf16[1024,1024]{1,0:T(8,128)(2,1)S(1)} %collective-permute-done.6.refs_1_, bf16[512,1024]{1,0:T(8,128)(2,1)S(1)} %inside_own.1.refs_2_.refs_1_), custom_call_target="tpu_custom_call" | custom-call | flops 2640000000 | bytes 2400000 | tf_op jit(solution)/shard_map/gate_other/pallas_call | solution.py:48
  26.2 1.6 %collective-permute-start.8 = (bf16[144,512]{1,0:T(8,128)(2,1)S(1)}, bf16[144,512]{1,0:T(8,128)(2,1)S(1)}, u32[]{:S(2)}, u32[]{:S(2)}) collective-permute-start(bf16[144,512]{1,0:T(8,128)(2,1)S(1)} %pair_other.1.refs_3_.refs_1_), channel_id=1, source_target_pairs={{0,4},{1,0},{2,6},{3,2},{4,8},{5,1},{6,10},{7,3},{8,12},{9,5},{10,... | collective-permute-start | bytes 442376 | tf_op jit(solution)/shard_map/ppermute | solution.py:597
  27.9 1.1 %collective-permute-start.7 = (bf16[144,512]{1,0:T(8,128)(2,1)S(1)}, bf16[144,512]{1,0:T(8,128)(2,1)S(1)}, u32[]{:S(2)}, u32[]{:S(2)}) collective-permute-start(bf16[144,512]{1,0:T(8,128)(2,1)S(1)} %chain_own.1.refs_3_), channel_id=1, source_target_pairs={{0,8},{1,0},{2,10},{3,2},{4,12},{5,4},{6,14},{7,6},{8,9},{9,1},{10... | collective-permute-start | bytes 442376 | tf_op jit(solution)/shard_map/ppermute | solution.py:597
  29.0 1.5 %collective-permute-done.8.refs_2_.refs_3_ = bf16[144,512]{1,0:T(8,128)(2,1)S(1)} collective-permute-done((bf16[144,512]{1,0:T(8,128)(2,1)S(1)}, bf16[144,512]{1,0:T(8,128)(2,1)S(1)}, u32[]{:S(2)}, u32[]{:S(2)}) %collective-permute-start.8) | collective-permute-done | bytes 147488 | tf_op jit(solution)/shard_map/ppermute | solution.py:597
  30.5 5.1 %collective-permute-start.9 = (bf16[144,512]{1,0:T(8,128)(2,1)S(1)}, bf16[144,512]{1,0:T(8,128)(2,1)S(1)}, u32[]{:S(2)}, u32[]{:S(2)}) collective-permute-start(bf16[144,512]{1,0:T(8,128)(2,1)S(1)} %chain_other.1.refs_5_), channel_id=1, source_target_pairs={{0,8},{1,0},{2,10},{3,2},{4,12},{5,4},{6,14},{7,6},{8,9},{9,1},{10... | collective-permute-start | bytes 442376 | tf_op jit(solution)/shard_map/ppermute | solution.py:597
  35.9 1.5 %inside_other.2.refs_5_.refs_9_.refs_2_ = bf16[512,512]{1,0:T(8,128)(2,1)S(1)} custom-call(bf16[512,1024]{1,0:T(8,128)(2,1)S(1)} %get-tuple-element.42.refs_1_.refs_0_, bf16[512,256]{1,0:T(8,128)(2,1)S(1)} %get-tuple-element.43.refs_1_.refs_2_.refs_4_, bf16[128,512]{1,0:T(8,128)(2,1)S(1)} %get-tuple-element.38.refs_4_.refs_2_, ...), custom_call_target="tpu_custom_call" | custom-call | flops 1760000000 | bytes 1600000 | tf_op jit(solution)/shard_map/inside_other/pallas_call | solution.py:48
  37.4 0.9 %collective-permute-done.9.refs_4_ = bf16[144,512]{1,0:T(8,128)(2,1)S(1)} collective-permute-done((bf16[144,512]{1,0:T(8,128)(2,1)S(1)}, bf16[144,512]{1,0:T(8,128)(2,1)S(1)}, u32[]{:S(2)}, u32[]{:S(2)}) %collective-permute-start.9) | collective-permute-done | bytes 147488 | tf_op jit(solution)/shard_map/ppermute | solution.py:597
  38.5 1.1 %collective-permute-start.10 = (bf16[128,512]{1,0:T(8,128)(2,1)S(1)}, bf16[128,512]{1,0:T(8,128)(2,1)S(1)}, u32[]{:S(2)}, u32[]{:S(2)}) collective-permute-start(bf16[128,512]{1,0:T(8,128)(2,1)S(1)} %get-tuple-element.55), channel_id=1, source_target_pairs={{0,2},{2,0},{4,6},{6,4},{8,10},{10,8},{12,14},{14,12},{1,3},{3,1},... | collective-permute-start | bytes 393224 | tf_op jit(solution)/shard_map/ppermute | solution.py:671
  39.6 1.5 %inside_other.3.refs_10_.refs_3_ = bf16[512,512]{1,0:T(8,128)(2,1)S(1)} custom-call(bf16[512,1024]{1,0:T(8,128)(2,1)S(1)} %get-tuple-element.42.refs_1_.refs_0_, bf16[512,256]{1,0:T(8,128)(2,1)S(1)} %get-tuple-element.43.refs_1_.refs_2_.refs_4_, bf16[128,512]{1,0:T(8,128)(2,1)S(1)} %get-tuple-element.38.refs_4_.refs_2_, ...), custom_call_target="tpu_custom_call" | custom-call | flops 1760000000 | bytes 1600000 | tf_op jit(solution)/shard_map/inside_other/pallas_call | solution.py:48
  41.4 2.0 %part.1 = (f32[512,1024]{1,0:T(8,128)S(1)}, f32[512,128]{1,0:T(8,128)S(1)}) custom-call(s32[1]{0:T(128)} %bitcast.2.refs_1_.refs_0_, bf16[512,1024]{1,0:T(8,128)(2,1)S(1)} %inside_own.1.refs_2_.refs_1_, bf16[512,256]{1,0:T(8,128)(2,1)S(1)} %get-tuple-element.43.refs_1_.refs_2_.refs_4_, f32[512,16]{1,0:T(8,128)S(1)} %get-tuple-element.51.refs_3_, ...), custom_call_target="tpu_custom_call" | custom-call | flops 3849999872 | bytes 3500000 | tf_op jit(solution)/shard_map/part/pallas_call | solution.py:48
  43.6 1.5 %finish.1 = (bf16[512,512]{1,0:T(8,128)(2,1)S(1)}, bf16[512,1024]{1,0:T(8,128)(2,1)S(1)}, f32[512,128]{1,0:T(8,128)S(1)}) custom-call(s32[1]{0:T(128)} %bitcast.refs_0_, s32[1]{0:T(128)} %bitcast.2.refs_1_.refs_0_, bf16[512,512]{1,0:T(8,128)(2,1)S(1)} %inside_other.2.refs_5_.refs_9_.refs_2_, bf16[512,512]{1,0:T(8,128)(2,1)S(1)} %inside_other.3.refs_10_.refs_3_, ...), custom_call_target="tpu_custom_call" | custom-call | flops 3849999872 | bytes 3500000 | tf_op jit(solution)/shard_map/finish/pallas_call | solution.py:48
  45.2 0.7 %own_half.1.refs_0_ = bf16[512,512]{1,0:T(8,128)(2,1)S(1)} custom-call(s32[1]{0:T(128)} %bitcast.refs_0_, bf16[512,1024]{1,0:T(8,128)(2,1)S(1)} %get-tuple-element.60.refs_1_, bf16[1024,1024]{1,0:T(8,128)(2,1)S(1)} %collective-permute-done.11.refs_10_.refs_2_, f32[512,1024]{1,0:T(8,128)S(1)} %get-tuple-element.58.refs_11_.refs_3_, ...), custom_call_target="tpu_custom_call" | custom-call | flops 770000000 | bytes 700000 | tf_op jit(solution)/shard_map/own_half/pallas_call | solution.py:48
  46.0 1.1 %collective-permute-done.13.refs_1_ = bf16[512,512]{1,0:T(8,128)(2,1)S(1)} collective-permute-done((bf16[512,512]{1,0:T(8,128)(2,1)S(1)}, bf16[512,512]{1,0:T(8,128)(2,1)S(1)}, u32[]{:S(2)}, u32[]{:S(2)}) %collective-permute-start.13) | collective-permute-done | bytes 524320 | tf_op jit(solution)/shard_map/ppermute | solution.py:850
  47.1 0.8 %total.1 = bf16[512,512]{1,0:T(8,128)(2,1)} custom-call(bf16[512,512]{1,0:T(8,128)(2,1)S(1)} %own_half.1.refs_0_, bf16[512,512]{1,0:T(8,128)(2,1)S(1)} %collective-permute-done.13.refs_1_), custom_call_target="tpu_custom_call" | custom-call | flops 880000000 | bytes 800000 | tf_op jit(solution)/shard_map/total/pallas_call | solution.py:48
  (34 shorter events, 3.0 us)
Async XLA Ops:
  0.0 15.2 %collective-permute-start.1 = (bf16[1024,1024]{1,0:T(8,128)(2,1)}, bf16[1024,1024]{1,0:T(8,128)(2,1)S(1)}, u32[]{:S(2)}, u32[]{:S(2)}) collective-permute-start(bf16[1024,1024]{1,0:T(8,128)(2,1)} %refs_5_.3), channel_id=1, source_target_pairs={{0,1},{1,0},{2,3},{3,2},{4,5},{5,4},{6,7},{7,6},{8,9},{9,8},{10,11... | collective-permute-start | bytes 6291464 | tf_op jit(solution)/shard_map/ppermute | solution.py:850
  0.5 24.0 %collective-permute-start.6 = (bf16[1024,1024]{1,0:T(8,128)(2,1)}, bf16[1024,1024]{1,0:T(8,128)(2,1)S(1)}, u32[]{:S(2)}, u32[]{:S(2)}) collective-permute-start(bf16[1024,1024]{1,0:T(8,128)(2,1)} %refs_1_.1), channel_id=1, source_target_pairs={{0,1},{1,0},{2,3},{3,2},{4,5},{5,4},{6,7},{7,6},{8,9},{9,8},{10,11... | collective-permute-start | bytes 6291464 | tf_op jit(solution)/shard_map/ppermute | solution.py:850
  0.5 5.7 %copy-start.4 = (bf16[1024,1024]{1,0:T(8,128)(2,1)S(1)}, bf16[1024,1024]{1,0:T(8,128)(2,1)}, u32[]{:S(2)}) copy-start(bf16[1024,1024]{1,0:T(8,128)(2,1)} %refs_8_.1) | copy-start | bytes 6291460
  0.5 6.2 %copy-start.3 = (bf16[1024,1024]{1,0:T(8,128)(2,1)S(1)}, bf16[1024,1024]{1,0:T(8,128)(2,1)}, u32[]{:S(2)}) copy-start(bf16[1024,1024]{1,0:T(8,128)(2,1)} %refs_1_.1) | copy-start | bytes 6291460
  3.2 5.0 %collective-permute-start = (bf16[16,1024]{1,0:T(8,128)(2,1)S(1)}, bf16[16,1024]{1,0:T(8,128)(2,1)S(1)}, u32[]{:S(2)}, u32[]{:S(2)}) collective-permute-start(bf16[16,1024]{1,0:T(8,128)(2,1)S(1)} %get-tuple-element.37), channel_id=1, source_target_pairs={{0,2},{1,0},{2,4},{3,1},{4,6},{5,3},{6,8},{7,5},{8,10},{9,7},{10,1... | collective-permute-start | bytes 98312 | tf_op jit(solution)/shard_map/ppermute | solution.py:597
  6.2 9.0 %collective-permute-start.2 = (f32[24,1024]{1,0:T(8,128)S(1)}, f32[24,1024]{1,0:T(8,128)S(1)}, u32[]{:S(2)}, u32[]{:S(2)}) collective-permute-start(f32[24,1024]{1,0:T(8,128)S(1)} %get-tuple-element.40.refs_6_.refs_7_), channel_id=1, source_target_pairs={{0,1},{1,0},{2,3},{3,2},{4,5},{5,4},{6,7},{7,6},{8,9},{9,8},{10,11... | collective-permute-start | bytes 294920 | tf_op jit(solution)/shard_map/ppermute | solution.py:850
  6.2 37.2 %collective-permute-start.11 = (bf16[1024,1024]{1,0:T(8,128)(2,1)S(1)}, bf16[1024,1024]{1,0:T(8,128)(2,1)S(1)}, u32[]{:S(2)}, u32[]{:S(2)}) collective-permute-start(bf16[1024,1024]{1,0:T(8,128)(2,1)S(1)} %copy-done.4), channel_id=1, source_target_pairs={{0,1},{1,0},{2,3},{3,2},{4,5},{5,4},{6,7},{7,6},{8,9},{9,8},{10,11... | collective-permute-start | bytes 6291464 | tf_op jit(solution)/shard_map/ppermute | solution.py:850
  6.8 1.5 %copy-start = (bf16[1024,256]{1,0:T(8,128)(2,1)S(1)}, bf16[1024,256]{1,0:T(8,128)(2,1)}, u32[]{:S(2)}) copy-start(bf16[1024,256]{1,0:T(8,128)(2,1)} %refs_3_.3) | copy-start | bytes 1572868
  6.8 1.5 %copy-start.1 = (f32[4,256]{1,0:T(4,128)S(1)}, f32[4,256]{1,0:T(4,128)}, u32[]{:S(2)}) copy-start(f32[4,256]{1,0:T(4,128)} %refs_4_.1) | copy-start | bytes 12292
  8.2 1.6 %copy-start.2 = (bf16[1024,1024]{1,0:T(8,128)(2,1)S(1)}, bf16[1024,1024]{1,0:T(8,128)(2,1)}, u32[]{:S(2)}) copy-start(bf16[1024,1024]{1,0:T(8,128)(2,1)} %refs_5_.3) | copy-start | bytes 6291460
  13.6 6.0 %collective-permute-start.3 = (bf16[144,512]{1,0:T(8,128)(2,1)S(1)}, bf16[144,512]{1,0:T(8,128)(2,1)S(1)}, u32[]{:S(2)}, u32[]{:S(2)}) collective-permute-start(bf16[144,512]{1,0:T(8,128)(2,1)S(1)} %get-tuple-element.46), channel_id=1, source_target_pairs={{0,2},{2,0},{4,6},{6,4},{8,10},{10,8},{12,14},{14,12},{1,3},{3,1},... | collective-permute-start | bytes 442376 | tf_op jit(solution)/shard_map/ppermute | solution.py:605
  19.0 6.9 %collective-permute-start.5 = (bf16[144,512]{1,0:T(8,128)(2,1)S(1)}, bf16[144,512]{1,0:T(8,128)(2,1)S(1)}, u32[]{:S(2)}, u32[]{:S(2)}) collective-permute-start(bf16[144,512]{1,0:T(8,128)(2,1)S(1)} %get-tuple-element.48), channel_id=1, source_target_pairs={{0,2},{2,0},{4,6},{6,4},{8,10},{10,8},{12,14},{14,12},{1,3},{3,1},... | collective-permute-start | bytes 442376 | tf_op jit(solution)/shard_map/ppermute | solution.py:605
  19.7 8.1 %collective-permute-start.4 = (bf16[144,512]{1,0:T(8,128)(2,1)S(1)}, bf16[144,512]{1,0:T(8,128)(2,1)S(1)}, u32[]{:S(2)}, u32[]{:S(2)}) collective-permute-start(bf16[144,512]{1,0:T(8,128)(2,1)S(1)} %pair_own.1.refs_5_.refs_1_), channel_id=1, source_target_pairs={{0,4},{1,0},{2,6},{3,2},{4,8},{5,1},{6,10},{7,3},{8,12},{9,5},{10,... | collective-permute-start | bytes 442376 | tf_op jit(solution)/shard_map/ppermute | solution.py:597
  26.2 4.3 %collective-permute-start.8 = (bf16[144,512]{1,0:T(8,128)(2,1)S(1)}, bf16[144,512]{1,0:T(8,128)(2,1)S(1)}, u32[]{:S(2)}, u32[]{:S(2)}) collective-permute-start(bf16[144,512]{1,0:T(8,128)(2,1)S(1)} %pair_other.1.refs_3_.refs_1_), channel_id=1, source_target_pairs={{0,4},{1,0},{2,6},{3,2},{4,8},{5,1},{6,10},{7,3},{8,12},{9,5},{10,... | collective-permute-start | bytes 442376 | tf_op jit(solution)/shard_map/ppermute | solution.py:597
  27.9 7.8 %collective-permute-start.7 = (bf16[144,512]{1,0:T(8,128)(2,1)S(1)}, bf16[144,512]{1,0:T(8,128)(2,1)S(1)}, u32[]{:S(2)}, u32[]{:S(2)}) collective-permute-start(bf16[144,512]{1,0:T(8,128)(2,1)S(1)} %chain_own.1.refs_3_), channel_id=1, source_target_pairs={{0,8},{1,0},{2,10},{3,2},{4,12},{5,4},{6,14},{7,6},{8,9},{9,1},{10... | collective-permute-start | bytes 442376 | tf_op jit(solution)/shard_map/ppermute | solution.py:597
  30.5 7.8 %collective-permute-start.9 = (bf16[144,512]{1,0:T(8,128)(2,1)S(1)}, bf16[144,512]{1,0:T(8,128)(2,1)S(1)}, u32[]{:S(2)}, u32[]{:S(2)}) collective-permute-start(bf16[144,512]{1,0:T(8,128)(2,1)S(1)} %chain_other.1.refs_5_), channel_id=1, source_target_pairs={{0,8},{1,0},{2,10},{3,2},{4,12},{5,4},{6,14},{7,6},{8,9},{9,1},{10... | collective-permute-start | bytes 442376 | tf_op jit(solution)/shard_map/ppermute | solution.py:597
  35.8 5.6 %collective-permute-start.12 = (bf16[128,512]{1,0:T(8,128)(2,1)S(1)}, bf16[128,512]{1,0:T(8,128)(2,1)S(1)}, u32[]{:S(2)}, u32[]{:S(2)}) collective-permute-start(bf16[128,512]{1,0:T(8,128)(2,1)S(1)} %get-tuple-element.57), channel_id=1, source_target_pairs={{0,2},{2,0},{4,6},{6,4},{8,10},{10,8},{12,14},{14,12},{1,3},{3,1},... | collective-permute-start | bytes 393224 | tf_op jit(solution)/shard_map/ppermute | solution.py:671
  38.5 5.2 %collective-permute-start.10 = (bf16[128,512]{1,0:T(8,128)(2,1)S(1)}, bf16[128,512]{1,0:T(8,128)(2,1)S(1)}, u32[]{:S(2)}, u32[]{:S(2)}) collective-permute-start(bf16[128,512]{1,0:T(8,128)(2,1)S(1)} %get-tuple-element.55), channel_id=1, source_target_pairs={{0,2},{2,0},{4,6},{6,4},{8,10},{10,8},{12,14},{14,12},{1,3},{3,1},... | collective-permute-start | bytes 393224 | tf_op jit(solution)/shard_map/ppermute | solution.py:671
  45.2 2.0 %collective-permute-start.13 = (bf16[512,512]{1,0:T(8,128)(2,1)S(1)}, bf16[512,512]{1,0:T(8,128)(2,1)S(1)}, u32[]{:S(2)}, u32[]{:S(2)}) collective-permute-start(bf16[512,512]{1,0:T(8,128)(2,1)S(1)} %get-tuple-element.62.refs_5_), channel_id=1, source_target_pairs={{0,1},{1,0},{2,3},{3,2},{4,5},{5,4},{6,7},{7,6},{8,9},{9,8},{10,11... | collective-permute-start | bytes 1572872 | tf_op jit(solution)/shard_map/ppermute | solution.py:850

commit v14 on v13

--- a/solution.py
+++ b/solution.py
@@ -877,10 +877,10 @@
     done = mark_call(normed, after=[x_2])
     done = chain_1.pair(after=[done])
     y_1 = inside_call("own", x_1, bc, bt, cum_1, times_1, after=[done])
-    gate_2 = gate_call("other", normed, w_gate_2, after=[y_1])
-    done = chain_2.pair(after=[gate_2])
+    done = chain_2.pair(after=[y_1])
     done = chain_1.middle(after=[done])
-    done = chain_2.middle(after=[done])
+    gate_2 = gate_call("other", normed, w_gate_2, after=[done])
+    done = chain_2.middle(after=[gate_2])
     entry_1 = chain_1.entry(after=[done])
     scan_2 = ("other", x_2, bc, bt, cum_2, times_2)
     y_2 = [inside_call(*scan_2, after=[entry_1[0]], part=0, parts=2)]

time: 48.3 us -> 46 us (0.952)
  waiting for transfers between devices: 4.16 us -> 3.05 us
  starting transfers between devices: 17.5 us -> 16.5 us
    ppermute x5, waiting for transfers between devices: 2.46 us -> 0.42 us  [onward(): return lax.ppermute(value, ('seq', 'ch'), pairs)]
    ppermute x5, starting transfers between devices: 13 us -> 11.5 us  [onward(): return lax.ppermute(value, ('seq', 'ch'), pairs)]
    ppermute x2, starting transfers between devices: 1.22 us -> 1.77 us  [entry(): return (keep, lax.ppermute(out, 'seq', self.swap))]
    ppermute x2, waiting for transfers between devices: 0.06 us -> 0.6 us  [__init__(): self.other = lax.ppermute(send, 'seq', self.swap)]
  transfers between devices with their start and end apart: 14 -> 14, of which waited for: 6 -> 5; matrix products, arithmetic and copies ran while one was open for 0% -> 0% of each run, Pallas kernels for 48% -> 50%
where the time goes in v14:
time: 46 us; the launch traced here: 45.9 us
  Pallas kernels  25.4 us (55%)
  starting transfers between devices  16.5 us (36%)
  waiting for transfers between devices  3.05 us (7%)
  local copies, waits for them, and re-layouts  0.65 us (1%)
    pallas_call x20, Pallas kernels, call(): return lambda *arrays: run(*arrays, *after)  25.4 us
    ppermute x5, starting transfers between devices, onward(): return lax.ppermute(value, ('seq', 'ch'), pairs)  11.5 us
    ppermute x2, starting transfers between devices, __init__(): self.other = lax.ppermute(send, 'seq', self.swap)  2.14 us
    ppermute x2, starting transfers between devices, entry(): return (keep, lax.ppermute(out, 'seq', self.swap))  1.77 us
    ppermute x5, waiting for transfers between devices, theirs(): return lax.ppermute(a, 'ch', swap)  1.15 us
    ppermute x5, starting transfers between devices, theirs(): return lax.ppermute(a, 'ch', swap)  1.09 us
  transfers between devices with their start and end apart: 14, of which 5 were waited for; matrix products, arithmetic and copies ran while one was open for 0% of the time, Pallas kernels for 50%

profile of v14, /device:TPU:0, one launch (start us, length us, event | category | flops | bytes accessed | tf_op | source)
XLA Modules:
  0.0 45.9 jit_solution(5548402537631371410)
XLA Ops:
  0.5 2.7 %prepare.1 = (bf16[512,1024]{1,0:T(8,128)(2,1)S(1)}, bf16[16,1024]{1,0:T(8,128)(2,1)S(1)}, f32[24,1024]{1,0:T(8,128)S(1)}) custom-call(s32[1]{0:T(128)} %bitcast.refs_0_, s32[1]{0:T(128)} %bitcast.2.refs_1_.refs_0_, s32[1]{0:T(128)} %bitcast.1.refs_2_.refs_0_, bf16[512,1024]{1,0:T(8,128)(2,1)} %refs_3_.2, s32[1,512]{1,0:T(1,128)} %bitcast.10, ...), custom_call_target="tpu_custom_call" | custom-call | flops 2969999872 | bytes 2700000 | tf_op jit(solution)/shard_map/prepare/pallas_call | solution.py:48
  3.2 3.0 %collective-permute-start = (bf16[16,1024]{1,0:T(8,128)(2,1)S(1)}, bf16[16,1024]{1,0:T(8,128)(2,1)S(1)}, u32[]{:S(2)}, u32[]{:S(2)}) collective-permute-start(bf16[16,1024]{1,0:T(8,128)(2,1)S(1)} %get-tuple-element.37), channel_id=1, source_target_pairs={{0,2},{1,0},{2,4},{3,1},{4,6},{5,3},{6,8},{7,5},{8,10},{9,7},{10,1... | collective-permute-start | bytes 98312 | tf_op jit(solution)/shard_map/ppermute | solution.py:597
  6.8 1.5 %gate_own.1.refs_5_.refs_6_ = bf16[512,1024]{1,0:T(8,128)(2,1)S(1)} custom-call(bf16[512,1024]{1,0:T(8,128)(2,1)S(1)} %get-tuple-element.36.refs_0_.refs_1_.refs_2_, bf16[1024,1024]{1,0:T(8,128)(2,1)S(1)} %copy-done.3), custom_call_target="tpu_custom_call" | custom-call | flops 2640000000 | bytes 2400000 | tf_op jit(solution)/shard_map/gate_own/pallas_call | solution.py:48
  8.3 0.9 %maps.1 = (bf16[512,256]{1,0:T(8,128)(2,1)S(1)}, bf16[128,512]{1,0:T(8,128)(2,1)S(1)}) custom-call(s32[1]{0:T(128)} %bitcast.1.refs_2_.refs_0_, bf16[512,1024]{1,0:T(8,128)(2,1)S(1)} %get-tuple-element.36.refs_0_.refs_1_.refs_2_, bf16[16,1024]{1,0:T(8,128)(2,1)S(1)} %collective-permute-done.refs_2_.refs_3_, bf16[1024,256]{1,0:T(8,128)(2,1)S(1)} %copy-done, ...), custom_call_target="tpu_custom_call" | custom-call | flops 330000000 | bytes 300000 | tf_op jit(solution)/shard_map/maps/pallas_call | solution.py:48
  9.2 0.6 %copy-done.2 = bf16[1024,1024]{1,0:T(8,128)(2,1)S(1)} copy-done((bf16[1024,1024]{1,0:T(8,128)(2,1)S(1)}, bf16[1024,1024]{1,0:T(8,128)(2,1)}, u32[]{:S(2)}) %copy-start.2) | copy-done | bytes 2097176
  9.8 3.8 %local_own.1 = (bf16[512,1024]{1,0:T(8,128)(2,1)S(1)}, f32[512,16]{1,0:T(8,128)S(1)}, f32[32,512]{1,0:T(8,128)S(1)}, bf16[144,512]{1,0:T(8,128)(2,1)S(1)}, bf16[144,512]{1,0:T(8,128)(2,1)S(1)}) custom-call(s32[1]{0:T(128)} %bitcast.1.refs_2_.refs_0_, s32[1]{0:T(128)} %bitcast.2.refs_1_.refs_0_, ...), custom_call_target="tpu_custom_call" | custom-call | flops 5500000256 | bytes 5000000 | tf_op jit(solution)/shard_map/local_own/pallas_call | solution.py:48
  13.6 1.6 %collective-permute-start.3 = (bf16[144,512]{1,0:T(8,128)(2,1)S(1)}, bf16[144,512]{1,0:T(8,128)(2,1)S(1)}, u32[]{:S(2)}, u32[]{:S(2)}) collective-permute-start(bf16[144,512]{1,0:T(8,128)(2,1)S(1)} %get-tuple-element.46), channel_id=1, source_target_pairs={{0,2},{2,0},{4,6},{6,4},{8,10},{10,8},{12,14},{14,12},{1,3},{3,1},... | collective-permute-start | bytes 442376 | tf_op jit(solution)/shard_map/ppermute | solution.py:605
  15.2 3.8 %local_other.1 = (bf16[512,1024]{1,0:T(8,128)(2,1)S(1)}, f32[512,16]{1,0:T(8,128)S(1)}, f32[32,512]{1,0:T(8,128)S(1)}, bf16[144,512]{1,0:T(8,128)(2,1)S(1)}, bf16[144,512]{1,0:T(8,128)(2,1)S(1)}) custom-call(s32[1]{0:T(128)} %bitcast.1.refs_2_.refs_0_, s32[1]{0:T(128)} %bitcast.2.refs_1_.refs_0_, ...), custom_call_target="tpu_custom_call" | custom-call | flops 5500000256 | bytes 5000000 | tf_op jit(solution)/shard_map/local_other/pallas_call | solution.py:48
  19.7 2.2 %collective-permute-start.4 = (bf16[144,512]{1,0:T(8,128)(2,1)S(1)}, bf16[144,512]{1,0:T(8,128)(2,1)S(1)}, u32[]{:S(2)}, u32[]{:S(2)}) collective-permute-start(bf16[144,512]{1,0:T(8,128)(2,1)S(1)} %pair_own.1.refs_5_.refs_1_), channel_id=1, source_target_pairs={{0,4},{1,0},{2,6},{3,2},{4,8},{5,1},{6,10},{7,3},{8,12},{9,5},{10,... | collective-permute-start | bytes 442376 | tf_op jit(solution)/shard_map/ppermute | solution.py:597
  21.9 2.5 %inside_own.1.refs_3_.refs_1_ = bf16[512,1024]{1,0:T(8,128)(2,1)S(1)} custom-call(bf16[512,1024]{1,0:T(8,128)(2,1)S(1)} %get-tuple-element.49.refs_0_, bf16[512,256]{1,0:T(8,128)(2,1)S(1)} %get-tuple-element.43.refs_1_.refs_2_.refs_4_, bf16[128,512]{1,0:T(8,128)(2,1)S(1)} %get-tuple-element.38.refs_4_.refs_2_, f32[512,16]{1,0:T(8,128)S(1)} %get-tuple-element.50.refs_3_, ...), custom_call_target="tpu_custom_call" | custom-call | flops 3520000000 | bytes 3200000 | tf_op jit(solution)/shard_map/inside_own/pallas_call | solution.py:48
  25.1 1.6 %collective-permute-start.7 = (bf16[144,512]{1,0:T(8,128)(2,1)S(1)}, bf16[144,512]{1,0:T(8,128)(2,1)S(1)}, u32[]{:S(2)}, u32[]{:S(2)}) collective-permute-start(bf16[144,512]{1,0:T(8,128)(2,1)S(1)} %pair_other.1.refs_3_.refs_1_), channel_id=1, source_target_pairs={{0,4},{1,0},{2,6},{3,2},{4,8},{5,1},{6,10},{7,3},{8,12},{9,5},{10,... | collective-permute-start | bytes 442376 | tf_op jit(solution)/shard_map/ppermute | solution.py:597
  26.8 2.2 %collective-permute-start.6 = (bf16[144,512]{1,0:T(8,128)(2,1)S(1)}, bf16[144,512]{1,0:T(8,128)(2,1)S(1)}, u32[]{:S(2)}, u32[]{:S(2)}) collective-permute-start(bf16[144,512]{1,0:T(8,128)(2,1)S(1)} %chain_own.1.refs_2_), channel_id=1, source_target_pairs={{0,8},{1,0},{2,10},{3,2},{4,12},{5,4},{6,14},{7,6},{8,9},{9,1},{10... | collective-permute-start | bytes 442376 | tf_op jit(solution)/shard_map/ppermute | solution.py:597
  28.9 1.5 %gate_other.1.refs_3_.refs_8_ = bf16[512,1024]{1,0:T(8,128)(2,1)S(1)} custom-call(bf16[512,1024]{1,0:T(8,128)(2,1)S(1)} %get-tuple-element.36.refs_0_.refs_1_.refs_2_, bf16[1024,1024]{1,0:T(8,128)(2,1)S(1)} %collective-permute-done.8.refs_1_, bf16[144,512]{1,0:T(8,128)(2,1)S(1)} %chain_own.1.refs_2_), custom_call_target="tpu_custom_call" | custom-call | flops 2640000000 | bytes 2400000 | tf_op jit(solution)/shard_map/gate_other/pallas_call | solution.py:48
  30.5 2.5 %collective-permute-start.9 = (bf16[144,512]{1,0:T(8,128)(2,1)S(1)}, bf16[144,512]{1,0:T(8,128)(2,1)S(1)}, u32[]{:S(2)}, u32[]{:S(2)}) collective-permute-start(bf16[144,512]{1,0:T(8,128)(2,1)S(1)} %chain_other.1.refs_5_), channel_id=1, source_target_pairs={{0,8},{1,0},{2,10},{3,2},{4,12},{5,4},{6,14},{7,6},{8,9},{9,1},{10... | collective-permute-start | bytes 442376 | tf_op jit(solution)/shard_map/ppermute | solution.py:597
  33.1 0.7 %collective-permute-start.12 = (bf16[128,512]{1,0:T(8,128)(2,1)S(1)}, bf16[128,512]{1,0:T(8,128)(2,1)S(1)}, u32[]{:S(2)}, u32[]{:S(2)}) collective-permute-start(bf16[128,512]{1,0:T(8,128)(2,1)S(1)} %get-tuple-element.57), channel_id=1, source_target_pairs={{0,2},{2,0},{4,6},{6,4},{8,10},{10,8},{12,14},{14,12},{1,3},{3,1},... | collective-permute-start | bytes 393224 | tf_op jit(solution)/shard_map/ppermute | solution.py:671
  33.8 1.5 %inside_other.2.refs_5_.refs_9_.refs_2_ = bf16[512,512]{1,0:T(8,128)(2,1)S(1)} custom-call(bf16[512,1024]{1,0:T(8,128)(2,1)S(1)} %get-tuple-element.42.refs_1_.refs_0_, bf16[512,256]{1,0:T(8,128)(2,1)S(1)} %get-tuple-element.43.refs_1_.refs_2_.refs_4_, bf16[128,512]{1,0:T(8,128)(2,1)S(1)} %get-tuple-element.38.refs_4_.refs_2_, ...), custom_call_target="tpu_custom_call" | custom-call | flops 1760000000 | bytes 1600000 | tf_op jit(solution)/shard_map/inside_other/pallas_call | solution.py:48
  35.8 1.1 %collective-permute-start.10 = (bf16[128,512]{1,0:T(8,128)(2,1)S(1)}, bf16[128,512]{1,0:T(8,128)(2,1)S(1)}, u32[]{:S(2)}, u32[]{:S(2)}) collective-permute-start(bf16[128,512]{1,0:T(8,128)(2,1)S(1)} %get-tuple-element.55), channel_id=1, source_target_pairs={{0,2},{2,0},{4,6},{6,4},{8,10},{10,8},{12,14},{14,12},{1,3},{3,1},... | collective-permute-start | bytes 393224 | tf_op jit(solution)/shard_map/ppermute | solution.py:671
  36.9 1.5 %inside_other.3.refs_10_.refs_3_ = bf16[512,512]{1,0:T(8,128)(2,1)S(1)} custom-call(bf16[512,1024]{1,0:T(8,128)(2,1)S(1)} %get-tuple-element.42.refs_1_.refs_0_, bf16[512,256]{1,0:T(8,128)(2,1)S(1)} %get-tuple-element.43.refs_1_.refs_2_.refs_4_, bf16[128,512]{1,0:T(8,128)(2,1)S(1)} %get-tuple-element.38.refs_4_.refs_2_, ...), custom_call_target="tpu_custom_call" | custom-call | flops 1760000000 | bytes 1600000 | tf_op jit(solution)/shard_map/inside_other/pallas_call | solution.py:48
  38.5 2.0 %part.1 = (f32[512,1024]{1,0:T(8,128)S(1)}, f32[512,128]{1,0:T(8,128)S(1)}) custom-call(s32[1]{0:T(128)} %bitcast.2.refs_1_.refs_0_, bf16[512,1024]{1,0:T(8,128)(2,1)S(1)} %inside_own.1.refs_3_.refs_1_, bf16[512,256]{1,0:T(8,128)(2,1)S(1)} %get-tuple-element.43.refs_1_.refs_2_.refs_4_, f32[512,16]{1,0:T(8,128)S(1)} %get-tuple-element.50.refs_3_, ...), custom_call_target="tpu_custom_call" | custom-call | flops 3849999872 | bytes 3500000 | tf_op jit(solution)/shard_map/part/pallas_call | solution.py:48
  40.5 0.9 %collective-permute-done.10.refs_7_ = bf16[128,512]{1,0:T(8,128)(2,1)S(1)} collective-permute-done((bf16[128,512]{1,0:T(8,128)(2,1)S(1)}, bf16[128,512]{1,0:T(8,128)(2,1)S(1)}, u32[]{:S(2)}, u32[]{:S(2)}) %collective-permute-start.10) | collective-permute-done | bytes 131104 | tf_op jit(solution)/shard_map/ppermute | solution.py:671
  41.4 1.5 %finish.1 = (bf16[512,512]{1,0:T(8,128)(2,1)S(1)}, bf16[512,1024]{1,0:T(8,128)(2,1)S(1)}, f32[512,128]{1,0:T(8,128)S(1)}) custom-call(s32[1]{0:T(128)} %bitcast.refs_0_, s32[1]{0:T(128)} %bitcast.2.refs_1_.refs_0_, bf16[512,512]{1,0:T(8,128)(2,1)S(1)} %inside_other.2.refs_5_.refs_9_.refs_2_, bf16[512,512]{1,0:T(8,128)(2,1)S(1)} %inside_other.3.refs_10_.refs_3_, ...), custom_call_target="tpu_custom_call" | custom-call | flops 3849999872 | bytes 3500000 | tf_op jit(solution)/shard_map/finish/pallas_call | solution.py:48
  43.0 0.7 %own_half.1.refs_0_ = bf16[512,512]{1,0:T(8,128)(2,1)S(1)} custom-call(s32[1]{0:T(128)} %bitcast.refs_0_, bf16[512,1024]{1,0:T(8,128)(2,1)S(1)} %get-tuple-element.60.refs_1_, bf16[1024,1024]{1,0:T(8,128)(2,1)S(1)} %collective-permute-done.11.refs_10_.refs_2_, f32[512,1024]{1,0:T(8,128)S(1)} %get-tuple-element.58.refs_11_.refs_3_, ...), custom_call_target="tpu_custom_call" | custom-call | flops 770000000 | bytes 700000 | tf_op jit(solution)/shard_map/own_half/pallas_call | solution.py:48
  43.7 1.1 %collective-permute-done.13.refs_1_ = bf16[512,512]{1,0:T(8,128)(2,1)S(1)} collective-permute-done((bf16[512,512]{1,0:T(8,128)(2,1)S(1)}, bf16[512,512]{1,0:T(8,128)(2,1)S(1)}, u32[]{:S(2)}, u32[]{:S(2)}) %collective-permute-start.13) | collective-permute-done | bytes 524320 | tf_op jit(solution)/shard_map/ppermute | solution.py:850
  44.9 0.8 %total.1 = bf16[512,512]{1,0:T(8,128)(2,1)} custom-call(bf16[512,512]{1,0:T(8,128)(2,1)S(1)} %own_half.1.refs_0_, bf16[512,512]{1,0:T(8,128)(2,1)S(1)} %collective-permute-done.13.refs_1_), custom_call_target="tpu_custom_call" | custom-call | flops 880000000 | bytes 800000 | tf_op jit(solution)/shard_map/total/pallas_call | solution.py:48
  (34 shorter events, 3.2 us)
Async XLA Ops:
  0.0 15.2 %collective-permute-start.1 = (bf16[1024,1024]{1,0:T(8,128)(2,1)}, bf16[1024,1024]{1,0:T(8,128)(2,1)S(1)}, u32[]{:S(2)}, u32[]{:S(2)}) collective-permute-start(bf16[1024,1024]{1,0:T(8,128)(2,1)} %refs_5_.3), channel_id=1, source_target_pairs={{0,1},{1,0},{2,3},{3,2},{4,5},{5,4},{6,7},{7,6},{8,9},{9,8},{10,11... | collective-permute-start | bytes 6291464 | tf_op jit(solution)/shard_map/ppermute | solution.py:850
  0.5 28.5 %collective-permute-start.8 = (bf16[1024,1024]{1,0:T(8,128)(2,1)}, bf16[1024,1024]{1,0:T(8,128)(2,1)S(1)}, u32[]{:S(2)}, u32[]{:S(2)}) collective-permute-start(bf16[1024,1024]{1,0:T(8,128)(2,1)} %refs_1_.1), channel_id=1, source_target_pairs={{0,1},{1,0},{2,3},{3,2},{4,5},{5,4},{6,7},{7,6},{8,9},{9,8},{10,11... | collective-permute-start | bytes 6291464 | tf_op jit(solution)/shard_map/ppermute | solution.py:850
  0.5 5.7 %copy-start.4 = (bf16[1024,1024]{1,0:T(8,128)(2,1)S(1)}, bf16[1024,1024]{1,0:T(8,128)(2,1)}, u32[]{:S(2)}) copy-start(bf16[1024,1024]{1,0:T(8,128)(2,1)} %refs_8_.1) | copy-start | bytes 6291460
  0.5 6.2 %copy-start.3 = (bf16[1024,1024]{1,0:T(8,128)(2,1)S(1)}, bf16[1024,1024]{1,0:T(8,128)(2,1)}, u32[]{:S(2)}) copy-start(bf16[1024,1024]{1,0:T(8,128)(2,1)} %refs_1_.1) | copy-start | bytes 6291460
  3.2 5.0 %collective-permute-start = (bf16[16,1024]{1,0:T(8,128)(2,1)S(1)}, bf16[16,1024]{1,0:T(8,128)(2,1)S(1)}, u32[]{:S(2)}, u32[]{:S(2)}) collective-permute-start(bf16[16,1024]{1,0:T(8,128)(2,1)S(1)} %get-tuple-element.37), channel_id=1, source_target_pairs={{0,2},{1,0},{2,4},{3,1},{4,6},{5,3},{6,8},{7,5},{8,10},{9,7},{10,1... | collective-permute-start | bytes 98312 | tf_op jit(solution)/shard_map/ppermute | solution.py:597
  6.2 9.0 %collective-permute-start.2 = (f32[24,1024]{1,0:T(8,128)S(1)}, f32[24,1024]{1,0:T(8,128)S(1)}, u32[]{:S(2)}, u32[]{:S(2)}) collective-permute-start(f32[24,1024]{1,0:T(8,128)S(1)} %get-tuple-element.40.refs_6_.refs_7_), channel_id=1, source_target_pairs={{0,1},{1,0},{2,3},{3,2},{4,5},{5,4},{6,7},{7,6},{8,9},{9,8},{10,11... | collective-permute-start | bytes 294920 | tf_op jit(solution)/shard_map/ppermute | solution.py:850
  6.2 34.2 %collective-permute-start.11 = (bf16[1024,1024]{1,0:T(8,128)(2,1)S(1)}, bf16[1024,1024]{1,0:T(8,128)(2,1)S(1)}, u32[]{:S(2)}, u32[]{:S(2)}) collective-permute-start(bf16[1024,1024]{1,0:T(8,128)(2,1)S(1)} %copy-done.4), channel_id=1, source_target_pairs={{0,1},{1,0},{2,3},{3,2},{4,5},{5,4},{6,7},{7,6},{8,9},{9,8},{10,11... | collective-permute-start | bytes 6291464 | tf_op jit(solution)/shard_map/ppermute | solution.py:850
  6.8 1.5 %copy-start = (bf16[1024,256]{1,0:T(8,128)(2,1)S(1)}, bf16[1024,256]{1,0:T(8,128)(2,1)}, u32[]{:S(2)}) copy-start(bf16[1024,256]{1,0:T(8,128)(2,1)} %refs_3_.3) | copy-start | bytes 1572868
  6.8 1.5 %copy-start.1 = (f32[4,256]{1,0:T(4,128)S(1)}, f32[4,256]{1,0:T(4,128)}, u32[]{:S(2)}) copy-start(f32[4,256]{1,0:T(4,128)} %refs_4_.1) | copy-start | bytes 12292
  8.2 1.6 %copy-start.2 = (bf16[1024,1024]{1,0:T(8,128)(2,1)S(1)}, bf16[1024,1024]{1,0:T(8,128)(2,1)}, u32[]{:S(2)}) copy-start(bf16[1024,1024]{1,0:T(8,128)(2,1)} %refs_5_.3) | copy-start | bytes 6291460
  13.6 6.0 %collective-permute-start.3 = (bf16[144,512]{1,0:T(8,128)(2,1)S(1)}, bf16[144,512]{1,0:T(8,128)(2,1)S(1)}, u32[]{:S(2)}, u32[]{:S(2)}) collective-permute-start(bf16[144,512]{1,0:T(8,128)(2,1)S(1)} %get-tuple-element.46), channel_id=1, source_target_pairs={{0,2},{2,0},{4,6},{6,4},{8,10},{10,8},{12,14},{14,12},{1,3},{3,1},... | collective-permute-start | bytes 442376 | tf_op jit(solution)/shard_map/ppermute | solution.py:605
  19.0 6.0 %collective-permute-start.5 = (bf16[144,512]{1,0:T(8,128)(2,1)S(1)}, bf16[144,512]{1,0:T(8,128)(2,1)S(1)}, u32[]{:S(2)}, u32[]{:S(2)}) collective-permute-start(bf16[144,512]{1,0:T(8,128)(2,1)S(1)} %get-tuple-element.48), channel_id=1, source_target_pairs={{0,2},{2,0},{4,6},{6,4},{8,10},{10,8},{12,14},{14,12},{1,3},{3,1},... | collective-permute-start | bytes 442376 | tf_op jit(solution)/shard_map/ppermute | solution.py:605
  19.7 7.0 %collective-permute-start.4 = (bf16[144,512]{1,0:T(8,128)(2,1)S(1)}, bf16[144,512]{1,0:T(8,128)(2,1)S(1)}, u32[]{:S(2)}, u32[]{:S(2)}) collective-permute-start(bf16[144,512]{1,0:T(8,128)(2,1)S(1)} %pair_own.1.refs_5_.refs_1_), channel_id=1, source_target_pairs={{0,4},{1,0},{2,6},{3,2},{4,8},{5,1},{6,10},{7,3},{8,12},{9,5},{10,... | collective-permute-start | bytes 442376 | tf_op jit(solution)/shard_map/ppermute | solution.py:597
  25.1 5.3 %collective-permute-start.7 = (bf16[144,512]{1,0:T(8,128)(2,1)S(1)}, bf16[144,512]{1,0:T(8,128)(2,1)S(1)}, u32[]{:S(2)}, u32[]{:S(2)}) collective-permute-start(bf16[144,512]{1,0:T(8,128)(2,1)S(1)} %pair_other.1.refs_3_.refs_1_), channel_id=1, source_target_pairs={{0,4},{1,0},{2,6},{3,2},{4,8},{5,1},{6,10},{7,3},{8,12},{9,5},{10,... | collective-permute-start | bytes 442376 | tf_op jit(solution)/shard_map/ppermute | solution.py:597
  26.8 6.2 %collective-permute-start.6 = (bf16[144,512]{1,0:T(8,128)(2,1)S(1)}, bf16[144,512]{1,0:T(8,128)(2,1)S(1)}, u32[]{:S(2)}, u32[]{:S(2)}) collective-permute-start(bf16[144,512]{1,0:T(8,128)(2,1)S(1)} %chain_own.1.refs_2_), channel_id=1, source_target_pairs={{0,8},{1,0},{2,10},{3,2},{4,12},{5,4},{6,14},{7,6},{8,9},{9,1},{10... | collective-permute-start | bytes 442376 | tf_op jit(solution)/shard_map/ppermute | solution.py:597
  30.5 5.2 %collective-permute-start.9 = (bf16[144,512]{1,0:T(8,128)(2,1)S(1)}, bf16[144,512]{1,0:T(8,128)(2,1)S(1)}, u32[]{:S(2)}, u32[]{:S(2)}) collective-permute-start(bf16[144,512]{1,0:T(8,128)(2,1)S(1)} %chain_other.1.refs_5_), channel_id=1, source_target_pairs={{0,8},{1,0},{2,10},{3,2},{4,12},{5,4},{6,14},{7,6},{8,9},{9,1},{10... | collective-permute-start | bytes 442376 | tf_op jit(solution)/shard_map/ppermute | solution.py:597
  33.1 5.3 %collective-permute-start.12 = (bf16[128,512]{1,0:T(8,128)(2,1)S(1)}, bf16[128,512]{1,0:T(8,128)(2,1)S(1)}, u32[]{:S(2)}, u32[]{:S(2)}) collective-permute-start(bf16[128,512]{1,0:T(8,128)(2,1)S(1)} %get-tuple-element.57), channel_id=1, source_target_pairs={{0,2},{2,0},{4,6},{6,4},{8,10},{10,8},{12,14},{14,12},{1,3},{3,1},... | collective-permute-start | bytes 393224 | tf_op jit(solution)/shard_map/ppermute | solution.py:671
  35.8 5.6 %collective-permute-start.10 = (bf16[128,512]{1,0:T(8,128)(2,1)S(1)}, bf16[128,512]{1,0:T(8,128)(2,1)S(1)}, u32[]{:S(2)}, u32[]{:S(2)}) collective-permute-start(bf16[128,512]{1,0:T(8,128)(2,1)S(1)} %get-tuple-element.55), channel_id=1, source_target_pairs={{0,2},{2,0},{4,6},{6,4},{8,10},{10,8},{12,14},{14,12},{1,3},{3,1},... | collective-permute-start | bytes 393224 | tf_op jit(solution)/shard_map/ppermute | solution.py:671
  42.9 2.0 %collective-permute-start.13 = (bf16[512,512]{1,0:T(8,128)(2,1)S(1)}, bf16[512,512]{1,0:T(8,128)(2,1)S(1)}, u32[]{:S(2)}, u32[]{:S(2)}) collective-permute-start(bf16[512,512]{1,0:T(8,128)(2,1)S(1)} %get-tuple-element.62.refs_5_), channel_id=1, source_target_pairs={{0,1},{1,0},{2,3},{3,2},{4,5},{5,4},{6,7},{7,6},{8,9},{9,8},{10,11... | collective-permute-start | bytes 1572872 | tf_op jit(solution)/shard_map/ppermute | solution.py:850

commit v15 on v14

--- a/solution.py
+++ b/solution.py
@@ -866,7 +866,7 @@
     small_2 = theirs(small)
     w_gate_2 = theirs(w_gate_3)
     w_output_2 = theirs(w_output_3)
-    gate_1 = gate_call("own", normed, w_gate)
+    gate_1 = gate_call("own", normed, w_gate, after=[w_inner])
     bc, bt = maps_call(place, normed, halo, w_state, conv_state, after=[gate_1])
     x_1, cum_1, times_1, send_1, mine_1 = local_call("own", place, parity, normed, halo, bt, w_inner, small)
     chain_1 = Chain("own", place, send_1, mine_1)

time: 46 us -> 46.4 us (level)
  waiting for transfers between devices: 3.05 us -> 4.14 us
  local copies, waits for them, and re-layouts: 0.65 us -> 0.02 us
    ppermute x2, waiting for transfers between devices: 0.6 us -> 1.25 us  [__init__(): self.other = lax.ppermute(send, 'seq', self.swap)]
    unnamed x10, local copies, waits for them, and re-layouts: 0.65 us -> 0.02 us
  transfers between devices with their start and end apart: 14 -> 14, of which waited for: 5 -> 6; matrix products, arithmetic and copies ran while one was open for 0% -> 0% of each run, Pallas kernels for 50% -> 50%
where the time goes in v15:
time: 46.4 us; the launch traced here: 46.2 us
  Pallas kernels  25.4 us (55%)
  starting transfers between devices  16.4 us (35%)
  waiting for transfers between devices  4.14 us (9%)
    pallas_call x20, Pallas kernels, call(): return lambda *arrays: run(*arrays, *after)  25.4 us
    ppermute x5, starting transfers between devices, onward(): return lax.ppermute(value, ('seq', 'ch'), pairs)  11.5 us
    ppermute x2, starting transfers between devices, __init__(): self.other = lax.ppermute(send, 'seq', self.swap)  2.14 us
    ppermute x2, starting transfers between devices, entry(): return (keep, lax.ppermute(out, 'seq', self.swap))  1.55 us
    ppermute x2, waiting for transfers between devices, __init__(): self.other = lax.ppermute(send, 'seq', self.swap)  1.25 us
    ppermute x2, waiting for transfers between devices, entry(): return (keep, lax.ppermute(out, 'seq', self.swap))  1.23 us
    ppermute x5, starting transfers between devices, theirs(): return lax.ppermute(a, 'ch', swap)  1.23 us
    ppermute x5, waiting for transfers between devices, theirs(): return lax.ppermute(a, 'ch', swap)  1.03 us
  transfers between devices with their start and end apart: 14, of which 6 were waited for; matrix products, arithmetic and copies ran while one was open for 0% of the time, Pallas kernels for 50%

profile of v15, /device:TPU:0, one launch (start us, length us, event | category | flops | bytes accessed | tf_op | source)
XLA Modules:
  0.0 46.2 jit_solution(2833971688641713168)
XLA Ops:
  0.5 2.7 %prepare.1 = (bf16[512,1024]{1,0:T(8,128)(2,1)S(1)}, bf16[16,1024]{1,0:T(8,128)(2,1)S(1)}, f32[24,1024]{1,0:T(8,128)S(1)}) custom-call(s32[1]{0:T(128)} %bitcast.refs_0_, s32[1]{0:T(128)} %bitcast.2.refs_1_.refs_0_, s32[1]{0:T(128)} %bitcast.1.refs_2_.refs_0_, bf16[512,1024]{1,0:T(8,128)(2,1)} %refs_3_.2, s32[1,512]{1,0:T(1,128)} %bitcast.10, ...), custom_call_target="tpu_custom_call" | custom-call | flops 2969999872 | bytes 2700000 | tf_op jit(solution)/shard_map/prepare/pallas_call | solution.py:48
  3.2 3.0 %collective-permute-start = (bf16[16,1024]{1,0:T(8,128)(2,1)S(1)}, bf16[16,1024]{1,0:T(8,128)(2,1)S(1)}, u32[]{:S(2)}, u32[]{:S(2)}) collective-permute-start(bf16[16,1024]{1,0:T(8,128)(2,1)S(1)} %get-tuple-element.37), channel_id=1, source_target_pairs={{0,2},{1,0},{2,4},{3,1},{4,6},{5,3},{6,8},{7,5},{8,10},{9,7},{10,1... | collective-permute-start | bytes 98312 | tf_op jit(solution)/shard_map/ppermute | solution.py:597
  6.8 1.5 %gate_own.1.refs_5_.refs_6_ = bf16[512,1024]{1,0:T(8,128)(2,1)S(1)} custom-call(bf16[512,1024]{1,0:T(8,128)(2,1)S(1)} %get-tuple-element.36.refs_0_.refs_1_.refs_2_, bf16[1024,1024]{1,0:T(8,128)(2,1)S(1)} %copy-done.3, bf16[1024,1024]{1,0:T(8,128)(2,1)S(1)} %copy-done.2), custom_call_target="tpu_custom_call" | custom-call | flops 2640000000 | bytes 2400000 | tf_op jit(solution)/shard_map/gate_own/pallas_call | solution.py:48
  8.3 0.9 %maps.1 = (bf16[512,256]{1,0:T(8,128)(2,1)S(1)}, bf16[128,512]{1,0:T(8,128)(2,1)S(1)}) custom-call(s32[1]{0:T(128)} %bitcast.1.refs_2_.refs_0_, bf16[512,1024]{1,0:T(8,128)(2,1)S(1)} %get-tuple-element.36.refs_0_.refs_1_.refs_2_, bf16[16,1024]{1,0:T(8,128)(2,1)S(1)} %collective-permute-done.refs_2_.refs_3_, bf16[1024,256]{1,0:T(8,128)(2,1)S(1)} %copy-done, ...), custom_call_target="tpu_custom_call" | custom-call | flops 330000000 | bytes 300000 | tf_op jit(solution)/shard_map/maps/pallas_call | solution.py:48
  9.2 3.8 %local_own.1 = (bf16[512,1024]{1,0:T(8,128)(2,1)S(1)}, f32[512,16]{1,0:T(8,128)S(1)}, f32[32,512]{1,0:T(8,128)S(1)}, bf16[144,512]{1,0:T(8,128)(2,1)S(1)}, bf16[144,512]{1,0:T(8,128)(2,1)S(1)}) custom-call(s32[1]{0:T(128)} %bitcast.1.refs_2_.refs_0_, s32[1]{0:T(128)} %bitcast.2.refs_1_.refs_0_, ...), custom_call_target="tpu_custom_call" | custom-call | flops 5500000256 | bytes 5000000 | tf_op jit(solution)/shard_map/local_own/pallas_call | solution.py:48
  13.0 2.0 %collective-permute-start.3 = (bf16[144,512]{1,0:T(8,128)(2,1)S(1)}, bf16[144,512]{1,0:T(8,128)(2,1)S(1)}, u32[]{:S(2)}, u32[]{:S(2)}) collective-permute-start(bf16[144,512]{1,0:T(8,128)(2,1)S(1)} %get-tuple-element.46), channel_id=1, source_target_pairs={{0,2},{2,0},{4,6},{6,4},{8,10},{10,8},{12,14},{14,12},{1,3},{3,1},... | collective-permute-start | bytes 442376 | tf_op jit(solution)/shard_map/ppermute | solution.py:605
  15.0 3.8 %local_other.1 = (bf16[512,1024]{1,0:T(8,128)(2,1)S(1)}, f32[512,16]{1,0:T(8,128)S(1)}, f32[32,512]{1,0:T(8,128)S(1)}, bf16[144,512]{1,0:T(8,128)(2,1)S(1)}, bf16[144,512]{1,0:T(8,128)(2,1)S(1)}) custom-call(s32[1]{0:T(128)} %bitcast.1.refs_2_.refs_0_, s32[1]{0:T(128)} %bitcast.2.refs_1_.refs_0_, ...), custom_call_target="tpu_custom_call" | custom-call | flops 5500000256 | bytes 5000000 | tf_op jit(solution)/shard_map/local_other/pallas_call | solution.py:48
  19.0 0.7 %collective-permute-done.3.refs_2_ = bf16[144,512]{1,0:T(8,128)(2,1)S(1)} collective-permute-done((bf16[144,512]{1,0:T(8,128)(2,1)S(1)}, bf16[144,512]{1,0:T(8,128)(2,1)S(1)}, u32[]{:S(2)}, u32[]{:S(2)}) %collective-permute-start.3) | collective-permute-done | bytes 147488 | tf_op jit(solution)/shard_map/ppermute | solution.py:605
  19.7 2.2 %collective-permute-start.4 = (bf16[144,512]{1,0:T(8,128)(2,1)S(1)}, bf16[144,512]{1,0:T(8,128)(2,1)S(1)}, u32[]{:S(2)}, u32[]{:S(2)}) collective-permute-start(bf16[144,512]{1,0:T(8,128)(2,1)S(1)} %pair_own.1.refs_5_.refs_1_), channel_id=1, source_target_pairs={{0,4},{1,0},{2,6},{3,2},{4,8},{5,1},{6,10},{7,3},{8,12},{9,5},{10,... | collective-permute-start | bytes 442376 | tf_op jit(solution)/shard_map/ppermute | solution.py:597
  21.9 2.5 %inside_own.1.refs_3_.refs_1_ = bf16[512,1024]{1,0:T(8,128)(2,1)S(1)} custom-call(bf16[512,1024]{1,0:T(8,128)(2,1)S(1)} %get-tuple-element.49.refs_0_, bf16[512,256]{1,0:T(8,128)(2,1)S(1)} %get-tuple-element.43.refs_1_.refs_2_.refs_4_, bf16[128,512]{1,0:T(8,128)(2,1)S(1)} %get-tuple-element.38.refs_4_.refs_2_, f32[512,16]{1,0:T(8,128)S(1)} %get-tuple-element.50.refs_3_, ...), custom_call_target="tpu_custom_call" | custom-call | flops 3520000000 | bytes 3200000 | tf_op jit(solution)/shard_map/inside_own/pallas_call | solution.py:48
  25.1 1.6 %collective-permute-start.7 = (bf16[144,512]{1,0:T(8,128)(2,1)S(1)}, bf16[144,512]{1,0:T(8,128)(2,1)S(1)}, u32[]{:S(2)}, u32[]{:S(2)}) collective-permute-start(bf16[144,512]{1,0:T(8,128)(2,1)S(1)} %pair_other.1.refs_3_.refs_1_), channel_id=1, source_target_pairs={{0,4},{1,0},{2,6},{3,2},{4,8},{5,1},{6,10},{7,3},{8,12},{9,5},{10,... | collective-permute-start | bytes 442376 | tf_op jit(solution)/shard_map/ppermute | solution.py:597
  26.8 2.1 %collective-permute-start.6 = (bf16[144,512]{1,0:T(8,128)(2,1)S(1)}, bf16[144,512]{1,0:T(8,128)(2,1)S(1)}, u32[]{:S(2)}, u32[]{:S(2)}) collective-permute-start(bf16[144,512]{1,0:T(8,128)(2,1)S(1)} %chain_own.1.refs_2_), channel_id=1, source_target_pairs={{0,8},{1,0},{2,10},{3,2},{4,12},{5,4},{6,14},{7,6},{8,9},{9,1},{10... | collective-permute-start | bytes 442376 | tf_op jit(solution)/shard_map/ppermute | solution.py:597
  28.9 1.5 %gate_other.1.refs_3_.refs_8_ = bf16[512,1024]{1,0:T(8,128)(2,1)S(1)} custom-call(bf16[512,1024]{1,0:T(8,128)(2,1)S(1)} %get-tuple-element.36.refs_0_.refs_1_.refs_2_, bf16[1024,1024]{1,0:T(8,128)(2,1)S(1)} %collective-permute-done.8.refs_1_, bf16[144,512]{1,0:T(8,128)(2,1)S(1)} %chain_own.1.refs_2_), custom_call_target="tpu_custom_call" | custom-call | flops 2640000000 | bytes 2400000 | tf_op jit(solution)/shard_map/gate_other/pallas_call | solution.py:48
  30.5 2.5 %collective-permute-start.9 = (bf16[144,512]{1,0:T(8,128)(2,1)S(1)}, bf16[144,512]{1,0:T(8,128)(2,1)S(1)}, u32[]{:S(2)}, u32[]{:S(2)}) collective-permute-start(bf16[144,512]{1,0:T(8,128)(2,1)S(1)} %chain_other.1.refs_5_), channel_id=1, source_target_pairs={{0,8},{1,0},{2,10},{3,2},{4,12},{5,4},{6,14},{7,6},{8,9},{9,1},{10... | collective-permute-start | bytes 442376 | tf_op jit(solution)/shard_map/ppermute | solution.py:597
  33.6 1.5 %inside_other.2.refs_5_.refs_9_.refs_2_ = bf16[512,512]{1,0:T(8,128)(2,1)S(1)} custom-call(bf16[512,1024]{1,0:T(8,128)(2,1)S(1)} %get-tuple-element.42.refs_1_.refs_0_, bf16[512,256]{1,0:T(8,128)(2,1)S(1)} %get-tuple-element.43.refs_1_.refs_2_.refs_4_, bf16[128,512]{1,0:T(8,128)(2,1)S(1)} %get-tuple-element.38.refs_4_.refs_2_, ...), custom_call_target="tpu_custom_call" | custom-call | flops 1760000000 | bytes 1600000 | tf_op jit(solution)/shard_map/inside_other/pallas_call | solution.py:48
  35.1 0.6 %collective-permute-done.9.refs_4_ = bf16[144,512]{1,0:T(8,128)(2,1)S(1)} collective-permute-done((bf16[144,512]{1,0:T(8,128)(2,1)S(1)}, bf16[144,512]{1,0:T(8,128)(2,1)S(1)}, u32[]{:S(2)}, u32[]{:S(2)}) %collective-permute-start.9) | collective-permute-done | bytes 147488 | tf_op jit(solution)/shard_map/ppermute | solution.py:597
  35.8 1.1 %collective-permute-start.10 = (bf16[128,512]{1,0:T(8,128)(2,1)S(1)}, bf16[128,512]{1,0:T(8,128)(2,1)S(1)}, u32[]{:S(2)}, u32[]{:S(2)}) collective-permute-start(bf16[128,512]{1,0:T(8,128)(2,1)S(1)} %get-tuple-element.55), channel_id=1, source_target_pairs={{0,2},{2,0},{4,6},{6,4},{8,10},{10,8},{12,14},{14,12},{1,3},{3,1},... | collective-permute-start | bytes 393224 | tf_op jit(solution)/shard_map/ppermute | solution.py:671
  36.9 1.5 %inside_other.3.refs_10_.refs_3_ = bf16[512,512]{1,0:T(8,128)(2,1)S(1)} custom-call(bf16[512,1024]{1,0:T(8,128)(2,1)S(1)} %get-tuple-element.42.refs_1_.refs_0_, bf16[512,256]{1,0:T(8,128)(2,1)S(1)} %get-tuple-element.43.refs_1_.refs_2_.refs_4_, bf16[128,512]{1,0:T(8,128)(2,1)S(1)} %get-tuple-element.38.refs_4_.refs_2_, ...), custom_call_target="tpu_custom_call" | custom-call | flops 1760000000 | bytes 1600000 | tf_op jit(solution)/shard_map/inside_other/pallas_call | solution.py:48
  38.5 2.0 %part.1 = (f32[512,1024]{1,0:T(8,128)S(1)}, f32[512,128]{1,0:T(8,128)S(1)}) custom-call(s32[1]{0:T(128)} %bitcast.2.refs_1_.refs_0_, bf16[512,1024]{1,0:T(8,128)(2,1)S(1)} %inside_own.1.refs_3_.refs_1_, bf16[512,256]{1,0:T(8,128)(2,1)S(1)} %get-tuple-element.43.refs_1_.refs_2_.refs_4_, f32[512,16]{1,0:T(8,128)S(1)} %get-tuple-element.50.refs_3_, ...), custom_call_target="tpu_custom_call" | custom-call | flops 3849999872 | bytes 3500000 | tf_op jit(solution)/shard_map/part/pallas_call | solution.py:48
  40.6 1.2 %collective-permute-done.10.refs_7_ = bf16[128,512]{1,0:T(8,128)(2,1)S(1)} collective-permute-done((bf16[128,512]{1,0:T(8,128)(2,1)S(1)}, bf16[128,512]{1,0:T(8,128)(2,1)S(1)}, u32[]{:S(2)}, u32[]{:S(2)}) %collective-permute-start.10) | collective-permute-done | bytes 131104 | tf_op jit(solution)/shard_map/ppermute | solution.py:671
  41.7 1.5 %finish.1 = (bf16[512,512]{1,0:T(8,128)(2,1)S(1)}, bf16[512,1024]{1,0:T(8,128)(2,1)S(1)}, f32[512,128]{1,0:T(8,128)S(1)}) custom-call(s32[1]{0:T(128)} %bitcast.refs_0_, s32[1]{0:T(128)} %bitcast.2.refs_1_.refs_0_, bf16[512,512]{1,0:T(8,128)(2,1)S(1)} %inside_other.2.refs_5_.refs_9_.refs_2_, bf16[512,512]{1,0:T(8,128)(2,1)S(1)} %inside_other.3.refs_10_.refs_3_, ...), custom_call_target="tpu_custom_call" | custom-call | flops 3849999872 | bytes 3500000 | tf_op jit(solution)/shard_map/finish/pallas_call | solution.py:48
  43.4 0.7 %own_half.1.refs_0_ = bf16[512,512]{1,0:T(8,128)(2,1)S(1)} custom-call(s32[1]{0:T(128)} %bitcast.refs_0_, bf16[512,1024]{1,0:T(8,128)(2,1)S(1)} %get-tuple-element.60.refs_1_, bf16[1024,1024]{1,0:T(8,128)(2,1)S(1)} %collective-permute-done.11.refs_10_.refs_2_, f32[512,1024]{1,0:T(8,128)S(1)} %get-tuple-element.58.refs_11_.refs_3_, ...), custom_call_target="tpu_custom_call" | custom-call | flops 770000000 | bytes 700000 | tf_op jit(solution)/shard_map/own_half/pallas_call | solution.py:48
  44.2 1.0 %collective-permute-done.13.refs_1_ = bf16[512,512]{1,0:T(8,128)(2,1)S(1)} collective-permute-done((bf16[512,512]{1,0:T(8,128)(2,1)S(1)}, bf16[512,512]{1,0:T(8,128)(2,1)S(1)}, u32[]{:S(2)}, u32[]{:S(2)}) %collective-permute-start.13) | collective-permute-done | bytes 524320 | tf_op jit(solution)/shard_map/ppermute | solution.py:850
  45.2 0.8 %total.1 = bf16[512,512]{1,0:T(8,128)(2,1)} custom-call(bf16[512,512]{1,0:T(8,128)(2,1)S(1)} %own_half.1.refs_0_, bf16[512,512]{1,0:T(8,128)(2,1)S(1)} %collective-permute-done.13.refs_1_), custom_call_target="tpu_custom_call" | custom-call | flops 880000000 | bytes 800000 | tf_op jit(solution)/shard_map/total/pallas_call | solution.py:48
  (34 shorter events, 3.1 us)
Async XLA Ops:
  0.0 15.0 %collective-permute-start.1 = (bf16[1024,1024]{1,0:T(8,128)(2,1)}, bf16[1024,1024]{1,0:T(8,128)(2,1)S(1)}, u32[]{:S(2)}, u32[]{:S(2)}) collective-permute-start(bf16[1024,1024]{1,0:T(8,128)(2,1)} %refs_5_.3), channel_id=1, source_target_pairs={{0,1},{1,0},{2,3},{3,2},{4,5},{5,4},{6,7},{7,6},{8,9},{9,8},{10,11... | collective-permute-start | bytes 6291464 | tf_op jit(solution)/shard_map/ppermute | solution.py:850
  0.5 28.5 %collective-permute-start.8 = (bf16[1024,1024]{1,0:T(8,128)(2,1)}, bf16[1024,1024]{1,0:T(8,128)(2,1)S(1)}, u32[]{:S(2)}, u32[]{:S(2)}) collective-permute-start(bf16[1024,1024]{1,0:T(8,128)(2,1)} %refs_1_.1), channel_id=1, source_target_pairs={{0,1},{1,0},{2,3},{3,2},{4,5},{5,4},{6,7},{7,6},{8,9},{9,8},{10,11... | collective-permute-start | bytes 6291464 | tf_op jit(solution)/shard_map/ppermute | solution.py:850
  0.5 5.7 %copy-start.4 = (bf16[1024,1024]{1,0:T(8,128)(2,1)S(1)}, bf16[1024,1024]{1,0:T(8,128)(2,1)}, u32[]{:S(2)}) copy-start(bf16[1024,1024]{1,0:T(8,128)(2,1)} %refs_8_.1) | copy-start | bytes 6291460
  0.5 6.3 %copy-start.2 = (bf16[1024,1024]{1,0:T(8,128)(2,1)S(1)}, bf16[1024,1024]{1,0:T(8,128)(2,1)}, u32[]{:S(2)}) copy-start(bf16[1024,1024]{1,0:T(8,128)(2,1)} %refs_5_.3) | copy-start | bytes 6291460
  0.5 6.3 %copy-start.3 = (bf16[1024,1024]{1,0:T(8,128)(2,1)S(1)}, bf16[1024,1024]{1,0:T(8,128)(2,1)}, u32[]{:S(2)}) copy-start(bf16[1024,1024]{1,0:T(8,128)(2,1)} %refs_1_.1) | copy-start | bytes 6291460
  3.2 5.0 %collective-permute-start = (bf16[16,1024]{1,0:T(8,128)(2,1)S(1)}, bf16[16,1024]{1,0:T(8,128)(2,1)S(1)}, u32[]{:S(2)}, u32[]{:S(2)}) collective-permute-start(bf16[16,1024]{1,0:T(8,128)(2,1)S(1)} %get-tuple-element.37), channel_id=1, source_target_pairs={{0,2},{1,0},{2,4},{3,1},{4,6},{5,3},{6,8},{7,5},{8,10},{9,7},{10,1... | collective-permute-start | bytes 98312 | tf_op jit(solution)/shard_map/ppermute | solution.py:597
  6.2 8.7 %collective-permute-start.2 = (f32[24,1024]{1,0:T(8,128)S(1)}, f32[24,1024]{1,0:T(8,128)S(1)}, u32[]{:S(2)}, u32[]{:S(2)}) collective-permute-start(f32[24,1024]{1,0:T(8,128)S(1)} %get-tuple-element.40.refs_6_.refs_7_), channel_id=1, source_target_pairs={{0,1},{1,0},{2,3},{3,2},{4,5},{5,4},{6,7},{7,6},{8,9},{9,8},{10,11... | collective-permute-start | bytes 294920 | tf_op jit(solution)/shard_map/ppermute | solution.py:850
  6.3 34.3 %collective-permute-start.11 = (bf16[1024,1024]{1,0:T(8,128)(2,1)S(1)}, bf16[1024,1024]{1,0:T(8,128)(2,1)S(1)}, u32[]{:S(2)}, u32[]{:S(2)}) collective-permute-start(bf16[1024,1024]{1,0:T(8,128)(2,1)S(1)} %copy-done.4), channel_id=1, source_target_pairs={{0,1},{1,0},{2,3},{3,2},{4,5},{5,4},{6,7},{7,6},{8,9},{9,8},{10,11... | collective-permute-start | bytes 6291464 | tf_op jit(solution)/shard_map/ppermute | solution.py:850
  6.8 1.5 %copy-start = (bf16[1024,256]{1,0:T(8,128)(2,1)S(1)}, bf16[1024,256]{1,0:T(8,128)(2,1)}, u32[]{:S(2)}) copy-start(bf16[1024,256]{1,0:T(8,128)(2,1)} %refs_3_.3) | copy-start | bytes 1572868
  6.8 1.5 %copy-start.1 = (f32[4,256]{1,0:T(4,128)S(1)}, f32[4,256]{1,0:T(4,128)}, u32[]{:S(2)}) copy-start(f32[4,256]{1,0:T(4,128)} %refs_4_.1) | copy-start | bytes 12292
  13.0 6.6 %collective-permute-start.3 = (bf16[144,512]{1,0:T(8,128)(2,1)S(1)}, bf16[144,512]{1,0:T(8,128)(2,1)S(1)}, u32[]{:S(2)}, u32[]{:S(2)}) collective-permute-start(bf16[144,512]{1,0:T(8,128)(2,1)S(1)} %get-tuple-element.46), channel_id=1, source_target_pairs={{0,2},{2,0},{4,6},{6,4},{8,10},{10,8},{12,14},{14,12},{1,3},{3,1},... | collective-permute-start | bytes 442376 | tf_op jit(solution)/shard_map/ppermute | solution.py:605
  18.8 6.2 %collective-permute-start.5 = (bf16[144,512]{1,0:T(8,128)(2,1)S(1)}, bf16[144,512]{1,0:T(8,128)(2,1)S(1)}, u32[]{:S(2)}, u32[]{:S(2)}) collective-permute-start(bf16[144,512]{1,0:T(8,128)(2,1)S(1)} %get-tuple-element.48), channel_id=1, source_target_pairs={{0,2},{2,0},{4,6},{6,4},{8,10},{10,8},{12,14},{14,12},{1,3},{3,1},... | collective-permute-start | bytes 442376 | tf_op jit(solution)/shard_map/ppermute | solution.py:605
  19.7 7.0 %collective-permute-start.4 = (bf16[144,512]{1,0:T(8,128)(2,1)S(1)}, bf16[144,512]{1,0:T(8,128)(2,1)S(1)}, u32[]{:S(2)}, u32[]{:S(2)}) collective-permute-start(bf16[144,512]{1,0:T(8,128)(2,1)S(1)} %pair_own.1.refs_5_.refs_1_), channel_id=1, source_target_pairs={{0,4},{1,0},{2,6},{3,2},{4,8},{5,1},{6,10},{7,3},{8,12},{9,5},{10,... | collective-permute-start | bytes 442376 | tf_op jit(solution)/shard_map/ppermute | solution.py:597
  25.1 5.3 %collective-permute-start.7 = (bf16[144,512]{1,0:T(8,128)(2,1)S(1)}, bf16[144,512]{1,0:T(8,128)(2,1)S(1)}, u32[]{:S(2)}, u32[]{:S(2)}) collective-permute-start(bf16[144,512]{1,0:T(8,128)(2,1)S(1)} %pair_other.1.refs_3_.refs_1_), channel_id=1, source_target_pairs={{0,4},{1,0},{2,6},{3,2},{4,8},{5,1},{6,10},{7,3},{8,12},{9,5},{10,... | collective-permute-start | bytes 442376 | tf_op jit(solution)/shard_map/ppermute | solution.py:597
  26.8 6.2 %collective-permute-start.6 = (bf16[144,512]{1,0:T(8,128)(2,1)S(1)}, bf16[144,512]{1,0:T(8,128)(2,1)S(1)}, u32[]{:S(2)}, u32[]{:S(2)}) collective-permute-start(bf16[144,512]{1,0:T(8,128)(2,1)S(1)} %chain_own.1.refs_2_), channel_id=1, source_target_pairs={{0,8},{1,0},{2,10},{3,2},{4,12},{5,4},{6,14},{7,6},{8,9},{9,1},{10... | collective-permute-start | bytes 442376 | tf_op jit(solution)/shard_map/ppermute | solution.py:597
  30.5 5.2 %collective-permute-start.9 = (bf16[144,512]{1,0:T(8,128)(2,1)S(1)}, bf16[144,512]{1,0:T(8,128)(2,1)S(1)}, u32[]{:S(2)}, u32[]{:S(2)}) collective-permute-start(bf16[144,512]{1,0:T(8,128)(2,1)S(1)} %chain_other.1.refs_5_), channel_id=1, source_target_pairs={{0,8},{1,0},{2,10},{3,2},{4,12},{5,4},{6,14},{7,6},{8,9},{9,1},{10... | collective-permute-start | bytes 442376 | tf_op jit(solution)/shard_map/ppermute | solution.py:597
  33.1 5.4 %collective-permute-start.12 = (bf16[128,512]{1,0:T(8,128)(2,1)S(1)}, bf16[128,512]{1,0:T(8,128)(2,1)S(1)}, u32[]{:S(2)}, u32[]{:S(2)}) collective-permute-start(bf16[128,512]{1,0:T(8,128)(2,1)S(1)} %get-tuple-element.57), channel_id=1, source_target_pairs={{0,2},{2,0},{4,6},{6,4},{8,10},{10,8},{12,14},{14,12},{1,3},{3,1},... | collective-permute-start | bytes 393224 | tf_op jit(solution)/shard_map/ppermute | solution.py:671
  35.8 5.9 %collective-permute-start.10 = (bf16[128,512]{1,0:T(8,128)(2,1)S(1)}, bf16[128,512]{1,0:T(8,128)(2,1)S(1)}, u32[]{:S(2)}, u32[]{:S(2)}) collective-permute-start(bf16[128,512]{1,0:T(8,128)(2,1)S(1)} %get-tuple-element.55), channel_id=1, source_target_pairs={{0,2},{2,0},{4,6},{6,4},{8,10},{10,8},{12,14},{14,12},{1,3},{3,1},... | collective-permute-start | bytes 393224 | tf_op jit(solution)/shard_map/ppermute | solution.py:671
  43.2 2.0 %collective-permute-start.13 = (bf16[512,512]{1,0:T(8,128)(2,1)S(1)}, bf16[512,512]{1,0:T(8,128)(2,1)S(1)}, u32[]{:S(2)}, u32[]{:S(2)}) collective-permute-start(bf16[512,512]{1,0:T(8,128)(2,1)S(1)} %get-tuple-element.62.refs_5_), channel_id=1, source_target_pairs={{0,1},{1,0},{2,3},{3,2},{4,5},{5,4},{6,7},{7,6},{8,9},{9,8},{10,11... | collective-permute-start | bytes 1572872 | tf_op jit(solution)/shard_map/ppermute | solution.py:850

commit v16 on v14

--- a/solution.py
+++ b/solution.py
@@ -711,27 +711,29 @@
 
 def product(back, scaled_ref, weights_ref, part_ref, scale_ref, tile_ref, half_ref, out_ref, first):
     rows, half = out_ref.shape
-    for low in range(0, half, TILE):
+
+    def compute(low, target_ref):
         columns = slice(first + low, first + low + TILE)
         tile_ref[...] = dot(scaled_ref[...], weights_ref[:, columns])
         for r in range(0, rows, BLOCK):
             block = slice(r, r + BLOCK)
             value = (tile_ref[block, :] + part_ref[block, columns]) * scale_ref[block, :1]
-            half_ref[block, low : low + TILE] = value.astype(BF16)
+            target_ref[block, low : low + TILE] = value.astype(BF16)
 
     @pl.when(back == 1)
     def _():
         turn = flip_matrix(TILE)
-        for r in range(0, rows, TILE):
-            for low in range(0, half, TILE):
+        for low in range(0, half, TILE):
+            compute(low, half_ref)
+            to = half - TILE - low
+            for r in range(0, rows, TILE):
                 tile = dot(turn, half_ref[r : r + TILE, low : low + TILE]).astype(BF16)
-                tile = dot(tile, turn).astype(BF16)
-                to_row, to = rows - TILE - r, half - TILE - low
-                out_ref[to_row : to_row + TILE, to : to + TILE] = tile
+                out_ref[rows - TILE - r : rows - r, to : to + TILE] = dot(tile, turn).astype(BF16)
 
     @pl.when(back != 1)
     def _():
-        out_ref[...] = half_ref[...]
+        for low in range(0, half, TILE):
+            compute(low, out_ref)
 
 
 def finish_kernel(head_size, shares, full_width, back_ref, parity_ref, *refs):

time: 46 us -> 47.1 us (1.024)
  starting transfers between devices: 16.5 us -> 17.1 us
    ppermute x5, starting transfers between devices: 1.09 us -> 1.7 us  [theirs(): return lax.ppermute(a, 'ch', swap)]
  transfers between devices with their start and end apart: 14 -> 14, of which waited for: 5 -> 5; matrix products, arithmetic and copies ran while one was open for 0% -> 0% of each run, Pallas kernels for 50% -> 49%
where the time goes in v16:
time: 47.1 us; the launch traced here: 46.6 us
  Pallas kernels  25.8 us (55%)
  starting transfers between devices  17.1 us (36%)
  waiting for transfers between devices  2.73 us (6%)
  local copies, waits for them, and re-layouts  0.65 us (1%)
    pallas_call x20, Pallas kernels, call(): return lambda *arrays: run(*arrays, *after)  25.8 us
    ppermute x5, starting transfers between devices, onward(): return lax.ppermute(value, ('seq', 'ch'), pairs)  11.5 us
    ppermute x2, starting transfers between devices, __init__(): self.other = lax.ppermute(send, 'seq', self.swap)  2.14 us
    ppermute x2, starting transfers between devices, entry(): return (keep, lax.ppermute(out, 'seq', self.swap))  1.77 us
    ppermute x5, starting transfers between devices, theirs(): return lax.ppermute(a, 'ch', swap)  1.7 us
  transfers between devices with their start and end apart: 14, of which 5 were waited for; matrix products, arithmetic and copies ran while one was open for 0% of the time, Pallas kernels for 49%

profile of v16, /device:TPU:0, one launch (start us, length us, event | category | flops | bytes accessed | tf_op | source)
XLA Modules:
  0.0 46.6 jit_solution(11404446759988088214)
XLA Ops:
  0.5 2.7 %prepare.1 = (bf16[512,1024]{1,0:T(8,128)(2,1)S(1)}, bf16[16,1024]{1,0:T(8,128)(2,1)S(1)}, f32[24,1024]{1,0:T(8,128)S(1)}) custom-call(s32[1]{0:T(128)} %bitcast.refs_0_, s32[1]{0:T(128)} %bitcast.2.refs_1_.refs_0_, s32[1]{0:T(128)} %bitcast.1.refs_2_.refs_0_, bf16[512,1024]{1,0:T(8,128)(2,1)} %refs_3_.2, s32[1,512]{1,0:T(1,128)} %bitcast.10, ...), custom_call_target="tpu_custom_call" | custom-call | flops 2969999872 | bytes 2700000 | tf_op jit(solution)/shard_map/prepare/pallas_call | solution.py:48
  3.2 3.0 %collective-permute-start = (bf16[16,1024]{1,0:T(8,128)(2,1)S(1)}, bf16[16,1024]{1,0:T(8,128)(2,1)S(1)}, u32[]{:S(2)}, u32[]{:S(2)}) collective-permute-start(bf16[16,1024]{1,0:T(8,128)(2,1)S(1)} %get-tuple-element.37), channel_id=1, source_target_pairs={{0,2},{1,0},{2,4},{3,1},{4,6},{5,3},{6,8},{7,5},{8,10},{9,7},{10,1... | collective-permute-start | bytes 98312 | tf_op jit(solution)/shard_map/ppermute | solution.py:597
  6.8 1.5 %gate_own.1.refs_5_.refs_6_ = bf16[512,1024]{1,0:T(8,128)(2,1)S(1)} custom-call(bf16[512,1024]{1,0:T(8,128)(2,1)S(1)} %get-tuple-element.36.refs_0_.refs_1_.refs_2_, bf16[1024,1024]{1,0:T(8,128)(2,1)S(1)} %copy-done.3), custom_call_target="tpu_custom_call" | custom-call | flops 2640000000 | bytes 2400000 | tf_op jit(solution)/shard_map/gate_own/pallas_call | solution.py:48
  8.3 0.9 %maps.1 = (bf16[512,256]{1,0:T(8,128)(2,1)S(1)}, bf16[128,512]{1,0:T(8,128)(2,1)S(1)}) custom-call(s32[1]{0:T(128)} %bitcast.1.refs_2_.refs_0_, bf16[512,1024]{1,0:T(8,128)(2,1)S(1)} %get-tuple-element.36.refs_0_.refs_1_.refs_2_, bf16[16,1024]{1,0:T(8,128)(2,1)S(1)} %collective-permute-done.refs_2_.refs_3_, bf16[1024,256]{1,0:T(8,128)(2,1)S(1)} %copy-done, ...), custom_call_target="tpu_custom_call" | custom-call | flops 330000000 | bytes 300000 | tf_op jit(solution)/shard_map/maps/pallas_call | solution.py:48
  9.8 3.8 %local_own.1 = (bf16[512,1024]{1,0:T(8,128)(2,1)S(1)}, f32[512,16]{1,0:T(8,128)S(1)}, f32[32,512]{1,0:T(8,128)S(1)}, bf16[144,512]{1,0:T(8,128)(2,1)S(1)}, bf16[144,512]{1,0:T(8,128)(2,1)S(1)}) custom-call(s32[1]{0:T(128)} %bitcast.1.refs_2_.refs_0_, s32[1]{0:T(128)} %bitcast.2.refs_1_.refs_0_, ...), custom_call_target="tpu_custom_call" | custom-call | flops 5500000256 | bytes 5000000 | tf_op jit(solution)/shard_map/local_own/pallas_call | solution.py:48
  13.6 1.6 %collective-permute-start.3 = (bf16[144,512]{1,0:T(8,128)(2,1)S(1)}, bf16[144,512]{1,0:T(8,128)(2,1)S(1)}, u32[]{:S(2)}, u32[]{:S(2)}) collective-permute-start(bf16[144,512]{1,0:T(8,128)(2,1)S(1)} %get-tuple-element.46), channel_id=1, source_target_pairs={{0,2},{2,0},{4,6},{6,4},{8,10},{10,8},{12,14},{14,12},{1,3},{3,1},... | collective-permute-start | bytes 442376 | tf_op jit(solution)/shard_map/ppermute | solution.py:605
  15.2 3.8 %local_other.1 = (bf16[512,1024]{1,0:T(8,128)(2,1)S(1)}, f32[512,16]{1,0:T(8,128)S(1)}, f32[32,512]{1,0:T(8,128)S(1)}, bf16[144,512]{1,0:T(8,128)(2,1)S(1)}, bf16[144,512]{1,0:T(8,128)(2,1)S(1)}) custom-call(s32[1]{0:T(128)} %bitcast.1.refs_2_.refs_0_, s32[1]{0:T(128)} %bitcast.2.refs_1_.refs_0_, ...), custom_call_target="tpu_custom_call" | custom-call | flops 5500000256 | bytes 5000000 | tf_op jit(solution)/shard_map/local_other/pallas_call | solution.py:48
  19.7 2.2 %collective-permute-start.4 = (bf16[144,512]{1,0:T(8,128)(2,1)S(1)}, bf16[144,512]{1,0:T(8,128)(2,1)S(1)}, u32[]{:S(2)}, u32[]{:S(2)}) collective-permute-start(bf16[144,512]{1,0:T(8,128)(2,1)S(1)} %pair_own.1.refs_5_.refs_1_), channel_id=1, source_target_pairs={{0,4},{1,0},{2,6},{3,2},{4,8},{5,1},{6,10},{7,3},{8,12},{9,5},{10,... | collective-permute-start | bytes 442376 | tf_op jit(solution)/shard_map/ppermute | solution.py:597
  21.9 2.5 %inside_own.1.refs_3_.refs_1_ = bf16[512,1024]{1,0:T(8,128)(2,1)S(1)} custom-call(bf16[512,1024]{1,0:T(8,128)(2,1)S(1)} %get-tuple-element.49.refs_0_, bf16[512,256]{1,0:T(8,128)(2,1)S(1)} %get-tuple-element.43.refs_1_.refs_2_.refs_4_, bf16[128,512]{1,0:T(8,128)(2,1)S(1)} %get-tuple-element.38.refs_4_.refs_2_, f32[512,16]{1,0:T(8,128)S(1)} %get-tuple-element.50.refs_3_, ...), custom_call_target="tpu_custom_call" | custom-call | flops 3520000000 | bytes 3200000 | tf_op jit(solution)/shard_map/inside_own/pallas_call | solution.py:48
  25.1 1.6 %collective-permute-start.7 = (bf16[144,512]{1,0:T(8,128)(2,1)S(1)}, bf16[144,512]{1,0:T(8,128)(2,1)S(1)}, u32[]{:S(2)}, u32[]{:S(2)}) collective-permute-start(bf16[144,512]{1,0:T(8,128)(2,1)S(1)} %pair_other.1.refs_3_.refs_1_), channel_id=1, source_target_pairs={{0,4},{1,0},{2,6},{3,2},{4,8},{5,1},{6,10},{7,3},{8,12},{9,5},{10,... | collective-permute-start | bytes 442376 | tf_op jit(solution)/shard_map/ppermute | solution.py:597
  26.8 2.2 %collective-permute-start.6 = (bf16[144,512]{1,0:T(8,128)(2,1)S(1)}, bf16[144,512]{1,0:T(8,128)(2,1)S(1)}, u32[]{:S(2)}, u32[]{:S(2)}) collective-permute-start(bf16[144,512]{1,0:T(8,128)(2,1)S(1)} %chain_own.1.refs_2_), channel_id=1, source_target_pairs={{0,8},{1,0},{2,10},{3,2},{4,12},{5,4},{6,14},{7,6},{8,9},{9,1},{10... | collective-permute-start | bytes 442376 | tf_op jit(solution)/shard_map/ppermute | solution.py:597
  28.9 1.5 %gate_other.1.refs_3_.refs_8_ = bf16[512,1024]{1,0:T(8,128)(2,1)S(1)} custom-call(bf16[512,1024]{1,0:T(8,128)(2,1)S(1)} %get-tuple-element.36.refs_0_.refs_1_.refs_2_, bf16[1024,1024]{1,0:T(8,128)(2,1)S(1)} %collective-permute-done.8.refs_1_, bf16[144,512]{1,0:T(8,128)(2,1)S(1)} %chain_own.1.refs_2_), custom_call_target="tpu_custom_call" | custom-call | flops 2640000000 | bytes 2400000 | tf_op jit(solution)/shard_map/gate_other/pallas_call | solution.py:48
  30.5 2.5 %collective-permute-start.9 = (bf16[144,512]{1,0:T(8,128)(2,1)S(1)}, bf16[144,512]{1,0:T(8,128)(2,1)S(1)}, u32[]{:S(2)}, u32[]{:S(2)}) collective-permute-start(bf16[144,512]{1,0:T(8,128)(2,1)S(1)} %chain_other.1.refs_5_), channel_id=1, source_target_pairs={{0,8},{1,0},{2,10},{3,2},{4,12},{5,4},{6,14},{7,6},{8,9},{9,1},{10... | collective-permute-start | bytes 442376 | tf_op jit(solution)/shard_map/ppermute | solution.py:597
  33.1 0.7 %collective-permute-start.12 = (bf16[128,512]{1,0:T(8,128)(2,1)S(1)}, bf16[128,512]{1,0:T(8,128)(2,1)S(1)}, u32[]{:S(2)}, u32[]{:S(2)}) collective-permute-start(bf16[128,512]{1,0:T(8,128)(2,1)S(1)} %get-tuple-element.57), channel_id=1, source_target_pairs={{0,2},{2,0},{4,6},{6,4},{8,10},{10,8},{12,14},{14,12},{1,3},{3,1},... | collective-permute-start | bytes 393224 | tf_op jit(solution)/shard_map/ppermute | solution.py:671
  33.8 1.5 %inside_other.2.refs_5_.refs_9_.refs_2_ = bf16[512,512]{1,0:T(8,128)(2,1)S(1)} custom-call(bf16[512,1024]{1,0:T(8,128)(2,1)S(1)} %get-tuple-element.42.refs_1_.refs_0_, bf16[512,256]{1,0:T(8,128)(2,1)S(1)} %get-tuple-element.43.refs_1_.refs_2_.refs_4_, bf16[128,512]{1,0:T(8,128)(2,1)S(1)} %get-tuple-element.38.refs_4_.refs_2_, ...), custom_call_target="tpu_custom_call" | custom-call | flops 1760000000 | bytes 1600000 | tf_op jit(solution)/shard_map/inside_other/pallas_call | solution.py:48
  35.8 1.1 %collective-permute-start.10 = (bf16[128,512]{1,0:T(8,128)(2,1)S(1)}, bf16[128,512]{1,0:T(8,128)(2,1)S(1)}, u32[]{:S(2)}, u32[]{:S(2)}) collective-permute-start(bf16[128,512]{1,0:T(8,128)(2,1)S(1)} %get-tuple-element.55), channel_id=1, source_target_pairs={{0,2},{2,0},{4,6},{6,4},{8,10},{10,8},{12,14},{14,12},{1,3},{3,1},... | collective-permute-start | bytes 393224 | tf_op jit(solution)/shard_map/ppermute | solution.py:671
  36.9 1.5 %inside_other.3.refs_10_.refs_3_ = bf16[512,512]{1,0:T(8,128)(2,1)S(1)} custom-call(bf16[512,1024]{1,0:T(8,128)(2,1)S(1)} %get-tuple-element.42.refs_1_.refs_0_, bf16[512,256]{1,0:T(8,128)(2,1)S(1)} %get-tuple-element.43.refs_1_.refs_2_.refs_4_, bf16[128,512]{1,0:T(8,128)(2,1)S(1)} %get-tuple-element.38.refs_4_.refs_2_, ...), custom_call_target="tpu_custom_call" | custom-call | flops 1760000000 | bytes 1600000 | tf_op jit(solution)/shard_map/inside_other/pallas_call | solution.py:48
  38.5 2.0 %part.1 = (f32[512,1024]{1,0:T(8,128)S(1)}, f32[512,128]{1,0:T(8,128)S(1)}) custom-call(s32[1]{0:T(128)} %bitcast.2.refs_1_.refs_0_, bf16[512,1024]{1,0:T(8,128)(2,1)S(1)} %inside_own.1.refs_3_.refs_1_, bf16[512,256]{1,0:T(8,128)(2,1)S(1)} %get-tuple-element.43.refs_1_.refs_2_.refs_4_, f32[512,16]{1,0:T(8,128)S(1)} %get-tuple-element.50.refs_3_, ...), custom_call_target="tpu_custom_call" | custom-call | flops 3849999872 | bytes 3500000 | tf_op jit(solution)/shard_map/part/pallas_call | solution.py:48
  40.5 0.9 %collective-permute-done.10.refs_7_ = bf16[128,512]{1,0:T(8,128)(2,1)S(1)} collective-permute-done((bf16[128,512]{1,0:T(8,128)(2,1)S(1)}, bf16[128,512]{1,0:T(8,128)(2,1)S(1)}, u32[]{:S(2)}, u32[]{:S(2)}) %collective-permute-start.10) | collective-permute-done | bytes 131104 | tf_op jit(solution)/shard_map/ppermute | solution.py:671
  41.4 2.0 %finish.1 = (bf16[512,512]{1,0:T(8,128)(2,1)S(1)}, bf16[512,1024]{1,0:T(8,128)(2,1)S(1)}, f32[512,128]{1,0:T(8,128)S(1)}) custom-call(s32[1]{0:T(128)} %bitcast.refs_0_, s32[1]{0:T(128)} %bitcast.2.refs_1_.refs_0_, bf16[512,512]{1,0:T(8,128)(2,1)S(1)} %inside_other.2.refs_5_.refs_9_.refs_2_, bf16[512,512]{1,0:T(8,128)(2,1)S(1)} %inside_other.3.refs_10_.refs_3_, ...), custom_call_target="tpu_custom_call" | custom-call | flops 3849999872 | bytes 3500000 | tf_op jit(solution)/shard_map/finish/pallas_call | solution.py:48
  43.4 0.7 %collective-permute-start.13 = (bf16[512,512]{1,0:T(8,128)(2,1)S(1)}, bf16[512,512]{1,0:T(8,128)(2,1)S(1)}, u32[]{:S(2)}, u32[]{:S(2)}) collective-permute-start(bf16[512,512]{1,0:T(8,128)(2,1)S(1)} %get-tuple-element.62.refs_5_), channel_id=1, source_target_pairs={{0,1},{1,0},{2,3},{3,2},{4,5},{5,4},{6,7},{7,6},{8,9},{9,8},{10,11... | collective-permute-start | bytes 1572872 | tf_op jit(solution)/shard_map/ppermute | solution.py:852
  44.1 0.7 %own_half.1.refs_0_ = bf16[512,512]{1,0:T(8,128)(2,1)S(1)} custom-call(s32[1]{0:T(128)} %bitcast.refs_0_, bf16[512,1024]{1,0:T(8,128)(2,1)S(1)} %get-tuple-element.60.refs_1_, bf16[1024,1024]{1,0:T(8,128)(2,1)S(1)} %collective-permute-done.11.refs_10_.refs_2_, f32[512,1024]{1,0:T(8,128)S(1)} %get-tuple-element.58.refs_11_.refs_3_, ...), custom_call_target="tpu_custom_call" | custom-call | flops 770000000 | bytes 700000 | tf_op jit(solution)/shard_map/own_half/pallas_call | solution.py:48
  44.8 0.8 %collective-permute-done.13.refs_1_ = bf16[512,512]{1,0:T(8,128)(2,1)S(1)} collective-permute-done((bf16[512,512]{1,0:T(8,128)(2,1)S(1)}, bf16[512,512]{1,0:T(8,128)(2,1)S(1)}, u32[]{:S(2)}, u32[]{:S(2)}) %collective-permute-start.13) | collective-permute-done | bytes 524320 | tf_op jit(solution)/shard_map/ppermute | solution.py:852
  45.6 0.8 %total.1 = bf16[512,512]{1,0:T(8,128)(2,1)} custom-call(bf16[512,512]{1,0:T(8,128)(2,1)S(1)} %own_half.1.refs_0_, bf16[512,512]{1,0:T(8,128)(2,1)S(1)} %collective-permute-done.13.refs_1_), custom_call_target="tpu_custom_call" | custom-call | flops 880000000 | bytes 800000 | tf_op jit(solution)/shard_map/total/pallas_call | solution.py:48
  (34 shorter events, 3.8 us)
Async XLA Ops:
  0.0 15.2 %collective-permute-start.1 = (bf16[1024,1024]{1,0:T(8,128)(2,1)}, bf16[1024,1024]{1,0:T(8,128)(2,1)S(1)}, u32[]{:S(2)}, u32[]{:S(2)}) collective-permute-start(bf16[1024,1024]{1,0:T(8,128)(2,1)} %refs_5_.3), channel_id=1, source_target_pairs={{0,1},{1,0},{2,3},{3,2},{4,5},{5,4},{6,7},{7,6},{8,9},{9,8},{10,11... | collective-permute-start | bytes 6291464 | tf_op jit(solution)/shard_map/ppermute | solution.py:852
  0.5 28.5 %collective-permute-start.8 = (bf16[1024,1024]{1,0:T(8,128)(2,1)}, bf16[1024,1024]{1,0:T(8,128)(2,1)S(1)}, u32[]{:S(2)}, u32[]{:S(2)}) collective-permute-start(bf16[1024,1024]{1,0:T(8,128)(2,1)} %refs_1_.1), channel_id=1, source_target_pairs={{0,1},{1,0},{2,3},{3,2},{4,5},{5,4},{6,7},{7,6},{8,9},{9,8},{10,11... | collective-permute-start | bytes 6291464 | tf_op jit(solution)/shard_map/ppermute | solution.py:852
  0.5 5.7 %copy-start.4 = (bf16[1024,1024]{1,0:T(8,128)(2,1)S(1)}, bf16[1024,1024]{1,0:T(8,128)(2,1)}, u32[]{:S(2)}) copy-start(bf16[1024,1024]{1,0:T(8,128)(2,1)} %refs_8_.1) | copy-start | bytes 6291460
  0.5 6.2 %copy-start.3 = (bf16[1024,1024]{1,0:T(8,128)(2,1)S(1)}, bf16[1024,1024]{1,0:T(8,128)(2,1)}, u32[]{:S(2)}) copy-start(bf16[1024,1024]{1,0:T(8,128)(2,1)} %refs_1_.1) | copy-start | bytes 6291460
  3.2 5.0 %collective-permute-start = (bf16[16,1024]{1,0:T(8,128)(2,1)S(1)}, bf16[16,1024]{1,0:T(8,128)(2,1)S(1)}, u32[]{:S(2)}, u32[]{:S(2)}) collective-permute-start(bf16[16,1024]{1,0:T(8,128)(2,1)S(1)} %get-tuple-element.37), channel_id=1, source_target_pairs={{0,2},{1,0},{2,4},{3,1},{4,6},{5,3},{6,8},{7,5},{8,10},{9,7},{10,1... | collective-permute-start | bytes 98312 | tf_op jit(solution)/shard_map/ppermute | solution.py:597
  6.2 9.0 %collective-permute-start.2 = (f32[24,1024]{1,0:T(8,128)S(1)}, f32[24,1024]{1,0:T(8,128)S(1)}, u32[]{:S(2)}, u32[]{:S(2)}) collective-permute-start(f32[24,1024]{1,0:T(8,128)S(1)} %get-tuple-element.40.refs_6_.refs_7_), channel_id=1, source_target_pairs={{0,1},{1,0},{2,3},{3,2},{4,5},{5,4},{6,7},{7,6},{8,9},{9,8},{10,11... | collective-permute-start | bytes 294920 | tf_op jit(solution)/shard_map/ppermute | solution.py:852
  6.2 34.2 %collective-permute-start.11 = (bf16[1024,1024]{1,0:T(8,128)(2,1)S(1)}, bf16[1024,1024]{1,0:T(8,128)(2,1)S(1)}, u32[]{:S(2)}, u32[]{:S(2)}) collective-permute-start(bf16[1024,1024]{1,0:T(8,128)(2,1)S(1)} %copy-done.4), channel_id=1, source_target_pairs={{0,1},{1,0},{2,3},{3,2},{4,5},{5,4},{6,7},{7,6},{8,9},{9,8},{10,11... | collective-permute-start | bytes 6291464 | tf_op jit(solution)/shard_map/ppermute | solution.py:852
  6.8 1.5 %copy-start = (bf16[1024,256]{1,0:T(8,128)(2,1)S(1)}, bf16[1024,256]{1,0:T(8,128)(2,1)}, u32[]{:S(2)}) copy-start(bf16[1024,256]{1,0:T(8,128)(2,1)} %refs_3_.3) | copy-start | bytes 1572868
  6.8 1.5 %copy-start.1 = (f32[4,256]{1,0:T(4,128)S(1)}, f32[4,256]{1,0:T(4,128)}, u32[]{:S(2)}) copy-start(f32[4,256]{1,0:T(4,128)} %refs_4_.1) | copy-start | bytes 12292
  8.2 1.6 %copy-start.2 = (bf16[1024,1024]{1,0:T(8,128)(2,1)S(1)}, bf16[1024,1024]{1,0:T(8,128)(2,1)}, u32[]{:S(2)}) copy-start(bf16[1024,1024]{1,0:T(8,128)(2,1)} %refs_5_.3) | copy-start | bytes 6291460
  13.6 6.0 %collective-permute-start.3 = (bf16[144,512]{1,0:T(8,128)(2,1)S(1)}, bf16[144,512]{1,0:T(8,128)(2,1)S(1)}, u32[]{:S(2)}, u32[]{:S(2)}) collective-permute-start(bf16[144,512]{1,0:T(8,128)(2,1)S(1)} %get-tuple-element.46), channel_id=1, source_target_pairs={{0,2},{2,0},{4,6},{6,4},{8,10},{10,8},{12,14},{14,12},{1,3},{3,1},... | collective-permute-start | bytes 442376 | tf_op jit(solution)/shard_map/ppermute | solution.py:605
  19.0 6.0 %collective-permute-start.5 = (bf16[144,512]{1,0:T(8,128)(2,1)S(1)}, bf16[144,512]{1,0:T(8,128)(2,1)S(1)}, u32[]{:S(2)}, u32[]{:S(2)}) collective-permute-start(bf16[144,512]{1,0:T(8,128)(2,1)S(1)} %get-tuple-element.48), channel_id=1, source_target_pairs={{0,2},{2,0},{4,6},{6,4},{8,10},{10,8},{12,14},{14,12},{1,3},{3,1},... | collective-permute-start | bytes 442376 | tf_op jit(solution)/shard_map/ppermute | solution.py:605
  19.7 7.0 %collective-permute-start.4 = (bf16[144,512]{1,0:T(8,128)(2,1)S(1)}, bf16[144,512]{1,0:T(8,128)(2,1)S(1)}, u32[]{:S(2)}, u32[]{:S(2)}) collective-permute-start(bf16[144,512]{1,0:T(8,128)(2,1)S(1)} %pair_own.1.refs_5_.refs_1_), channel_id=1, source_target_pairs={{0,4},{1,0},{2,6},{3,2},{4,8},{5,1},{6,10},{7,3},{8,12},{9,5},{10,... | collective-permute-start | bytes 442376 | tf_op jit(solution)/shard_map/ppermute | solution.py:597
  25.1 5.3 %collective-permute-start.7 = (bf16[144,512]{1,0:T(8,128)(2,1)S(1)}, bf16[144,512]{1,0:T(8,128)(2,1)S(1)}, u32[]{:S(2)}, u32[]{:S(2)}) collective-permute-start(bf16[144,512]{1,0:T(8,128)(2,1)S(1)} %pair_other.1.refs_3_.refs_1_), channel_id=1, source_target_pairs={{0,4},{1,0},{2,6},{3,2},{4,8},{5,1},{6,10},{7,3},{8,12},{9,5},{10,... | collective-permute-start | bytes 442376 | tf_op jit(solution)/shard_map/ppermute | solution.py:597
  26.8 6.2 %collective-permute-start.6 = (bf16[144,512]{1,0:T(8,128)(2,1)S(1)}, bf16[144,512]{1,0:T(8,128)(2,1)S(1)}, u32[]{:S(2)}, u32[]{:S(2)}) collective-permute-start(bf16[144,512]{1,0:T(8,128)(2,1)S(1)} %chain_own.1.refs_2_), channel_id=1, source_target_pairs={{0,8},{1,0},{2,10},{3,2},{4,12},{5,4},{6,14},{7,6},{8,9},{9,1},{10... | collective-permute-start | bytes 442376 | tf_op jit(solution)/shard_map/ppermute | solution.py:597
  30.5 5.2 %collective-permute-start.9 = (bf16[144,512]{1,0:T(8,128)(2,1)S(1)}, bf16[144,512]{1,0:T(8,128)(2,1)S(1)}, u32[]{:S(2)}, u32[]{:S(2)}) collective-permute-start(bf16[144,512]{1,0:T(8,128)(2,1)S(1)} %chain_other.1.refs_5_), channel_id=1, source_target_pairs={{0,8},{1,0},{2,10},{3,2},{4,12},{5,4},{6,14},{7,6},{8,9},{9,1},{10... | collective-permute-start | bytes 442376 | tf_op jit(solution)/shard_map/ppermute | solution.py:597
  33.1 5.3 %collective-permute-start.12 = (bf16[128,512]{1,0:T(8,128)(2,1)S(1)}, bf16[128,512]{1,0:T(8,128)(2,1)S(1)}, u32[]{:S(2)}, u32[]{:S(2)}) collective-permute-start(bf16[128,512]{1,0:T(8,128)(2,1)S(1)} %get-tuple-element.57), channel_id=1, source_target_pairs={{0,2},{2,0},{4,6},{6,4},{8,10},{10,8},{12,14},{14,12},{1,3},{3,1},... | collective-permute-start | bytes 393224 | tf_op jit(solution)/shard_map/ppermute | solution.py:671
  35.8 5.6 %collective-permute-start.10 = (bf16[128,512]{1,0:T(8,128)(2,1)S(1)}, bf16[128,512]{1,0:T(8,128)(2,1)S(1)}, u32[]{:S(2)}, u32[]{:S(2)}) collective-permute-start(bf16[128,512]{1,0:T(8,128)(2,1)S(1)} %get-tuple-element.55), channel_id=1, source_target_pairs={{0,2},{2,0},{4,6},{6,4},{8,10},{10,8},{12,14},{14,12},{1,3},{3,1},... | collective-permute-start | bytes 393224 | tf_op jit(solution)/shard_map/ppermute | solution.py:671
  43.4 2.2 %collective-permute-start.13 = (bf16[512,512]{1,0:T(8,128)(2,1)S(1)}, bf16[512,512]{1,0:T(8,128)(2,1)S(1)}, u32[]{:S(2)}, u32[]{:S(2)}) collective-permute-start(bf16[512,512]{1,0:T(8,128)(2,1)S(1)} %get-tuple-element.62.refs_5_), channel_id=1, source_target_pairs={{0,1},{1,0},{2,3},{3,2},{4,5},{5,4},{6,7},{7,6},{8,9},{9,8},{10,11... | collective-permute-start | bytes 1572872 | tf_op jit(solution)/shard_map/ppermute | solution.py:852
